TPU v7x, 128 devices: a whole 4x4x4 slice. The times are simulated.
128 devices in a mesh: slab: 32 (over y_hi, x, z), sub: 4 (over y_lo, core).
Axes of the slice: x: 4, y: 4 (y_hi: 2, y_lo: 2; y = y_hi * 2 + y_lo), z: 4, core: 2. Of those that a mesh axis runs over, the one named last changes fastest.
Arguments:
- inputs: bfloat16 [64, 64, 64, 128], P('slab', 'sub'), may hold values from -6 to 6
- fine_cot: bfloat16 [64, 64, 64, 128], P('slab', 'sub'), may hold values from -6 to 6
- coarse_cot: bfloat16 [32, 32, 128, 64], P('slab', 'sub'), may hold values from -6 to 6
- weight_fine: bfloat16 [3, 3, 3, 64, 64], replicated, may hold values from -0.15625 to 0.15625
- weight_coarse: bfloat16 [3, 3, 3, 64, 128], replicated, may hold values from -0.15625 to 0.15625
Outputs:
- grad_input: bfloat16 [64, 64, 64, 128], P('slab', 'sub')
- grad_fine: float32 [3, 3, 3, 64, 64], replicated
- grad_coarse: float32 [3, 3, 3, 64, 128], replicated
All inputs are finite; a program needn't handle non-finite values.
Results may differ from a plain program's by a relative error of at most 0.014.
Values may be sent and summed in bfloat16 or wider, within the bound.
No kernel may reach another device: no remote copies, remote signals or barrier semaphores. Data moves between devices by JAX's collectives and lax.ppermute only.
A program may use at most 64 MiB of HBM per device.

v0:
```python
import jax
import jax.numpy as jnp
from jax import lax
from jax.sharding import PartitionSpec as P


def padded_2(block, sides, width):
    for axis, dim in sides:
        count = lax.axis_size(axis)
        forward = [(i, i + 1) for i in range(count - 1)]
        backward = [(target, source) for source, target in forward]
        low = lax.ppermute(
            lax.slice_in_dim(block, block.shape[dim] - width, None, axis=dim), axis, forward
        )
        high = lax.ppermute(lax.slice_in_dim(block, 0, width, axis=dim), axis, backward)
        block = jnp.concatenate([low, block, high], axis=dim)
    return block


def pad_depth(field):
    return jnp.pad(field, ((0, 0), (0, 0), (0, 0), (1, 1)))


def convolve(padded, weight, rows, cols, depth):
    total = jnp.zeros((rows, cols, weight.shape[4], depth), jnp.float32)
    for i in range(3):
        for j in range(3):
            for k in range(3):
                window = padded[i : i + rows, j : j + cols, :, k : k + depth]
                total = total + jnp.einsum(
                    "xycz,co->xyoz", window, weight[i, j, k], preferred_element_type=jnp.float32
                )
    return total


def correlate(padded, grad, rows, cols, depth):
    terms = []
    for i in range(3):
        for j in range(3):
            for k in range(3):
                window = padded[i : i + rows, j : j + cols, :, k : k + depth]
                terms.append(
                    jnp.einsum("xycz,xyoz->co", window, grad, preferred_element_type=jnp.float32)
                )
    return jnp.stack(terms).reshape((3, 3, 3, padded.shape[2], grad.shape[3 - 1]))


def transpose_kernel(weight):
    return jnp.swapaxes(jnp.flip(weight, (0, 1, 2)), 3, 4)


def gate_slope(value):
    sig = jax.nn.sigmoid(value)
    return sig * (1.0 + value * (1.0 - sig))


def on_device(inputs, fine_cot, coarse_cot, weight_fine, weight_coarse):
    rows, cols, chans, depth = inputs.shape
    half_rows, half_cols, half_depth = (rows // 2, cols // 2, depth // 2)
    devices = lax.axis_size("slab") * lax.axis_size("sub")
    padded_in = pad_depth(padded_2(inputs, (("slab", 0), ("sub", 1)), 1))
    pre_fine = convolve(padded_in, weight_fine, rows, cols, depth)
    act = jax.nn.silu(pre_fine).astype(jnp.bfloat16)
    blocks = act.astype(jnp.float32).reshape((half_rows, 2, half_cols, 2, chans, half_depth, 2))
    pooled = jnp.mean(blocks, axis=(1, 3, 6)).astype(jnp.bfloat16)
    padded_pool = padded_2(pooled, (("slab", 0), ("sub", 1)), 1)
    padded_pool = pad_depth(padded_pool)
    pre_coarse = convolve(padded_pool, weight_coarse, half_rows, half_cols, half_depth)
    grad_pc = (coarse_cot.astype(jnp.float32) * gate_slope(pre_coarse)).astype(jnp.bfloat16)
    coarse_cells = jnp.float32(half_rows * half_cols * half_depth * devices)
    coarse_part = correlate(padded_pool, grad_pc, half_rows, half_cols, half_depth) / jnp.sqrt(
        coarse_cells
    )
    grad_coarse = lax.psum(coarse_part, ("slab", "sub"))
    padded_gc = padded_2(grad_pc, (("slab", 0), ("sub", 1)), 1)
    grad_pooled = convolve(
        pad_depth(padded_gc), transpose_kernel(weight_coarse), half_rows, half_cols, half_depth
    )
    spread = jnp.broadcast_to(
        grad_pooled[:, None, :, None, :, :, None],
        (half_rows, 2, half_cols, 2, chans, half_depth, 2),
    )
    spread = spread.reshape((rows, cols, chans, depth)) * 0.125
    grad_pf = ((fine_cot.astype(jnp.float32) + spread) * gate_slope(pre_fine)).astype(jnp.bfloat16)
    fine_cells = jnp.float32(rows * cols * depth * devices)
    fine_part = correlate(padded_in, grad_pf, rows, cols, depth) / jnp.sqrt(fine_cells)
    padded_gf = pad_depth(padded_2(grad_pf, (("slab", 0), ("sub", 1)), 1))
    grad_input = convolve(padded_gf, transpose_kernel(weight_fine), rows, cols, depth).astype(
        jnp.bfloat16
    )
    grad_fine = lax.psum(fine_part, ("slab", "sub"))
    return (grad_input, grad_fine, grad_coarse)


def solution(mesh):
    in_specs = (
        P("slab", "sub", None, None),
        P("slab", "sub", None, None),
        P("slab", "sub", None, None),
        P(),
        P(),
    )
    out_specs = (P("slab", "sub", None, None), P(), P())
    return jax.shard_map(
        on_device, mesh=mesh, in_specs=in_specs, out_specs=out_specs, check_vma=False
    )
```

profile of v0, /device:TPU:1, one launch (start us, length us, event | category | flops | bytes accessed | tf_op | source)
XLA Modules:
  0.0 291.9 jit_solution(6520779247083145975)
XLA Ops:
  8.3 4.4 %collective-permute-start = (bf16[1,16,64,128]{3,2,1,0:T(8,128)(2,1)S(1)}, bf16[1,16,64,128]{3,2,1,0:T(8,128)(2,1)S(1)}, u32[]{:S(2)}, u32[]{:S(2)}) collective-permute-start(bf16[1,16,64,128]{3,2,1,0:T(8,128)(2,1)S(1)} %get-tuple-element.17), channel_id=1, source_target_pairs={{0,4},{4,8},{8,12},{12,16},{16,20},{20,24},{24,28},{28,32},{32,36}... | collective-permute-start | bytes 786440 | tf_op jit(solution)/shard_map/ppermute | solution.py:12
  18.2 3.6 %collective-permute-done.1 = bf16[1,16,64,128]{3,2,1,0:T(8,128)(2,1)S(1)} collective-permute-done((bf16[1,16,64,128]{3,2,1,0:T(8,128)(2,1)S(1)}, bf16[1,16,64,128]{3,2,1,0:T(8,128)(2,1)S(1)}, u32[]{:S(2)}, u32[]{:S(2)}) %collective-permute-start.1) | collective-permute-done | bytes 262176 | tf_op jit(solution)/shard_map/ppermute | solution.py:15
  22.0 4.8 %collective-permute-start.2 = (bf16[4,1,64,128]{3,2,1,0:T(8,128)(2,1)S(1)}, bf16[4,1,64,128]{3,2,1,0:T(8,128)(2,1)S(1)}, u32[]{:S(2)}, u32[]{:S(2)}) collective-permute-start(bf16[4,1,64,128]{3,2,1,0:T(8,128)(2,1)S(1)} %get-tuple-element.9), channel_id=1, source_target_pairs={{0,1},{1,2},{2,3},{4,5},{5,6},{6,7},{8,9},{9,10},{10,11},{12,13},{... | collective-permute-start | bytes 196616 | tf_op jit(solution)/shard_map/ppermute | solution.py:12
  26.8 1.9 collective-permute-start.3
  29.4 3.0 %collective-permute-done.3 = bf16[4,1,64,128]{3,2,1,0:T(8,128)(2,1)S(1)} collective-permute-done((bf16[4,1,64,128]{3,2,1,0:T(8,128)(2,1)S(1)}, bf16[4,1,64,128]{3,2,1,0:T(8,128)(2,1)S(1)}, u32[]{:S(2)}, u32[]{:S(2)}) %collective-permute-start.3) | collective-permute-done | bytes 65568 | tf_op jit(solution)/shard_map/ppermute | solution.py:15
  45.2 2.2 reduce_sum.18
  47.4 3.4 %collective-permute-start.4 = (bf16[1,8,64,64]{2,3,1,0:T(8,128)(2,1)S(1)}, bf16[1,8,64,64]{2,3,1,0:T(8,128)(2,1)S(1)}, u32[]{:S(2)}, u32[]{:S(2)}) collective-permute-start(bf16[1,8,64,64]{2,3,1,0:T(8,128)(2,1)S(1)} %fusion.474), channel_id=1, source_target_pairs={{0,4},{4,8},{8,12},{12,16},{16,20},{20,24},{24,28},{28,32},{32,36}... | collective-permute-start | bytes 196616 | tf_op jit(solution)/shard_map/ppermute | solution.py:12
  53.2 3.4 %collective-permute-done.5 = bf16[1,8,64,64]{2,3,1,0:T(8,128)(2,1)S(1)} collective-permute-done((bf16[1,8,64,64]{2,3,1,0:T(8,128)(2,1)S(1)}, bf16[1,8,64,64]{2,3,1,0:T(8,128)(2,1)S(1)}, u32[]{:S(2)}, u32[]{:S(2)}) %collective-permute-start.5) | collective-permute-done | bytes 65568 | tf_op jit(solution)/shard_map/ppermute | solution.py:15
  56.6 3.2 %collective-permute-start.6 = (bf16[3,1,64,64]{2,3,1,0:T(8,128)(2,1)S(1)}, bf16[3,1,64,64]{2,3,1,0:T(8,128)(2,1)S(1)}, u32[]{:S(2)}, u32[]{:S(2)}) collective-permute-start(bf16[3,1,64,64]{2,3,1,0:T(8,128)(2,1)S(1)} %get-tuple-element.26), channel_id=1, source_target_pairs={{0,1},{1,2},{2,3},{4,5},{5,6},{6,7},{8,9},{9,10},{10,11},{12,13},{... | collective-permute-start | bytes 73736 | tf_op jit(solution)/shard_map/ppermute | solution.py:12
  59.9 2.1 collective-permute-start.7
  62.2 3.1 %collective-permute-done.7 = bf16[3,1,64,64]{2,3,1,0:T(8,128)(2,1)S(1)} collective-permute-done((bf16[3,1,64,64]{2,3,1,0:T(8,128)(2,1)S(1)}, bf16[3,1,64,64]{2,3,1,0:T(8,128)(2,1)S(1)}, u32[]{:S(2)}, u32[]{:S(2)}) %collective-permute-start.7) | collective-permute-done | bytes 24608 | tf_op jit(solution)/shard_map/ppermute | solution.py:15
  70.5 3.6 %collective-permute-start.8 = (bf16[1,8,128,64]{2,3,1,0:T(8,128)(2,1)S(1)}, bf16[1,8,128,64]{2,3,1,0:T(8,128)(2,1)S(1)}, u32[]{:S(2)}, u32[]{:S(2)}) collective-permute-start(bf16[1,8,128,64]{2,3,1,0:T(8,128)(2,1)S(1)} %multiply_convert_fusion.2), channel_id=1, source_target_pairs={{0,4},{4,8},{8,12},{12,16},{16,20},{20,24},{24,28},{28,32},{32,36}... | collective-permute-start | bytes 393224 | tf_op jit(solution)/shard_map/ppermute | solution.py:12
  82.0 2.2 collective-permute-start.10
  84.2 2.1 collective-permute-start.11
  86.6 3.1 %collective-permute-done.11 = bf16[3,1,128,64]{2,3,1,0:T(8,128)(2,1)S(1)} collective-permute-done((bf16[3,1,128,64]{2,3,1,0:T(8,128)(2,1)S(1)}, bf16[3,1,128,64]{2,3,1,0:T(8,128)(2,1)S(1)}, u32[]{:S(2)}, u32[]{:S(2)}) %collective-permute-start.11) | collective-permute-done | bytes 49184 | tf_op jit(solution)/shard_map/ppermute | solution.py:15
  96.0 2.3 copy.148
  110.9 4.3 %collective-permute-start.12 = (bf16[1,16,64,128]{3,2,1,0:T(8,128)(2,1)S(1)}, bf16[1,16,64,128]{3,2,1,0:T(8,128)(2,1)S(1)}, u32[]{:S(2)}, u32[]{:S(2)}) collective-permute-start(bf16[1,16,64,128]{3,2,1,0:T(8,128)(2,1)S(1)} %get-tuple-element.11), channel_id=1, source_target_pairs={{0,4},{4,8},{8,12},{12,16},{16,20},{20,24},{24,28},{28,32},{32,36}... | collective-permute-start | bytes 786440 | tf_op jit(solution)/shard_map/ppermute | solution.py:12
  117.0 2.7 collective-permute-done.12
  119.7 4.2 %collective-permute-done.13 = bf16[1,16,64,128]{3,2,1,0:T(8,128)(2,1)S(1)} collective-permute-done((bf16[1,16,64,128]{3,2,1,0:T(8,128)(2,1)S(1)}, bf16[1,16,64,128]{3,2,1,0:T(8,128)(2,1)S(1)}, u32[]{:S(2)}, u32[]{:S(2)}) %collective-permute-start.13) | collective-permute-done | bytes 262176 | tf_op jit(solution)/shard_map/ppermute | solution.py:15
  125.8 2.4 collective-permute-start.15
  128.8 2.6 collective-permute-done.15
  132.2 2.2 select_maximum_fusion
  143.3 138.5 %all-reduce.7.cloned.1.call-done = (f32[3,3,3,64,64]{4,3,2,1,0:T(8,128)}, f32[3,3,3,64,128]{4,3,2,1,0:T(8,128)}) async-done(((f32[3,3,3,64,64]{4,3,2,1,0:T(8,128)}, f32[3,3,3,64,128]{4,3,2,1,0:T(8,128)}), (f32[3,3,3,64,64]{4,3,2,1,0:T(8,128)}, f32[3,3,3,64,128]{4,3,2,1,0:T(8,128)})) %all-reduce.7.cloned.1.call-update) | async-done | bytes 1327120 | tf_op jit(solution)/shard_map/psum | solution.py:91
  281.9 2.3 copy.371
  (225 shorter events, 68.9 us)
Async XLA Ops:
  7.2 10.6 %copy-start.2 = (bf16[2,16,64,128]{3,2,1,0:T(8,128)(2,1)S(1)}, bf16[2,16,64,128]{3,2,1,0:T(8,128)(2,1)}, u32[]{:S(2)}) copy-start(bf16[2,16,64,128]{3,2,1,0:T(8,128)(2,1)} %param.5) | copy-start | bytes 1572868
  7.2 274.7 %all-reduce.7.cloned.1.call-start = ((), (), s32[]{:S(2)}) async-start(), calls=%async_computation | async-start | bytes 3538944 | tf_op jit(solution)/shard_map/psum | solution.py:91
  8.3 9.3 %collective-permute-start = (bf16[1,16,64,128]{3,2,1,0:T(8,128)(2,1)S(1)}, bf16[1,16,64,128]{3,2,1,0:T(8,128)(2,1)S(1)}, u32[]{:S(2)}, u32[]{:S(2)}) collective-permute-start(bf16[1,16,64,128]{3,2,1,0:T(8,128)(2,1)S(1)} %get-tuple-element.17), channel_id=1, source_target_pairs={{0,4},{4,8},{8,12},{12,16},{16,20},{20,24},{24,28},{28,32},{32,36}... | collective-permute-start | bytes 786440 | tf_op jit(solution)/shard_map/ppermute | solution.py:12
  12.7 9.1 %collective-permute-start.1 = (bf16[1,16,64,128]{3,2,1,0:T(8,128)(2,1)S(1)}, bf16[1,16,64,128]{3,2,1,0:T(8,128)(2,1)S(1)}, u32[]{:S(2)}, u32[]{:S(2)}) collective-permute-start(bf16[1,16,64,128]{3,2,1,0:T(8,128)(2,1)S(1)} %get-tuple-element.16), channel_id=1, source_target_pairs={{4,0},{8,4},{12,8},{16,12},{20,16},{24,20},{28,24},{32,28},{36,32}... | collective-permute-start | bytes 786440 | tf_op jit(solution)/shard_map/ppermute | solution.py:15
  17.3 11.5 %copy-start.7 = (bf16[3,3,3,64,64]{4,3,2,1,0:T(8,128)(2,1)S(1)}, bf16[3,3,3,64,64]{4,3,2,1,0:T(8,128)(2,1)}, u32[]{:S(2)}) copy-start(bf16[3,3,3,64,64]{4,3,2,1,0:T(8,128)(2,1)} %param.8) | copy-start | bytes 663556
  18.2 10.8 %copy-start.5 = (bf16[3,16,64,128]{3,2,1,0:T(8,128)(2,1)}, bf16[3,16,64,128]{3,2,1,0:T(8,128)(2,1)S(1)}, u32[]{:S(2)}) copy-start(bf16[3,16,64,128]{3,2,1,0:T(8,128)(2,1)S(1)} %get-tuple-element.13) | copy-start | bytes 2359300
  22.0 12.0 %copy-start.3 = (bf16[3,16,64,128]{3,2,1,0:T(8,128)(2,1)}, bf16[3,16,64,128]{3,2,1,0:T(8,128)(2,1)S(1)}, u32[]{:S(2)}) copy-start(bf16[3,16,64,128]{3,2,1,0:T(8,128)(2,1)S(1)} %get-tuple-element.30) | copy-start | bytes 2359300
  22.0 7.4 %collective-permute-start.2 = (bf16[4,1,64,128]{3,2,1,0:T(8,128)(2,1)S(1)}, bf16[4,1,64,128]{3,2,1,0:T(8,128)(2,1)S(1)}, u32[]{:S(2)}, u32[]{:S(2)}) collective-permute-start(bf16[4,1,64,128]{3,2,1,0:T(8,128)(2,1)S(1)} %get-tuple-element.9), channel_id=1, source_target_pairs={{0,1},{1,2},{2,3},{4,5},{5,6},{6,7},{8,9},{9,10},{10,11},{12,13},{... | collective-permute-start | bytes 196616 | tf_op jit(solution)/shard_map/ppermute | solution.py:12
  26.8 5.6 %collective-permute-start.3 = (bf16[4,1,64,128]{3,2,1,0:T(8,128)(2,1)S(1)}, bf16[4,1,64,128]{3,2,1,0:T(8,128)(2,1)S(1)}, u32[]{:S(2)}, u32[]{:S(2)}) collective-permute-start(bf16[4,1,64,128]{3,2,1,0:T(8,128)(2,1)S(1)} %get-tuple-element.10), channel_id=1, source_target_pairs={{1,0},{2,1},{3,2},{5,4},{6,5},{7,6},{9,8},{10,9},{11,10},{13,12},{... | collective-permute-start | bytes 196616 | tf_op jit(solution)/shard_map/ppermute | solution.py:15
  34.0 8.8 %copy-start = (bf16[4,18,64,130]{3,2,1,0:T(8,128)(2,1)}, bf16[4,18,64,130]{3,2,1,0:T(8,128)(2,1)S(1)}, u32[]{:S(2)}) copy-start(bf16[4,18,64,130]{3,2,1,0:T(8,128)(2,1)S(1)} %fusion.8) | copy-start | bytes 3594244
  45.2 16.8 %copy-start.9 = (bf16[3,3,3,64,128]{4,3,2,1,0:T(8,128)(2,1)S(1)}, bf16[3,3,3,64,128]{4,3,2,1,0:T(8,128)(2,1)}, u32[]{:S(2)}) copy-start(bf16[3,3,3,64,128]{4,3,2,1,0:T(8,128)(2,1)} %param.9) | copy-start | bytes 1327108
  47.4 5.8 %collective-permute-start.4 = (bf16[1,8,64,64]{2,3,1,0:T(8,128)(2,1)S(1)}, bf16[1,8,64,64]{2,3,1,0:T(8,128)(2,1)S(1)}, u32[]{:S(2)}, u32[]{:S(2)}) collective-permute-start(bf16[1,8,64,64]{2,3,1,0:T(8,128)(2,1)S(1)} %fusion.474), channel_id=1, source_target_pairs={{0,4},{4,8},{8,12},{12,16},{16,20},{20,24},{24,28},{28,32},{32,36}... | collective-permute-start | bytes 196616 | tf_op jit(solution)/shard_map/ppermute | solution.py:12
  50.9 5.7 %collective-permute-start.5 = (bf16[1,8,64,64]{2,3,1,0:T(8,128)(2,1)S(1)}, bf16[1,8,64,64]{2,3,1,0:T(8,128)(2,1)S(1)}, u32[]{:S(2)}, u32[]{:S(2)}) collective-permute-start(bf16[1,8,64,64]{2,3,1,0:T(8,128)(2,1)S(1)} %fusion.474), channel_id=1, source_target_pairs={{4,0},{8,4},{12,8},{16,12},{20,16},{24,20},{28,24},{32,28},{36,32}... | collective-permute-start | bytes 196616 | tf_op jit(solution)/shard_map/ppermute | solution.py:15
  56.6 5.5 %collective-permute-start.6 = (bf16[3,1,64,64]{2,3,1,0:T(8,128)(2,1)S(1)}, bf16[3,1,64,64]{2,3,1,0:T(8,128)(2,1)S(1)}, u32[]{:S(2)}, u32[]{:S(2)}) collective-permute-start(bf16[3,1,64,64]{2,3,1,0:T(8,128)(2,1)S(1)} %get-tuple-element.26), channel_id=1, source_target_pairs={{0,1},{1,2},{2,3},{4,5},{5,6},{6,7},{8,9},{9,10},{10,11},{12,13},{... | collective-permute-start | bytes 73736 | tf_op jit(solution)/shard_map/ppermute | solution.py:12
  59.9 5.4 %collective-permute-start.7 = (bf16[3,1,64,64]{2,3,1,0:T(8,128)(2,1)S(1)}, bf16[3,1,64,64]{2,3,1,0:T(8,128)(2,1)S(1)}, u32[]{:S(2)}, u32[]{:S(2)}) collective-permute-start(bf16[3,1,64,64]{2,3,1,0:T(8,128)(2,1)S(1)} %get-tuple-element.27), channel_id=1, source_target_pairs={{1,0},{2,1},{3,2},{5,4},{6,5},{7,6},{9,8},{10,9},{11,10},{13,12},{... | collective-permute-start | bytes 73736 | tf_op jit(solution)/shard_map/ppermute | solution.py:15
  70.5 11.5 %collective-permute-start.8 = (bf16[1,8,128,64]{2,3,1,0:T(8,128)(2,1)S(1)}, bf16[1,8,128,64]{2,3,1,0:T(8,128)(2,1)S(1)}, u32[]{:S(2)}, u32[]{:S(2)}) collective-permute-start(bf16[1,8,128,64]{2,3,1,0:T(8,128)(2,1)S(1)} %multiply_convert_fusion.2), channel_id=1, source_target_pairs={{0,4},{4,8},{8,12},{12,16},{16,20},{20,24},{24,28},{28,32},{32,36}... | collective-permute-start | bytes 393224 | tf_op jit(solution)/shard_map/ppermute | solution.py:12
  74.2 7.8 %collective-permute-start.9 = (bf16[1,8,128,64]{2,3,1,0:T(8,128)(2,1)S(1)}, bf16[1,8,128,64]{2,3,1,0:T(8,128)(2,1)S(1)}, u32[]{:S(2)}, u32[]{:S(2)}) collective-permute-start(bf16[1,8,128,64]{2,3,1,0:T(8,128)(2,1)S(1)} %multiply_convert_fusion.2), channel_id=1, source_target_pairs={{4,0},{8,4},{12,8},{16,12},{20,16},{24,20},{28,24},{32,28},{36,32}... | collective-permute-start | bytes 393224 | tf_op jit(solution)/shard_map/ppermute | solution.py:15
  82.0 4.5 %collective-permute-start.10 = (bf16[3,1,128,64]{2,3,1,0:T(8,128)(2,1)S(1)}, bf16[3,1,128,64]{2,3,1,0:T(8,128)(2,1)S(1)}, u32[]{:S(2)}, u32[]{:S(2)}) collective-permute-start(bf16[3,1,128,64]{2,3,1,0:T(8,128)(2,1)S(1)} %get-tuple-element.24), channel_id=1, source_target_pairs={{0,1},{1,2},{2,3},{4,5},{5,6},{6,7},{8,9},{9,10},{10,11},{12,13},{... | collective-permute-start | bytes 147464 | tf_op jit(solution)/shard_map/ppermute | solution.py:12
  84.2 5.4 %collective-permute-start.11 = (bf16[3,1,128,64]{2,3,1,0:T(8,128)(2,1)S(1)}, bf16[3,1,128,64]{2,3,1,0:T(8,128)(2,1)S(1)}, u32[]{:S(2)}, u32[]{:S(2)}) collective-permute-start(bf16[3,1,128,64]{2,3,1,0:T(8,128)(2,1)S(1)} %get-tuple-element.25), channel_id=1, source_target_pairs={{1,0},{2,1},{3,2},{5,4},{6,5},{7,6},{9,8},{10,9},{11,10},{13,12},{... | collective-permute-start | bytes 147464 | tf_op jit(solution)/shard_map/ppermute | solution.py:15
  109.5 7.2 %copy-start.8 = (bf16[3,3,3,64,64]{3,4,2,1,0:T(8,128)(2,1)S(1)}, bf16[3,3,3,64,64]{3,4,2,1,0:T(8,128)(2,1)}, u32[]{:S(2)}) copy-start(bf16[3,3,3,64,64]{3,4,2,1,0:T(8,128)(2,1)} %reverse_bitcast_fusion) | copy-start | bytes 663556
  110.9 8.8 %collective-permute-start.12 = (bf16[1,16,64,128]{3,2,1,0:T(8,128)(2,1)S(1)}, bf16[1,16,64,128]{3,2,1,0:T(8,128)(2,1)S(1)}, u32[]{:S(2)}, u32[]{:S(2)}) collective-permute-start(bf16[1,16,64,128]{3,2,1,0:T(8,128)(2,1)S(1)} %get-tuple-element.11), channel_id=1, source_target_pairs={{0,4},{4,8},{8,12},{12,16},{16,20},{20,24},{24,28},{28,32},{32,36}... | collective-permute-start | bytes 786440 | tf_op jit(solution)/shard_map/ppermute | solution.py:12
  115.2 8.7 %collective-permute-start.13 = (bf16[1,16,64,128]{3,2,1,0:T(8,128)(2,1)S(1)}, bf16[1,16,64,128]{3,2,1,0:T(8,128)(2,1)S(1)}, u32[]{:S(2)}, u32[]{:S(2)}) collective-permute-start(bf16[1,16,64,128]{3,2,1,0:T(8,128)(2,1)S(1)} %get-tuple-element.12), channel_id=1, source_target_pairs={{4,0},{8,4},{12,8},{16,12},{20,16},{24,20},{28,24},{32,28},{36,32}... | collective-permute-start | bytes 786440 | tf_op jit(solution)/shard_map/ppermute | solution.py:15
  123.9 4.9 %collective-permute-start.14 = (bf16[4,1,64,128]{3,2,1,0:T(8,128)(2,1)S(1)}, bf16[4,1,64,128]{3,2,1,0:T(8,128)(2,1)S(1)}, u32[]{:S(2)}, u32[]{:S(2)}) collective-permute-start(bf16[4,1,64,128]{3,2,1,0:T(8,128)(2,1)S(1)} %get-tuple-element.7), channel_id=1, source_target_pairs={{0,1},{1,2},{2,3},{4,5},{5,6},{6,7},{8,9},{9,10},{10,11},{12,13},{... | collective-permute-start | bytes 196616 | tf_op jit(solution)/shard_map/ppermute | solution.py:12
  125.8 5.6 %collective-permute-start.15 = (bf16[4,1,64,128]{3,2,1,0:T(8,128)(2,1)S(1)}, bf16[4,1,64,128]{3,2,1,0:T(8,128)(2,1)S(1)}, u32[]{:S(2)}, u32[]{:S(2)}) collective-permute-start(bf16[4,1,64,128]{3,2,1,0:T(8,128)(2,1)S(1)} %get-tuple-element.8), channel_id=1, source_target_pairs={{1,0},{2,1},{3,2},{5,4},{6,5},{7,6},{9,8},{10,9},{11,10},{13,12},{... | collective-permute-start | bytes 196616 | tf_op jit(solution)/shard_map/ppermute | solution.py:15
  (5 other events, 7.8 us)
Sparse Core Ops, SparseCore 0:
  116.8 164.9 all-reduce.6
where the time goes:
time: 293 us; the launch traced here: 292 us
  waiting for transfers between devices  165 us (56%)
  matrix products  46.4 us (16%)
  starting transfers between devices  41.8 us (14%)
  between operations  15.4 us (5%)
  local copies, waits for them, and re-layouts  13.2 us (5%)
  other arithmetic  10.5 us (4%)
    psum x1, waiting for transfers between devices, on_device(): grad_fine = lax.psum(fine_part, ('slab', 'sub'))  139 us
    dot_general x108, matrix products, convolve(): jnp.einsum('xycz,co->xyoz', window, weight[i, j, k], preferred_element_ty...  31.3 us
    ppermute x8, starting transfers between devices, padded_2(): lax.ppermute(lax.slice_in_dim(block, block.shape[dim] - width, None, axis...  27.9 us
    ppermute x8, waiting for transfers between devices, padded_2(): lax.ppermute(lax.slice_in_dim(block, 0, width, axis=dim), axis, backward)  23 us
    dot_general x54, matrix products, correlate(): jnp.einsum('xycz,xyoz->co', window, grad, preferred_element_type=jnp.floa...  15.1 us
    ppermute x8, starting transfers between devices, padded_2(): lax.ppermute(lax.slice_in_dim(block, 0, width, axis=dim), axis, backward)  14 us
  transfers between devices with their start and end apart: 17, of which 10 were waited for; matrix products, arithmetic and copies ran while one was open for 9% of the time, Pallas kernels for 0%

commit v1 on v0

v1 whole, which is shorter than its diff:
```python
import functools

import jax
import jax.numpy as jnp
from jax import lax
from jax.experimental import pallas as pl
from jax.experimental.pallas import tpu as pltpu
from jax.sharding import PartitionSpec as P

L = 128
YH = 7
BF = jnp.bfloat16
F32 = jnp.float32
ROWS = 24
FINE_AT = 1728
VMEM = 56 * 1024 * 1024


def iota(shape, dim):
    return lax.broadcasted_iota(jnp.int32, shape, dim)


def shifted(tile, by, lane):
    out = pltpu.roll(tile, by % L, 1)
    keep = lane >= by if by > 0 else lane < L + by
    return jnp.where(keep, out, 0.0)


def combine(acc, rows, tiles, step, lane):
    out = []
    for t in range(tiles):
        part = acc[:, t * L : (t + 1) * L]
        out.append(
            shifted(part[:rows], step, lane)
            + part[rows : 2 * rows]
            + shifted(part[2 * rows :], -step, lane)
        )
    return out


def slopes(value):
    sig = jax.nn.sigmoid(value)
    return sig, sig * (1.0 + value * (1.0 - sig))


def dot(a, b):
    return jnp.dot(a, b, preferred_element_type=F32)


def spread_matrix():
    row, col = iota((L, 2 * L), 0), iota((L, 2 * L), 1)
    return jnp.where(row == (col // L) * 64 + (col % L) // 2, 1.0, 0.0).astype(BF)


def fine_kernel(flags, own, xlo, xhi, ylo, yhi, weight, v2, slope, pooled):
    f = [flags[i] > 0 for i in range(4)]
    ny = 16 + 2 * YH
    for x in range(4):
        ok = f[0] if x == 0 else f[1] if x == 3 else None
        for y in range(ny):
            if y < YH:
                tile, edge = ylo[x, y], f[2]
            elif y >= YH + 16:
                tile, edge = yhi[x, y - YH - 16], f[3]
            else:
                src = xlo[0] if x == 0 else xhi[0] if x == 3 else own[x - 1]
                tile, edge = src[y - YH], None
            for cond in (ok, edge):
                if cond is not None:
                    tile = jnp.where(cond, tile, jnp.zeros_like(tile))
            v2[x * 64 : (x + 1) * 64, y * L : (y + 1) * L] = tile
    lane = iota((128, L), 1)
    lane64 = iota((64, L), 1)
    row, col = iota((1024, L), 0), iota((1024, L), 1)
    pool = jnp.where(col == ((row // 256) % 2) * 64 + (row % L) // 2, 1.0, 0.0).astype(BF)
    for t in range(7):
        acc = None
        for j in range(3):
            term = dot(weight[j], v2[:, (4 * t + j) * L : (4 * t + j + 4) * L])
            acc = term if acc is None else acc + term
        acts = []
        for n, pre in enumerate(combine(acc, 128, 4, 1, lane)):
            sig, slp = slopes(pre)
            acts.append((pre * sig).astype(BF))
            at = 4 * t + n - 5
            if 0 <= at < 18:
                slope[:, at * L : (at + 1) * L] = slp
        cells = jnp.concatenate([a[:64] for a in acts] + [a[64:] for a in acts], axis=1)
        mean = dot(cells, pool) * 0.125
        yc = 2 * t + lane64 // 64
        keep = ((yc >= 3) | f[2]) & ((yc < 11) | f[3])
        pooled[:, t * L : (t + 1) * L] = jnp.where(keep, mean, 0.0).astype(BF)


def coarse_kernel(flags, own, lo, hi, cot_lo, cot, cot_hi, weight, p2, gpc, gpack):
    f = [flags[i] > 0 for i in range(4)]
    spread = spread_matrix()
    for t in range(7):
        at = slice(t * L, (t + 1) * L)
        zero = jnp.zeros((64, L), BF)
        rows = jnp.concatenate(
            [jnp.where(f[0], lo[:, at], zero), own[:, at], jnp.where(f[1], hi[:, at], zero)], axis=0
        )
        p2[:, 2 * t * L : (2 * t + 2) * L] = dot(rows, spread).astype(BF)
    lane = iota((128, L), 1)
    row, col = iota((2 * L, L), 0), iota((2 * L, L), 1)
    pack = jnp.where(
        (row % 2 == 0) & (col == (row // L) * 64 + (row % L) // 2), 1.0, 0.0
    ).astype(BF)
    for t in range(6):
        acc = None
        for j in range(3):
            term = dot(weight[j], p2[:, (2 * t + j) * L : (2 * t + j + 2) * L])
            acc = term if acc is None else acc + term
        if t == 0:
            cc = dot(cot_lo[...], spread)
        elif t == 5:
            cc = dot(cot_hi[...], spread)
        else:
            cc = jnp.concatenate(
                [dot(cot[2 * t - 2 + n], spread[:64, :L]) for n in range(2)], axis=1
            )
        out = []
        for n, pre in enumerate(combine(acc, 128, 2, 2, lane)):
            _, slp = slopes(pre)
            val = (cc[:, n * L : (n + 1) * L] * slp).astype(BF)
            if t == 0 or t == 5:
                val = jnp.where(f[2] if t == 0 else f[3], val, jnp.zeros_like(val))
            out.append(val)
        pair = jnp.concatenate(out, axis=1)
        gpc[:, 2 * t * L : (2 * t + 2) * L] = pair
        gpack[:, t * L : (t + 1) * L] = dot(pair, pack).astype(BF)


def nt(a, b):
    return lax.dot_general(a, b, (((1,), (1,)), ((), ())), preferred_element_type=F32)


def coarse_corr_kernel(scale, p2, gpc, out, g3):
    lane = iota((128, L), 1)
    for y in range(8):
        tile = gpc[:, (2 + y) * L : (3 + y) * L].astype(F32)
        at = slice(y * L, (y + 1) * L)
        g3[0:128, at] = shifted(tile, -2, lane).astype(BF)
        g3[128:256, at] = tile.astype(BF)
        g3[256:384, at] = shifted(tile, 2, lane).astype(BF)
    for j in range(3):
        res = nt(p2[:, (2 + j) * L : (10 + j) * L], g3[...]) * (0.5 * scale)
        for k in range(3):
            at = (3 * j + k) * 192
            out[at : at + 192, :] = res[:, k * L : (k + 1) * L].astype(BF)


def gpf_kernel(flags, own, lo, hi, weight, fc, fc_lo, fc_hi, slope, gpf, g2):
    f = [flags[i] > 0 for i in range(4)]
    spread = spread_matrix()
    zero = jnp.zeros((128, L), BF)
    for t in range(6):
        at = slice(t * L, (t + 1) * L)
        rows = jnp.concatenate(
            [jnp.where(f[0], lo[:, at], zero), own[:, at], jnp.where(f[1], hi[:, at], zero)], axis=0
        )
        g2[:, 2 * t * L : (2 * t + 2) * L] = dot(rows, spread).astype(BF)
    lane = iota((64, L), 1)
    for t in range(5):
        acc = None
        for j in range(3):
            term = dot(weight[j], g2[:, (2 * t + j) * L : (2 * t + j + 2) * L])
            acc = term if acc is None else acc + term
        for m, gp in enumerate(combine(acc, 64, 2, 2, lane)):
            m = 2 * t + m
            add = gp * 0.125
            for n in (2 * m - 1, 2 * m):
                if not 0 <= n < 18:
                    continue
                for x in range(2):
                    cot = fc_lo[x] if n == 0 else fc_hi[x] if n == 17 else fc[x, n - 1]
                    val = (cot.astype(F32) + add) * slope[x * 64 : (x + 1) * 64, n * L : (n + 1) * L]
                    if n == 0 or n == 17:
                        val = jnp.where(f[2] if n == 0 else f[3], val, 0.0)
                    gpf[x, n] = val.astype(BF)


def fine_corr_kernel(scale, v2, gpf, out, u3):
    lane = iota((64, L), 1)
    for y in range(16):
        at = slice(y * L, (y + 1) * L)
        for x in range(2):
            tile = gpf[x, y + 1].astype(F32)
            u3[x * 64 : x * 64 + 64, at] = shifted(tile, -1, lane).astype(BF)
            u3[128 + x * 64 : 192 + x * 64, at] = gpf[x, y + 1]
            u3[256 + x * 64 : 320 + x * 64, at] = shifted(tile, 1, lane).astype(BF)
    lane = iota((96, L), 1)
    for j in range(3):
        res = nt(v2[:, (YH - 1 + j) * L : (YH + 15 + j) * L], u3[...]) * scale
        for k in range(3):
            part = res[:, k * L : (k + 1) * L]
            both = part[:192] + pltpu.roll(part[64:], 64, 1)
            packed = jnp.where(lane < 64, both[:96], pltpu.roll(both[96:], 64, 1))
            at = (3 * j + k) * 96
            out[at : at + 96, :] = packed.astype(BF)


def input_grad_kernel(flags, own, lo, hi, weight, out, g2):
    f = [flags[i] > 0 for i in range(4)]
    for y in range(18):
        at = slice(y * L, (y + 1) * L)
        zero = jnp.zeros((64, L), BF)
        g2[0:64, at] = jnp.where(f[0], lo[0, y], zero)
        g2[64:128, at] = own[0, y]
        g2[128:192, at] = own[1, y]
        g2[192:256, at] = jnp.where(f[1], hi[0, y], zero)
    lane = iota((128, L), 1)
    for t in range(4):
        acc = None
        for j in range(3):
            term = dot(weight[j], g2[:, (4 * t + j) * L : (4 * t + j + 4) * L])
            acc = term if acc is None else acc + term
        for n, val in enumerate(combine(acc, 128, 4, 1, lane)):
            val = val.astype(BF)
            out[0, 4 * t + n] = val[:64]
            out[1, 4 * t + n] = val[64:]


def sum_kernel(parts, out):
    total = parts[0].astype(F32)
    for n in range(1, 128):
        total = total + parts[n].astype(F32)
    total = total.astype(BF)
    for n in range(128):
        out[n] = total


def unpack_kernel(got, fine, coarse):
    for j in range(3):
        for k in range(3):
            at = (3 * j + k) * 192
            for i in range(3):
                coarse[i, j, k] = got[at + i * 64 : at + (i + 1) * 64, :].astype(F32)
            at = FINE_AT + (3 * j + k) * 96
            tile = got[at : at + 96, :].astype(F32)
            fine[0, j, k] = tile[:64, :64]
            fine[1, j, k, :32] = tile[64:, :64]
            fine[1, j, k, 32:] = tile[:32, 64:]
            fine[2, j, k] = tile[32:, 64:]


def call(kernel, name, outs, args, scratch=(), flags=True, macs=0):
    specs = [pl.BlockSpec(memory_space=pltpu.VMEM) for _ in args]
    if flags:
        specs[0] = pl.BlockSpec(memory_space=pltpu.SMEM)
    moved = sum(a.size * a.dtype.itemsize for a in args)
    many = isinstance(outs[0][0], tuple)
    shapes = tuple(jax.ShapeDtypeStruct(*o) for o in (outs if many else (outs,)))
    return pl.pallas_call(
        kernel,
        out_shape=shapes if many else shapes[0],
        in_specs=specs,
        out_specs=tuple(pl.BlockSpec(memory_space=pltpu.VMEM) for _ in shapes)
        if many
        else pl.BlockSpec(memory_space=pltpu.VMEM),
        scratch_shapes=list(scratch),
        compiler_params=pltpu.CompilerParams(vmem_limit_bytes=VMEM),
        cost_estimate=pl.CostEstimate(flops=2 * macs, bytes_accessed=moved, transcendentals=0),
        name=name,
    )(*args)


def both_ways(low, high, axis):
    count = lax.axis_size(axis)
    ahead = [(i, (i + 1) % count) for i in range(count)]
    back = [(i, (i - 1) % count) for i in range(count)]
    return lax.ppermute(high, axis, ahead), lax.ppermute(low, axis, back)


def banded(weight):
    both = [jnp.pad(weight, ((x, 1 - x),) + ((0, 0),) * 4) for x in range(2)]
    full = jnp.stack(both)
    full = jnp.transpose(full, (2, 3, 0, 4, 1, 5))
    return full.reshape(3, 3 * 2 * weight.shape[3], 4 * weight.shape[4])


def stacked(weight):
    full = jnp.transpose(weight, (1, 2, 3, 0, 4))
    return full.reshape(3, 3 * weight.shape[3], 3 * weight.shape[4])


def on_device(inputs, fine_cot, coarse_cot, weight_fine, weight_coarse):
    slab, sub = lax.axis_index("slab"), lax.axis_index("sub")
    flags = jnp.stack([slab > 0, slab < 31, sub > 0, sub < 3]).astype(jnp.int32)
    w_fwd = banded(jnp.swapaxes(weight_fine, 3, 4))
    w_bwd = banded(jnp.flip(weight_fine, (0, 1, 2)))
    c_fwd = stacked(jnp.swapaxes(weight_coarse, 3, 4))
    c_bwd = stacked(jnp.flip(weight_coarse, (0, 1, 2)))

    xlo, xhi = both_ways(inputs[:1], inputs[1:], "slab")

    def edge(cols, n, cc):
        at = slice(0, cols) if n == 0 else slice(16 - cols, 16)
        one = slice(0, 1) if n == 0 else slice(15, 16)
        pieces = [a[:, at] for a in (xlo, inputs, xhi)] + [
            fine_cot[:, one].reshape(1, 2, 64, 128)
        ]
        pieces = [p.reshape(-1, 64, 128) for p in pieces]
        two = jnp.concatenate([coarse_cot[0, cc], coarse_cot[0, cc + 1]], axis=1)
        return jnp.concatenate(pieces + [two.reshape(2, 64, 128)], axis=0)

    got_lo, got_hi = both_ways(edge(YH, 0, 0), edge(YH, 1, 6), "sub")

    def parts(got):
        n = 4 * YH
        return got[:n].reshape(4, YH, 64, 128), got[n : n + 2], got[n + 2 :].reshape(128, 128)

    ylo, fc_lo, cc_lo = parts(got_lo)
    yhi, fc_hi, cc_hi = parts(got_hi)

    v2, slope, pooled = call(
        fine_kernel,
        "fine_forward",
        (((256, 30 * L), BF), ((128, 18 * L), F32), ((64, 7 * L), BF)),
        (flags, inputs, xlo, xhi, ylo, yhi, w_fwd),
        macs=384 * 256 * 3584 * 3,
    )
    plo, phi = both_ways(pooled, pooled, "slab")
    p2, gpc, gpack = call(
        coarse_kernel,
        "coarse_forward",
        (((192, 14 * L), BF), ((128, 12 * L), BF), ((128, 6 * L), BF)),
        (flags, pooled, plo, phi, cc_lo, coarse_cot[0], cc_hi, c_fwd),
        macs=384 * 192 * 1536 * 3,
    )
    glo, ghi = both_ways(gpack, gpack, "slab")
    coarse_part = call(
        functools.partial(coarse_corr_kernel, 1.0 / 256.0),
        "coarse_correlate",
        ((1728, L), BF),
        (p2, gpc),
        scratch=[pltpu.VMEM((384, 8 * L), BF)],
        flags=False,
        macs=384 * 192 * 1024 * 3,
    )
    gpf = call(
        gpf_kernel,
        "fine_gradient",
        ((2, 18, 64, L), BF),
        (flags, gpack, glo, ghi, c_bwd, fine_cot, fc_lo, fc_hi, slope),
        scratch=[pltpu.VMEM((384, 12 * L), BF)],
        macs=384 * 192 * 1280 * 3,
    )
    fine_part = call(
        functools.partial(fine_corr_kernel, 524288.0**-0.5),
        "fine_correlate",
        ((864, L), BF),
        (v2, gpf),
        scratch=[pltpu.VMEM((384, 16 * L), BF)],
        flags=False,
        macs=384 * 256 * 2048 * 3,
    )
    mine = jnp.concatenate(
        [coarse_part, fine_part, jnp.zeros((128 * ROWS - 2592, L), BF)], axis=0
    )
    shares = lax.all_to_all(mine, ("slab", "sub"), 0, 0, tiled=True)
    total = call(
        sum_kernel, "sum_shares", ((128, ROWS, L), BF), (shares.reshape(128, ROWS, L),), flags=False
    )
    hlo, hhi = both_ways(gpf[:1], gpf[1:], "slab")
    everything = lax.all_to_all(total.reshape(128 * ROWS, L), ("slab", "sub"), 0, 0, tiled=True)
    grad_fine, grad_coarse = call(
        unpack_kernel,
        "unpack",
        (((3, 3, 3, 64, 64), F32), ((3, 3, 3, 64, 128), F32)),
        (everything,),
        flags=False,
    )
    grad_input = call(
        input_grad_kernel,
        "input_gradient",
        ((2, 16, 64, L), BF),
        (flags, gpf, hlo, hhi, w_bwd),
        scratch=[pltpu.VMEM((256, 18 * L), BF)],
        macs=384 * 256 * 2048 * 3,
    )
    return (grad_input, grad_fine, grad_coarse)


def solution(mesh):
    in_specs = (
        P("slab", "sub", None, None),
        P("slab", "sub", None, None),
        P("slab", "sub", None, None),
        P(),
        P(),
    )
    out_specs = (P("slab", "sub", None, None), P(), P())
    return jax.shard_map(
        on_device, mesh=mesh, in_specs=in_specs, out_specs=out_specs, check_vma=False
    )
```

time: 293 us -> 151 us (0.52)
  waiting for transfers between devices: 165 us -> 20.9 us
  matrix products: 46.4 us -> 0 us
  Pallas kernels: 0 us -> 32.6 us
  blocking collectives: 0 us -> 26.3 us
  between operations: 15.4 us -> 0.83 us
  local copies, waits for them, and re-layouts: 13.2 us -> 27.4 us
  other arithmetic: 10.5 us -> 3.97 us
  starting transfers between devices: 41.8 us -> 38.5 us
    psum x1 -> x0, waiting for transfers between devices: 139 us -> none  [on_device(): grad_fine = lax.psum(fine_part, ('slab', 'sub'))]
    dot_general x162 -> x0, matrix products: 46.4 us -> none  [the longest x108 31.3 us: convolve(): jnp.einsum('xycz,co->xyoz', window, weight[i, j, k], preferred_element_ty...]
    pallas_call x0 -> x8, Pallas kernels: none -> 32.6 us  [call(): pl.pallas_call(kernel, out_shape=shapes if many else shapes[0], in_specs=...]
    all_to_all x0 -> x1, blocking collectives: none -> 26.3 us  [on_device(): shares = lax.all_to_all(mine, ('slab', 'sub'), 0, 0, tiled=True)]
    slice x3 -> x12, local copies, waits for them, and re-layouts: 1.16 us -> 9.62 us  [the longest x2 3.64 us: parts(): got[:n].reshape(4, YH, 64, 128)]
    ppermute x16 -> x10, starting transfers between devices: 41.8 us -> 33.7 us  [both_ways(): return (lax.ppermute(high, axis, ahead), lax.ppermute(low, axis, back))]
    reshape x0 -> x5, local copies, waits for them, and re-layouts: none -> 6.51 us  [the longest x3 3.41 us: stacked(): return full.reshape(3, 3 * weight.shape[3], 3 * weight.shape[4])]
    ppermute x16 -> x10, waiting for transfers between devices: 26.1 us -> 20.9 us  [both_ways(): return (lax.ppermute(high, axis, ahead), lax.ppermute(low, axis, back))]
  transfers between devices with their start and end apart: 17 -> 11, of which waited for: 10 -> 4; matrix products, arithmetic and copies ran while one was open for 9% -> 14% of each run, Pallas kernels for 0% -> 5%
where the time goes in v1:
time: 151 us
  starting transfers between devices  38.5 us (25%)
  Pallas kernels  32.6 us (22%)
  local copies, waits for them, and re-layouts  27.4 us (18%)
  blocking collectives  26.3 us (17%)
  waiting for transfers between devices  20.9 us (14%)
  other arithmetic  3.97 us (3%)
    ppermute x10, starting transfers between devices, both_ways(): return (lax.ppermute(high, axis, ahead), lax.ppermute(low, axis, back))  33.7 us
    pallas_call x8, Pallas kernels, call(): pl.pallas_call(kernel, out_shape=shapes if many else shapes[0], in_specs=...  32.6 us
    all_to_all x1, blocking collectives, on_device(): shares = lax.all_to_all(mine, ('slab', 'sub'), 0, 0, tiled=True)  26.3 us
    ppermute x10, waiting for transfers between devices, both_ways(): return (lax.ppermute(high, axis, ahead), lax.ppermute(low, axis, back))  20.9 us
    unnamed x35, local copies, waits for them, and re-layouts  8.37 us
    all_to_all x1, starting transfers between devices, on_device(): lax.all_to_all(total.reshape(128 * ROWS, L), ('slab', 'sub'), 0, 0, tiled...  4.88 us
    slice x2, local copies, waits for them, and re-layouts, parts(): got[:n].reshape(4, YH, 64, 128)  3.64 us
    reshape x3, local copies, waits for them, and re-layouts, stacked(): return full.reshape(3, 3 * weight.shape[3], 3 * weight.shape[4])  3.41 us
  transfers between devices with their start and end apart: 11, of which 4 were waited for; matrix products, arithmetic and copies ran while one was open for 14% of the time, Pallas kernels for 5%

profile of v1, /device:TPU:1, one launch (start us, length us, event | category | flops | bytes accessed | tf_op | source)
XLA Modules:
  0.0 150.6 jit_solution(7115749503521228049)
XLA Ops:
  1.8 2.5 %collective-permute-start = (bf16[1,16,64,128]{3,2,1,0:T(8,128)(2,1)S(1)}, bf16[1,16,64,128]{3,2,1,0:T(8,128)(2,1)S(1)}, u32[]{:S(2)}, u32[]{:S(2)}) collective-permute-start(bf16[1,16,64,128]{3,2,1,0:T(8,128)(2,1)S(1)} %get-tuple-element.30), channel_id=1, source_target_pairs={{0,4},{4,8},{8,12},{12,16},{16,20},{20,24},{24,28},{28,32},{32,36}... | collective-permute-start | bytes 786440 | tf_op jit(solution)/shard_map/ppermute | solution.py:273
  4.3 7.0 %collective-permute-start.1 = (bf16[1,16,64,128]{3,2,1,0:T(8,128)(2,1)S(1)}, bf16[1,16,64,128]{3,2,1,0:T(8,128)(2,1)S(1)}, u32[]{:S(2)}, u32[]{:S(2)}) collective-permute-start(bf16[1,16,64,128]{3,2,1,0:T(8,128)(2,1)S(1)} %get-tuple-element.29), channel_id=1, source_target_pairs={{0,124},{4,0},{8,4},{12,8},{16,12},{20,16},{24,20},{28,24},{32,28}... | collective-permute-start | bytes 786440 | tf_op jit(solution)/shard_map/ppermute | solution.py:273
  12.7 4.6 %collective-permute-done.xlo = bf16[1,16,64,128]{3,2,1,0:T(8,128)(2,1)S(1)} collective-permute-done((bf16[1,16,64,128]{3,2,1,0:T(8,128)(2,1)S(1)}, bf16[1,16,64,128]{3,2,1,0:T(8,128)(2,1)S(1)}, u32[]{:S(2)}, u32[]{:S(2)}) %collective-permute-start) | collective-permute-done | bytes 262176 | tf_op jit(solution)/shard_map/ppermute | solution.py:273
  26.5 1.6 %reshape.74.weight = bf16[3,384,256]{2,1,0:T(8,128)(2,1)} reshape(bf16[3,3,2,64,4,64]{5,4,3,2,1,0:T(4,128)(2,1)S(1)} %copy.25) | data formatting | bytes 1179648 | tf_op jit(solution)/shard_map/reshape | solution.py:280
  28.8 1.4 reshape.80.weight
  30.9 4.4 %collective-permute-done.3 = bf16[32,64,128]{2,1,0:T(8,128)(2,1)} collective-permute-done((bf16[32,64,128]{2,1,0:T(8,128)(2,1)}, bf16[32,64,128]{2,1,0:T(8,128)(2,1)}, u32[]{:S(2)}, u32[]{:S(2)}) %collective-permute-start.3) | collective-permute-done | bytes 524320 | tf_op jit(solution)/shard_map/ppermute | solution.py:273
  35.3 1.8 %slice.93 = bf16[28,64,128]{2,1,0:T(8,128)(2,1)} slice(bf16[32,64,128]{2,1,0:T(8,128)(2,1)} %collective-permute-done.3), slice={[0:28], [0:64], [0:128]} | slice | bytes 917504 | tf_op jit(solution)/shard_map/slice | solution.py:312
  37.1 1.8 %slice.90 = bf16[28,64,128]{2,1,0:T(8,128)(2,1)} slice(bf16[32,64,128]{2,1,0:T(8,128)(2,1)} %collective-permute-done.2), slice={[0:28], [0:64], [0:128]} | slice | bytes 917504 | tf_op jit(solution)/shard_map/slice | solution.py:312
  39.0 7.0 %fine_forward.1 = (bf16[256,3840]{1,0:T(8,128)(2,1)}, f32[128,2304]{1,0:T(8,128)}, bf16[64,896]{1,0:T(8,128)(2,1)}) custom-call(s32[4]{0:T(128)} %add_convert_fusion.flags, bf16[2,16,64,128]{3,2,1,0:T(8,128)(2,1)} %own.1, bf16[1,16,64,128]{3,2,1,0:T(8,128)(2,1)} %copy-done.7, bf16[1,16,64,128]{3,2,1,0:T(8,128)(2,1)} %copy-done.8, ...), custom_call_target="tpu_custom_call" | custom-call | flops 2113929216 | bytes 2555920 | tf_op jit(solution)/shard_map/fine_forward/pallas_call | solution.py:255
  46.0 7.2 %collective-permute-start.5 = (bf16[64,896]{1,0:T(8,128)(2,1)}, bf16[64,896]{1,0:T(8,128)(2,1)S(1)}, u32[]{:S(2)}, u32[]{:S(2)}) collective-permute-start(bf16[64,896]{1,0:T(8,128)(2,1)} %get-tuple-element.11.own), channel_id=1, source_target_pairs={{0,124},{4,0},{8,4},{12,8},{16,12},{20,16},{24,20},{28,24},{32,28}... | collective-permute-start | bytes 344072 | tf_op jit(solution)/shard_map/ppermute | solution.py:273
  57.5 5.6 %coarse_forward.1 = (bf16[192,1792]{1,0:T(8,128)(2,1)}, bf16[128,1536]{1,0:T(8,128)(2,1)}, bf16[128,768]{1,0:T(8,128)(2,1)}) custom-call(s32[4]{0:T(128)} %add_convert_fusion.flags, bf16[64,896]{1,0:T(8,128)(2,1)} %get-tuple-element.11.own, bf16[64,896]{1,0:T(8,128)(2,1)} %copy-done.13, bf16[64,896]{1,0:T(8,128)(2,1)} %copy-done.14, ...), custom_call_target="tpu_custom_call" | custom-call | flops 679477248 | bytes 983056 | tf_op jit(solution)/shard_map/coarse_forward/pallas_call | solution.py:255
  63.0 7.2 %collective-permute-start.7 = (bf16[128,768]{1,0:T(8,128)(2,1)}, bf16[128,768]{1,0:T(8,128)(2,1)S(1)}, u32[]{:S(2)}, u32[]{:S(2)}) collective-permute-start(bf16[128,768]{1,0:T(8,128)(2,1)} %get-tuple-element.12.own), channel_id=1, source_target_pairs={{0,124},{4,0},{8,4},{12,8},{16,12},{20,16},{24,20},{28,24},{32,28}... | collective-permute-start | bytes 589832 | tf_op jit(solution)/shard_map/ppermute | solution.py:273
  71.9 3.0 %coarse_correlate.1 = bf16[1728,128]{1,0:T(8,128)(2,1)} custom-call(bf16[192,1792]{1,0:T(8,128)(2,1)} %get-tuple-element.14.p2, bf16[128,1536]{1,0:T(8,128)(2,1)} %get-tuple-element.15.gpc), custom_call_target="tpu_custom_call" | custom-call | flops 452984832 | bytes 1081344 | tf_op jit(solution)/shard_map/coarse_correlate/pallas_call | solution.py:255
  75.6 4.1 %fine_gradient.1.own.gpf = bf16[2,18,64,128]{3,2,1,0:T(8,128)(2,1)} custom-call(s32[4]{0:T(128)} %add_convert_fusion.flags, bf16[128,768]{1,0:T(8,128)(2,1)} %get-tuple-element.12.own, bf16[128,768]{1,0:T(8,128)(2,1)} %copy-done.9, bf16[128,768]{1,0:T(8,128)(2,1)} %copy-done.10, bf16[3,192,384]{2,1,0:T(8,128)(2,1)} %reshape.78.weight, ...), custom_call_target="tpu_custom_call" | custom-call | flops 566231040 | bytes 2801680 | tf_op jit(solution)/shard_map/fine_gradient/pallas_call | solution.py:255
  79.8 4.5 %fine_correlate.1 = bf16[864,128]{1,0:T(8,128)(2,1)} custom-call(bf16[256,3840]{1,0:T(8,128)(2,1)} %get-tuple-element.16.v2, bf16[2,18,64,128]{3,2,1,0:T(8,128)(2,1)} %fine_gradient.1.own.gpf), custom_call_target="tpu_custom_call" | custom-call | flops 1207959552 | bytes 2555904 | tf_op jit(solution)/shard_map/fine_correlate/pallas_call | solution.py:255
  85.6 26.3 %all_to_all.17.parts = bf16[128,24,128]{2,1,0:T(8,128)(2,1)} all-to-all(bf16[128,24,128]{2,1,0:T(8,128)(2,1)S(1)} %bitcast.58), channel_id=1, replica_groups=mesh['slab'=32,'sub'=4] {'slab','sub'}, dimensions={0} | all-to-all | bytes 1572864 | tf_op jit(solution)/shard_map/all_to_all | solution.py:362
  112.0 2.2 %sum_shares.1 = bf16[128,24,128]{2,1,0:T(8,128)(2,1)} custom-call(bf16[128,24,128]{2,1,0:T(8,128)(2,1)} %all_to_all.17.parts), custom_call_target="tpu_custom_call" | custom-call | bytes 786432 | tf_op jit(solution)/shard_map/sum_shares/pallas_call | solution.py:255
  114.2 4.9 %all-to-all-start.1 = ((bf16[128,24,128]{2,1,0:T(8,128)(2,1)}), bf16[128,24,128]{2,1,0:T(8,128)(2,1)S(1)}, u32[]{:S(2)}, u32[]{:S(2)}) async-start(bf16[128,24,128]{2,1,0:T(8,128)(2,1)} %sum_shares.1), calls=%async_computation.1 | async-start | bytes 1572864 | tf_op jit(solution)/shard_map/all_to_all | solution.py:367
  119.8 1.5 %collective-permute-start.8 = (bf16[1,18,64,128]{3,2,1,0:T(8,128)(2,1)}, bf16[1,18,64,128]{3,2,1,0:T(8,128)(2,1)S(1)}, u32[]{:S(2)}, u32[]{:S(2)}) collective-permute-start(bf16[1,18,64,128]{3,2,1,0:T(8,128)(2,1)} %get-tuple-element.20), channel_id=1, source_target_pairs={{0,4},{4,8},{8,12},{12,16},{16,20},{20,24},{24,28},{28,32},{32,36}... | collective-permute-start | bytes 884744 | tf_op jit(solution)/shard_map/ppermute | solution.py:273
  121.3 6.5 %collective-permute-start.9 = (bf16[1,18,64,128]{3,2,1,0:T(8,128)(2,1)S(1)}, bf16[1,18,64,128]{3,2,1,0:T(8,128)(2,1)S(1)}, u32[]{:S(2)}, u32[]{:S(2)}) collective-permute-start(bf16[1,18,64,128]{3,2,1,0:T(8,128)(2,1)S(1)} %get-tuple-element.19), channel_id=1, source_target_pairs={{0,124},{4,0},{8,4},{12,8},{16,12},{20,16},{24,20},{28,24},{32,28}... | collective-permute-start | bytes 884744 | tf_op jit(solution)/shard_map/ppermute | solution.py:273
  129.4 1.6 %reshape.79.weight = bf16[3,384,256]{2,1,0:T(8,128)(2,1)} reshape(bf16[3,3,2,64,4,64]{5,4,3,2,1,0:T(4,128)(2,1)S(1)} %copy.30) | data formatting | bytes 1179648 | tf_op jit(solution)/shard_map/reshape | solution.py:280
  130.9 11.1 %collective-permute-done.8.lo = bf16[1,18,64,128]{3,2,1,0:T(8,128)(2,1)S(1)} collective-permute-done((bf16[1,18,64,128]{3,2,1,0:T(8,128)(2,1)}, bf16[1,18,64,128]{3,2,1,0:T(8,128)(2,1)S(1)}, u32[]{:S(2)}, u32[]{:S(2)}) %collective-permute-start.8) | collective-permute-done | bytes 294944 | tf_op jit(solution)/shard_map/ppermute | solution.py:273
  143.5 3.8 %input_gradient.1 = bf16[2,16,64,128]{3,2,1,0:T(8,128)(2,1)} custom-call(s32[4]{0:T(128)} %add_convert_fusion.flags, bf16[2,18,64,128]{3,2,1,0:T(8,128)(2,1)} %fine_gradient.1.own.gpf, bf16[1,18,64,128]{3,2,1,0:T(8,128)(2,1)} %copy-done.11, bf16[1,18,64,128]{3,2,1,0:T(8,128)(2,1)} %copy-done.12, bf16[3,384,256]{2,1,0:T(8,128)(2,1)} %reshape.79.weight), custom_call_target="tpu_custom_call" | custom-call | flops 1207959552 | bytes 1769488 | tf_op jit(solution)/shard_map/input_gradient/pallas_call | solution.py:255
  148.1 2.4 %unpack.1 = (f32[3,3,3,64,64]{4,3,2,1,0:T(8,128)}, f32[3,3,3,64,128]{4,3,2,1,0:T(8,128)}) custom-call(bf16[3072,128]{1,0:T(8,128)(2,1)} %bitcast.57), custom_call_target="tpu_custom_call" | custom-call | bytes 786432 | tf_op jit(solution)/shard_map/unpack/pallas_call | solution.py:255
  (74 shorter events, 25.8 us)
Async XLA Ops:
  0.6 12.0 %copy-start.2 = (bf16[2,16,64,128]{3,2,1,0:T(8,128)(2,1)S(1)}, bf16[2,16,64,128]{3,2,1,0:T(8,128)(2,1)}, u32[]{:S(2)}) copy-start(bf16[2,16,64,128]{3,2,1,0:T(8,128)(2,1)} %own.1) | copy-start | bytes 1572868
  1.8 15.5 %collective-permute-start = (bf16[1,16,64,128]{3,2,1,0:T(8,128)(2,1)S(1)}, bf16[1,16,64,128]{3,2,1,0:T(8,128)(2,1)S(1)}, u32[]{:S(2)}, u32[]{:S(2)}) collective-permute-start(bf16[1,16,64,128]{3,2,1,0:T(8,128)(2,1)S(1)} %get-tuple-element.30), channel_id=1, source_target_pairs={{0,4},{4,8},{8,12},{12,16},{16,20},{20,24},{24,28},{28,32},{32,36}... | collective-permute-start | bytes 786440 | tf_op jit(solution)/shard_map/ppermute | solution.py:273
  4.3 14.6 %collective-permute-start.1 = (bf16[1,16,64,128]{3,2,1,0:T(8,128)(2,1)S(1)}, bf16[1,16,64,128]{3,2,1,0:T(8,128)(2,1)S(1)}, u32[]{:S(2)}, u32[]{:S(2)}) collective-permute-start(bf16[1,16,64,128]{3,2,1,0:T(8,128)(2,1)S(1)} %get-tuple-element.29), channel_id=1, source_target_pairs={{0,124},{4,0},{8,4},{12,8},{16,12},{20,16},{24,20},{28,24},{32,28}... | collective-permute-start | bytes 786440 | tf_op jit(solution)/shard_map/ppermute | solution.py:273
  12.6 11.5 %copy-start.6 = (bf16[1,8,128,64]{2,3,1,0:T(8,128)(2,1)S(1)}, bf16[1,8,128,64]{2,3,1,0:T(8,128)(2,1)}, u32[]{:S(2)}) copy-start(bf16[1,8,128,64]{2,3,1,0:T(8,128)(2,1)} %param.7) | copy-start | bytes 393220
  17.3 7.7 %copy-start.7 = (bf16[1,16,64,128]{3,2,1,0:T(8,128)(2,1)}, bf16[1,16,64,128]{3,2,1,0:T(8,128)(2,1)S(1)}, u32[]{:S(2)}) copy-start(bf16[1,16,64,128]{3,2,1,0:T(8,128)(2,1)S(1)} %collective-permute-done.xlo) | copy-start | bytes 786436
  18.1 7.0 %copy-start.4 = (bf16[3,3,3,64,64]{4,3,2,1,0:T(8,128)(2,1)S(1)}, bf16[3,3,3,64,64]{4,3,2,1,0:T(8,128)(2,1)}, u32[]{:S(2)}) copy-start(bf16[3,3,3,64,64]{4,3,2,1,0:T(8,128)(2,1)} %param.8) | copy-start | bytes 663556
  18.9 6.4 %copy-start.8 = (bf16[1,16,64,128]{3,2,1,0:T(8,128)(2,1)}, bf16[1,16,64,128]{3,2,1,0:T(8,128)(2,1)S(1)}, u32[]{:S(2)}) copy-start(bf16[1,16,64,128]{3,2,1,0:T(8,128)(2,1)S(1)} %collective-permute-done.1.xhi) | copy-start | bytes 786436
  21.7 13.6 %collective-permute-start.3 = (bf16[32,64,128]{2,1,0:T(8,128)(2,1)}, bf16[32,64,128]{2,1,0:T(8,128)(2,1)}, u32[]{:S(2)}, u32[]{:S(2)}) collective-permute-start(bf16[32,64,128]{2,1,0:T(8,128)(2,1)} %maximum_dynamic-update-slice_fusion.1), channel_id=1, source_target_pairs={{0,3},{1,0},{2,1},{3,2},{4,7},{5,4},{6,5},{7,6},{8,11},{9,8},{10,9... | collective-permute-start | bytes 1572872 | tf_op jit(solution)/shard_map/ppermute | solution.py:273
  23.6 13.5 %collective-permute-start.2 = (bf16[32,64,128]{2,1,0:T(8,128)(2,1)}, bf16[32,64,128]{2,1,0:T(8,128)(2,1)}, u32[]{:S(2)}, u32[]{:S(2)}) collective-permute-start(bf16[32,64,128]{2,1,0:T(8,128)(2,1)} %maximum_dynamic-update-slice_fusion), channel_id=1, source_target_pairs={{0,1},{1,2},{2,3},{3,0},{4,5},{5,6},{6,7},{7,4},{8,9},{9,10},{10,1... | collective-permute-start | bytes 1572872 | tf_op jit(solution)/shard_map/ppermute | solution.py:273
  26.4 1.6 %copy-start.3 = (bf16[3,3,3,64,128]{4,3,2,1,0:T(8,128)(2,1)S(1)}, bf16[3,3,3,64,128]{4,3,2,1,0:T(8,128)(2,1)}, u32[]{:S(2)}) copy-start(bf16[3,3,3,64,128]{4,3,2,1,0:T(8,128)(2,1)} %param.9) | copy-start | bytes 1327108
  46.0 10.8 %collective-permute-start.4 = (bf16[64,896]{1,0:T(8,128)(2,1)}, bf16[64,896]{1,0:T(8,128)(2,1)S(1)}, u32[]{:S(2)}, u32[]{:S(2)}) collective-permute-start(bf16[64,896]{1,0:T(8,128)(2,1)} %get-tuple-element.11.own), channel_id=1, source_target_pairs={{0,4},{4,8},{8,12},{12,16},{16,20},{20,24},{24,28},{28,32},{32,36}... | collective-permute-start | bytes 344072 | tf_op jit(solution)/shard_map/ppermute | solution.py:273
  46.0 10.8 %collective-permute-start.5 = (bf16[64,896]{1,0:T(8,128)(2,1)}, bf16[64,896]{1,0:T(8,128)(2,1)S(1)}, u32[]{:S(2)}, u32[]{:S(2)}) collective-permute-start(bf16[64,896]{1,0:T(8,128)(2,1)} %get-tuple-element.11.own), channel_id=1, source_target_pairs={{0,124},{4,0},{8,4},{12,8},{16,12},{20,16},{24,20},{28,24},{32,28}... | collective-permute-start | bytes 344072 | tf_op jit(solution)/shard_map/ppermute | solution.py:273
  56.8 0.7 copy-start.14
  63.0 11.8 %collective-permute-start.6 = (bf16[128,768]{1,0:T(8,128)(2,1)}, bf16[128,768]{1,0:T(8,128)(2,1)S(1)}, u32[]{:S(2)}, u32[]{:S(2)}) collective-permute-start(bf16[128,768]{1,0:T(8,128)(2,1)} %get-tuple-element.12.own), channel_id=1, source_target_pairs={{0,4},{4,8},{8,12},{12,16},{16,20},{20,24},{24,28},{28,32},{32,36}... | collective-permute-start | bytes 589832 | tf_op jit(solution)/shard_map/ppermute | solution.py:273
  63.0 11.8 %collective-permute-start.7 = (bf16[128,768]{1,0:T(8,128)(2,1)}, bf16[128,768]{1,0:T(8,128)(2,1)S(1)}, u32[]{:S(2)}, u32[]{:S(2)}) collective-permute-start(bf16[128,768]{1,0:T(8,128)(2,1)} %get-tuple-element.12.own), channel_id=1, source_target_pairs={{0,124},{4,0},{8,4},{12,8},{16,12},{20,16},{24,20},{28,24},{32,28}... | collective-permute-start | bytes 589832 | tf_op jit(solution)/shard_map/ppermute | solution.py:273
  74.9 0.7 copy-start.10
  79.8 4.5 %copy-start.5 = (bf16[1728,128]{1,0:T(8,128)(2,1)S(1)}, bf16[1728,128]{1,0:T(8,128)(2,1)}, u32[]{:S(2)}) copy-start(bf16[1728,128]{1,0:T(8,128)(2,1)} %coarse_correlate.1) | copy-start | bytes 1327108
  114.2 4.9 %copy-start.1 = (bf16[2,18,64,128]{3,2,1,0:T(8,128)(2,1)S(1)}, bf16[2,18,64,128]{3,2,1,0:T(8,128)(2,1)}, u32[]{:S(2)}) copy-start(bf16[2,18,64,128]{3,2,1,0:T(8,128)(2,1)} %fine_gradient.1.own.gpf) | copy-start | bytes 1769476
  114.2 33.1 %all-to-all-start.1 = ((bf16[128,24,128]{2,1,0:T(8,128)(2,1)}), bf16[128,24,128]{2,1,0:T(8,128)(2,1)S(1)}, u32[]{:S(2)}, u32[]{:S(2)}) async-start(bf16[128,24,128]{2,1,0:T(8,128)(2,1)} %sum_shares.1), calls=%async_computation.1 | async-start | bytes 1572864 | tf_op jit(solution)/shard_map/all_to_all | solution.py:367
  119.8 22.2 %collective-permute-start.8 = (bf16[1,18,64,128]{3,2,1,0:T(8,128)(2,1)}, bf16[1,18,64,128]{3,2,1,0:T(8,128)(2,1)S(1)}, u32[]{:S(2)}, u32[]{:S(2)}) collective-permute-start(bf16[1,18,64,128]{3,2,1,0:T(8,128)(2,1)} %get-tuple-element.20), channel_id=1, source_target_pairs={{0,4},{4,8},{8,12},{12,16},{16,20},{20,24},{24,28},{28,32},{32,36}... | collective-permute-start | bytes 884744 | tf_op jit(solution)/shard_map/ppermute | solution.py:273
  121.3 20.7 %collective-permute-start.9 = (bf16[1,18,64,128]{3,2,1,0:T(8,128)(2,1)S(1)}, bf16[1,18,64,128]{3,2,1,0:T(8,128)(2,1)S(1)}, u32[]{:S(2)}, u32[]{:S(2)}) collective-permute-start(bf16[1,18,64,128]{3,2,1,0:T(8,128)(2,1)S(1)} %get-tuple-element.19), channel_id=1, source_target_pairs={{0,124},{4,0},{8,4},{12,8},{16,12},{20,16},{24,20},{28,24},{32,28}... | collective-permute-start | bytes 884744 | tf_op jit(solution)/shard_map/ppermute | solution.py:273
  142.0 0.7 copy-start.11
  142.7 0.7 copy-start.12
  147.3 0.9 copy-start
  (2 other events, 1.3 us)

commit v2 on v1

v2 whole, which is shorter than its diff:
```python
import functools

import jax
import jax.numpy as jnp
from jax import lax
from jax.experimental import pallas as pl
from jax.experimental.pallas import tpu as pltpu
from jax.sharding import PartitionSpec as P

L = 128
YH = 7
BF = jnp.bfloat16
F32 = jnp.float32
ROWS = 24
FINE_AT = 1728
VMEM = 20 * 1024 * 1024


def iota(shape, dim):
    return lax.broadcasted_iota(jnp.int32, shape, dim)


def shifted(tile, by, lane):
    out = pltpu.roll(tile, by % L, 1)
    keep = lane >= by if by > 0 else lane < L + by
    return jnp.where(keep, out, 0.0)


def combine(acc, rows, tiles, step, lane):
    out = []
    for t in range(tiles):
        part = acc[:, t * L : (t + 1) * L]
        out.append(
            shifted(part[:rows], step, lane)
            + part[rows : 2 * rows]
            + shifted(part[2 * rows :], -step, lane)
        )
    return out


def slopes(value):
    sig = jax.nn.sigmoid(value)
    return sig, sig * (1.0 + value * (1.0 - sig))


def dot(a, b):
    return jnp.dot(a, b, preferred_element_type=F32)


def spread_matrix():
    row, col = iota((L, 2 * L), 0), iota((L, 2 * L), 1)
    return jnp.where(row == (col // L) * 64 + (col % L) // 2, 1.0, 0.0).astype(BF)


def take(ok, tile):
    return tile if ok is None else jnp.where(ok, tile, jnp.zeros_like(tile))


def pool_matrix():
    row, col = iota((1024, L), 0), iota((1024, L), 1)
    return jnp.where(col == ((row // 256) % 2) * 64 + (row % L) // 2, 1.0, 0.0).astype(BF)


def taps(ref, at, tiles):
    return jnp.concatenate([ref[:, (at + j) * L : (at + j + tiles) * L] for j in range(3)], axis=0)


def forward_chunk(weight, window, at, lane, pool):
    acc = dot(weight[...], taps(window, at, 4))
    acts, slopes_ = [], []
    for pre in combine(acc, 128, 4, 1, lane):
        sig, slp = slopes(pre)
        acts.append((pre * sig).astype(BF))
        slopes_.append(slp)
    cells = jnp.concatenate([a[:64] for a in acts] + [a[64:] for a in acts], axis=1)
    return slopes_, dot(cells, pool) * 0.125


def prepare_kernel(wf, wc, wfwd, wbwd, cfwd, cbwd):
    def fine(i, j, k):
        return wf[i, j, k] if 0 <= i < 3 else jnp.zeros((64, 64), BF)

    for j in range(3):
        for k in range(3):
            for x in range(2):
                rows = slice(k * 128 + x * 64, k * 128 + x * 64 + 64)
                for h in range(2):
                    i = 2 * h - x
                    cols = slice(j * 256 + h * L, j * 256 + (h + 1) * L)
                    pair = jnp.concatenate([fine(i, j, k), fine(i + 1, j, k)], axis=0)
                    wfwd[rows, cols] = pair.astype(F32).T.astype(BF)
                    wbwd[rows, cols] = jnp.concatenate(
                        [fine(2 - i, 2 - j, 2 - k), fine(1 - i, 2 - j, 2 - k)], axis=1
                    )
    for k in range(3):
        full = jnp.concatenate([wc[i, j, k] for j in range(3) for i in range(3)], axis=0)
        cfwd[k * 128 : (k + 1) * 128, :] = full.astype(F32).T.astype(BF)
        for j in range(3):
            for i in range(3):
                at = (3 * j + i) * L
                cbwd[k * 64 : (k + 1) * 64, at : at + L] = wc[2 - i, 2 - j, 2 - k]


def start_and_wait(pairs, sems):
    copies = [pltpu.make_async_copy(a, b, sems.at[n]) for n, (a, b) in enumerate(pairs)]
    for c in copies:
        c.start()
    for c in copies:
        c.wait()


def own_edges_kernel(own, fc, cot, low, high, sems):
    pairs = []
    for out, y, one, cc in ((low, 0, 0, 0), (high, 16 - YH, 15, 6)):
        for x in range(2):
            pairs.append((own.at[x, y : y + YH], out.at[x * YH : (x + 1) * YH]))
            pairs.append((fc.at[x, one : one + 1], out.at[2 * YH + x : 2 * YH + x + 1]))
        pairs.append((cot.at[cc : cc + 2], out.at[2 * YH + 2 : 2 * YH + 4]))
    start_and_wait(pairs, sems)


def corner_edges_kernel(xlo, xhi, low, high, sems):
    pairs = []
    for out, y in ((low, 0), (high, 16 - YH)):
        pairs.append((xlo.at[0, y : y + YH], out.at[0:YH]))
        pairs.append((xhi.at[0, y : y + YH], out.at[YH : 2 * YH]))
    start_and_wait(pairs, sems)


def interior_kernel(flags, own, xlo, xhi, weight, v2, slope, pooled):
    f = [flags[i] > 0 for i in range(2)]
    for y in range(16):
        at = slice(y * L, (y + 1) * L)
        v2[0:64, at] = take(f[0], xlo[0, y])
        v2[64:128, at] = own[0, y]
        v2[128:192, at] = own[1, y]
        v2[192:256, at] = take(f[1], xhi[0, y])
    lane, pool = iota((128, L), 1), pool_matrix()
    for t in range(3):
        slps, mean = forward_chunk(weight, v2, 4 * t + 1, lane, pool)
        for n in range(4):
            slope[:, (4 * t + n) * L : (4 * t + n + 1) * L] = slps[n]
        pooled[:, t * L : (t + 1) * L] = mean.astype(BF)


def border_kernel(
    flags, v2, mid, alo, ahi, blo, bhi, weight, slope_lo, slope_hi, pooled, vedge, window
):
    f = [flags[i] > 0 for i in range(4)]
    lane, lane64, pool = iota((128, L), 1), iota((64, L), 1), pool_matrix()
    pooled[:, 2 * L : 5 * L] = mid[...]
    for side, (a, b, ok) in enumerate(((alo, blo, f[2]), (ahi, bhi, f[3]))):
        win = window.at[side]
        first = 0 if side == 0 else 3
        for y in range(YH):
            at = slice((first + y) * L, (first + y + 1) * L)
            win[0:64, at] = take(ok & f[0], b[y])
            win[64:128, at] = take(ok, a[y])
            win[128:192, at] = take(ok, a[YH + y])
            win[192:256, at] = take(ok & f[1], b[YH + y])
        if side == 0:
            win[:, YH * L :] = v2[:, : 3 * L]
            vedge[:, :L] = win[:, 6 * L : 7 * L]
        else:
            win[:, : 3 * L] = v2[:, 13 * L :]
            vedge[:, L:] = win[:, 3 * L : 4 * L]
        for u in range(2):
            slps, mean = forward_chunk(weight, win, 4 * u, lane, pool)
            if side == 0 and u == 1:
                for n in range(3):
                    slope_lo[:, n * L : (n + 1) * L] = slps[n + 1]
            if side == 1 and u == 0:
                for n in range(3):
                    slope_hi[:, n * L : (n + 1) * L] = slps[n]
            t = u if side == 0 else 5 + u
            yc = 2 * t + lane64 // 64
            keep = ((yc >= 3) | f[2]) & ((yc < 11) | f[3])
            pooled[:, t * L : (t + 1) * L] = jnp.where(keep, mean, 0.0).astype(BF)


def spread_rows(f, lo, own, hi, tiles, out):
    rows = []
    for t in range(tiles):
        at = slice(t * L, (t + 1) * L)
        rows += [take(f[0], lo[:, at]), own[:, at], take(f[1], hi[:, at])]
    full = dot(jnp.concatenate(rows, axis=0), spread_matrix()).astype(BF)
    n = full.shape[0] // tiles
    for t in range(tiles):
        out[:, 2 * t * L : (2 * t + 2) * L] = full[t * n : (t + 1) * n]


def coarse_kernel(flags, own, lo, hi, alo, cot, ahi, weight, p2, gpc, gpack):
    f = [flags[i] > 0 for i in range(4)]
    spread_rows(f, lo, own, hi, 7, p2)
    lane = iota((128, L), 1)
    row, col = iota((2 * L, L), 0), iota((2 * L, L), 1)
    pack = jnp.where(
        (row % 2 == 0) & (col == (row // L) * 64 + (row % L) // 2), 1.0, 0.0
    ).astype(BF)
    at = 2 * YH + 2
    tiles = (
        [take(f[2], alo[at + n]) for n in range(2)]
        + [cot[n] for n in range(8)]
        + [take(f[3], ahi[at + n]) for n in range(2)]
    )
    cc = lax.dot_general(
        jnp.concatenate(tiles, axis=1),
        spread_matrix()[:64, :L],
        (((0,), (0,)), ((), ())),
        preferred_element_type=F32,
    )
    acc = dot(weight[...], taps(p2, 0, 12))
    out = []
    for n, pre in enumerate(combine(acc, 128, 12, 2, lane)):
        _, slp = slopes(pre)
        out.append((cc[n * L : (n + 1) * L] * slp).astype(BF))
        gpc[:, n * L : (n + 1) * L] = out[n]
    pairs = jnp.concatenate(
        [jnp.concatenate(out[2 * t : 2 * t + 2], axis=1) for t in range(6)], axis=0
    )
    packed = dot(pairs, pack).astype(BF)
    for t in range(6):
        gpack[:, t * L : (t + 1) * L] = packed[t * L : (t + 1) * L]


def nt(a, b):
    return lax.dot_general(a, b, (((1,), (1,)), ((), ())), preferred_element_type=F32)


def coarse_corr_kernel(scale, p2, gpc, out, g3):
    lane = iota((128, L), 1)
    for y in range(8):
        tile = gpc[:, (2 + y) * L : (3 + y) * L].astype(F32)
        at = slice(y * L, (y + 1) * L)
        g3[0:128, at] = shifted(tile, -2, lane).astype(BF)
        g3[128:256, at] = tile.astype(BF)
        g3[256:384, at] = shifted(tile, 2, lane).astype(BF)
    res = nt(taps(p2, 2, 8), g3[...]) * (0.5 * scale)
    for j in range(3):
        for k in range(3):
            at = (3 * j + k) * 192
            out[at : at + 192, :] = res[j * 192 : (j + 1) * 192, k * L : (k + 1) * L].astype(BF)


def gpf_kernel(flags, own, lo, hi, weight, fc, alo, ahi, slope_lo, slope, slope_hi, row0, row1, g2):
    f = [flags[i] > 0 for i in range(4)]
    spread_rows(f, lo, own, hi, 6, g2)
    lane = iota((64, L), 1)
    acc = dot(weight[...], taps(g2, 0, 10))
    for m, gp in enumerate(combine(acc, 64, 10, 2, lane)):
        add = gp * 0.125
        for n in (2 * m - 1, 2 * m):
            if not 0 <= n < 18:
                continue
            if n < 3:
                slp = slope_lo[:, n * L : (n + 1) * L]
            elif n < 15:
                slp = slope[:, (n - 3) * L : (n - 2) * L]
            else:
                slp = slope_hi[:, (n - 15) * L : (n - 14) * L]
            for x, out in enumerate((row0, row1)):
                edge = 2 * YH + x
                cot = alo[edge] if n == 0 else ahi[edge] if n == 17 else fc[x, n - 1]
                val = (cot.astype(F32) + add) * slp[x * 64 : (x + 1) * 64]
                if n == 0 or n == 17:
                    val = take(f[2] if n == 0 else f[3], val)
                out[n] = val.astype(BF)


def fine_corr_kernel(scale, v2, vedge, row0, row1, coarse, out, u3):
    lane = iota((64, L), 1)
    for y in range(16):
        at = slice(y * L, (y + 1) * L)
        for x, row in enumerate((row0, row1)):
            tile = row[y + 1].astype(F32)
            u3[x * 64 : x * 64 + 64, at] = shifted(tile, -1, lane).astype(BF)
            u3[128 + x * 64 : 192 + x * 64, at] = row[y + 1]
            u3[256 + x * 64 : 320 + x * 64, at] = shifted(tile, 1, lane).astype(BF)
    lane = iota((96, L), 1)
    lhs = jnp.concatenate(
        [
            jnp.concatenate([vedge[:, :L], v2[:, : 15 * L]], axis=1),
            v2[...],
            jnp.concatenate([v2[:, L:], vedge[:, L:]], axis=1),
        ],
        axis=0,
    )
    res = nt(lhs, u3[...]) * scale
    out[:FINE_AT, :] = coarse[...]
    out[2592:, :] = jnp.zeros((128 * ROWS - 2592, L), BF)
    for j in range(3):
        for k in range(3):
            part = res[j * 256 : (j + 1) * 256, k * L : (k + 1) * L]
            both = part[:192] + pltpu.roll(part[64:], 64, 1)
            packed = jnp.where(lane < 64, both[:96], pltpu.roll(both[96:], 64, 1))
            at = FINE_AT + (3 * j + k) * 96
            out[at : at + 96, :] = packed.astype(BF)


def input_grad_kernel(flags, row0, row1, lo, hi, weight, out, g2):
    f = [flags[i] > 0 for i in range(4)]
    for y in range(18):
        at = slice(y * L, (y + 1) * L)
        g2[0:64, at] = take(f[0], lo[y])
        g2[64:128, at] = row0[y]
        g2[128:192, at] = row1[y]
        g2[192:256, at] = take(f[1], hi[y])
    lane = iota((128, L), 1)
    for t in range(4):
        acc = dot(weight[...], taps(g2, 4 * t, 4))
        for n, val in enumerate(combine(acc, 128, 4, 1, lane)):
            val = val.astype(BF)
            out[0, 4 * t + n] = val[:64]
            out[1, 4 * t + n] = val[64:]


def sum_kernel(parts, out):
    total = parts[0].astype(F32)
    for n in range(1, 128):
        total = total + parts[n].astype(F32)
    total = total.astype(BF)
    for n in range(128):
        out[n] = total


def unpack_kernel(got, fine, coarse):
    for j in range(3):
        for k in range(3):
            at = (3 * j + k) * 192
            for i in range(3):
                coarse[i, j, k] = got[at + i * 64 : at + (i + 1) * 64, :].astype(F32)
            at = FINE_AT + (3 * j + k) * 96
            tile = got[at : at + 96, :].astype(F32)
            fine[0, j, k] = tile[:64, :64]
            fine[1, j, k, :32] = tile[64:, :64]
            fine[1, j, k, 32:] = tile[:32, 64:]
            fine[2, j, k] = tile[32:, 64:]


def call(kernel, name, outs, args, scratch=(), flags=True, macs=0, copies=0):
    space = pl.ANY if copies else pltpu.VMEM
    specs = [pl.BlockSpec(memory_space=space) for _ in args]
    if flags:
        specs[0] = pl.BlockSpec(memory_space=pltpu.SMEM)
    moved = sum(a.size * a.dtype.itemsize for a in args)
    shapes = tuple(jax.ShapeDtypeStruct(*o) for o in outs)
    if copies:
        scratch = [pltpu.SemaphoreType.DMA((copies,))]
    got = pl.pallas_call(
        kernel,
        out_shape=shapes,
        in_specs=specs,
        out_specs=tuple(pl.BlockSpec(memory_space=space) for _ in shapes),
        scratch_shapes=list(scratch),
        compiler_params=pltpu.CompilerParams(vmem_limit_bytes=VMEM),
        cost_estimate=pl.CostEstimate(flops=2 * macs, bytes_accessed=moved, transcendentals=0),
        name=name,
    )(*args)
    return got if len(shapes) > 1 else got[0]


def both_ways(low, high, axis):
    count = lax.axis_size(axis)
    ahead = [(i, (i + 1) % count) for i in range(count)]
    back = [(i, (i - 1) % count) for i in range(count)]
    return lax.ppermute(high, axis, ahead), lax.ppermute(low, axis, back)


def on_device(inputs, fine_cot, coarse_cot, weight_fine, weight_coarse):
    slab, sub = lax.axis_index("slab"), lax.axis_index("sub")
    flags = jnp.stack([slab > 0, slab < 31, sub > 0, sub < 3]).astype(jnp.int32)
    cot = jnp.swapaxes(coarse_cot[0], 1, 2)

    xlo, xhi = both_ways(inputs[:1], inputs[1:], "slab")
    own_edge = ((2 * YH + 4, 64, L), BF)
    low, high = call(
        own_edges_kernel,
        "own_edges",
        (own_edge, own_edge),
        (inputs, fine_cot, cot),
        flags=False,
        copies=10,
    )
    alo, ahi = both_ways(low, high, "sub")
    w_fwd, w_bwd, c_fwd, c_bwd = call(
        prepare_kernel,
        "prepare_weights",
        (((384, 768), BF), ((384, 768), BF), ((384, 576), BF), ((192, 1152), BF)),
        (weight_fine, weight_coarse),
        flags=False,
    )
    corner = ((2 * YH, 64, L), BF)
    low, high = call(
        corner_edges_kernel, "corner_edges", (corner, corner), (xlo, xhi), flags=False, copies=4
    )
    blo, bhi = both_ways(low, high, "sub")
    v2, slope, mid = call(
        interior_kernel,
        "fine_forward_interior",
        (((256, 16 * L), BF), ((128, 12 * L), F32), ((64, 3 * L), BF)),
        (flags, inputs, xlo, xhi, w_fwd),
        macs=384 * 768 * 12 * L,
    )
    slope_lo, slope_hi, pooled, vedge = call(
        border_kernel,
        "fine_forward_border",
        (((128, 3 * L), F32), ((128, 3 * L), F32), ((64, 7 * L), BF), ((256, 2 * L), BF)),
        (flags, v2, mid, alo, ahi, blo, bhi, w_fwd),
        scratch=[pltpu.VMEM((2, 256, 10 * L), BF)],
        macs=384 * 768 * 16 * L,
    )
    plo, phi = both_ways(pooled, pooled, "slab")
    p2, gpc, gpack = call(
        coarse_kernel,
        "coarse_forward",
        (((192, 14 * L), BF), ((128, 12 * L), BF), ((128, 6 * L), BF)),
        (flags, pooled, plo, phi, alo, cot, ahi, c_fwd),
        macs=384 * 576 * 12 * L,
    )
    glo, ghi = both_ways(gpack, gpack, "slab")
    coarse_part = call(
        functools.partial(coarse_corr_kernel, 1.0 / 256.0),
        "coarse_correlate",
        (((FINE_AT, L), BF),),
        (p2, gpc),
        scratch=[pltpu.VMEM((384, 8 * L), BF)],
        flags=False,
        macs=384 * 576 * 8 * L,
    )
    row0, row1 = call(
        gpf_kernel,
        "fine_gradient",
        (((18, 64, L), BF), ((18, 64, L), BF)),
        (flags, gpack, glo, ghi, c_bwd, fine_cot, alo, ahi, slope_lo, slope, slope_hi),
        scratch=[pltpu.VMEM((384, 12 * L), BF)],
        macs=192 * 1152 * 10 * L,
    )
    hlo, hhi = both_ways(row0, row1, "slab")
    mine = call(
        functools.partial(fine_corr_kernel, 524288.0**-0.5),
        "fine_correlate",
        (((128 * ROWS, L), BF),),
        (v2, vedge, row0, row1, coarse_part),
        scratch=[pltpu.VMEM((384, 16 * L), BF)],
        flags=False,
        macs=384 * 768 * 16 * L,
    )
    shares = lax.all_to_all(mine, ("slab", "sub"), 0, 0, tiled=True)
    grad_input = call(
        input_grad_kernel,
        "input_gradient",
        (((2, 16, 64, L), BF),),
        (flags, row0, row1, hlo, hhi, w_bwd),
        scratch=[pltpu.VMEM((256, 18 * L), BF)],
        macs=384 * 768 * 16 * L,
    )
    shares, grad_input = lax.optimization_barrier((shares, grad_input))
    total = call(
        sum_kernel,
        "sum_shares",
        (((128, ROWS, L), BF),),
        (shares.reshape(128, ROWS, L),),
        flags=False,
    )
    everything = lax.all_to_all(total.reshape(128 * ROWS, L), ("slab", "sub"), 0, 0, tiled=True)
    grad_fine, grad_coarse = call(
        unpack_kernel,
        "unpack",
        (((3, 3, 3, 64, 64), F32), ((3, 3, 3, 64, 128), F32)),
        (everything,),
        flags=False,
    )
    return (grad_input, grad_fine, grad_coarse)


def solution(mesh):
    in_specs = (
        P("slab", "sub", None, None),
        P("slab", "sub", None, None),
        P("slab", "sub", None, None),
        P(),
        P(),
    )
    out_specs = (P("slab", "sub", None, None), P(), P())
    return jax.shard_map(
        on_device, mesh=mesh, in_specs=in_specs, out_specs=out_specs, check_vma=False
    )
```

time: 151 us -> 122 us (0.81)
  waiting for transfers between devices: 20.9 us -> 46.9 us
  local copies, waits for them, and re-layouts: 27.4 us -> 2.88 us
  Pallas kernels: 32.6 us -> 21.7 us
  starting transfers between devices: 38.5 us -> 29.4 us
  blocking collectives: 26.3 us -> 19.9 us
  other arithmetic: 3.97 us -> 0.08 us
    ppermute x10 -> x12, waiting for transfers between devices: 20.9 us -> 46.9 us  [both_ways(): return (lax.ppermute(high, axis, ahead), lax.ppermute(low, axis, back))]
    pallas_call x8 -> x12, Pallas kernels: 32.6 us -> 21.7 us  [call(): pl.pallas_call(kernel, out_shape=shapes, in_specs=specs, out_specs=tuple(...]
    ppermute x10 -> x12, starting transfers between devices: 33.7 us -> 24.3 us  [both_ways(): return (lax.ppermute(high, axis, ahead), lax.ppermute(low, axis, back))]
    slice x11 -> x0, local copies, waits for them, and re-layouts: 8.5 us -> none  [the longest x2 3.64 us: parts(): got[:n].reshape(4, YH, 64, 128)]
    unnamed x35 -> x16, local copies, waits for them, and re-layouts: 8.37 us -> 1.73 us
    reshape x5 -> x0, local copies, waits for them, and re-layouts: 6.51 us -> none  [the longest x3 3.41 us: stacked(): return full.reshape(3, 3 * weight.shape[3], 3 * weight.shape[4])]
    all_to_all x1, blocking collectives: 26.3 us -> 19.9 us  [on_device(): lax.all_to_all(total.reshape(128 * ROWS, L), ('slab', 'sub'), 0, 0, tiled...]
    concatenate x3 -> x0, other arithmetic: 2.79 us -> none  [the longest x1 1.4 us: on_device(): jnp.concatenate([coarse_part, fine_part, jnp.zeros((128 * ROWS - 2592, L)...]
  transfers between devices with their start and end apart: 11 -> 13, of which waited for: 4 -> 9; matrix products, arithmetic and copies ran while one was open for 14% -> 0% of each run, Pallas kernels for 5% -> 7%
where the time goes in v2:
time: 122 us
  waiting for transfers between devices  46.9 us (38%)
  starting transfers between devices  29.4 us (24%)
  Pallas kernels  21.7 us (18%)
  blocking collectives  19.9 us (16%)
  local copies, waits for them, and re-layouts  2.88 us (2%)
    ppermute x12, waiting for transfers between devices, both_ways(): return (lax.ppermute(high, axis, ahead), lax.ppermute(low, axis, back))  46.9 us
    ppermute x12, starting transfers between devices, both_ways(): return (lax.ppermute(high, axis, ahead), lax.ppermute(low, axis, back))  24.3 us
    pallas_call x12, Pallas kernels, call(): pl.pallas_call(kernel, out_shape=shapes, in_specs=specs, out_specs=tuple(...  21.7 us
    all_to_all x1, blocking collectives, on_device(): lax.all_to_all(total.reshape(128 * ROWS, L), ('slab', 'sub'), 0, 0, tiled...  19.9 us
    all_to_all x1, starting transfers between devices, on_device(): shares = lax.all_to_all(mine, ('slab', 'sub'), 0, 0, tiled=True)  5.04 us
  transfers between devices with their start and end apart: 13, of which 9 were waited for; matrix products, arithmetic and copies ran while one was open for 0% of the time, Pallas kernels for 7%

profile of v2, /device:TPU:1, one launch (start us, length us, event | category | flops | bytes accessed | tf_op | source)
XLA Modules:
  0.0 121.7 jit_solution(2307681551557965516)
XLA Ops:
  1.8 9.5 %collective-permute-start.1 = (bf16[1,16,64,128]{3,2,1,0:T(8,128)(2,1)S(1)}, bf16[1,16,64,128]{3,2,1,0:T(8,128)(2,1)S(1)}, u32[]{:S(2)}, u32[]{:S(2)}) collective-permute-start(bf16[1,16,64,128]{3,2,1,0:T(8,128)(2,1)S(1)} %get-tuple-element.51), channel_id=1, source_target_pairs={{0,124},{4,0},{8,4},{12,8},{16,12},{20,16},{24,20},{28,24},{32,28}... | collective-permute-start | bytes 786440 | tf_op jit(solution)/shard_map/ppermute | solution.py:366
  13.4 1.3 %collective-permute-start.2 = (bf16[18,64,128]{2,1,0:T(8,128)(2,1)}, bf16[18,64,128]{2,1,0:T(8,128)(2,1)S(1)}, u32[]{:S(2)}, u32[]{:S(2)}) collective-permute-start(bf16[18,64,128]{2,1,0:T(8,128)(2,1)} %get-tuple-element.30), channel_id=1, source_target_pairs={{0,1},{1,2},{2,3},{3,0},{4,5},{5,6},{6,7},{7,4},{8,9},{9,10},{10,1... | collective-permute-start | bytes 884744 | tf_op jit(solution)/shard_map/ppermute | solution.py:366
  14.7 1.6 %collective-permute-done.1.xhi = bf16[1,16,64,128]{3,2,1,0:T(8,128)(2,1)S(1)} collective-permute-done((bf16[1,16,64,128]{3,2,1,0:T(8,128)(2,1)S(1)}, bf16[1,16,64,128]{3,2,1,0:T(8,128)(2,1)S(1)}, u32[]{:S(2)}, u32[]{:S(2)}) %collective-permute-start.1) | collective-permute-done | bytes 262176 | tf_op jit(solution)/shard_map/ppermute | solution.py:366
  16.3 7.6 %collective-permute-done.xlo = bf16[1,16,64,128]{3,2,1,0:T(8,128)(2,1)S(1)} collective-permute-done((bf16[1,16,64,128]{3,2,1,0:T(8,128)(2,1)S(1)}, bf16[1,16,64,128]{3,2,1,0:T(8,128)(2,1)S(1)}, u32[]{:S(2)}, u32[]{:S(2)}) %collective-permute-start) | collective-permute-done | bytes 262176 | tf_op jit(solution)/shard_map/ppermute | solution.py:366
  24.7 2.3 %collective-permute-start.4 = (bf16[14,64,128]{2,1,0:T(8,128)(2,1)}, bf16[14,64,128]{2,1,0:T(8,128)(2,1)}, u32[]{:S(2)}, u32[]{:S(2)}) collective-permute-start(bf16[14,64,128]{2,1,0:T(8,128)(2,1)} %get-tuple-element.32), channel_id=1, source_target_pairs={{0,1},{1,2},{2,3},{3,0},{4,5},{5,6},{6,7},{7,4},{8,9},{9,10},{10,1... | collective-permute-start | bytes 688136 | tf_op jit(solution)/shard_map/ppermute | solution.py:366
  28.6 2.6 %fine_forward_interior.1 = (bf16[256,2048]{1,0:T(8,128)(2,1)S(1)}, f32[128,1536]{1,0:T(8,128)S(1)}, bf16[64,384]{1,0:T(8,128)(2,1)S(1)}) custom-call(s32[4]{0:T(128)S(1)} %add_convert_fusion.flags, bf16[2,16,64,128]{3,2,1,0:T(8,128)(2,1)S(1)} %copy-done, bf16[1,16,64,128]{3,2,1,0:T(8,128)(2,1)S(1)} %collective-permute-done.xlo, ...), custom_call_target="tpu_custom_call" | custom-call | flops 905969664 | bytes 1638416 | tf_op jit(solution)/shard_map/fine_forward_interior/pallas_call | solution.py:349
  31.2 3.0 %collective-permute-done.5.bhi = bf16[14,64,128]{2,1,0:T(8,128)(2,1)} collective-permute-done((bf16[14,64,128]{2,1,0:T(8,128)(2,1)}, bf16[14,64,128]{2,1,0:T(8,128)(2,1)}, u32[]{:S(2)}, u32[]{:S(2)}) %collective-permute-start.5) | collective-permute-done | bytes 229408 | tf_op jit(solution)/shard_map/ppermute | solution.py:366
  34.2 3.7 %fine_forward_border.1 = (f32[128,384]{1,0:T(8,128)S(1)}, f32[128,384]{1,0:T(8,128)S(1)}, bf16[64,896]{1,0:T(8,128)(2,1)S(1)}, bf16[256,256]{1,0:T(8,128)(2,1)S(1)}) custom-call(s32[4]{0:T(128)S(1)} %add_convert_fusion.flags, bf16[256,2048]{1,0:T(8,128)(2,1)S(1)} %get-tuple-element.28.v2, bf16[64,384]{1,0:T(8,128)(2,1)S(1)} %get-tuple-element.29.mid, ...), custom_call_target="tpu_custom_call" | custom-call | flops 1207959552 | bytes 2736144 | tf_op jit(solution)/shard_map/fine_forward_border/pallas_call | solution.py:349
  37.9 1.5 %collective-permute-start.7 = (bf16[64,896]{1,0:T(8,128)(2,1)S(1)}, bf16[64,896]{1,0:T(8,128)(2,1)S(1)}, u32[]{:S(2)}, u32[]{:S(2)}) collective-permute-start(bf16[64,896]{1,0:T(8,128)(2,1)S(1)} %get-tuple-element.35.own), channel_id=1, source_target_pairs={{0,124},{4,0},{8,4},{12,8},{16,12},{20,16},{24,20},{28,24},{32,28}... | collective-permute-start | bytes 344072 | tf_op jit(solution)/shard_map/ppermute | solution.py:366
  39.4 3.5 %collective-permute-done.7.hi = bf16[64,896]{1,0:T(8,128)(2,1)S(1)} collective-permute-done((bf16[64,896]{1,0:T(8,128)(2,1)S(1)}, bf16[64,896]{1,0:T(8,128)(2,1)S(1)}, u32[]{:S(2)}, u32[]{:S(2)}) %collective-permute-start.7) | collective-permute-done | bytes 114720 | tf_op jit(solution)/shard_map/ppermute | solution.py:366
  42.9 7.2 %collective-permute-done.6.lo = bf16[64,896]{1,0:T(8,128)(2,1)S(1)} collective-permute-done((bf16[64,896]{1,0:T(8,128)(2,1)S(1)}, bf16[64,896]{1,0:T(8,128)(2,1)S(1)}, u32[]{:S(2)}, u32[]{:S(2)}) %collective-permute-start.6) | collective-permute-done | bytes 114720 | tf_op jit(solution)/shard_map/ppermute | solution.py:366
  50.1 2.2 %coarse_forward.1 = (bf16[192,1792]{1,0:T(8,128)(2,1)S(1)}, bf16[128,1536]{1,0:T(8,128)(2,1)S(1)}, bf16[128,768]{1,0:T(8,128)(2,1)S(1)}) custom-call(s32[4]{0:T(128)S(1)} %add_convert_fusion.flags, bf16[64,896]{1,0:T(8,128)(2,1)S(1)} %get-tuple-element.35.own, bf16[64,896]{1,0:T(8,128)(2,1)S(1)} %collective-permute-done.6.lo, ...), custom_call_target="tpu_custom_call" | custom-call | flops 679477248 | bytes 1507344 | tf_op jit(solution)/shard_map/coarse_forward/pallas_call | solution.py:349
  52.5 1.3 %collective-permute-start.8 = (bf16[128,768]{1,0:T(8,128)(2,1)S(1)}, bf16[128,768]{1,0:T(8,128)(2,1)S(1)}, u32[]{:S(2)}, u32[]{:S(2)}) collective-permute-start(bf16[128,768]{1,0:T(8,128)(2,1)S(1)} %get-tuple-element.37.own), channel_id=1, source_target_pairs={{0,4},{4,8},{8,12},{12,16},{16,20},{20,24},{24,28},{28,32},{32,36}... | collective-permute-start | bytes 589832 | tf_op jit(solution)/shard_map/ppermute | solution.py:366
  54.8 3.4 %collective-permute-done.9.hi = bf16[128,768]{1,0:T(8,128)(2,1)S(1)} collective-permute-done((bf16[128,768]{1,0:T(8,128)(2,1)S(1)}, bf16[128,768]{1,0:T(8,128)(2,1)S(1)}, u32[]{:S(2)}, u32[]{:S(2)}) %collective-permute-start.9) | collective-permute-done | bytes 196640 | tf_op jit(solution)/shard_map/ppermute | solution.py:366
  58.2 6.0 %collective-permute-done.8.lo = bf16[128,768]{1,0:T(8,128)(2,1)S(1)} collective-permute-done((bf16[128,768]{1,0:T(8,128)(2,1)S(1)}, bf16[128,768]{1,0:T(8,128)(2,1)S(1)}, u32[]{:S(2)}, u32[]{:S(2)}) %collective-permute-start.8) | collective-permute-done | bytes 196640 | tf_op jit(solution)/shard_map/ppermute | solution.py:366
  64.2 2.1 %fine_gradient.1 = (bf16[18,64,128]{2,1,0:T(8,128)(2,1)S(1)}, bf16[18,64,128]{2,1,0:T(8,128)(2,1)S(1)}) custom-call(s32[4]{0:T(128)S(1)} %add_convert_fusion.flags, bf16[128,768]{1,0:T(8,128)(2,1)S(1)} %get-tuple-element.37.own, bf16[128,768]{1,0:T(8,128)(2,1)S(1)} %collective-permute-done.8.lo, bf16[128,768]{1,0:T(8,128)(2,1)S(1)} %collective-permute-done.9.hi, ...), custom_call_target="tpu_custom_call" | custom-call | flops 566231040 | bytes 3325968 | tf_op jit(solution)/shard_map/fine_gradient/pallas_call | solution.py:349
  66.3 3.2 %fine_correlate.1 = bf16[3072,128]{1,0:T(8,128)(2,1)} custom-call(bf16[256,2048]{1,0:T(8,128)(2,1)S(1)} %get-tuple-element.28.v2, bf16[256,256]{1,0:T(8,128)(2,1)S(1)} %get-tuple-element.34.vedge, bf16[18,64,128]{2,1,0:T(8,128)(2,1)S(1)} %get-tuple-element.42.row0, bf16[18,64,128]{2,1,0:T(8,128)(2,1)S(1)} %get-tuple-element.43.row1, ...), custom_call_target="tpu_custom_call" | custom-call | flops 1207959552 | bytes 2211840 | tf_op jit(solution)/shard_map/fine_correlate/pallas_call | solution.py:349
  69.5 5.0 %all-to-all-start = ((bf16[128,24,128]{2,1,0:T(8,128)(2,1)}), bf16[128,24,128]{2,1,0:T(8,128)(2,1)S(1)}, u32[]{:S(2)}, u32[]{:S(2)}) async-start(bf16[128,24,128]{2,1,0:T(8,128)(2,1)} %bitcast.7), calls=%async_computation | async-start | bytes 1572864 | tf_op jit(solution)/shard_map/all_to_all | solution.py:448
  74.6 8.2 %collective-permute-start.11 = (bf16[18,64,128]{2,1,0:T(8,128)(2,1)S(1)}, bf16[18,64,128]{2,1,0:T(8,128)(2,1)S(1)}, u32[]{:S(2)}, u32[]{:S(2)}) collective-permute-start(bf16[18,64,128]{2,1,0:T(8,128)(2,1)S(1)} %get-tuple-element.42.row0), channel_id=1, source_target_pairs={{0,124},{4,0},{8,4},{12,8},{16,12},{20,16},{24,20},{28,24},{32,28}... | collective-permute-start | bytes 884744 | tf_op jit(solution)/shard_map/ppermute | solution.py:366
  82.7 8.7 %collective-permute-done.11.hi = bf16[18,64,128]{2,1,0:T(8,128)(2,1)S(1)} collective-permute-done((bf16[18,64,128]{2,1,0:T(8,128)(2,1)S(1)}, bf16[18,64,128]{2,1,0:T(8,128)(2,1)S(1)}, u32[]{:S(2)}, u32[]{:S(2)}) %collective-permute-start.11) | collective-permute-done | bytes 294944 | tf_op jit(solution)/shard_map/ppermute | solution.py:366
  91.4 6.0 %collective-permute-done.10.lo = bf16[18,64,128]{2,1,0:T(8,128)(2,1)S(1)} collective-permute-done((bf16[18,64,128]{2,1,0:T(8,128)(2,1)S(1)}, bf16[18,64,128]{2,1,0:T(8,128)(2,1)S(1)}, u32[]{:S(2)}, u32[]{:S(2)}) %collective-permute-start.10) | collective-permute-done | bytes 294944 | tf_op jit(solution)/shard_map/ppermute | solution.py:366
  97.4 2.9 %input_gradient.1 = bf16[2,16,64,128]{3,2,1,0:T(8,128)(2,1)} custom-call(s32[4]{0:T(128)S(1)} %add_convert_fusion.flags, bf16[18,64,128]{2,1,0:T(8,128)(2,1)S(1)} %get-tuple-element.42.row0, bf16[18,64,128]{2,1,0:T(8,128)(2,1)S(1)} %get-tuple-element.43.row1, bf16[18,64,128]{2,1,0:T(8,128)(2,1)S(1)} %collective-permute-done.10.lo, ...), custom_call_target="tpu_custom_call" | custom-call | flops 1207959552 | bytes 1769488 | tf_op jit(solution)/shard_map/input_gradient/pallas_call | solution.py:349
  100.5 19.9 %all_to_all.20 = bf16[128,24,128]{2,1,0:T(8,128)(2,1)S(1)} all-to-all(bf16[128,24,128]{2,1,0:T(8,128)(2,1)S(1)} %sum_shares.1), channel_id=1, replica_groups=mesh['slab'=32,'sub'=4] {'slab','sub'}, dimensions={0} | all-to-all | bytes 1572864 | tf_op jit(solution)/shard_map/all_to_all | solution.py:465
  120.4 1.3 %unpack.1 = (f32[3,3,3,64,64]{4,3,2,1,0:T(8,128)}, f32[3,3,3,64,128]{4,3,2,1,0:T(8,128)}) custom-call(bf16[3072,128]{1,0:T(8,128)(2,1)S(1)} %bitcast.11), custom_call_target="tpu_custom_call" | custom-call | bytes 786432 | tf_op jit(solution)/shard_map/unpack/pallas_call | solution.py:349
  (33 shorter events, 6.9 us)
Async XLA Ops:
  0.6 10.7 %copy-start = (bf16[2,16,64,128]{3,2,1,0:T(8,128)(2,1)S(1)}, bf16[2,16,64,128]{3,2,1,0:T(8,128)(2,1)}, u32[]{:S(2)}) copy-start(bf16[2,16,64,128]{3,2,1,0:T(8,128)(2,1)} %own.3) | copy-start | bytes 1572868
  0.6 10.7 %copy-start.1 = (bf16[2,16,64,128]{3,2,1,0:T(8,128)(2,1)S(1)}, bf16[2,16,64,128]{3,2,1,0:T(8,128)(2,1)}, u32[]{:S(2)}) copy-start(bf16[2,16,64,128]{3,2,1,0:T(8,128)(2,1)} %fc.3) | copy-start | bytes 1572868
  1.8 14.5 %collective-permute-start.1 = (bf16[1,16,64,128]{3,2,1,0:T(8,128)(2,1)S(1)}, bf16[1,16,64,128]{3,2,1,0:T(8,128)(2,1)S(1)}, u32[]{:S(2)}, u32[]{:S(2)}) collective-permute-start(bf16[1,16,64,128]{3,2,1,0:T(8,128)(2,1)S(1)} %get-tuple-element.51), channel_id=1, source_target_pairs={{0,124},{4,0},{8,4},{12,8},{16,12},{20,16},{24,20},{28,24},{32,28}... | collective-permute-start | bytes 786440 | tf_op jit(solution)/shard_map/ppermute | solution.py:366
  11.3 12.6 %collective-permute-start = (bf16[1,16,64,128]{3,2,1,0:T(8,128)(2,1)S(1)}, bf16[1,16,64,128]{3,2,1,0:T(8,128)(2,1)S(1)}, u32[]{:S(2)}, u32[]{:S(2)}) collective-permute-start(bf16[1,16,64,128]{3,2,1,0:T(8,128)(2,1)S(1)} %get-tuple-element.52), channel_id=1, source_target_pairs={{0,4},{4,8},{8,12},{12,16},{16,20},{20,24},{24,28},{28,32},{32,36}... | collective-permute-start | bytes 786440 | tf_op jit(solution)/shard_map/ppermute | solution.py:366
  11.3 0.9 copy-start.4
  12.2 14.8 %copy-start.3 = (bf16[3,3,3,64,128]{4,3,2,1,0:T(8,128)(2,1)S(1)}, bf16[3,3,3,64,128]{4,3,2,1,0:T(8,128)(2,1)}, u32[]{:S(2)}) copy-start(bf16[3,3,3,64,128]{4,3,2,1,0:T(8,128)(2,1)} %wc.1) | copy-start | bytes 1327108
  13.4 13.6 %copy-start.2 = (bf16[3,3,3,64,64]{4,3,2,1,0:T(8,128)(2,1)S(1)}, bf16[3,3,3,64,64]{4,3,2,1,0:T(8,128)(2,1)}, u32[]{:S(2)}) copy-start(bf16[3,3,3,64,64]{4,3,2,1,0:T(8,128)(2,1)} %wf.1) | copy-start | bytes 663556
  13.4 17.8 %collective-permute-start.2 = (bf16[18,64,128]{2,1,0:T(8,128)(2,1)}, bf16[18,64,128]{2,1,0:T(8,128)(2,1)S(1)}, u32[]{:S(2)}, u32[]{:S(2)}) collective-permute-start(bf16[18,64,128]{2,1,0:T(8,128)(2,1)} %get-tuple-element.30), channel_id=1, source_target_pairs={{0,1},{1,2},{2,3},{3,0},{4,5},{5,6},{6,7},{7,4},{8,9},{9,10},{10,1... | collective-permute-start | bytes 884744 | tf_op jit(solution)/shard_map/ppermute | solution.py:366
  14.7 16.5 %collective-permute-start.3 = (bf16[18,64,128]{2,1,0:T(8,128)(2,1)S(1)}, bf16[18,64,128]{2,1,0:T(8,128)(2,1)S(1)}, u32[]{:S(2)}, u32[]{:S(2)}) collective-permute-start(bf16[18,64,128]{2,1,0:T(8,128)(2,1)S(1)} %get-tuple-element.31), channel_id=1, source_target_pairs={{0,3},{1,0},{2,1},{3,2},{4,7},{5,4},{6,5},{7,6},{8,11},{9,8},{10,9... | collective-permute-start | bytes 884744 | tf_op jit(solution)/shard_map/ppermute | solution.py:366
  24.7 6.5 %collective-permute-start.4 = (bf16[14,64,128]{2,1,0:T(8,128)(2,1)}, bf16[14,64,128]{2,1,0:T(8,128)(2,1)}, u32[]{:S(2)}, u32[]{:S(2)}) collective-permute-start(bf16[14,64,128]{2,1,0:T(8,128)(2,1)} %get-tuple-element.32), channel_id=1, source_target_pairs={{0,1},{1,2},{2,3},{3,0},{4,5},{5,6},{6,7},{7,4},{8,9},{9,10},{10,1... | collective-permute-start | bytes 688136 | tf_op jit(solution)/shard_map/ppermute | solution.py:366
  27.0 7.2 %collective-permute-start.5 = (bf16[14,64,128]{2,1,0:T(8,128)(2,1)}, bf16[14,64,128]{2,1,0:T(8,128)(2,1)}, u32[]{:S(2)}, u32[]{:S(2)}) collective-permute-start(bf16[14,64,128]{2,1,0:T(8,128)(2,1)} %get-tuple-element.33), channel_id=1, source_target_pairs={{0,3},{1,0},{2,1},{3,2},{4,7},{5,4},{6,5},{7,6},{8,11},{9,8},{10,9... | collective-permute-start | bytes 688136 | tf_op jit(solution)/shard_map/ppermute | solution.py:366
  27.7 0.8 copy-start.6
  34.2 15.9 %copy-start.5 = (bf16[1,8,128,64]{2,3,1,0:T(8,128)(2,1)S(1)}, bf16[1,8,128,64]{2,3,1,0:T(8,128)(2,1)}, u32[]{:S(2)}) copy-start(bf16[1,8,128,64]{2,3,1,0:T(8,128)(2,1)} %param.7) | copy-start | bytes 393220
  37.9 5.0 %collective-permute-start.7 = (bf16[64,896]{1,0:T(8,128)(2,1)S(1)}, bf16[64,896]{1,0:T(8,128)(2,1)S(1)}, u32[]{:S(2)}, u32[]{:S(2)}) collective-permute-start(bf16[64,896]{1,0:T(8,128)(2,1)S(1)} %get-tuple-element.35.own), channel_id=1, source_target_pairs={{0,124},{4,0},{8,4},{12,8},{16,12},{20,16},{24,20},{28,24},{32,28}... | collective-permute-start | bytes 344072 | tf_op jit(solution)/shard_map/ppermute | solution.py:366
  39.4 10.7 %collective-permute-start.6 = (bf16[64,896]{1,0:T(8,128)(2,1)S(1)}, bf16[64,896]{1,0:T(8,128)(2,1)S(1)}, u32[]{:S(2)}, u32[]{:S(2)}) collective-permute-start(bf16[64,896]{1,0:T(8,128)(2,1)S(1)} %get-tuple-element.35.own), channel_id=1, source_target_pairs={{0,4},{4,8},{8,12},{12,16},{16,20},{20,24},{24,28},{28,32},{32,36}... | collective-permute-start | bytes 344072 | tf_op jit(solution)/shard_map/ppermute | solution.py:366
  52.3 5.9 %collective-permute-start.9 = (bf16[128,768]{1,0:T(8,128)(2,1)S(1)}, bf16[128,768]{1,0:T(8,128)(2,1)S(1)}, u32[]{:S(2)}, u32[]{:S(2)}) collective-permute-start(bf16[128,768]{1,0:T(8,128)(2,1)S(1)} %get-tuple-element.37.own), channel_id=1, source_target_pairs={{0,124},{4,0},{8,4},{12,8},{16,12},{20,16},{24,20},{28,24},{32,28}... | collective-permute-start | bytes 589832 | tf_op jit(solution)/shard_map/ppermute | solution.py:366
  52.5 11.7 %collective-permute-start.8 = (bf16[128,768]{1,0:T(8,128)(2,1)S(1)}, bf16[128,768]{1,0:T(8,128)(2,1)S(1)}, u32[]{:S(2)}, u32[]{:S(2)}) collective-permute-start(bf16[128,768]{1,0:T(8,128)(2,1)S(1)} %get-tuple-element.37.own), channel_id=1, source_target_pairs={{0,4},{4,8},{8,12},{12,16},{16,20},{20,24},{24,28},{28,32},{32,36}... | collective-permute-start | bytes 589832 | tf_op jit(solution)/shard_map/ppermute | solution.py:366
  69.5 27.9 %copy-start.7 = (bf16[384,768]{1,0:T(8,128)(2,1)S(1)}, bf16[384,768]{1,0:T(8,128)(2,1)}, u32[]{:S(2)}) copy-start(bf16[384,768]{1,0:T(8,128)(2,1)} %copy-done.6) | copy-start | bytes 1769476
  69.5 30.8 %all-to-all-start = ((bf16[128,24,128]{2,1,0:T(8,128)(2,1)}), bf16[128,24,128]{2,1,0:T(8,128)(2,1)S(1)}, u32[]{:S(2)}, u32[]{:S(2)}) async-start(bf16[128,24,128]{2,1,0:T(8,128)(2,1)} %bitcast.7), calls=%async_computation | async-start | bytes 1572864 | tf_op jit(solution)/shard_map/all_to_all | solution.py:448
  74.6 16.8 %collective-permute-start.11 = (bf16[18,64,128]{2,1,0:T(8,128)(2,1)S(1)}, bf16[18,64,128]{2,1,0:T(8,128)(2,1)S(1)}, u32[]{:S(2)}, u32[]{:S(2)}) collective-permute-start(bf16[18,64,128]{2,1,0:T(8,128)(2,1)S(1)} %get-tuple-element.42.row0), channel_id=1, source_target_pairs={{0,124},{4,0},{8,4},{12,8},{16,12},{20,16},{24,20},{28,24},{32,28}... | collective-permute-start | bytes 884744 | tf_op jit(solution)/shard_map/ppermute | solution.py:366
  82.7 14.7 %collective-permute-start.10 = (bf16[18,64,128]{2,1,0:T(8,128)(2,1)S(1)}, bf16[18,64,128]{2,1,0:T(8,128)(2,1)S(1)}, u32[]{:S(2)}, u32[]{:S(2)}) collective-permute-start(bf16[18,64,128]{2,1,0:T(8,128)(2,1)S(1)} %get-tuple-element.43.row1), channel_id=1, source_target_pairs={{0,4},{4,8},{8,12},{12,16},{16,20},{20,24},{24,28},{28,32},{32,36}... | collective-permute-start | bytes 884744 | tf_op jit(solution)/shard_map/ppermute | solution.py:366

commit v3 on v2

v3 whole, which is shorter than its diff:
```python
import functools

import jax
import jax.numpy as jnp
from jax import lax
from jax.experimental import pallas as pl
from jax.experimental.pallas import tpu as pltpu
from jax.sharding import PartitionSpec as P

L = 128
YH = 7
BF = jnp.bfloat16
F32 = jnp.float32
R = 8
HALF = 864
VMEM = 20 * 1024 * 1024


def iota(shape, dim):
    return lax.broadcasted_iota(jnp.int32, shape, dim)


def shifted(tile, by, lane):
    out = pltpu.roll(tile, by % L, 1)
    keep = lane >= by if by > 0 else lane < L + by
    return jnp.where(keep, out, 0.0)


def combine(acc, rows, tiles, step, lane):
    out = []
    for t in range(tiles):
        part = acc[:, t * L : (t + 1) * L]
        out.append(
            shifted(part[:rows], step, lane)
            + part[rows : 2 * rows]
            + shifted(part[2 * rows :], -step, lane)
        )
    return out


def slopes(value):
    sig = jax.nn.sigmoid(value)
    return sig, sig * (1.0 + value * (1.0 - sig))


def dot(a, b):
    return jnp.dot(a, b, preferred_element_type=F32)


def spread_matrix():
    row, col = iota((L, 2 * L), 0), iota((L, 2 * L), 1)
    return jnp.where(row == (col // L) * 64 + (col % L) // 2, 1.0, 0.0).astype(BF)


def pick(cond, a, b):
    return jnp.where(cond, a, b)


def take(ok, tile):
    return tile if ok is None else jnp.where(ok, tile, jnp.zeros_like(tile))


def pool_matrix():
    row, col = iota((1024, L), 0), iota((1024, L), 1)
    return jnp.where(col == ((row // 256) % 2) * 64 + (row % L) // 2, 1.0, 0.0).astype(BF)


def taps(ref, at, tiles):
    return jnp.concatenate([ref[:, (at + j) * L : (at + j + tiles) * L] for j in range(3)], axis=0)


def forward_chunk(weight, window, at, lane, pool):
    acc = dot(weight[...], taps(window, at, 4))
    acts, slopes_ = [], []
    for pre in combine(acc, 128, 4, 1, lane):
        sig, slp = slopes(pre)
        acts.append((pre * sig).astype(BF))
        slopes_.append(slp)
    cells = jnp.concatenate([a[:64] for a in acts] + [a[64:] for a in acts], axis=1)
    return slopes_, dot(cells, pool) * 0.125


def prepare_kernel(wf, wc, wfwd, wbwd, cfwd, cbwd):
    def fine(i, j, k):
        return wf[i, j, k] if 0 <= i < 3 else jnp.zeros((64, 64), BF)

    for j in range(3):
        for k in range(3):
            for x in range(2):
                rows = slice(k * 128 + x * 64, k * 128 + x * 64 + 64)
                for h in range(2):
                    i = 2 * h - x
                    cols = slice(j * 256 + h * L, j * 256 + (h + 1) * L)
                    pair = jnp.concatenate([fine(i, j, k), fine(i + 1, j, k)], axis=0)
                    wfwd[rows, cols] = pair.astype(F32).T.astype(BF)
                    wbwd[rows, cols] = jnp.concatenate(
                        [fine(2 - i, 2 - j, 2 - k), fine(1 - i, 2 - j, 2 - k)], axis=1
                    )
    for k in range(3):
        full = jnp.concatenate([wc[i, j, k] for j in range(3) for i in range(3)], axis=0)
        cfwd[k * 128 : (k + 1) * 128, :] = full.astype(F32).T.astype(BF)
        for j in range(3):
            for i in range(3):
                at = (3 * j + i) * L
                cbwd[k * 64 : (k + 1) * 64, at : at + L] = wc[2 - i, 2 - j, 2 - k]


def start_and_wait(pairs, sems):
    copies = [pltpu.make_async_copy(a, b, sems.at[n]) for n, (a, b) in enumerate(pairs)]
    for c in copies:
        c.start()
    for c in copies:
        c.wait()


def own_edges_kernel(flags, own, fc, cot, first, second, sems):
    pairs = []
    for out, up in ((first, flags[5]), (second, 1 - flags[5])):
        y, one, cc = up * (16 - YH), up * 15, up * 6
        for x in range(2):
            pairs.append((own.at[x, pl.ds(y, YH)], out.at[x * YH : (x + 1) * YH]))
            pairs.append((fc.at[x, pl.ds(one, 1)], out.at[2 * YH + x : 2 * YH + x + 1]))
        pairs.append((cot.at[pl.ds(cc, 2)], out.at[2 * YH + 2 : 2 * YH + 4]))
    start_and_wait(pairs, sems)


def corner_edges_kernel(flags, xa, xb, first, second, sems):
    pairs = []
    for out, up in ((first, flags[5]), (second, 1 - flags[5])):
        y = up * (16 - YH)
        pairs.append((xa.at[pl.ds(y, YH)], out.at[0:YH]))
        pairs.append((xb.at[pl.ds(y, YH)], out.at[YH : 2 * YH]))
    start_and_wait(pairs, sems)


def interior_kernel(flags, own, xa, xb, weight, v2, slope, pooled):
    f = [flags[i] > 0 for i in range(6)]
    for y in range(16):
        at = slice(y * L, (y + 1) * L)
        v2[0:64, at] = take(f[0], pick(f[4], xb[y], xa[y]))
        v2[64:128, at] = own[0, y]
        v2[128:192, at] = own[1, y]
        v2[192:256, at] = take(f[1], pick(f[4], xa[y], xb[y]))
    lane, pool = iota((128, L), 1), pool_matrix()
    for t in range(3):
        slps, mean = forward_chunk(weight, v2, 4 * t + 1, lane, pool)
        for n in range(4):
            slope[:, (4 * t + n) * L : (4 * t + n + 1) * L] = slps[n]
        pooled[:, t * L : (t + 1) * L] = mean.astype(BF)


def border_kernel(
    flags, v2, mid, aa, ab, ba, bb, weight, slope_lo, slope_hi, pooled, vedge, window
):
    f = [flags[i] > 0 for i in range(6)]
    lane, lane64, pool = iota((128, L), 1), iota((64, L), 1), pool_matrix()
    pooled[:, 2 * L : 5 * L] = mid[...]
    for side, ok in enumerate((f[2], f[3])):
        even = f[5] if side == 1 else jnp.logical_not(f[5])
        win = window.at[side]
        first = 0 if side == 0 else 3
        for y in range(YH):
            at = slice((first + y) * L, (first + y + 1) * L)
            xs = [pick(even, ba[n * YH + y], bb[n * YH + y]) for n in range(2)]
            win[0:64, at] = take(ok & f[0], pick(f[4], xs[1], xs[0]))
            win[64:128, at] = take(ok, pick(even, aa[y], ab[y]))
            win[128:192, at] = take(ok, pick(even, aa[YH + y], ab[YH + y]))
            win[192:256, at] = take(ok & f[1], pick(f[4], xs[0], xs[1]))
        if side == 0:
            win[:, YH * L :] = v2[:, : 3 * L]
            vedge[:, :L] = win[:, 6 * L : 7 * L]
        else:
            win[:, : 3 * L] = v2[:, 13 * L :]
            vedge[:, L:] = win[:, 3 * L : 4 * L]
        for u in range(2):
            slps, mean = forward_chunk(weight, win, 4 * u, lane, pool)
            if side == 0 and u == 1:
                for n in range(3):
                    slope_lo[:, n * L : (n + 1) * L] = slps[n + 1]
            if side == 1 and u == 0:
                for n in range(3):
                    slope_hi[:, n * L : (n + 1) * L] = slps[n]
            t = u if side == 0 else 5 + u
            yc = 2 * t + lane64 // 64
            keep = ((yc >= 3) | f[2]) & ((yc < 11) | f[3])
            pooled[:, t * L : (t + 1) * L] = jnp.where(keep, mean, 0.0).astype(BF)


def spread_rows(f, own, a, b, tiles, out):
    rows = []
    for t in range(tiles):
        at = slice(t * L, (t + 1) * L)
        lo, hi = pick(f[4], b[:, at], a[:, at]), pick(f[4], a[:, at], b[:, at])
        rows += [take(f[0], lo), own[:, at], take(f[1], hi)]
    full = dot(jnp.concatenate(rows, axis=0), spread_matrix()).astype(BF)
    n = full.shape[0] // tiles
    for t in range(tiles):
        out[:, 2 * t * L : (2 * t + 2) * L] = full[t * n : (t + 1) * n]


def coarse_kernel(flags, own, a, b, aa, cot, ab, weight, p2, gpc, gpack):
    f = [flags[i] > 0 for i in range(6)]
    spread_rows(f, own, a, b, 7, p2)
    lane = iota((128, L), 1)
    row, col = iota((2 * L, L), 0), iota((2 * L, L), 1)
    pack = jnp.where(
        (row % 2 == 0) & (col == (row // L) * 64 + (row % L) // 2), 1.0, 0.0
    ).astype(BF)
    at = 2 * YH + 2
    tiles = (
        [take(f[2], pick(f[5], ab[at + n], aa[at + n])) for n in range(2)]
        + [cot[n] for n in range(8)]
        + [take(f[3], pick(f[5], aa[at + n], ab[at + n])) for n in range(2)]
    )
    cc = lax.dot_general(
        jnp.concatenate(tiles, axis=1),
        spread_matrix()[:64, :L],
        (((0,), (0,)), ((), ())),
        preferred_element_type=F32,
    )
    acc = dot(weight[...], taps(p2, 0, 12))
    out = []
    for n, pre in enumerate(combine(acc, 128, 12, 2, lane)):
        _, slp = slopes(pre)
        out.append((cc[n * L : (n + 1) * L] * slp).astype(BF))
        gpc[:, n * L : (n + 1) * L] = out[n]
    pairs = jnp.concatenate(
        [jnp.concatenate(out[2 * t : 2 * t + 2], axis=1) for t in range(6)], axis=0
    )
    packed = dot(pairs, pack).astype(BF)
    for t in range(6):
        gpack[:, t * L : (t + 1) * L] = packed[t * L : (t + 1) * L]


def nt(a, b):
    return lax.dot_general(a, b, (((1,), (1,)), ((), ())), preferred_element_type=F32)


def coarse_corr_kernel(scale, flags, p2, gpc, kept, sent0, sent1, g3, out):
    lane = iota((128, L), 1)
    for y in range(8):
        tile = gpc[:, (2 + y) * L : (3 + y) * L].astype(F32)
        at = slice(y * L, (y + 1) * L)
        g3[0:128, at] = shifted(tile, -2, lane).astype(BF)
        g3[128:256, at] = tile.astype(BF)
        g3[256:384, at] = shifted(tile, 2, lane).astype(BF)
    res = nt(taps(p2, 2, 8), g3[...]) * (0.5 * scale)
    for j in range(3):
        for k in range(3):
            at = (3 * j + k) * 192
            out[at : at + 192, :] = res[j * 192 : (j + 1) * 192, k * L : (k + 1) * L].astype(BF)
    low, high = out[:HALF, :], out[HALF:, :]
    even = flags[5] > 0
    kept[...] = pick(even, low, high)
    sent0[...] = pick(even, high[: HALF // 2], low[: HALF // 2])
    sent1[...] = pick(even, high[HALF // 2 :], low[HALF // 2 :])


def turn_kernel(v2, vedge, vt):
    for y in range(18):
        tile = vedge[:, :L] if y == 0 else vedge[:, L:] if y == 17 else v2[:, (y - 1) * L : y * L]
        vt[y * L : (y + 1) * L, :] = tile.astype(F32).T.astype(BF)


def gpf_kernel(
    scale,
    flags,
    own,
    a,
    b,
    weight,
    fc,
    aa,
    ab,
    slope_lo,
    slope,
    slope_hi,
    vt,
    kept,
    got0,
    got1,
    first,
    second,
    mine,
    g2,
    u3,
    pack,
):
    f = [flags[i] > 0 for i in range(6)]
    spread_rows(f, own, a, b, 6, g2)
    lane = iota((64, L), 1)
    acc = dot(weight[...], taps(g2, 0, 10))
    for m, gp in enumerate(combine(acc, 64, 10, 2, lane)):
        add = gp * 0.125
        for n in (2 * m - 1, 2 * m):
            if not 0 <= n < 18:
                continue
            if n < 3:
                slp = slope_lo[:, n * L : (n + 1) * L]
            elif n < 15:
                slp = slope[:, (n - 3) * L : (n - 2) * L]
            else:
                slp = slope_hi[:, (n - 15) * L : (n - 14) * L]
            rows = []
            for x in range(2):
                edge = 2 * YH + x
                if n == 0:
                    cot = pick(f[5], ab[edge], aa[edge])
                elif n == 17:
                    cot = pick(f[5], aa[edge], ab[edge])
                else:
                    cot = fc[x, n - 1]
                val = (cot.astype(F32) + add) * slp[x * 64 : (x + 1) * 64]
                if n == 0 or n == 17:
                    val = take(f[2] if n == 0 else f[3], val)
                rows.append(val.astype(BF))
                if 0 < n < 17:
                    tile, at = rows[x].astype(F32), slice((n - 1) * L, n * L)
                    u3[x * 64 : x * 64 + 64, at] = shifted(tile, -1, lane).astype(BF)
                    u3[128 + x * 64 : 192 + x * 64, at] = rows[x]
                    u3[256 + x * 64 : 320 + x * 64, at] = shifted(tile, 1, lane).astype(BF)
            first[n] = pick(f[4], rows[1], rows[0])
            second[n] = pick(f[4], rows[0], rows[1])
    halves = []
    for j in range(3):
        res = dot(u3[...], vt[j * L : (j + 16) * L, :]) * scale
        for k in range(3):
            both = res[k * L : k * L + 64] + pltpu.roll(res[k * L + 64 : (k + 1) * L], 192, 1)
            at = (3 * j + k) * 64
            pack[at : at + 64, :] = both[:, :L]
            halves.append(both[:, L:])
    halves.append(jnp.zeros((64, L), F32))
    lane = iota((64, L), 1)
    for n in range(5):
        packed = jnp.where(lane < 64, halves[2 * n], pltpu.roll(halves[2 * n + 1], 64, 1))
        pack[576 + 64 * n : 640 + 64 * n, :] = packed
    got = jnp.concatenate([got0[...], got1[...]], axis=0)
    coarse = kept[...].astype(F32) + got.astype(F32)
    none = jnp.zeros((R, L), F32)
    for n in range(128):
        at = slice(n * R, (n + 1) * R)
        top = coarse[at] if n < HALF // R else none
        low = pack[at, :] if n < 896 // R else none
        mine[n] = jnp.concatenate([top, low], axis=0).astype(BF)


def input_grad_kernel(flags, first, second, a, b, weight, out, g2):
    f = [flags[i] > 0 for i in range(6)]
    for y in range(18):
        at = slice(y * L, (y + 1) * L)
        g2[0:64, at] = take(f[0], pick(f[4], b[y], a[y]))
        g2[64:128, at] = pick(f[4], second[y], first[y])
        g2[128:192, at] = pick(f[4], first[y], second[y])
        g2[192:256, at] = take(f[1], pick(f[4], a[y], b[y]))
    lane = iota((128, L), 1)
    for t in range(4):
        acc = dot(weight[...], taps(g2, 4 * t, 4))
        for n, val in enumerate(combine(acc, 128, 4, 1, lane)):
            val = val.astype(BF)
            out[0, 4 * t + n] = val[:64]
            out[1, 4 * t + n] = val[64:]


def sum_kernel(parts, out):
    sums = []
    for core in range(2):
        total = parts[core].astype(F32)
        for n in range(core + 2, 128, 2):
            total = total + parts[n].astype(F32)
        sums.append(total)
    total = jnp.concatenate([sums[0][:R], sums[1][:R], sums[0][R:] + sums[1][R:]], axis=0)
    total = total.astype(BF)
    for n in range(128):
        out[n] = total


def unpack_kernel(got, fine, coarse):
    def coarse_rows(q):
        half, at = q // (HALF // R), q % (HALF // R)
        return got[at].astype(F32)[half * R : (half + 1) * R]

    for j in range(3):
        for k in range(3):
            for i in range(3):
                q = ((3 * j + k) * 192 + i * 64) // R
                rows = [coarse_rows(q + m) for m in range(64 // R)]
                coarse[i, j, k] = jnp.concatenate(rows, axis=0)

    def tile(n):
        rows = [got[m].astype(F32)[2 * R :] for m in range(n * 64 // R, (n + 1) * 64 // R)]
        return jnp.concatenate(rows, axis=0).T

    for n in range(9):
        part = tile(n)
        fine[0, n // 3, n % 3] = part[:64]
        fine[1, n // 3, n % 3] = part[64:]
    for n in range(5):
        part = tile(9 + n)
        for h in range(2):
            at = 2 * n + h
            if at < 9:
                fine[2, at // 3, at % 3] = part[64 * h : 64 * h + 64]


def call(kernel, name, outs, args, scratch=(), flags=True, macs=0, copies=0):
    space = pl.ANY if copies else pltpu.VMEM
    specs = [pl.BlockSpec(memory_space=space) for _ in args]
    if flags:
        specs[0] = pl.BlockSpec(memory_space=pltpu.SMEM)
    moved = sum(a.size * a.dtype.itemsize for a in args)
    shapes = tuple(jax.ShapeDtypeStruct(*o) for o in outs)
    if copies:
        scratch = [pltpu.SemaphoreType.DMA((copies,))]
    got = pl.pallas_call(
        kernel,
        out_shape=shapes,
        in_specs=specs,
        out_specs=tuple(pl.BlockSpec(memory_space=space) for _ in shapes),
        scratch_shapes=list(scratch),
        compiler_params=pltpu.CompilerParams(vmem_limit_bytes=VMEM),
        cost_estimate=pl.CostEstimate(flops=2 * macs, bytes_accessed=moved, transcendentals=0),
        name=name,
    )(*args)
    return got if len(shapes) > 1 else got[0]


def swaps(first, second, axis):
    count = lax.axis_size(axis)
    pairs = [(i, i ^ 1) for i in range(count)]
    others = [(0, 0), (count - 1, count - 1)] + [(i, ((i - 1) ^ 1) + 1) for i in range(1, count - 1)]
    other = lax.ppermute(second, axis, others)
    return lax.ppermute(first, axis, pairs), other


def on_device(inputs, fine_cot, coarse_cot, weight_fine, weight_coarse):
    slab, sub = lax.axis_index("slab"), lax.axis_index("sub")
    flags = jnp.stack(
        [slab > 0, slab < 31, sub > 0, sub < 3, slab % 2 == 0, sub % 2 == 0]
    ).astype(jnp.int32)
    cot = jnp.swapaxes(coarse_cot[0], 1, 2)

    odd = slab % 2
    xa, xb = swaps(
        lax.dynamic_index_in_dim(inputs, 1 - odd, 0, False),
        lax.dynamic_index_in_dim(inputs, odd, 0, False),
        "slab",
    )
    own_edge = ((2 * YH + 4, 64, L), BF)
    first, second = call(
        own_edges_kernel,
        "own_edges",
        (own_edge, own_edge),
        (flags, inputs, fine_cot, cot),
        copies=10,
    )
    aa, ab = swaps(first, second, "sub")
    w_fwd, w_bwd, c_fwd, c_bwd = call(
        prepare_kernel,
        "prepare_weights",
        (((384, 768), BF), ((384, 768), BF), ((384, 576), BF), ((192, 1152), BF)),
        (weight_fine, weight_coarse),
        flags=False,
    )
    corner = ((2 * YH, 64, L), BF)
    first, second = call(
        corner_edges_kernel, "corner_edges", (corner, corner), (flags, xa, xb), copies=4
    )
    ba, bb = swaps(first, second, "sub")
    v2, slope, mid = call(
        interior_kernel,
        "fine_forward_interior",
        (((256, 16 * L), BF), ((128, 12 * L), F32), ((64, 3 * L), BF)),
        (flags, inputs, xa, xb, w_fwd),
        macs=384 * 768 * 12 * L,
    )
    slope_lo, slope_hi, pooled, vedge = call(
        border_kernel,
        "fine_forward_border",
        (((128, 3 * L), F32), ((128, 3 * L), F32), ((64, 7 * L), BF), ((256, 2 * L), BF)),
        (flags, v2, mid, aa, ab, ba, bb, w_fwd),
        scratch=[pltpu.VMEM((2, 256, 10 * L), BF)],
        macs=384 * 768 * 16 * L,
    )
    pa, pb = swaps(pooled, pooled, "slab")
    vt = call(
        turn_kernel, "turn_inputs", (((18 * L, 256), BF),), (v2, vedge), flags=False
    )
    p2, gpc, gpack = call(
        coarse_kernel,
        "coarse_forward",
        (((192, 14 * L), BF), ((128, 12 * L), BF), ((128, 6 * L), BF)),
        (flags, pooled, pa, pb, aa, cot, ab, c_fwd),
        macs=384 * 576 * 12 * L,
    )
    ga, gb = swaps(gpack, gpack, "slab")
    kept, *sent = call(
        functools.partial(coarse_corr_kernel, 1.0 / 256.0),
        "coarse_correlate",
        (((HALF, L), BF), ((HALF // 2, L), BF), ((HALF // 2, L), BF)),
        (flags, p2, gpc),
        scratch=[pltpu.VMEM((384, 8 * L), BF), pltpu.VMEM((2 * HALF, L), BF)],
        macs=384 * 576 * 8 * L,
    )
    got0, got1 = (lax.ppermute(part, "sub", [(0, 1), (1, 0), (2, 3), (3, 2)]) for part in sent)
    first, second, mine = call(
        functools.partial(gpf_kernel, 524288.0**-0.5),
        "fine_gradient",
        (((18, 64, L), BF), ((18, 64, L), BF), ((128, 2 * R, L), BF)),
        (
            flags,
            gpack,
            ga,
            gb,
            c_bwd,
            fine_cot,
            aa,
            ab,
            slope_lo,
            slope,
            slope_hi,
            vt,
            kept,
            got0,
            got1,
        ),
        scratch=[
            pltpu.VMEM((384, 12 * L), BF),
            pltpu.VMEM((384, 16 * L), BF),
            pltpu.VMEM((896, L), F32),
        ],
        macs=384 * 768 * 16 * L,
    )
    ha, hb = swaps(first, second, "slab")
    shares = lax.all_to_all(mine.reshape(128 * 2 * R, L), ("slab", "sub"), 0, 0, tiled=True)
    total = call(
        sum_kernel,
        "sum_shares",
        (((128, 3 * R, L), BF),),
        (shares.reshape(128, 2 * R, L),),
        flags=False,
    )
    everything = lax.all_to_all(total.reshape(128 * 3 * R, L), ("slab", "sub"), 0, 0, tiled=True)
    grad_input = call(
        input_grad_kernel,
        "input_gradient",
        (((2, 16, 64, L), BF),),
        (flags, first, second, ha, hb, w_bwd),
        scratch=[pltpu.VMEM((256, 18 * L), BF)],
        macs=20 * 384 * 768 * 16 * L,
    )
    grad_fine, grad_coarse = call(
        unpack_kernel,
        "unpack",
        (((3, 3, 3, 64, 64), F32), ((3, 3, 3, 64, 128), F32)),
        (everything.reshape(128, 3 * R, L),),
        flags=False,
    )
    return (grad_input, grad_fine, grad_coarse)


def solution(mesh):
    in_specs = (
        P("slab", "sub", None, None),
        P("slab", "sub", None, None),
        P("slab", "sub", None, None),
        P(),
        P(),
    )
    out_specs = (P("slab", "sub", None, None), P(), P())
    return jax.shard_map(
        on_device, mesh=mesh, in_specs=in_specs, out_specs=out_specs, check_vma=False
    )
```

time: 122 us -> 109 us (0.89)
  starting transfers between devices: 29.4 us -> 53.6 us
  blocking collectives: 19.9 us -> 0 us
  waiting for transfers between devices: 46.9 us -> 28.4 us
  Pallas kernels: 21.7 us -> 23.3 us
    ppermute x12 -> x14, waiting for transfers between devices: 46.9 us -> 4.09 us  [the longest x6 2.54 us: swaps(): return (lax.ppermute(first, axis, pairs), other)]
    all_to_all x1 -> x2, waiting for transfers between devices: 0.01 us -> 24.3 us  [the longest x1 13 us: on_device(): lax.all_to_all(total.reshape(128 * 3 * R, L), ('slab', 'sub'), 0, 0, tile...]
    all_to_all x1 -> x2, starting transfers between devices: 5.04 us -> 26.3 us  [the longest x1 21.6 us: on_device(): lax.all_to_all(mine.reshape(128 * 2 * R, L), ('slab', 'sub'), 0, 0, tiled...]
    all_to_all x1 -> x0, blocking collectives: 19.9 us -> none  [on_device(): lax.all_to_all(total.reshape(128 * ROWS, L), ('slab', 'sub'), 0, 0, tiled...]
    ppermute x12 -> x14, starting transfers between devices: 24.3 us -> 27.2 us  [the longest x6 17.8 us: swaps(): return (lax.ppermute(first, axis, pairs), other)]
    pallas_call x12, Pallas kernels: 21.7 us -> 23.3 us  [call(): pl.pallas_call(kernel, out_shape=shapes, in_specs=specs, out_specs=tuple(...]
  transfers between devices with their start and end apart: 13 -> 16, of which waited for: 9 -> 7; matrix products, arithmetic and copies ran while one was open for 0% -> 0% of each run, Pallas kernels for 7% -> 11%
where the time goes in v3:
time: 109 us; the launch traced here: 108 us
  starting transfers between devices  53.6 us (49%)
  waiting for transfers between devices  28.4 us (26%)
  Pallas kernels  23.3 us (21%)
  local copies, waits for them, and re-layouts  2.22 us (2%)
    pallas_call x12, Pallas kernels, call(): pl.pallas_call(kernel, out_shape=shapes, in_specs=specs, out_specs=tuple(...  23.3 us
    all_to_all x1, starting transfers between devices, on_device(): lax.all_to_all(mine.reshape(128 * 2 * R, L), ('slab', 'sub'), 0, 0, tiled...  21.6 us
    ppermute x6, starting transfers between devices, swaps(): return (lax.ppermute(first, axis, pairs), other)  17.8 us
    all_to_all x1, waiting for transfers between devices, on_device(): lax.all_to_all(total.reshape(128 * 3 * R, L), ('slab', 'sub'), 0, 0, tile...  13 us
    all_to_all x1, waiting for transfers between devices, on_device(): lax.all_to_all(mine.reshape(128 * 2 * R, L), ('slab', 'sub'), 0, 0, tiled...  11.3 us
    ppermute x6, starting transfers between devices, swaps(): other = lax.ppermute(second, axis, others)  8.89 us
    all_to_all x1, starting transfers between devices, on_device(): lax.all_to_all(total.reshape(128 * 3 * R, L), ('slab', 'sub'), 0, 0, tile...  4.67 us
    ppermute x6, waiting for transfers between devices, swaps(): return (lax.ppermute(first, axis, pairs), other)  2.54 us
  transfers between devices with their start and end apart: 16, of which 7 were waited for; matrix products, arithmetic and copies ran while one was open for 0% of the time, Pallas kernels for 11%

profile of v3, /device:TPU:1, one launch (start us, length us, event | category | flops | bytes accessed | tf_op | source)
XLA Modules:
  0.0 108.4 jit_solution(15293010725895271441)
XLA Ops:
  0.7 1.2 %dynamic-slice_bitcast_fusion = (bf16[16,64,128]{2,1,0:T(8,128)(2,1)S(1)}, bf16[16,64,128]{2,1,0:T(8,128)(2,1)S(1)}) fusion(bf16[2,16,64,128]{3,2,1,0:T(8,128)(2,1)} %own.3, s32[]{:T(128)S(6)} %select_n.23, s32[]{:T(128)S(6)} %select_n.22), kind=kLoop, calls=%fused_computation | loop fusion | bytes 1048584 | tf_op jit(solution)/shard_map/jit(dynamic_index_in_dim)/squeeze | solution.py:445
  2.6 5.4 %collective-permute-start = (bf16[16,64,128]{2,1,0:T(8,128)(2,1)S(1)}, bf16[16,64,128]{2,1,0:T(8,128)(2,1)S(1)}, u32[]{:S(2)}, u32[]{:S(2)}) collective-permute-start(bf16[16,64,128]{2,1,0:T(8,128)(2,1)S(1)} %get-tuple-element.56), channel_id=1, source_target_pairs={{0,4},{4,0},{8,12},{12,8},{16,20},{20,16},{24,28},{28,24},{32,36},... | collective-permute-start | bytes 786440 | tf_op jit(solution)/shard_map/ppermute | solution.py:432
  8.1 0.9 copy-done.4
  9.0 1.4 %own_edges.1 = (bf16[18,64,128]{2,1,0:T(8,128)(2,1)S(1)}, bf16[18,64,128]{2,1,0:T(8,128)(2,1)S(1)}) custom-call(s32[6]{0:T(128)S(1)} %convert_element_type.3.flags, bf16[2,16,64,128]{3,2,1,0:T(8,128)(2,1)S(1)} %copy-done.1, bf16[2,16,64,128]{3,2,1,0:T(8,128)(2,1)S(1)} %copy-done, bf16[8,64,128]{2,1,0:T(8,128)(2,1)S(1)} %bitcast.13), custom_call_target="tpu_custom_call" | custom-call | bytes 1179672 | tf_op jit(solution)/shard_map/own_edges/pallas_call | solution.py:414
  10.4 1.3 %collective-permute-start.2 = (bf16[18,64,128]{2,1,0:T(8,128)(2,1)S(1)}, bf16[18,64,128]{2,1,0:T(8,128)(2,1)S(1)}, u32[]{:S(2)}, u32[]{:S(2)}) collective-permute-start(bf16[18,64,128]{2,1,0:T(8,128)(2,1)S(1)} %get-tuple-element.32), channel_id=1, source_target_pairs={{0,1},{1,0},{2,3},{3,2},{4,5},{5,4},{6,7},{7,6},{8,9},{9,8},{10,11... | collective-permute-start | bytes 884744 | tf_op jit(solution)/shard_map/ppermute | solution.py:432
  11.8 3.1 %collective-permute-start.3 = (bf16[18,64,128]{2,1,0:T(8,128)(2,1)S(1)}, bf16[18,64,128]{2,1,0:T(8,128)(2,1)S(1)}, u32[]{:S(2)}, u32[]{:S(2)}) collective-permute-start(bf16[18,64,128]{2,1,0:T(8,128)(2,1)S(1)} %get-tuple-element.33), channel_id=1, source_target_pairs={{0,0},{3,3},{1,2},{2,1},{4,4},{7,7},{5,6},{6,5},{8,8},{11,11},{9,1... | collective-permute-start | bytes 884744 | tf_op jit(solution)/shard_map/ppermute | solution.py:431
  14.9 1.2 %corner_edges.1 = (bf16[14,64,128]{2,1,0:T(8,128)(2,1)S(1)}, bf16[14,64,128]{2,1,0:T(8,128)(2,1)S(1)}) custom-call(s32[6]{0:T(128)S(1)} %convert_element_type.3.flags, bf16[16,64,128]{2,1,0:T(8,128)(2,1)S(1)} %collective-permute-done.xa, bf16[16,64,128]{2,1,0:T(8,128)(2,1)S(1)} %collective-permute-done.1.xb), custom_call_target="tpu_custom_call" | custom-call | bytes 524312 | tf_op jit(solution)/shard_map/corner_edges/pallas_call | solution.py:414
  16.5 3.1 %collective-permute-start.5 = (bf16[14,64,128]{2,1,0:T(8,128)(2,1)S(1)}, bf16[14,64,128]{2,1,0:T(8,128)(2,1)S(1)}, u32[]{:S(2)}, u32[]{:S(2)}) collective-permute-start(bf16[14,64,128]{2,1,0:T(8,128)(2,1)S(1)} %get-tuple-element.35), channel_id=1, source_target_pairs={{0,0},{3,3},{1,2},{2,1},{4,4},{7,7},{5,6},{6,5},{8,8},{11,11},{9,1... | collective-permute-start | bytes 688136 | tf_op jit(solution)/shard_map/ppermute | solution.py:431
  20.3 2.6 %fine_forward_interior.1 = (bf16[256,2048]{1,0:T(8,128)(2,1)S(1)}, f32[128,1536]{1,0:T(8,128)S(1)}, bf16[64,384]{1,0:T(8,128)(2,1)S(1)}) custom-call(s32[6]{0:T(128)S(1)} %convert_element_type.3.flags, bf16[2,16,64,128]{3,2,1,0:T(8,128)(2,1)S(1)} %copy-done.1, bf16[16,64,128]{2,1,0:T(8,128)(2,1)S(1)} %collective-permute-done.xa, ...), custom_call_target="tpu_custom_call" | custom-call | flops 905969664 | bytes 1638424 | tf_op jit(solution)/shard_map/fine_forward_interior/pallas_call | solution.py:414
  23.9 3.2 %fine_forward_border.1 = (f32[128,384]{1,0:T(8,128)S(1)}, f32[128,384]{1,0:T(8,128)S(1)}, bf16[64,896]{1,0:T(8,128)(2,1)S(1)}, bf16[256,256]{1,0:T(8,128)(2,1)S(1)}) custom-call(s32[6]{0:T(128)S(1)} %convert_element_type.3.flags, bf16[256,2048]{1,0:T(8,128)(2,1)S(1)} %get-tuple-element.30.v2, bf16[64,384]{1,0:T(8,128)(2,1)S(1)} %get-tuple-element.31.mid, ...), custom_call_target="tpu_custom_call" | custom-call | flops 1207959552 | bytes 2736152 | tf_op jit(solution)/shard_map/fine_forward_border/pallas_call | solution.py:414
  27.8 2.8 %collective-permute-start.6 = (bf16[64,896]{1,0:T(8,128)(2,1)S(1)}, bf16[64,896]{1,0:T(8,128)(2,1)S(1)}, u32[]{:S(2)}, u32[]{:S(2)}) collective-permute-start(bf16[64,896]{1,0:T(8,128)(2,1)S(1)} %get-tuple-element.36.own), channel_id=1, source_target_pairs={{0,4},{4,0},{8,12},{12,8},{16,20},{20,16},{24,28},{28,24},{32,36},... | collective-permute-start | bytes 344072 | tf_op jit(solution)/shard_map/ppermute | solution.py:432
  30.6 2.2 %collective-permute-done.6.a = bf16[64,896]{1,0:T(8,128)(2,1)S(1)} collective-permute-done((bf16[64,896]{1,0:T(8,128)(2,1)S(1)}, bf16[64,896]{1,0:T(8,128)(2,1)S(1)}, u32[]{:S(2)}, u32[]{:S(2)}) %collective-permute-start.6) | collective-permute-done | bytes 114720 | tf_op jit(solution)/shard_map/ppermute | solution.py:432
  32.7 2.2 %coarse_forward.1 = (bf16[192,1792]{1,0:T(8,128)(2,1)S(1)}, bf16[128,1536]{1,0:T(8,128)(2,1)S(1)}, bf16[128,768]{1,0:T(8,128)(2,1)S(1)}) custom-call(s32[6]{0:T(128)S(1)} %convert_element_type.3.flags, bf16[64,896]{1,0:T(8,128)(2,1)S(1)} %get-tuple-element.36.own, bf16[64,896]{1,0:T(8,128)(2,1)S(1)} %collective-permute-done.6.a, ...), custom_call_target="tpu_custom_call" | custom-call | flops 679477248 | bytes 1507352 | tf_op jit(solution)/shard_map/coarse_forward/pallas_call | solution.py:414
  35.6 6.2 %collective-permute-start.8 = (bf16[128,768]{1,0:T(8,128)(2,1)S(1)}, bf16[128,768]{1,0:T(8,128)(2,1)S(1)}, u32[]{:S(2)}, u32[]{:S(2)}) collective-permute-start(bf16[128,768]{1,0:T(8,128)(2,1)S(1)} %get-tuple-element.38.own), channel_id=1, source_target_pairs={{0,4},{4,0},{8,12},{12,8},{16,20},{20,16},{24,28},{28,24},{32,36},... | collective-permute-start | bytes 589832 | tf_op jit(solution)/shard_map/ppermute | solution.py:432
  41.9 1.5 %coarse_correlate.1 = (bf16[864,128]{1,0:T(8,128)(2,1)S(1)}, bf16[432,128]{1,0:T(8,128)(2,1)S(1)}, bf16[432,128]{1,0:T(8,128)(2,1)S(1)}) custom-call(s32[6]{0:T(128)S(1)} %convert_element_type.3.flags, bf16[192,1792]{1,0:T(8,128)(2,1)S(1)} %get-tuple-element.44.p2, bf16[128,1536]{1,0:T(8,128)(2,1)S(1)} %get-tuple-element.45.gpc), custom_call_target="tpu_custom_call" | custom-call | flops 452984832 | bytes 1081368 | tf_op jit(solution)/shard_map/coarse_correlate/pallas_call | solution.py:414
  45.4 4.6 %fine_gradient.1 = (bf16[18,64,128]{2,1,0:T(8,128)(2,1)S(1)}, bf16[18,64,128]{2,1,0:T(8,128)(2,1)S(1)}, bf16[128,16,128]{2,1,0:T(8,128)(2,1)}) custom-call(s32[6]{0:T(128)S(1)} %convert_element_type.3.flags, bf16[128,768]{1,0:T(8,128)(2,1)S(1)} %get-tuple-element.38.own, bf16[128,768]{1,0:T(8,128)(2,1)S(1)} %collective-permute-done.8.a, ...), custom_call_target="tpu_custom_call" | custom-call | flops 1207959552 | bytes 4947992 | tf_op jit(solution)/shard_map/fine_gradient/pallas_call | solution.py:414
  50.0 21.6 %all-to-all-start = ((bf16[128,16,128]{2,1,0:T(8,128)(2,1)}), bf16[128,16,128]{2,1,0:T(8,128)(2,1)S(1)}, u32[]{:S(2)}, u32[]{:S(2)}) async-start(bf16[128,16,128]{2,1,0:T(8,128)(2,1)} %get-tuple-element.52), calls=%async_computation | async-start | bytes 1048576 | tf_op jit(solution)/shard_map/all_to_all | solution.py:534
  71.7 1.6 %collective-permute-start.12 = (bf16[18,64,128]{2,1,0:T(8,128)(2,1)S(1)}, bf16[18,64,128]{2,1,0:T(8,128)(2,1)S(1)}, u32[]{:S(2)}, u32[]{:S(2)}) collective-permute-start(bf16[18,64,128]{2,1,0:T(8,128)(2,1)S(1)} %get-tuple-element.49.first), channel_id=1, source_target_pairs={{0,4},{4,0},{8,12},{12,8},{16,20},{20,16},{24,28},{28,24},{32,36},... | collective-permute-start | bytes 884744 | tf_op jit(solution)/shard_map/ppermute | solution.py:432
  73.9 11.3 %all-to-all-done.parts = bf16[128,16,128]{2,1,0:T(8,128)(2,1)S(1)} async-done(((bf16[128,16,128]{2,1,0:T(8,128)(2,1)}), bf16[128,16,128]{2,1,0:T(8,128)(2,1)S(1)}, u32[]{:S(2)}, u32[]{:S(2)}) %all-to-all-start) | async-done | bytes 524320 | tf_op jit(solution)/shard_map/all_to_all | solution.py:534
  85.3 1.0 sum_shares.1
  86.3 4.7 %all-to-all-start.1 = ((bf16[128,24,128]{2,1,0:T(8,128)(2,1)}), bf16[128,24,128]{2,1,0:T(8,128)(2,1)S(1)}, u32[]{:S(2)}, u32[]{:S(2)}) async-start(bf16[128,24,128]{2,1,0:T(8,128)(2,1)} %sum_shares.1), calls=%async_computation.1 | async-start | bytes 1572864 | tf_op jit(solution)/shard_map/all_to_all | solution.py:542
  91.0 3.0 %input_gradient.1 = bf16[2,16,64,128]{3,2,1,0:T(8,128)(2,1)} custom-call(s32[6]{0:T(128)S(1)} %convert_element_type.3.flags, bf16[18,64,128]{2,1,0:T(8,128)(2,1)S(1)} %get-tuple-element.49.first, bf16[18,64,128]{2,1,0:T(8,128)(2,1)S(1)} %get-tuple-element.50.second, bf16[18,64,128]{2,1,0:T(8,128)(2,1)S(1)} %collective-permute-done.12.a, ...), custom_call_target="tpu_custom_call" | custom-call | flops 24159191040 | bytes 1769496 | tf_op jit(solution)/shard_map/input_gradient/pallas_call | solution.py:414
  93.9 13.0 %all-to-all-done.1.got = bf16[128,24,128]{2,1,0:T(8,128)(2,1)S(1)} async-done(((bf16[128,24,128]{2,1,0:T(8,128)(2,1)}), bf16[128,24,128]{2,1,0:T(8,128)(2,1)S(1)}, u32[]{:S(2)}, u32[]{:S(2)}) %all-to-all-start.1) | async-done | bytes 786464 | tf_op jit(solution)/shard_map/all_to_all | solution.py:542
  107.0 1.4 %unpack.1 = (f32[3,3,3,64,64]{4,3,2,1,0:T(8,128)}, f32[3,3,3,64,128]{4,3,2,1,0:T(8,128)}) custom-call(bf16[128,24,128]{2,1,0:T(8,128)(2,1)S(1)} %all-to-all-done.1.got), custom_call_target="tpu_custom_call" | custom-call | bytes 786432 | tf_op jit(solution)/shard_map/unpack/pallas_call | solution.py:414
  (35 shorter events, 6.8 us)
Async XLA Ops:
  0.6 7.5 %copy-start.1 = (bf16[2,16,64,128]{3,2,1,0:T(8,128)(2,1)S(1)}, bf16[2,16,64,128]{3,2,1,0:T(8,128)(2,1)}, u32[]{:S(2)}) copy-start(bf16[2,16,64,128]{3,2,1,0:T(8,128)(2,1)} %own.3) | copy-start | bytes 1572868
  0.6 7.5 %copy-start = (bf16[2,16,64,128]{3,2,1,0:T(8,128)(2,1)S(1)}, bf16[2,16,64,128]{3,2,1,0:T(8,128)(2,1)}, u32[]{:S(2)}) copy-start(bf16[2,16,64,128]{3,2,1,0:T(8,128)(2,1)} %fc.3) | copy-start | bytes 1572868
  0.7 19.0 %copy-start.2 = (bf16[3,3,3,64,64]{4,3,2,1,0:T(8,128)(2,1)S(1)}, bf16[3,3,3,64,64]{4,3,2,1,0:T(8,128)(2,1)}, u32[]{:S(2)}) copy-start(bf16[3,3,3,64,64]{4,3,2,1,0:T(8,128)(2,1)} %wf.1) | copy-start | bytes 663556
  0.7 19.0 %copy-start.3 = (bf16[3,3,3,64,128]{4,3,2,1,0:T(8,128)(2,1)S(1)}, bf16[3,3,3,64,128]{4,3,2,1,0:T(8,128)(2,1)}, u32[]{:S(2)}) copy-start(bf16[3,3,3,64,128]{4,3,2,1,0:T(8,128)(2,1)} %wc.1) | copy-start | bytes 1327108
  1.9 13.0 %collective-permute-start.1 = (bf16[16,64,128]{2,1,0:T(8,128)(2,1)S(1)}, bf16[16,64,128]{2,1,0:T(8,128)(2,1)S(1)}, u32[]{:S(2)}, u32[]{:S(2)}) collective-permute-start(bf16[16,64,128]{2,1,0:T(8,128)(2,1)S(1)} %get-tuple-element.55), channel_id=1, source_target_pairs={{0,0},{124,124},{4,8},{8,4},{12,16},{16,12},{20,24},{24,20},{28,32... | collective-permute-start | bytes 786440 | tf_op jit(solution)/shard_map/ppermute | solution.py:431
  2.6 12.3 %collective-permute-start = (bf16[16,64,128]{2,1,0:T(8,128)(2,1)S(1)}, bf16[16,64,128]{2,1,0:T(8,128)(2,1)S(1)}, u32[]{:S(2)}, u32[]{:S(2)}) collective-permute-start(bf16[16,64,128]{2,1,0:T(8,128)(2,1)S(1)} %get-tuple-element.56), channel_id=1, source_target_pairs={{0,4},{4,0},{8,12},{12,8},{16,20},{20,16},{24,28},{28,24},{32,36},... | collective-permute-start | bytes 786440 | tf_op jit(solution)/shard_map/ppermute | solution.py:432
  8.1 0.9 copy-start.4
  10.4 12.5 %collective-permute-start.2 = (bf16[18,64,128]{2,1,0:T(8,128)(2,1)S(1)}, bf16[18,64,128]{2,1,0:T(8,128)(2,1)S(1)}, u32[]{:S(2)}, u32[]{:S(2)}) collective-permute-start(bf16[18,64,128]{2,1,0:T(8,128)(2,1)S(1)} %get-tuple-element.32), channel_id=1, source_target_pairs={{0,1},{1,0},{2,3},{3,2},{4,5},{5,4},{6,7},{7,6},{8,9},{9,8},{10,11... | collective-permute-start | bytes 884744 | tf_op jit(solution)/shard_map/ppermute | solution.py:432
  11.8 11.2 %collective-permute-start.3 = (bf16[18,64,128]{2,1,0:T(8,128)(2,1)S(1)}, bf16[18,64,128]{2,1,0:T(8,128)(2,1)S(1)}, u32[]{:S(2)}, u32[]{:S(2)}) collective-permute-start(bf16[18,64,128]{2,1,0:T(8,128)(2,1)S(1)} %get-tuple-element.33), channel_id=1, source_target_pairs={{0,0},{3,3},{1,2},{2,1},{4,4},{7,7},{5,6},{6,5},{8,8},{11,11},{9,1... | collective-permute-start | bytes 884744 | tf_op jit(solution)/shard_map/ppermute | solution.py:431
  16.1 6.9 %collective-permute-start.4 = (bf16[14,64,128]{2,1,0:T(8,128)(2,1)S(1)}, bf16[14,64,128]{2,1,0:T(8,128)(2,1)S(1)}, u32[]{:S(2)}, u32[]{:S(2)}) collective-permute-start(bf16[14,64,128]{2,1,0:T(8,128)(2,1)S(1)} %get-tuple-element.34), channel_id=1, source_target_pairs={{0,1},{1,0},{2,3},{3,2},{4,5},{5,4},{6,7},{7,6},{8,9},{9,8},{10,11... | collective-permute-start | bytes 688136 | tf_op jit(solution)/shard_map/ppermute | solution.py:432
  16.5 7.3 %collective-permute-start.5 = (bf16[14,64,128]{2,1,0:T(8,128)(2,1)S(1)}, bf16[14,64,128]{2,1,0:T(8,128)(2,1)S(1)}, u32[]{:S(2)}, u32[]{:S(2)}) collective-permute-start(bf16[14,64,128]{2,1,0:T(8,128)(2,1)S(1)} %get-tuple-element.35), channel_id=1, source_target_pairs={{0,0},{3,3},{1,2},{2,1},{4,4},{7,7},{5,6},{6,5},{8,8},{11,11},{9,1... | collective-permute-start | bytes 688136 | tf_op jit(solution)/shard_map/ppermute | solution.py:431
  23.8 8.9 %copy-start.5 = (bf16[1,8,128,64]{2,3,1,0:T(8,128)(2,1)S(1)}, bf16[1,8,128,64]{2,3,1,0:T(8,128)(2,1)}, u32[]{:S(2)}) copy-start(bf16[1,8,128,64]{2,3,1,0:T(8,128)(2,1)} %param.7) | copy-start | bytes 393220
  27.1 3.5 %collective-permute-start.7 = (bf16[64,896]{1,0:T(8,128)(2,1)S(1)}, bf16[64,896]{1,0:T(8,128)(2,1)S(1)}, u32[]{:S(2)}, u32[]{:S(2)}) collective-permute-start(bf16[64,896]{1,0:T(8,128)(2,1)S(1)} %get-tuple-element.36.own), channel_id=1, source_target_pairs={{0,0},{124,124},{4,8},{8,4},{12,16},{16,12},{20,24},{24,20},{28,32... | collective-permute-start | bytes 344072 | tf_op jit(solution)/shard_map/ppermute | solution.py:431
  27.8 5.0 %collective-permute-start.6 = (bf16[64,896]{1,0:T(8,128)(2,1)S(1)}, bf16[64,896]{1,0:T(8,128)(2,1)S(1)}, u32[]{:S(2)}, u32[]{:S(2)}) collective-permute-start(bf16[64,896]{1,0:T(8,128)(2,1)S(1)} %get-tuple-element.36.own), channel_id=1, source_target_pairs={{0,4},{4,0},{8,12},{12,8},{16,20},{20,16},{24,28},{28,24},{32,36},... | collective-permute-start | bytes 344072 | tf_op jit(solution)/shard_map/ppermute | solution.py:432
  35.0 10.1 %collective-permute-start.9 = (bf16[128,768]{1,0:T(8,128)(2,1)S(1)}, bf16[128,768]{1,0:T(8,128)(2,1)S(1)}, u32[]{:S(2)}, u32[]{:S(2)}) collective-permute-start(bf16[128,768]{1,0:T(8,128)(2,1)S(1)} %get-tuple-element.38.own), channel_id=1, source_target_pairs={{0,0},{124,124},{4,8},{8,4},{12,16},{16,12},{20,24},{24,20},{28,32... | collective-permute-start | bytes 589832 | tf_op jit(solution)/shard_map/ppermute | solution.py:431
  35.6 9.8 %collective-permute-start.8 = (bf16[128,768]{1,0:T(8,128)(2,1)S(1)}, bf16[128,768]{1,0:T(8,128)(2,1)S(1)}, u32[]{:S(2)}, u32[]{:S(2)}) collective-permute-start(bf16[128,768]{1,0:T(8,128)(2,1)S(1)} %get-tuple-element.38.own), channel_id=1, source_target_pairs={{0,4},{4,0},{8,12},{12,8},{16,20},{20,16},{24,28},{28,24},{32,36},... | collective-permute-start | bytes 589832 | tf_op jit(solution)/shard_map/ppermute | solution.py:432
  43.4 1.4 %collective-permute-start.10 = (bf16[432,128]{1,0:T(8,128)(2,1)S(1)}, bf16[432,128]{1,0:T(8,128)(2,1)S(1)}, u32[]{:S(2)}, u32[]{:S(2)}) collective-permute-start(bf16[432,128]{1,0:T(8,128)(2,1)S(1)} %get-tuple-element.47), channel_id=1, source_target_pairs={{0,1},{1,0},{2,3},{3,2},{4,5},{5,4},{6,7},{7,6},{8,9},{9,8},{10,11... | collective-permute-start | bytes 331784 | tf_op jit(solution)/shard_map/ppermute | solution.py:504
  43.5 1.6 %collective-permute-start.11 = (bf16[432,128]{1,0:T(8,128)(2,1)S(1)}, bf16[432,128]{1,0:T(8,128)(2,1)S(1)}, u32[]{:S(2)}, u32[]{:S(2)}) collective-permute-start(bf16[432,128]{1,0:T(8,128)(2,1)S(1)} %get-tuple-element.48), channel_id=1, source_target_pairs={{0,1},{1,0},{2,3},{3,2},{4,5},{5,4},{6,7},{7,6},{8,9},{9,8},{10,11... | collective-permute-start | bytes 331784 | tf_op jit(solution)/shard_map/ppermute | solution.py:504
  50.0 35.2 %all-to-all-start = ((bf16[128,16,128]{2,1,0:T(8,128)(2,1)}), bf16[128,16,128]{2,1,0:T(8,128)(2,1)S(1)}, u32[]{:S(2)}, u32[]{:S(2)}) async-start(bf16[128,16,128]{2,1,0:T(8,128)(2,1)} %get-tuple-element.52), calls=%async_computation | async-start | bytes 1048576 | tf_op jit(solution)/shard_map/all_to_all | solution.py:534
  71.7 19.3 %collective-permute-start.12 = (bf16[18,64,128]{2,1,0:T(8,128)(2,1)S(1)}, bf16[18,64,128]{2,1,0:T(8,128)(2,1)S(1)}, u32[]{:S(2)}, u32[]{:S(2)}) collective-permute-start(bf16[18,64,128]{2,1,0:T(8,128)(2,1)S(1)} %get-tuple-element.49.first), channel_id=1, source_target_pairs={{0,4},{4,0},{8,12},{12,8},{16,20},{20,16},{24,28},{28,24},{32,36},... | collective-permute-start | bytes 884744 | tf_op jit(solution)/shard_map/ppermute | solution.py:432
  73.3 17.7 %collective-permute-start.13 = (bf16[18,64,128]{2,1,0:T(8,128)(2,1)S(1)}, bf16[18,64,128]{2,1,0:T(8,128)(2,1)S(1)}, u32[]{:S(2)}, u32[]{:S(2)}) collective-permute-start(bf16[18,64,128]{2,1,0:T(8,128)(2,1)S(1)} %get-tuple-element.50.second), channel_id=1, source_target_pairs={{0,0},{124,124},{4,8},{8,4},{12,16},{16,12},{20,24},{24,20},{28,32... | collective-permute-start | bytes 884744 | tf_op jit(solution)/shard_map/ppermute | solution.py:431
  86.3 20.7 %all-to-all-start.1 = ((bf16[128,24,128]{2,1,0:T(8,128)(2,1)}), bf16[128,24,128]{2,1,0:T(8,128)(2,1)S(1)}, u32[]{:S(2)}, u32[]{:S(2)}) async-start(bf16[128,24,128]{2,1,0:T(8,128)(2,1)} %sum_shares.1), calls=%async_computation.1 | async-start | bytes 1572864 | tf_op jit(solution)/shard_map/all_to_all | solution.py:542

commit v4 on v3

--- a/solution.py
+++ b/solution.py
@@ -20,20 +20,20 @@
     return lax.broadcasted_iota(jnp.int32, shape, dim)
 
 
-def shifted(tile, by, lane):
+def shifted(tile, by, lane, width=L):
     out = pltpu.roll(tile, by % L, 1)
-    keep = lane >= by if by > 0 else lane < L + by
-    return jnp.where(keep, out, 0.0)
-
-
-def combine(acc, rows, tiles, step, lane):
+    z = lane % width
+    return jnp.where(z >= by if by > 0 else z < width + by, out, 0.0)
+
+
+def combine(acc, rows, tiles, lane, width=L):
     out = []
     for t in range(tiles):
         part = acc[:, t * L : (t + 1) * L]
         out.append(
-            shifted(part[:rows], step, lane)
+            shifted(part[:rows], 1, lane, width)
             + part[rows : 2 * rows]
-            + shifted(part[2 * rows :], -step, lane)
+            + shifted(part[2 * rows :], -1, lane, width)
         )
     return out
 
@@ -60,27 +60,32 @@
     return tile if ok is None else jnp.where(ok, tile, jnp.zeros_like(tile))
 
 
-def pool_matrix():
-    row, col = iota((1024, L), 0), iota((1024, L), 1)
-    return jnp.where(col == ((row // 256) % 2) * 64 + (row % L) // 2, 1.0, 0.0).astype(BF)
+def pack_matrix():
+    row, col = iota((2 * L, L), 0), iota((2 * L, L), 1)
+    keep = (row % 2 == 0) & (col == (row // L) * 64 + (row % L) // 2)
+    return jnp.where(keep, 1.0, 0.0).astype(BF)
 
 
 def taps(ref, at, tiles):
     return jnp.concatenate([ref[:, (at + j) * L : (at + j + tiles) * L] for j in range(3)], axis=0)
 
 
-def forward_chunk(weight, window, at, lane, pool):
-    acc = dot(weight[...], taps(window, at, 4))
-    acts, slopes_ = [], []
-    for pre in combine(acc, 128, 4, 1, lane):
+def forward(weight, cells, tiles, lane):
+    acc = dot(weight[...], cells)
+    sums, slps = [], []
+    for pre in combine(acc, 128, tiles, lane):
         sig, slp = slopes(pre)
-        acts.append((pre * sig).astype(BF))
-        slopes_.append(slp)
-    cells = jnp.concatenate([a[:64] for a in acts] + [a[64:] for a in acts], axis=1)
-    return slopes_, dot(cells, pool) * 0.125
-
-
-def prepare_kernel(wf, wc, wfwd, wbwd, cfwd, cbwd):
+        act = (pre * sig).astype(BF).astype(F32)
+        sums.append(act[:64] + act[64:])
+        slps.append(slp)
+    means = []
+    for t in range(0, tiles, 2):
+        total = sums[t] + sums[t + 1]
+        means.append(((total + pltpu.roll(total, L - 1, 1)) * 0.125).astype(BF))
+    return slps, means
+
+
+def prepare_kernel(wf, wc, wfwd, wbwd, cfwd, cown, cpart):
     def fine(i, j, k):
         return wf[i, j, k] if 0 <= i < 3 else jnp.zeros((64, 64), BF)
 
@@ -100,9 +105,10 @@
         full = jnp.concatenate([wc[i, j, k] for j in range(3) for i in range(3)], axis=0)
         cfwd[k * 128 : (k + 1) * 128, :] = full.astype(F32).T.astype(BF)
         for j in range(3):
-            for i in range(3):
-                at = (3 * j + i) * L
-                cbwd[k * 64 : (k + 1) * 64, at : at + L] = wc[2 - i, 2 - j, 2 - k]
+            at = slice(j * L, (j + 1) * L)
+            cown[k * 64 : (k + 1) * 64, at] = wc[1, 2 - j, 2 - k]
+            cpart[k * 128 : k * 128 + 64, at] = wc[2, 2 - j, 2 - k]
+            cpart[k * 128 + 64 : (k + 1) * 128, at] = wc[0, 2 - j, 2 - k]
 
 
 def start_and_wait(pairs, sems):
@@ -124,13 +130,11 @@
     start_and_wait(pairs, sems)
 
 
-def corner_edges_kernel(flags, xa, xb, first, second, sems):
-    pairs = []
+def corner_edges_kernel(flags, xa, xb, first, second):
     for out, up in ((first, flags[5]), (second, 1 - flags[5])):
-        y = up * (16 - YH)
-        pairs.append((xa.at[pl.ds(y, YH)], out.at[0:YH]))
-        pairs.append((xb.at[pl.ds(y, YH)], out.at[YH : 2 * YH]))
-    start_and_wait(pairs, sems)
+        for n in range(YH):
+            out[n] = xa[up * (16 - YH) + n]
+            out[YH + n] = xb[up * (16 - YH) + n]
 
 
 def interior_kernel(flags, own, xa, xb, weight, v2, slope, pooled):
@@ -141,20 +145,19 @@
         v2[64:128, at] = own[0, y]
         v2[128:192, at] = own[1, y]
         v2[192:256, at] = take(f[1], pick(f[4], xa[y], xb[y]))
-    lane, pool = iota((128, L), 1), pool_matrix()
-    for t in range(3):
-        slps, mean = forward_chunk(weight, v2, 4 * t + 1, lane, pool)
-        for n in range(4):
-            slope[:, (4 * t + n) * L : (4 * t + n + 1) * L] = slps[n]
-        pooled[:, t * L : (t + 1) * L] = mean.astype(BF)
+    lane = iota((128, L), 1)
+    slps, means = forward(weight, taps(v2, 1, 12), 12, lane)
+    for n in range(12):
+        slope[:, n * L : (n + 1) * L] = slps[n]
+    for t in range(6):
+        pooled[:, t * L : (t + 1) * L] = means[t]
 
 
 def border_kernel(
     flags, v2, mid, aa, ab, ba, bb, weight, slope_lo, slope_hi, pooled, vedge, window
 ):
     f = [flags[i] > 0 for i in range(6)]
-    lane, lane64, pool = iota((128, L), 1), iota((64, L), 1), pool_matrix()
-    pooled[:, 2 * L : 5 * L] = mid[...]
+    lane = iota((128, L), 1)
     for side, ok in enumerate((f[2], f[3])):
         even = f[5] if side == 1 else jnp.logical_not(f[5])
         win = window.at[side]
@@ -172,79 +175,81 @@
         else:
             win[:, : 3 * L] = v2[:, 13 * L :]
             vedge[:, L:] = win[:, 3 * L : 4 * L]
-        for u in range(2):
-            slps, mean = forward_chunk(weight, win, 4 * u, lane, pool)
-            if side == 0 and u == 1:
-                for n in range(3):
-                    slope_lo[:, n * L : (n + 1) * L] = slps[n + 1]
-            if side == 1 and u == 0:
-                for n in range(3):
-                    slope_hi[:, n * L : (n + 1) * L] = slps[n]
-            t = u if side == 0 else 5 + u
-            yc = 2 * t + lane64 // 64
-            keep = ((yc >= 3) | f[2]) & ((yc < 11) | f[3])
-            pooled[:, t * L : (t + 1) * L] = jnp.where(keep, mean, 0.0).astype(BF)
-
-
-def spread_rows(f, own, a, b, tiles, out):
-    rows = []
-    for t in range(tiles):
-        at = slice(t * L, (t + 1) * L)
-        lo, hi = pick(f[4], b[:, at], a[:, at]), pick(f[4], a[:, at], b[:, at])
-        rows += [take(f[0], lo), own[:, at], take(f[1], hi)]
-    full = dot(jnp.concatenate(rows, axis=0), spread_matrix()).astype(BF)
-    n = full.shape[0] // tiles
-    for t in range(tiles):
-        out[:, 2 * t * L : (2 * t + 2) * L] = full[t * n : (t + 1) * n]
-
-
-def coarse_kernel(flags, own, a, b, aa, cot, ab, weight, p2, gpc, gpack):
+    both = jnp.concatenate([taps(window.at[side], 0, 8) for side in range(2)], axis=1)
+    slps, means = forward(weight, both, 16, lane)
+    for n in range(3):
+        slope_lo[:, n * L : (n + 1) * L] = slps[5 + n]
+        slope_hi[:, n * L : (n + 1) * L] = slps[8 + n]
+    means = (
+        [take(f[2], m) for m in means[:3]]
+        + [means[3]]
+        + [mid[:, t * L : (t + 1) * L] for t in range(6)]
+        + [means[4]]
+        + [take(f[3], m) for m in means[5:]]
+    )
+    rows = [jnp.concatenate([means[t], means[t + 6]], axis=1) for t in range(8)]
+    packed = dot(jnp.concatenate(rows, axis=0), pack_matrix()).astype(BF)
+    for t in range(8):
+        pooled[:, t * L : (t + 1) * L] = packed[t * 64 : (t + 1) * 64]
+
+
+def beside_kernel(flags, aa, cot, ab, v2, vedge, cc, vt):
     f = [flags[i] > 0 for i in range(6)]
-    spread_rows(f, own, a, b, 7, p2)
-    lane = iota((128, L), 1)
-    row, col = iota((2 * L, L), 0), iota((2 * L, L), 1)
-    pack = jnp.where(
-        (row % 2 == 0) & (col == (row // L) * 64 + (row % L) // 2), 1.0, 0.0
-    ).astype(BF)
     at = 2 * YH + 2
     tiles = (
         [take(f[2], pick(f[5], ab[at + n], aa[at + n])) for n in range(2)]
         + [cot[n] for n in range(8)]
         + [take(f[3], pick(f[5], aa[at + n], ab[at + n])) for n in range(2)]
     )
-    cc = lax.dot_general(
-        jnp.concatenate(tiles, axis=1),
-        spread_matrix()[:64, :L],
-        (((0,), (0,)), ((), ())),
-        preferred_element_type=F32,
-    )
-    acc = dot(weight[...], taps(p2, 0, 12))
-    out = []
-    for n, pre in enumerate(combine(acc, 128, 12, 2, lane)):
+    for t in range(6):
+        pair = jnp.concatenate([tiles[t], tiles[t + 6]], axis=0)
+        cc[:, t * L : (t + 1) * L] = pair.astype(F32).T
+    for y in range(18):
+        tile = vedge[:, :L] if y == 0 else vedge[:, L:] if y == 17 else v2[:, (y - 1) * L : y * L]
+        vt[y * L : (y + 1) * L, :] = tile.astype(F32).T.astype(BF)
+
+
+def coarse_kernel(flags, own, a, b, cc, weight, w_part, p2, gpc, first, second):
+    f = [flags[i] > 0 for i in range(6)]
+    p2[0:64, :] = take(f[0], pick(f[4], b[...], a[...]))
+    p2[64:128, :] = own[...]
+    p2[128:192, :] = take(f[1], pick(f[4], a[...], b[...]))
+    lane = iota((128, L), 1)
+    acc = dot(weight[...], taps(p2, 0, 6))
+    for t, pre in enumerate(combine(acc, 128, 6, lane, 64)):
         _, slp = slopes(pre)
-        out.append((cc[n * L : (n + 1) * L] * slp).astype(BF))
-        gpc[:, n * L : (n + 1) * L] = out[n]
-    pairs = jnp.concatenate(
-        [jnp.concatenate(out[2 * t : 2 * t + 2], axis=1) for t in range(6)], axis=0
-    )
-    packed = dot(pairs, pack).astype(BF)
-    for t in range(6):
-        gpack[:, t * L : (t + 1) * L] = packed[t * L : (t + 1) * L]
+        tile = (cc[:, t * L : (t + 1) * L] * slp).astype(BF)
+        gpc[:, t * L : (t + 1) * L] = tile
+        if t < 2:
+            other = pltpu.roll(tile.astype(F32), 64, 1).astype(BF)
+            gpc[:, (t + 6) * L : (t + 7) * L] = other
+    acc = dot(w_part[...], taps(gpc, 0, 6))
+    for t, val in enumerate(combine(acc, 128, 6, lane, 64)):
+        at = slice(t * L, (t + 1) * L)
+        val = val.astype(BF)
+        first[:, at] = pick(f[4], val[:64], val[64:])
+        second[:, at] = pick(f[4], val[64:], val[:64])
 
 
 def nt(a, b):
     return lax.dot_general(a, b, (((1,), (1,)), ((), ())), preferred_element_type=F32)
 
 
-def coarse_corr_kernel(scale, flags, p2, gpc, kept, sent0, sent1, g3, out):
+def coarse_corr_kernel(scale, flags, p2, gpc, w_own, own, kept, sent0, sent1, sent2, g3, out):
+    lane = iota((64, L), 1)
+    acc = dot(w_own[...], taps(gpc, 0, 6))
+    for t, val in enumerate(combine(acc, 64, 6, lane, 64)):
+        own[:, t * L : (t + 1) * L] = val
     lane = iota((128, L), 1)
-    for y in range(8):
-        tile = gpc[:, (2 + y) * L : (3 + y) * L].astype(F32)
-        at = slice(y * L, (y + 1) * L)
-        g3[0:128, at] = shifted(tile, -2, lane).astype(BF)
+    for t in range(6):
+        at = slice(t * L, (t + 1) * L)
+        tile = gpc[:, at].astype(F32)
+        if t < 2 or t > 3:
+            tile = jnp.where(lane >= 64 if t < 2 else lane < 64, tile, 0.0)
+        g3[0:128, at] = shifted(tile, -1, lane, 64).astype(BF)
         g3[128:256, at] = tile.astype(BF)
-        g3[256:384, at] = shifted(tile, 2, lane).astype(BF)
-    res = nt(taps(p2, 2, 8), g3[...]) * (0.5 * scale)
+        g3[256:384, at] = shifted(tile, 1, lane, 64).astype(BF)
+    res = nt(taps(p2, 0, 6), g3[...]) * scale
     for j in range(3):
         for k in range(3):
             at = (3 * j + k) * 192
@@ -252,14 +257,9 @@
     low, high = out[:HALF, :], out[HALF:, :]
     even = flags[5] > 0
     kept[...] = pick(even, low, high)
-    sent0[...] = pick(even, high[: HALF // 2], low[: HALF // 2])
-    sent1[...] = pick(even, high[HALF // 2 :], low[HALF // 2 :])
-
-
-def turn_kernel(v2, vedge, vt):
-    for y in range(18):
-        tile = vedge[:, :L] if y == 0 else vedge[:, L:] if y == 17 else v2[:, (y - 1) * L : y * L]
-        vt[y * L : (y + 1) * L, :] = tile.astype(F32).T.astype(BF)
+    sent = pick(even, high, low)
+    part = HALF // 3
+    sent0[...], sent1[...], sent2[...] = sent[:part], sent[part : 2 * part], sent[2 * part :]
 
 
 def gpf_kernel(
@@ -268,7 +268,6 @@
     own,
     a,
     b,
-    weight,
     fc,
     aa,
     ab,
@@ -279,18 +278,28 @@
     kept,
     got0,
     got1,
+    got2,
     first,
     second,
     mine,
-    g2,
     u3,
     pack,
 ):
     f = [flags[i] > 0 for i in range(6)]
-    spread_rows(f, own, a, b, 6, g2)
     lane = iota((64, L), 1)
-    acc = dot(weight[...], taps(g2, 0, 10))
-    for m, gp in enumerate(combine(acc, 64, 10, 2, lane)):
+    rows = []
+    for t in range(6):
+        at = slice(t * L, (t + 1) * L)
+        lo, hi = pick(f[4], b[:, at], a[:, at]), pick(f[4], a[:, at], b[:, at])
+        total = own[:, at] + take(f[0], lo).astype(F32) + take(f[1], hi).astype(F32)
+        main = total.astype(BF)
+        rest = (total - main.astype(F32)).astype(BF)
+        rows.append(jnp.concatenate([main, rest], axis=1))
+    spread = spread_matrix()
+    full = dot(jnp.concatenate(rows, axis=0), jnp.concatenate([spread, spread], axis=0))
+    gps = [full[64 * t : 64 * t + 64, :L] for t in range(6)]
+    gps += [full[64 * t : 64 * t + 64, L:] for t in range(4)]
+    for m, gp in enumerate(gps):
         add = gp * 0.125
         for n in (2 * m - 1, 2 * m):
             if not 0 <= n < 18:
@@ -334,7 +343,7 @@
     for n in range(5):
         packed = jnp.where(lane < 64, halves[2 * n], pltpu.roll(halves[2 * n + 1], 64, 1))
         pack[576 + 64 * n : 640 + 64 * n, :] = packed
-    got = jnp.concatenate([got0[...], got1[...]], axis=0)
+    got = jnp.concatenate([got0[...], got1[...], got2[...]], axis=0)
     coarse = kept[...].astype(F32) + got.astype(F32)
     none = jnp.zeros((R, L), F32)
     for n in range(128):
@@ -355,7 +364,7 @@
     lane = iota((128, L), 1)
     for t in range(4):
         acc = dot(weight[...], taps(g2, 4 * t, 4))
-        for n, val in enumerate(combine(acc, 128, 4, 1, lane)):
+        for n, val in enumerate(combine(acc, 128, 4, lane)):
             val = val.astype(BF)
             out[0, 4 * t + n] = val[:64]
             out[1, 4 * t + n] = val[64:]
@@ -454,64 +463,78 @@
         copies=10,
     )
     aa, ab = swaps(first, second, "sub")
-    w_fwd, w_bwd, c_fwd, c_bwd = call(
+    w_fwd, w_bwd, c_fwd, c_own, c_part = call(
         prepare_kernel,
         "prepare_weights",
-        (((384, 768), BF), ((384, 768), BF), ((384, 576), BF), ((192, 1152), BF)),
+        (
+            ((384, 768), BF),
+            ((384, 768), BF),
+            ((384, 576), BF),
+            ((192, 384), BF),
+            ((384, 384), BF),
+        ),
         (weight_fine, weight_coarse),
         flags=False,
     )
     corner = ((2 * YH, 64, L), BF)
     first, second = call(
-        corner_edges_kernel, "corner_edges", (corner, corner), (flags, xa, xb), copies=4
+        corner_edges_kernel, "corner_edges", (corner, corner), (flags, xa, xb)
     )
     ba, bb = swaps(first, second, "sub")
     v2, slope, mid = call(
         interior_kernel,
         "fine_forward_interior",
-        (((256, 16 * L), BF), ((128, 12 * L), F32), ((64, 3 * L), BF)),
+        (((256, 16 * L), BF), ((128, 12 * L), F32), ((64, 6 * L), BF)),
         (flags, inputs, xa, xb, w_fwd),
         macs=384 * 768 * 12 * L,
     )
     slope_lo, slope_hi, pooled, vedge = call(
         border_kernel,
         "fine_forward_border",
-        (((128, 3 * L), F32), ((128, 3 * L), F32), ((64, 7 * L), BF), ((256, 2 * L), BF)),
+        (((128, 3 * L), F32), ((128, 3 * L), F32), ((64, 8 * L), BF), ((256, 2 * L), BF)),
         (flags, v2, mid, aa, ab, ba, bb, w_fwd),
         scratch=[pltpu.VMEM((2, 256, 10 * L), BF)],
         macs=384 * 768 * 16 * L,
     )
     pa, pb = swaps(pooled, pooled, "slab")
-    vt = call(
-        turn_kernel, "turn_inputs", (((18 * L, 256), BF),), (v2, vedge), flags=False
-    )
-    p2, gpc, gpack = call(
+    cc, vt = call(
+        beside_kernel,
+        "cotangent_and_turned_inputs",
+        (((128, 6 * L), F32), ((18 * L, 256), BF)),
+        (flags, aa, cot, ab, v2, vedge),
+    )
+    p2, gpc, first, second = call(
         coarse_kernel,
         "coarse_forward",
-        (((192, 14 * L), BF), ((128, 12 * L), BF), ((128, 6 * L), BF)),
-        (flags, pooled, pa, pb, aa, cot, ab, c_fwd),
-        macs=384 * 576 * 12 * L,
-    )
-    ga, gb = swaps(gpack, gpack, "slab")
-    kept, *sent = call(
+        (
+            ((192, 8 * L), BF),
+            ((128, 8 * L), BF),
+            ((64, 6 * L), BF),
+            ((64, 6 * L), BF),
+        ),
+        (flags, pooled, pa, pb, cc, c_fwd, c_part),
+        macs=384 * 960 * 6 * L,
+    )
+    ga, gb = swaps(first, second, "slab")
+    third = ((HALF // 3, L), BF)
+    own, kept, *sent = call(
         functools.partial(coarse_corr_kernel, 1.0 / 256.0),
         "coarse_correlate",
-        (((HALF, L), BF), ((HALF // 2, L), BF), ((HALF // 2, L), BF)),
-        (flags, p2, gpc),
-        scratch=[pltpu.VMEM((384, 8 * L), BF), pltpu.VMEM((2 * HALF, L), BF)],
-        macs=384 * 576 * 8 * L,
-    )
-    got0, got1 = (lax.ppermute(part, "sub", [(0, 1), (1, 0), (2, 3), (3, 2)]) for part in sent)
+        (((64, 6 * L), F32), ((HALF, L), BF), third, third, third),
+        (flags, p2, gpc, c_own),
+        scratch=[pltpu.VMEM((384, 6 * L), BF), pltpu.VMEM((2 * HALF, L), BF)],
+        macs=384 * 768 * 6 * L,
+    )
+    got0, got1, got2 = (lax.ppermute(part, "sub", [(0, 1), (1, 0), (2, 3), (3, 2)]) for part in sent)
     first, second, mine = call(
         functools.partial(gpf_kernel, 524288.0**-0.5),
         "fine_gradient",
         (((18, 64, L), BF), ((18, 64, L), BF), ((128, 2 * R, L), BF)),
         (
             flags,
-            gpack,
+            own,
             ga,
             gb,
-            c_bwd,
             fine_cot,
             aa,
             ab,
@@ -522,9 +545,9 @@
             kept,
             got0,
             got1,
+            got2,
         ),
         scratch=[
-            pltpu.VMEM((384, 12 * L), BF),
             pltpu.VMEM((384, 16 * L), BF),
             pltpu.VMEM((896, L), F32),
         ],

time: 109 us -> 105 us (0.963)
  Pallas kernels: 23.3 us -> 20.1 us
    pallas_call x12, Pallas kernels: 23.3 us -> 20.1 us  [call(): pl.pallas_call(kernel, out_shape=shapes, in_specs=specs, out_specs=tuple(...]
    all_to_all x1, starting transfers between devices: 21.6 us -> 24 us  [on_device(): lax.all_to_all(mine.reshape(128 * 2 * R, L), ('slab', 'sub'), 0, 0, tiled...]
    ppermute x6, starting transfers between devices: 17.8 us -> 15.6 us  [swaps(): return (lax.ppermute(first, axis, pairs), other)]
    ppermute x6, waiting for transfers between devices: 2.54 us -> 0.71 us  [swaps(): return (lax.ppermute(first, axis, pairs), other)]
  transfers between devices with their start and end apart: 16 -> 17, of which waited for: 7 -> 7; matrix products, arithmetic and copies ran while one was open for 0% -> 0% of each run, Pallas kernels for 11% -> 11%
where the time goes in v4:
time: 105 us
  starting transfers between devices  53.7 us (51%)
  waiting for transfers between devices  27.9 us (27%)
  Pallas kernels  20.1 us (19%)
  local copies, waits for them, and re-layouts  2.31 us (2%)
    all_to_all x1, starting transfers between devices, on_device(): lax.all_to_all(mine.reshape(128 * 2 * R, L), ('slab', 'sub'), 0, 0, tiled...  24 us
    pallas_call x12, Pallas kernels, call(): pl.pallas_call(kernel, out_shape=shapes, in_specs=specs, out_specs=tuple(...  20.1 us
    ppermute x6, starting transfers between devices, swaps(): return (lax.ppermute(first, axis, pairs), other)  15.6 us
    all_to_all x1, waiting for transfers between devices, on_device(): lax.all_to_all(total.reshape(128 * 3 * R, L), ('slab', 'sub'), 0, 0, tile...  13 us
    all_to_all x1, waiting for transfers between devices, on_device(): lax.all_to_all(mine.reshape(128 * 2 * R, L), ('slab', 'sub'), 0, 0, tiled...  11.3 us
    ppermute x6, starting transfers between devices, swaps(): other = lax.ppermute(second, axis, others)  8.65 us
    all_to_all x1, starting transfers between devices, on_device(): lax.all_to_all(total.reshape(128 * 3 * R, L), ('slab', 'sub'), 0, 0, tile...  4.67 us
  transfers between devices with their start and end apart: 17, of which 7 were waited for; matrix products, arithmetic and copies ran while one was open for 0% of the time, Pallas kernels for 11%

profile of v4, /device:TPU:1, one launch (start us, length us, event | category | flops | bytes accessed | tf_op | source)
XLA Modules:
  0.0 104.9 jit_solution(13178068047520564472)
XLA Ops:
  0.7 1.1 %dynamic-slice_bitcast_fusion = (bf16[16,64,128]{2,1,0:T(8,128)(2,1)S(1)}, bf16[16,64,128]{2,1,0:T(8,128)(2,1)S(1)}) fusion(bf16[2,16,64,128]{3,2,1,0:T(8,128)(2,1)} %own.3, s32[]{:T(128)S(6)} %select_n.23, s32[]{:T(128)S(6)} %select_n.22), kind=kLoop, calls=%fused_computation | loop fusion | bytes 1048584 | tf_op jit(solution)/shard_map/jit(dynamic_index_in_dim)/squeeze | solution.py:454
  1.8 2.5 %collective-permute-start = (bf16[16,64,128]{2,1,0:T(8,128)(2,1)S(1)}, bf16[16,64,128]{2,1,0:T(8,128)(2,1)S(1)}, u32[]{:S(2)}, u32[]{:S(2)}) collective-permute-start(bf16[16,64,128]{2,1,0:T(8,128)(2,1)S(1)} %get-tuple-element.68), channel_id=1, source_target_pairs={{0,4},{4,0},{8,12},{12,8},{16,20},{20,16},{24,28},{28,24},{32,36},... | collective-permute-start | bytes 786440 | tf_op jit(solution)/shard_map/ppermute | solution.py:441
  5.2 1.0 copy-done.2
  6.2 1.4 %own_edges.1 = (bf16[18,64,128]{2,1,0:T(8,128)(2,1)S(1)}, bf16[18,64,128]{2,1,0:T(8,128)(2,1)S(1)}) custom-call(s32[6]{0:T(128)S(1)} %convert_element_type.3.flags, bf16[2,16,64,128]{3,2,1,0:T(8,128)(2,1)S(1)} %copy-done, bf16[2,16,64,128]{3,2,1,0:T(8,128)(2,1)S(1)} %copy-done.2, bf16[8,64,128]{2,1,0:T(8,128)(2,1)S(1)} %bitcast.13), custom_call_target="tpu_custom_call" | custom-call | bytes 1179672 | tf_op jit(solution)/shard_map/own_edges/pallas_call | solution.py:423
  7.7 1.0 collective-permute-start.2
  8.7 3.1 %collective-permute-start.3 = (bf16[18,64,128]{2,1,0:T(8,128)(2,1)S(1)}, bf16[18,64,128]{2,1,0:T(8,128)(2,1)S(1)}, u32[]{:S(2)}, u32[]{:S(2)}) collective-permute-start(bf16[18,64,128]{2,1,0:T(8,128)(2,1)S(1)} %get-tuple-element.39), channel_id=1, source_target_pairs={{0,0},{3,3},{1,2},{2,1},{4,4},{7,7},{5,6},{6,5},{8,8},{11,11},{9,1... | collective-permute-start | bytes 884744 | tf_op jit(solution)/shard_map/ppermute | solution.py:440
  12.5 2.9 %collective-permute-start.5 = (bf16[14,64,128]{2,1,0:T(8,128)(2,1)S(1)}, bf16[14,64,128]{2,1,0:T(8,128)(2,1)S(1)}, u32[]{:S(2)}, u32[]{:S(2)}) collective-permute-start(bf16[14,64,128]{2,1,0:T(8,128)(2,1)S(1)} %get-tuple-element.41), channel_id=1, source_target_pairs={{0,0},{3,3},{1,2},{2,1},{4,4},{7,7},{5,6},{6,5},{8,8},{11,11},{9,1... | collective-permute-start | bytes 688136 | tf_op jit(solution)/shard_map/ppermute | solution.py:440
  16.1 2.0 %fine_forward_interior.1 = (bf16[256,2048]{1,0:T(8,128)(2,1)S(1)}, f32[128,1536]{1,0:T(8,128)S(1)}, bf16[64,768]{1,0:T(8,128)(2,1)S(1)}) custom-call(s32[6]{0:T(128)S(1)} %convert_element_type.3.flags, bf16[2,16,64,128]{3,2,1,0:T(8,128)(2,1)S(1)} %copy-done, bf16[16,64,128]{2,1,0:T(8,128)(2,1)S(1)} %collective-permute-done.xa, ...), custom_call_target="tpu_custom_call" | custom-call | flops 905969664 | bytes 1638424 | tf_op jit(solution)/shard_map/fine_forward_interior/pallas_call | solution.py:423
  18.2 1.7 %collective-permute-done.5.bb = bf16[14,64,128]{2,1,0:T(8,128)(2,1)S(1)} collective-permute-done((bf16[14,64,128]{2,1,0:T(8,128)(2,1)S(1)}, bf16[14,64,128]{2,1,0:T(8,128)(2,1)S(1)}, u32[]{:S(2)}, u32[]{:S(2)}) %collective-permute-start.5) | collective-permute-done | bytes 229408 | tf_op jit(solution)/shard_map/ppermute | solution.py:440
  19.9 2.5 %fine_forward_border.1 = (f32[128,384]{1,0:T(8,128)S(1)}, f32[128,384]{1,0:T(8,128)S(1)}, bf16[64,1024]{1,0:T(8,128)(2,1)S(1)}, bf16[256,256]{1,0:T(8,128)(2,1)S(1)}) custom-call(s32[6]{0:T(128)S(1)} %convert_element_type.3.flags, bf16[256,2048]{1,0:T(8,128)(2,1)S(1)} %get-tuple-element.36.v2, bf16[64,768]{1,0:T(8,128)(2,1)S(1)} %get-tuple-element.37.mid, ...), custom_call_target="tpu_custom_call" | custom-call | flops 1207959552 | bytes 2785304 | tf_op jit(solution)/shard_map/fine_forward_border/pallas_call | solution.py:423
  22.3 4.7 %collective-permute-start.6 = (bf16[64,1024]{1,0:T(8,128)(2,1)S(1)}, bf16[64,1024]{1,0:T(8,128)(2,1)S(1)}, u32[]{:S(2)}, u32[]{:S(2)}) collective-permute-start(bf16[64,1024]{1,0:T(8,128)(2,1)S(1)} %get-tuple-element.42.own), channel_id=1, source_target_pairs={{0,4},{4,0},{8,12},{12,8},{16,20},{20,16},{24,28},{28,24},{32,36},... | collective-permute-start | bytes 393224 | tf_op jit(solution)/shard_map/ppermute | solution.py:441
  27.7 1.0 cotangent_and_turned_inputs.1
  29.4 1.8 %coarse_forward.1 = (bf16[192,1024]{1,0:T(8,128)(2,1)S(1)}, bf16[128,1024]{1,0:T(8,128)(2,1)S(1)}, bf16[64,768]{1,0:T(8,128)(2,1)S(1)}, bf16[64,768]{1,0:T(8,128)(2,1)S(1)}) custom-call(s32[6]{0:T(128)S(1)} %convert_element_type.3.flags, bf16[64,1024]{1,0:T(8,128)(2,1)S(1)} %get-tuple-element.42.own, bf16[64,1024]{1,0:T(8,128)(2,1)S(1)} %collective-permute-done.6.a, ...), custom_call_target="tpu_custom_call" | custom-call | flops 566231040 | bytes 1523736 | tf_op jit(solution)/shard_map/coarse_forward/pallas_call | solution.py:423
  31.3 5.6 %collective-permute-start.8 = (bf16[64,768]{1,0:T(8,128)(2,1)S(1)}, bf16[64,768]{1,0:T(8,128)(2,1)S(1)}, u32[]{:S(2)}, u32[]{:S(2)}) collective-permute-start(bf16[64,768]{1,0:T(8,128)(2,1)S(1)} %get-tuple-element.51), channel_id=1, source_target_pairs={{0,4},{4,0},{8,12},{12,8},{16,20},{20,16},{24,28},{28,24},{32,36},... | collective-permute-start | bytes 294920 | tf_op jit(solution)/shard_map/ppermute | solution.py:441
  37.6 1.4 %coarse_correlate.1 = (f32[64,768]{1,0:T(8,128)S(1)}, bf16[864,128]{1,0:T(8,128)(2,1)S(1)}, bf16[288,128]{1,0:T(8,128)(2,1)S(1)}, bf16[288,128]{1,0:T(8,128)(2,1)S(1)}, bf16[288,128]{1,0:T(8,128)(2,1)S(1)}) custom-call(s32[6]{0:T(128)S(1)} %convert_element_type.3.flags, bf16[192,1024]{1,0:T(8,128)(2,1)S(1)} %get-tuple-element.47.p2, ...), custom_call_target="tpu_custom_call" | custom-call | flops 452984832 | bytes 802840 | tf_op jit(solution)/shard_map/coarse_correlate/pallas_call | solution.py:423
  40.9 3.4 %fine_gradient.1 = (bf16[18,64,128]{2,1,0:T(8,128)(2,1)S(1)}, bf16[18,64,128]{2,1,0:T(8,128)(2,1)S(1)}, bf16[128,16,128]{2,1,0:T(8,128)(2,1)}) custom-call(s32[6]{0:T(128)S(1)} %convert_element_type.3.flags, f32[64,768]{1,0:T(8,128)S(1)} %get-tuple-element.50.own, bf16[64,768]{1,0:T(8,128)(2,1)S(1)} %collective-permute-done.8.a, ...), custom_call_target="tpu_custom_call" | custom-call | flops 1207959552 | bytes 4309016 | tf_op jit(solution)/shard_map/fine_gradient/pallas_call | solution.py:423
  44.2 24.0 %all-to-all-start = ((bf16[128,16,128]{2,1,0:T(8,128)(2,1)}), bf16[128,16,128]{2,1,0:T(8,128)(2,1)S(1)}, u32[]{:S(2)}, u32[]{:S(2)}) async-start(bf16[128,16,128]{2,1,0:T(8,128)(2,1)} %get-tuple-element.64), calls=%async_computation | async-start | bytes 1048576 | tf_op jit(solution)/shard_map/all_to_all | solution.py:557
  68.2 1.6 %collective-permute-start.13 = (bf16[18,64,128]{2,1,0:T(8,128)(2,1)S(1)}, bf16[18,64,128]{2,1,0:T(8,128)(2,1)S(1)}, u32[]{:S(2)}, u32[]{:S(2)}) collective-permute-start(bf16[18,64,128]{2,1,0:T(8,128)(2,1)S(1)} %get-tuple-element.61.first), channel_id=1, source_target_pairs={{0,4},{4,0},{8,12},{12,8},{16,20},{20,16},{24,28},{28,24},{32,36},... | collective-permute-start | bytes 884744 | tf_op jit(solution)/shard_map/ppermute | solution.py:441
  70.5 11.3 %all-to-all-done.parts = bf16[128,16,128]{2,1,0:T(8,128)(2,1)S(1)} async-done(((bf16[128,16,128]{2,1,0:T(8,128)(2,1)}), bf16[128,16,128]{2,1,0:T(8,128)(2,1)S(1)}, u32[]{:S(2)}, u32[]{:S(2)}) %all-to-all-start) | async-done | bytes 524320 | tf_op jit(solution)/shard_map/all_to_all | solution.py:557
  81.8 1.0 sum_shares.1
  82.8 4.7 %all-to-all-start.1 = ((bf16[128,24,128]{2,1,0:T(8,128)(2,1)}), bf16[128,24,128]{2,1,0:T(8,128)(2,1)S(1)}, u32[]{:S(2)}, u32[]{:S(2)}) async-start(bf16[128,24,128]{2,1,0:T(8,128)(2,1)} %sum_shares.1), calls=%async_computation.1 | async-start | bytes 1572864 | tf_op jit(solution)/shard_map/all_to_all | solution.py:565
  87.5 3.0 %input_gradient.1 = bf16[2,16,64,128]{3,2,1,0:T(8,128)(2,1)} custom-call(s32[6]{0:T(128)S(1)} %convert_element_type.3.flags, bf16[18,64,128]{2,1,0:T(8,128)(2,1)S(1)} %get-tuple-element.61.first, bf16[18,64,128]{2,1,0:T(8,128)(2,1)S(1)} %get-tuple-element.62.second, bf16[18,64,128]{2,1,0:T(8,128)(2,1)S(1)} %collective-permute-done.13.a, ...), custom_call_target="tpu_custom_call" | custom-call | flops 24159191040 | bytes 1769496 | tf_op jit(solution)/shard_map/input_gradient/pallas_call | solution.py:423
  90.5 13.0 %all-to-all-done.1.got = bf16[128,24,128]{2,1,0:T(8,128)(2,1)S(1)} async-done(((bf16[128,24,128]{2,1,0:T(8,128)(2,1)}), bf16[128,24,128]{2,1,0:T(8,128)(2,1)S(1)}, u32[]{:S(2)}, u32[]{:S(2)}) %all-to-all-start.1) | async-done | bytes 786464 | tf_op jit(solution)/shard_map/all_to_all | solution.py:565
  103.5 1.4 %unpack.1 = (f32[3,3,3,64,64]{4,3,2,1,0:T(8,128)}, f32[3,3,3,64,128]{4,3,2,1,0:T(8,128)}) custom-call(bf16[128,24,128]{2,1,0:T(8,128)(2,1)S(1)} %all-to-all-done.1.got), custom_call_target="tpu_custom_call" | custom-call | bytes 786432 | tf_op jit(solution)/shard_map/unpack/pallas_call | solution.py:423
  (37 shorter events, 6.7 us)
Async XLA Ops:
  0.6 4.6 %copy-start = (bf16[2,16,64,128]{3,2,1,0:T(8,128)(2,1)S(1)}, bf16[2,16,64,128]{3,2,1,0:T(8,128)(2,1)}, u32[]{:S(2)}) copy-start(bf16[2,16,64,128]{3,2,1,0:T(8,128)(2,1)} %own.3) | copy-start | bytes 1572868
  0.6 4.6 %copy-start.1 = (bf16[1,8,128,64]{2,3,1,0:T(8,128)(2,1)S(1)}, bf16[1,8,128,64]{2,3,1,0:T(8,128)(2,1)}, u32[]{:S(2)}) copy-start(bf16[1,8,128,64]{2,3,1,0:T(8,128)(2,1)} %param.7) | copy-start | bytes 393220
  0.7 14.8 %copy-start.4 = (bf16[3,3,3,64,64]{4,3,2,1,0:T(8,128)(2,1)S(1)}, bf16[3,3,3,64,64]{4,3,2,1,0:T(8,128)(2,1)}, u32[]{:S(2)}) copy-start(bf16[3,3,3,64,64]{4,3,2,1,0:T(8,128)(2,1)} %wf.1) | copy-start | bytes 663556
  1.8 10.0 %collective-permute-start = (bf16[16,64,128]{2,1,0:T(8,128)(2,1)S(1)}, bf16[16,64,128]{2,1,0:T(8,128)(2,1)S(1)}, u32[]{:S(2)}, u32[]{:S(2)}) collective-permute-start(bf16[16,64,128]{2,1,0:T(8,128)(2,1)S(1)} %get-tuple-element.68), channel_id=1, source_target_pairs={{0,4},{4,0},{8,12},{12,8},{16,20},{20,16},{24,28},{28,24},{32,36},... | collective-permute-start | bytes 786440 | tf_op jit(solution)/shard_map/ppermute | solution.py:441
  4.4 7.4 %collective-permute-start.1 = (bf16[16,64,128]{2,1,0:T(8,128)(2,1)S(1)}, bf16[16,64,128]{2,1,0:T(8,128)(2,1)S(1)}, u32[]{:S(2)}, u32[]{:S(2)}) collective-permute-start(bf16[16,64,128]{2,1,0:T(8,128)(2,1)S(1)} %get-tuple-element.67), channel_id=1, source_target_pairs={{0,0},{124,124},{4,8},{8,4},{12,16},{16,12},{20,24},{24,20},{28,32... | collective-permute-start | bytes 786440 | tf_op jit(solution)/shard_map/ppermute | solution.py:440
  5.2 1.0 copy-start.2
  6.2 9.2 %copy-start.5 = (bf16[3,3,3,64,128]{4,3,2,1,0:T(8,128)(2,1)S(1)}, bf16[3,3,3,64,128]{4,3,2,1,0:T(8,128)(2,1)}, u32[]{:S(2)}) copy-start(bf16[3,3,3,64,128]{4,3,2,1,0:T(8,128)(2,1)} %wc.1) | copy-start | bytes 1327108
  7.7 10.5 %collective-permute-start.2 = (bf16[18,64,128]{2,1,0:T(8,128)(2,1)S(1)}, bf16[18,64,128]{2,1,0:T(8,128)(2,1)S(1)}, u32[]{:S(2)}, u32[]{:S(2)}) collective-permute-start(bf16[18,64,128]{2,1,0:T(8,128)(2,1)S(1)} %get-tuple-element.38), channel_id=1, source_target_pairs={{0,1},{1,0},{2,3},{3,2},{4,5},{5,4},{6,7},{7,6},{8,9},{9,8},{10,11... | collective-permute-start | bytes 884744 | tf_op jit(solution)/shard_map/ppermute | solution.py:441
  8.7 9.4 %collective-permute-start.3 = (bf16[18,64,128]{2,1,0:T(8,128)(2,1)S(1)}, bf16[18,64,128]{2,1,0:T(8,128)(2,1)S(1)}, u32[]{:S(2)}, u32[]{:S(2)}) collective-permute-start(bf16[18,64,128]{2,1,0:T(8,128)(2,1)S(1)} %get-tuple-element.39), channel_id=1, source_target_pairs={{0,0},{3,3},{1,2},{2,1},{4,4},{7,7},{5,6},{6,5},{8,8},{11,11},{9,1... | collective-permute-start | bytes 884744 | tf_op jit(solution)/shard_map/ppermute | solution.py:440
  12.4 5.7 %collective-permute-start.4 = (bf16[14,64,128]{2,1,0:T(8,128)(2,1)S(1)}, bf16[14,64,128]{2,1,0:T(8,128)(2,1)S(1)}, u32[]{:S(2)}, u32[]{:S(2)}) collective-permute-start(bf16[14,64,128]{2,1,0:T(8,128)(2,1)S(1)} %get-tuple-element.40), channel_id=1, source_target_pairs={{0,1},{1,0},{2,3},{3,2},{4,5},{5,4},{6,7},{7,6},{8,9},{9,8},{10,11... | collective-permute-start | bytes 688136 | tf_op jit(solution)/shard_map/ppermute | solution.py:441
  12.5 7.3 %collective-permute-start.5 = (bf16[14,64,128]{2,1,0:T(8,128)(2,1)S(1)}, bf16[14,64,128]{2,1,0:T(8,128)(2,1)S(1)}, u32[]{:S(2)}, u32[]{:S(2)}) collective-permute-start(bf16[14,64,128]{2,1,0:T(8,128)(2,1)S(1)} %get-tuple-element.41), channel_id=1, source_target_pairs={{0,0},{3,3},{1,2},{2,1},{4,4},{7,7},{5,6},{6,5},{8,8},{11,11},{9,1... | collective-permute-start | bytes 688136 | tf_op jit(solution)/shard_map/ppermute | solution.py:440
  22.3 7.1 %collective-permute-start.6 = (bf16[64,1024]{1,0:T(8,128)(2,1)S(1)}, bf16[64,1024]{1,0:T(8,128)(2,1)S(1)}, u32[]{:S(2)}, u32[]{:S(2)}) collective-permute-start(bf16[64,1024]{1,0:T(8,128)(2,1)S(1)} %get-tuple-element.42.own), channel_id=1, source_target_pairs={{0,4},{4,0},{8,12},{12,8},{16,20},{20,16},{24,28},{28,24},{32,36},... | collective-permute-start | bytes 393224 | tf_op jit(solution)/shard_map/ppermute | solution.py:441
  27.1 2.4 %collective-permute-start.7 = (bf16[64,1024]{1,0:T(8,128)(2,1)S(1)}, bf16[64,1024]{1,0:T(8,128)(2,1)S(1)}, u32[]{:S(2)}, u32[]{:S(2)}) collective-permute-start(bf16[64,1024]{1,0:T(8,128)(2,1)S(1)} %get-tuple-element.42.own), channel_id=1, source_target_pairs={{0,0},{124,124},{4,8},{8,4},{12,16},{16,12},{20,24},{24,20},{28,32... | collective-permute-start | bytes 393224 | tf_op jit(solution)/shard_map/ppermute | solution.py:440
  31.3 9.6 %copy-start.3 = (bf16[2,16,64,128]{3,2,1,0:T(8,128)(2,1)S(1)}, bf16[2,16,64,128]{3,2,1,0:T(8,128)(2,1)}, u32[]{:S(2)}) copy-start(bf16[2,16,64,128]{3,2,1,0:T(8,128)(2,1)} %fc.3) | copy-start | bytes 1572868
  31.3 9.6 %collective-permute-start.8 = (bf16[64,768]{1,0:T(8,128)(2,1)S(1)}, bf16[64,768]{1,0:T(8,128)(2,1)S(1)}, u32[]{:S(2)}, u32[]{:S(2)}) collective-permute-start(bf16[64,768]{1,0:T(8,128)(2,1)S(1)} %get-tuple-element.51), channel_id=1, source_target_pairs={{0,4},{4,0},{8,12},{12,8},{16,20},{20,16},{24,28},{28,24},{32,36},... | collective-permute-start | bytes 294920 | tf_op jit(solution)/shard_map/ppermute | solution.py:441
  36.9 3.9 %collective-permute-start.9 = (bf16[64,768]{1,0:T(8,128)(2,1)S(1)}, bf16[64,768]{1,0:T(8,128)(2,1)S(1)}, u32[]{:S(2)}, u32[]{:S(2)}) collective-permute-start(bf16[64,768]{1,0:T(8,128)(2,1)S(1)} %get-tuple-element.52), channel_id=1, source_target_pairs={{0,0},{124,124},{4,8},{8,4},{12,16},{16,12},{20,24},{24,20},{28,32... | collective-permute-start | bytes 294920 | tf_op jit(solution)/shard_map/ppermute | solution.py:440
  39.0 1.3 %collective-permute-start.10 = (bf16[288,128]{1,0:T(8,128)(2,1)S(1)}, bf16[288,128]{1,0:T(8,128)(2,1)S(1)}, u32[]{:S(2)}, u32[]{:S(2)}) collective-permute-start(bf16[288,128]{1,0:T(8,128)(2,1)S(1)} %get-tuple-element.58), channel_id=1, source_target_pairs={{0,1},{1,0},{2,3},{3,2},{4,5},{5,4},{6,7},{7,6},{8,9},{9,8},{10,11... | collective-permute-start | bytes 221192 | tf_op jit(solution)/shard_map/ppermute | solution.py:528
  39.1 1.4 %collective-permute-start.11 = (bf16[288,128]{1,0:T(8,128)(2,1)S(1)}, bf16[288,128]{1,0:T(8,128)(2,1)S(1)}, u32[]{:S(2)}, u32[]{:S(2)}) collective-permute-start(bf16[288,128]{1,0:T(8,128)(2,1)S(1)} %get-tuple-element.59), channel_id=1, source_target_pairs={{0,1},{1,0},{2,3},{3,2},{4,5},{5,4},{6,7},{7,6},{8,9},{9,8},{10,11... | collective-permute-start | bytes 221192 | tf_op jit(solution)/shard_map/ppermute | solution.py:528
  39.6 1.3 %collective-permute-start.12 = (bf16[288,128]{1,0:T(8,128)(2,1)S(1)}, bf16[288,128]{1,0:T(8,128)(2,1)S(1)}, u32[]{:S(2)}, u32[]{:S(2)}) collective-permute-start(bf16[288,128]{1,0:T(8,128)(2,1)S(1)} %get-tuple-element.60), channel_id=1, source_target_pairs={{0,1},{1,0},{2,3},{3,2},{4,5},{5,4},{6,7},{7,6},{8,9},{9,8},{10,11... | collective-permute-start | bytes 221192 | tf_op jit(solution)/shard_map/ppermute | solution.py:528
  44.2 37.6 %all-to-all-start = ((bf16[128,16,128]{2,1,0:T(8,128)(2,1)}), bf16[128,16,128]{2,1,0:T(8,128)(2,1)S(1)}, u32[]{:S(2)}, u32[]{:S(2)}) async-start(bf16[128,16,128]{2,1,0:T(8,128)(2,1)} %get-tuple-element.64), calls=%async_computation | async-start | bytes 1048576 | tf_op jit(solution)/shard_map/all_to_all | solution.py:557
  68.2 19.3 %collective-permute-start.13 = (bf16[18,64,128]{2,1,0:T(8,128)(2,1)S(1)}, bf16[18,64,128]{2,1,0:T(8,128)(2,1)S(1)}, u32[]{:S(2)}, u32[]{:S(2)}) collective-permute-start(bf16[18,64,128]{2,1,0:T(8,128)(2,1)S(1)} %get-tuple-element.61.first), channel_id=1, source_target_pairs={{0,4},{4,0},{8,12},{12,8},{16,20},{20,16},{24,28},{28,24},{32,36},... | collective-permute-start | bytes 884744 | tf_op jit(solution)/shard_map/ppermute | solution.py:441
  69.8 17.7 %collective-permute-start.14 = (bf16[18,64,128]{2,1,0:T(8,128)(2,1)S(1)}, bf16[18,64,128]{2,1,0:T(8,128)(2,1)S(1)}, u32[]{:S(2)}, u32[]{:S(2)}) collective-permute-start(bf16[18,64,128]{2,1,0:T(8,128)(2,1)S(1)} %get-tuple-element.62.second), channel_id=1, source_target_pairs={{0,0},{124,124},{4,8},{8,4},{12,16},{16,12},{20,24},{24,20},{28,32... | collective-permute-start | bytes 884744 | tf_op jit(solution)/shard_map/ppermute | solution.py:440
  82.8 20.7 %all-to-all-start.1 = ((bf16[128,24,128]{2,1,0:T(8,128)(2,1)}), bf16[128,24,128]{2,1,0:T(8,128)(2,1)S(1)}, u32[]{:S(2)}, u32[]{:S(2)}) async-start(bf16[128,24,128]{2,1,0:T(8,128)(2,1)} %sum_shares.1), calls=%async_computation.1 | async-start | bytes 1572864 | tf_op jit(solution)/shard_map/all_to_all | solution.py:565

commit v5 on v4

--- a/solution.py
+++ b/solution.py
@@ -8,7 +8,7 @@
 from jax.sharding import PartitionSpec as P
 
 L = 128
-YH = 7
+YH = 5
 BF = jnp.bfloat16
 F32 = jnp.float32
 R = 8
@@ -119,14 +119,13 @@
         c.wait()
 
 
-def own_edges_kernel(flags, own, fc, cot, first, second, sems):
+def own_edges_kernel(flags, own, cot, first, second, sems):
     pairs = []
     for out, up in ((first, flags[5]), (second, 1 - flags[5])):
-        y, one, cc = up * (16 - YH), up * 15, up * 6
+        y, cc = up * (16 - YH), up * 7
         for x in range(2):
             pairs.append((own.at[x, pl.ds(y, YH)], out.at[x * YH : (x + 1) * YH]))
-            pairs.append((fc.at[x, pl.ds(one, 1)], out.at[2 * YH + x : 2 * YH + x + 1]))
-        pairs.append((cot.at[pl.ds(cc, 2)], out.at[2 * YH + 2 : 2 * YH + 4]))
+        pairs.append((cot.at[pl.ds(cc, 1)], out.at[2 * YH : 2 * YH + 1]))
     start_and_wait(pairs, sems)
 
 
@@ -171,38 +170,38 @@
             win[192:256, at] = take(ok & f[1], pick(f[4], xs[0], xs[1]))
         if side == 0:
             win[:, YH * L :] = v2[:, : 3 * L]
-            vedge[:, :L] = win[:, 6 * L : 7 * L]
+            vedge[:, :L] = win[:, 4 * L : 5 * L]
         else:
             win[:, : 3 * L] = v2[:, 13 * L :]
             vedge[:, L:] = win[:, 3 * L : 4 * L]
-    both = jnp.concatenate([taps(window.at[side], 0, 8) for side in range(2)], axis=1)
-    slps, means = forward(weight, both, 16, lane)
-    for n in range(3):
-        slope_lo[:, n * L : (n + 1) * L] = slps[5 + n]
-        slope_hi[:, n * L : (n + 1) * L] = slps[8 + n]
+    both = jnp.concatenate([taps(window.at[side], 0, 6) for side in range(2)], axis=1)
+    slps, means = forward(weight, both, 12, lane)
+    for n in range(2):
+        slope_lo[:, n * L : (n + 1) * L] = slps[4 + n]
+        slope_hi[:, n * L : (n + 1) * L] = slps[6 + n]
     means = (
-        [take(f[2], m) for m in means[:3]]
+        [take(f[2], m) for m in means[:2]]
+        + [means[2]]
+        + [mid[:, t * L : (t + 1) * L] for t in range(6)]
         + [means[3]]
-        + [mid[:, t * L : (t + 1) * L] for t in range(6)]
-        + [means[4]]
-        + [take(f[3], m) for m in means[5:]]
-    )
-    rows = [jnp.concatenate([means[t], means[t + 6]], axis=1) for t in range(8)]
+        + [take(f[3], m) for m in means[4:]]
+    )
+    rows = [jnp.concatenate([means[t], means[t + 5]], axis=1) for t in range(7)]
     packed = dot(jnp.concatenate(rows, axis=0), pack_matrix()).astype(BF)
-    for t in range(8):
+    for t in range(7):
         pooled[:, t * L : (t + 1) * L] = packed[t * 64 : (t + 1) * 64]
 
 
 def beside_kernel(flags, aa, cot, ab, v2, vedge, cc, vt):
     f = [flags[i] > 0 for i in range(6)]
-    at = 2 * YH + 2
+    at = 2 * YH
     tiles = (
-        [take(f[2], pick(f[5], ab[at + n], aa[at + n])) for n in range(2)]
+        [take(f[2], pick(f[5], ab[at], aa[at]))]
         + [cot[n] for n in range(8)]
-        + [take(f[3], pick(f[5], aa[at + n], ab[at + n])) for n in range(2)]
-    )
-    for t in range(6):
-        pair = jnp.concatenate([tiles[t], tiles[t + 6]], axis=0)
+        + [take(f[3], pick(f[5], aa[at], ab[at]))]
+    )
+    for t in range(5):
+        pair = jnp.concatenate([tiles[t], tiles[t + 5]], axis=0)
         cc[:, t * L : (t + 1) * L] = pair.astype(F32).T
     for y in range(18):
         tile = vedge[:, :L] if y == 0 else vedge[:, L:] if y == 17 else v2[:, (y - 1) * L : y * L]
@@ -215,16 +214,16 @@
     p2[64:128, :] = own[...]
     p2[128:192, :] = take(f[1], pick(f[4], a[...], b[...]))
     lane = iota((128, L), 1)
-    acc = dot(weight[...], taps(p2, 0, 6))
-    for t, pre in enumerate(combine(acc, 128, 6, lane, 64)):
+    acc = dot(weight[...], taps(p2, 0, 5))
+    for t, pre in enumerate(combine(acc, 128, 5, lane, 64)):
         _, slp = slopes(pre)
         tile = (cc[:, t * L : (t + 1) * L] * slp).astype(BF)
         gpc[:, t * L : (t + 1) * L] = tile
         if t < 2:
             other = pltpu.roll(tile.astype(F32), 64, 1).astype(BF)
-            gpc[:, (t + 6) * L : (t + 7) * L] = other
-    acc = dot(w_part[...], taps(gpc, 0, 6))
-    for t, val in enumerate(combine(acc, 128, 6, lane, 64)):
+            gpc[:, (t + 5) * L : (t + 6) * L] = other
+    acc = dot(w_part[...], taps(gpc, 0, 5))
+    for t, val in enumerate(combine(acc, 128, 5, lane, 64)):
         at = slice(t * L, (t + 1) * L)
         val = val.astype(BF)
         first[:, at] = pick(f[4], val[:64], val[64:])
@@ -237,19 +236,19 @@
 
 def coarse_corr_kernel(scale, flags, p2, gpc, w_own, own, kept, sent0, sent1, sent2, g3, out):
     lane = iota((64, L), 1)
-    acc = dot(w_own[...], taps(gpc, 0, 6))
-    for t, val in enumerate(combine(acc, 64, 6, lane, 64)):
+    acc = dot(w_own[...], taps(gpc, 0, 5))
+    for t, val in enumerate(combine(acc, 64, 5, lane, 64)):
         own[:, t * L : (t + 1) * L] = val
     lane = iota((128, L), 1)
-    for t in range(6):
+    for t in range(5):
         at = slice(t * L, (t + 1) * L)
         tile = gpc[:, at].astype(F32)
-        if t < 2 or t > 3:
-            tile = jnp.where(lane >= 64 if t < 2 else lane < 64, tile, 0.0)
+        if t == 0 or t == 4:
+            tile = jnp.where(lane >= 64 if t == 0 else lane < 64, tile, 0.0)
         g3[0:128, at] = shifted(tile, -1, lane, 64).astype(BF)
         g3[128:256, at] = tile.astype(BF)
         g3[256:384, at] = shifted(tile, 1, lane, 64).astype(BF)
-    res = nt(taps(p2, 0, 6), g3[...]) * scale
+    res = nt(taps(p2, 0, 5), g3[...]) * scale
     for j in range(3):
         for k in range(3):
             at = (3 * j + k) * 192
@@ -269,8 +268,6 @@
     a,
     b,
     fc,
-    aa,
-    ab,
     slope_lo,
     slope,
     slope_hi,
@@ -288,7 +285,7 @@
     f = [flags[i] > 0 for i in range(6)]
     lane = iota((64, L), 1)
     rows = []
-    for t in range(6):
+    for t in range(5):
         at = slice(t * L, (t + 1) * L)
         lo, hi = pick(f[4], b[:, at], a[:, at]), pick(f[4], a[:, at], b[:, at])
         total = own[:, at] + take(f[0], lo).astype(F32) + take(f[1], hi).astype(F32)
@@ -297,37 +294,25 @@
         rows.append(jnp.concatenate([main, rest], axis=1))
     spread = spread_matrix()
     full = dot(jnp.concatenate(rows, axis=0), jnp.concatenate([spread, spread], axis=0))
-    gps = [full[64 * t : 64 * t + 64, :L] for t in range(6)]
-    gps += [full[64 * t : 64 * t + 64, L:] for t in range(4)]
+    gps = [full[64 * t : 64 * t + 64, :L] for t in range(5)]
+    gps += [full[64 * t : 64 * t + 64, L:] for t in range(3)]
     for m, gp in enumerate(gps):
         add = gp * 0.125
-        for n in (2 * m - 1, 2 * m):
-            if not 0 <= n < 18:
-                continue
-            if n < 3:
+        for n in (2 * m, 2 * m + 1):
+            if n < 2:
                 slp = slope_lo[:, n * L : (n + 1) * L]
-            elif n < 15:
-                slp = slope[:, (n - 3) * L : (n - 2) * L]
+            elif n < 14:
+                slp = slope[:, (n - 2) * L : (n - 1) * L]
             else:
-                slp = slope_hi[:, (n - 15) * L : (n - 14) * L]
-            rows = []
+                slp = slope_hi[:, (n - 14) * L : (n - 13) * L]
+            rows, at = [], slice(n * L, (n + 1) * L)
             for x in range(2):
-                edge = 2 * YH + x
-                if n == 0:
-                    cot = pick(f[5], ab[edge], aa[edge])
-                elif n == 17:
-                    cot = pick(f[5], aa[edge], ab[edge])
-                else:
-                    cot = fc[x, n - 1]
-                val = (cot.astype(F32) + add) * slp[x * 64 : (x + 1) * 64]
-                if n == 0 or n == 17:
-                    val = take(f[2] if n == 0 else f[3], val)
+                val = (fc[x, n].astype(F32) + add) * slp[x * 64 : (x + 1) * 64]
                 rows.append(val.astype(BF))
-                if 0 < n < 17:
-                    tile, at = rows[x].astype(F32), slice((n - 1) * L, n * L)
-                    u3[x * 64 : x * 64 + 64, at] = shifted(tile, -1, lane).astype(BF)
-                    u3[128 + x * 64 : 192 + x * 64, at] = rows[x]
-                    u3[256 + x * 64 : 320 + x * 64, at] = shifted(tile, 1, lane).astype(BF)
+                tile = rows[x].astype(F32)
+                u3[x * 64 : x * 64 + 64, at] = shifted(tile, -1, lane).astype(BF)
+                u3[128 + x * 64 : 192 + x * 64, at] = rows[x]
+                u3[256 + x * 64 : 320 + x * 64, at] = shifted(tile, 1, lane).astype(BF)
             first[n] = pick(f[4], rows[1], rows[0])
             second[n] = pick(f[4], rows[0], rows[1])
     halves = []
@@ -353,14 +338,27 @@
         mine[n] = jnp.concatenate([top, low], axis=0).astype(BF)
 
 
-def input_grad_kernel(flags, first, second, a, b, weight, out, g2):
+def gradient_edges_kernel(flags, a, b, c, d, first, second):
+    for out, up in ((first, flags[5]), (second, 1 - flags[5])):
+        for n, rows in enumerate((a, b, c, d)):
+            out[n] = rows[up * 15]
+
+
+def input_grad_kernel(flags, first, second, a, b, ea, eb, weight, out, g2):
     f = [flags[i] > 0 for i in range(6)]
     for y in range(18):
+        if y == 0:
+            tiles, ok = [pick(f[5], eb[n], ea[n]) for n in range(4)], f[2]
+        elif y == 17:
+            tiles, ok = [pick(f[5], ea[n], eb[n]) for n in range(4)], f[3]
+        else:
+            tiles, ok = [ref[y - 1] for ref in (first, second, a, b)], None
+        one, two, lo, hi = tiles
         at = slice(y * L, (y + 1) * L)
-        g2[0:64, at] = take(f[0], pick(f[4], b[y], a[y]))
-        g2[64:128, at] = pick(f[4], second[y], first[y])
-        g2[128:192, at] = pick(f[4], first[y], second[y])
-        g2[192:256, at] = take(f[1], pick(f[4], a[y], b[y]))
+        g2[0:64, at] = take(ok, take(f[0], pick(f[4], hi, lo)))
+        g2[64:128, at] = take(ok, pick(f[4], two, one))
+        g2[128:192, at] = take(ok, pick(f[4], one, two))
+        g2[192:256, at] = take(ok, take(f[1], pick(f[4], lo, hi)))
     lane = iota((128, L), 1)
     for t in range(4):
         acc = dot(weight[...], taps(g2, 4 * t, 4))
@@ -454,13 +452,13 @@
         lax.dynamic_index_in_dim(inputs, odd, 0, False),
         "slab",
     )
-    own_edge = ((2 * YH + 4, 64, L), BF)
+    own_edge = ((2 * YH + 1, 64, L), BF)
     first, second = call(
         own_edges_kernel,
         "own_edges",
         (own_edge, own_edge),
-        (flags, inputs, fine_cot, cot),
-        copies=10,
+        (flags, inputs, cot),
+        copies=6,
     )
     aa, ab = swaps(first, second, "sub")
     w_fwd, w_bwd, c_fwd, c_own, c_part = call(
@@ -491,26 +489,26 @@
     slope_lo, slope_hi, pooled, vedge = call(
         border_kernel,
         "fine_forward_border",
-        (((128, 3 * L), F32), ((128, 3 * L), F32), ((64, 8 * L), BF), ((256, 2 * L), BF)),
+        (((128, 2 * L), F32), ((128, 2 * L), F32), ((64, 7 * L), BF), ((256, 2 * L), BF)),
         (flags, v2, mid, aa, ab, ba, bb, w_fwd),
-        scratch=[pltpu.VMEM((2, 256, 10 * L), BF)],
-        macs=384 * 768 * 16 * L,
+        scratch=[pltpu.VMEM((2, 256, 8 * L), BF)],
+        macs=384 * 768 * 12 * L,
     )
     pa, pb = swaps(pooled, pooled, "slab")
     cc, vt = call(
         beside_kernel,
         "cotangent_and_turned_inputs",
-        (((128, 6 * L), F32), ((18 * L, 256), BF)),
+        (((128, 5 * L), F32), ((18 * L, 256), BF)),
         (flags, aa, cot, ab, v2, vedge),
     )
     p2, gpc, first, second = call(
         coarse_kernel,
         "coarse_forward",
         (
-            ((192, 8 * L), BF),
-            ((128, 8 * L), BF),
-            ((64, 6 * L), BF),
-            ((64, 6 * L), BF),
+            ((192, 7 * L), BF),
+            ((128, 7 * L), BF),
+            ((64, 5 * L), BF),
+            ((64, 5 * L), BF),
         ),
         (flags, pooled, pa, pb, cc, c_fwd, c_part),
         macs=384 * 960 * 6 * L,
@@ -520,24 +518,22 @@
     own, kept, *sent = call(
         functools.partial(coarse_corr_kernel, 1.0 / 256.0),
         "coarse_correlate",
-        (((64, 6 * L), F32), ((HALF, L), BF), third, third, third),
+        (((64, 5 * L), F32), ((HALF, L), BF), third, third, third),
         (flags, p2, gpc, c_own),
-        scratch=[pltpu.VMEM((384, 6 * L), BF), pltpu.VMEM((2 * HALF, L), BF)],
+        scratch=[pltpu.VMEM((384, 5 * L), BF), pltpu.VMEM((2 * HALF, L), BF)],
         macs=384 * 768 * 6 * L,
     )
     got0, got1, got2 = (lax.ppermute(part, "sub", [(0, 1), (1, 0), (2, 3), (3, 2)]) for part in sent)
     first, second, mine = call(
         functools.partial(gpf_kernel, 524288.0**-0.5),
         "fine_gradient",
-        (((18, 64, L), BF), ((18, 64, L), BF), ((128, 2 * R, L), BF)),
+        (((16, 64, L), BF), ((16, 64, L), BF), ((128, 2 * R, L), BF)),
         (
             flags,
             own,
             ga,
             gb,
             fine_cot,
-            aa,
-            ab,
             slope_lo,
             slope,
             slope_hi,
@@ -563,13 +559,21 @@
         flags=False,
     )
     everything = lax.all_to_all(total.reshape(128 * 3 * R, L), ("slab", "sub"), 0, 0, tiled=True)
+    one, two = call(
+        gradient_edges_kernel,
+        "gradient_edges",
+        (((4, 64, L), BF), ((4, 64, L), BF)),
+        (flags, first, second, ha, hb),
+        macs=20 * 384 * 768 * 16 * L,
+    )
+    ea, eb = swaps(one, two, "sub")
     grad_input = call(
         input_grad_kernel,
         "input_gradient",
         (((2, 16, 64, L), BF),),
-        (flags, first, second, ha, hb, w_bwd),
+        (flags, first, second, ha, hb, ea, eb, w_bwd),
         scratch=[pltpu.VMEM((256, 18 * L), BF)],
-        macs=20 * 384 * 768 * 16 * L,
+        macs=384 * 768 * 16 * L,
     )
     grad_fine, grad_coarse = call(
         unpack_kernel,

time: 105 us -> 104 us (level)
  waiting for transfers between devices: 27.9 us -> 23.2 us
  starting transfers between devices: 53.7 us -> 57.9 us
    all_to_all x1, waiting for transfers between devices: 13 us -> 2.88 us  [on_device(): lax.all_to_all(total.reshape(128 * 3 * R, L), ('slab', 'sub'), 0, 0, tile...]
    ppermute x6 -> x7, waiting for transfers between devices: 1.7 us -> 6.6 us  [swaps(): other = lax.ppermute(second, axis, others)]
    ppermute x6 -> x7, starting transfers between devices: 8.65 us -> 11.5 us  [swaps(): other = lax.ppermute(second, axis, others)]
    all_to_all x1, starting transfers between devices: 24 us -> 25.7 us  [on_device(): lax.all_to_all(mine.reshape(128 * 2 * R, L), ('slab', 'sub'), 0, 0, tiled...]
    pallas_call x12 -> x13, Pallas kernels: 20.1 us -> 19.8 us  [call(): pl.pallas_call(kernel, out_shape=shapes, in_specs=specs, out_specs=tuple(...]
    ppermute x6 -> x7, starting transfers between devices: 15.6 us -> 15.4 us  [swaps(): return (lax.ppermute(first, axis, pairs), other)]
  transfers between devices with their start and end apart: 17 -> 19, of which waited for: 7 -> 9; matrix products, arithmetic and copies ran while one was open for 0% -> 0% of each run, Pallas kernels for 11% -> 11%
where the time goes in v5:
time: 104 us; the launch traced here: 103 us
  starting transfers between devices  57.9 us (56%)
  waiting for transfers between devices  23.2 us (22%)
  Pallas kernels  19.8 us (19%)
  local copies, waits for them, and re-layouts  1.3 us (1%)
    all_to_all x1, starting transfers between devices, on_device(): lax.all_to_all(mine.reshape(128 * 2 * R, L), ('slab', 'sub'), 0, 0, tiled...  25.7 us
    pallas_call x13, Pallas kernels, call(): pl.pallas_call(kernel, out_shape=shapes, in_specs=specs, out_specs=tuple(...  19.8 us
    ppermute x7, starting transfers between devices, swaps(): return (lax.ppermute(first, axis, pairs), other)  15.4 us
    ppermute x7, starting transfers between devices, swaps(): other = lax.ppermute(second, axis, others)  11.5 us
    all_to_all x1, waiting for transfers between devices, on_device(): lax.all_to_all(mine.reshape(128 * 2 * R, L), ('slab', 'sub'), 0, 0, tiled...  11.3 us
    ppermute x7, waiting for transfers between devices, swaps(): other = lax.ppermute(second, axis, others)  6.6 us
    all_to_all x1, starting transfers between devices, on_device(): lax.all_to_all(total.reshape(128 * 3 * R, L), ('slab', 'sub'), 0, 0, tile...  4.67 us
    all_to_all x1, waiting for transfers between devices, on_device(): lax.all_to_all(total.reshape(128 * 3 * R, L), ('slab', 'sub'), 0, 0, tile...  2.88 us
  transfers between devices with their start and end apart: 19, of which 9 were waited for; matrix products, arithmetic and copies ran while one was open for 0% of the time, Pallas kernels for 11%

profile of v5, /device:TPU:1, one launch (start us, length us, event | category | flops | bytes accessed | tf_op | source)
XLA Modules:
  0.0 103.2 jit_solution(14028948779668712753)
XLA Ops:
  0.7 1.2 %dynamic-slice_bitcast_fusion = (bf16[16,64,128]{2,1,0:T(8,128)(2,1)S(1)}, bf16[16,64,128]{2,1,0:T(8,128)(2,1)S(1)}) fusion(bf16[2,16,64,128]{3,2,1,0:T(8,128)(2,1)} %own.3, s32[]{:T(128)S(6)} %select_n.23, s32[]{:T(128)S(6)} %select_n.22), kind=kLoop, calls=%fused_computation | loop fusion | bytes 1048584 | tf_op jit(solution)/shard_map/jit(dynamic_index_in_dim)/squeeze | solution.py:452
  2.6 5.4 %collective-permute-start = (bf16[16,64,128]{2,1,0:T(8,128)(2,1)S(1)}, bf16[16,64,128]{2,1,0:T(8,128)(2,1)S(1)}, u32[]{:S(2)}, u32[]{:S(2)}) collective-permute-start(bf16[16,64,128]{2,1,0:T(8,128)(2,1)S(1)} %get-tuple-element.72), channel_id=1, source_target_pairs={{0,4},{4,0},{8,12},{12,8},{16,20},{20,16},{24,28},{28,24},{32,36},... | collective-permute-start | bytes 786440 | tf_op jit(solution)/shard_map/ppermute | solution.py:439
  9.2 1.3 %collective-permute-start.2 = (bf16[11,64,128]{2,1,0:T(8,128)(2,1)S(1)}, bf16[11,64,128]{2,1,0:T(8,128)(2,1)S(1)}, u32[]{:S(2)}, u32[]{:S(2)}) collective-permute-start(bf16[11,64,128]{2,1,0:T(8,128)(2,1)S(1)} %get-tuple-element.40), channel_id=1, source_target_pairs={{0,1},{1,0},{2,3},{3,2},{4,5},{5,4},{6,7},{7,6},{8,9},{9,8},{10,11... | collective-permute-start | bytes 540680 | tf_op jit(solution)/shard_map/ppermute | solution.py:439
  10.5 3.1 %collective-permute-start.3 = (bf16[11,64,128]{2,1,0:T(8,128)(2,1)S(1)}, bf16[11,64,128]{2,1,0:T(8,128)(2,1)S(1)}, u32[]{:S(2)}, u32[]{:S(2)}) collective-permute-start(bf16[11,64,128]{2,1,0:T(8,128)(2,1)S(1)} %get-tuple-element.41), channel_id=1, source_target_pairs={{0,0},{3,3},{1,2},{2,1},{4,4},{7,7},{5,6},{6,5},{8,8},{11,11},{9,1... | collective-permute-start | bytes 540680 | tf_op jit(solution)/shard_map/ppermute | solution.py:438
  14.3 1.6 %collective-permute-start.4 = (bf16[10,64,128]{2,1,0:T(8,128)(2,1)S(1)}, bf16[10,64,128]{2,1,0:T(8,128)(2,1)S(1)}, u32[]{:S(2)}, u32[]{:S(2)}) collective-permute-start(bf16[10,64,128]{2,1,0:T(8,128)(2,1)S(1)} %get-tuple-element.42), channel_id=1, source_target_pairs={{0,1},{1,0},{2,3},{3,2},{4,5},{5,4},{6,7},{7,6},{8,9},{9,8},{10,11... | collective-permute-start | bytes 491528 | tf_op jit(solution)/shard_map/ppermute | solution.py:439
  15.9 3.1 %collective-permute-start.5 = (bf16[10,64,128]{2,1,0:T(8,128)(2,1)S(1)}, bf16[10,64,128]{2,1,0:T(8,128)(2,1)S(1)}, u32[]{:S(2)}, u32[]{:S(2)}) collective-permute-start(bf16[10,64,128]{2,1,0:T(8,128)(2,1)S(1)} %get-tuple-element.43), channel_id=1, source_target_pairs={{0,0},{3,3},{1,2},{2,1},{4,4},{7,7},{5,6},{6,5},{8,8},{11,11},{9,1... | collective-permute-start | bytes 491528 | tf_op jit(solution)/shard_map/ppermute | solution.py:438
  19.7 2.0 %fine_forward_interior.1 = (bf16[256,2048]{1,0:T(8,128)(2,1)S(1)}, f32[128,1536]{1,0:T(8,128)S(1)}, bf16[64,768]{1,0:T(8,128)(2,1)S(1)}) custom-call(s32[6]{0:T(128)S(1)} %convert_element_type.3.flags, bf16[2,16,64,128]{3,2,1,0:T(8,128)(2,1)S(1)} %copy-done, bf16[16,64,128]{2,1,0:T(8,128)(2,1)S(1)} %collective-permute-done.xa, ...), custom_call_target="tpu_custom_call" | custom-call | flops 905969664 | bytes 1638424 | tf_op jit(solution)/shard_map/fine_forward_interior/pallas_call | solution.py:421
  22.5 2.1 %fine_forward_border.1 = (f32[128,256]{1,0:T(8,128)S(1)}, f32[128,256]{1,0:T(8,128)S(1)}, bf16[64,896]{1,0:T(8,128)(2,1)S(1)}, bf16[256,256]{1,0:T(8,128)(2,1)S(1)}) custom-call(s32[6]{0:T(128)S(1)} %convert_element_type.3.flags, bf16[256,2048]{1,0:T(8,128)(2,1)S(1)} %get-tuple-element.38.v2, bf16[64,768]{1,0:T(8,128)(2,1)S(1)} %get-tuple-element.39.mid, ...), custom_call_target="tpu_custom_call" | custom-call | flops 905969664 | bytes 2424856 | tf_op jit(solution)/shard_map/fine_forward_border/pallas_call | solution.py:421
  25.3 2.8 %collective-permute-start.6 = (bf16[64,896]{1,0:T(8,128)(2,1)S(1)}, bf16[64,896]{1,0:T(8,128)(2,1)S(1)}, u32[]{:S(2)}, u32[]{:S(2)}) collective-permute-start(bf16[64,896]{1,0:T(8,128)(2,1)S(1)} %get-tuple-element.44.own), channel_id=1, source_target_pairs={{0,4},{4,0},{8,12},{12,8},{16,20},{20,16},{24,28},{28,24},{32,36},... | collective-permute-start | bytes 344072 | tf_op jit(solution)/shard_map/ppermute | solution.py:439
  29.1 1.2 %collective-permute-done.6.a = bf16[64,896]{1,0:T(8,128)(2,1)S(1)} collective-permute-done((bf16[64,896]{1,0:T(8,128)(2,1)S(1)}, bf16[64,896]{1,0:T(8,128)(2,1)S(1)}, u32[]{:S(2)}, u32[]{:S(2)}) %collective-permute-start.6) | collective-permute-done | bytes 114720 | tf_op jit(solution)/shard_map/ppermute | solution.py:439
  30.3 1.8 %coarse_forward.1 = (bf16[192,896]{1,0:T(8,128)(2,1)S(1)}, bf16[128,896]{1,0:T(8,128)(2,1)S(1)}, bf16[64,640]{1,0:T(8,128)(2,1)S(1)}, bf16[64,640]{1,0:T(8,128)(2,1)S(1)}) custom-call(s32[6]{0:T(128)S(1)} %convert_element_type.3.flags, bf16[64,896]{1,0:T(8,128)(2,1)S(1)} %get-tuple-element.44.own, bf16[64,896]{1,0:T(8,128)(2,1)S(1)} %collective-permute-done.6.a, ...), custom_call_target="tpu_custom_call" | custom-call | flops 566231040 | bytes 1409048 | tf_op jit(solution)/shard_map/coarse_forward/pallas_call | solution.py:421
  32.1 1.5 %collective-permute-start.8 = (bf16[64,640]{1,0:T(8,128)(2,1)S(1)}, bf16[64,640]{1,0:T(8,128)(2,1)S(1)}, u32[]{:S(2)}, u32[]{:S(2)}) collective-permute-start(bf16[64,640]{1,0:T(8,128)(2,1)S(1)} %get-tuple-element.53), channel_id=1, source_target_pairs={{0,4},{4,0},{8,12},{12,8},{16,20},{20,16},{24,28},{28,24},{32,36},... | collective-permute-start | bytes 245768 | tf_op jit(solution)/shard_map/ppermute | solution.py:439
  34.3 1.4 %coarse_correlate.1 = (f32[64,640]{1,0:T(8,128)S(1)}, bf16[864,128]{1,0:T(8,128)(2,1)S(1)}, bf16[288,128]{1,0:T(8,128)(2,1)S(1)}, bf16[288,128]{1,0:T(8,128)(2,1)S(1)}, bf16[288,128]{1,0:T(8,128)(2,1)S(1)}) custom-call(s32[6]{0:T(128)S(1)} %convert_element_type.3.flags, bf16[192,896]{1,0:T(8,128)(2,1)S(1)} %get-tuple-element.49.p2, ...), custom_call_target="tpu_custom_call" | custom-call | flops 452984832 | bytes 720920 | tf_op jit(solution)/shard_map/coarse_correlate/pallas_call | solution.py:421
  37.5 3.3 %fine_gradient.1 = (bf16[16,64,128]{2,1,0:T(8,128)(2,1)S(1)}, bf16[16,64,128]{2,1,0:T(8,128)(2,1)S(1)}, bf16[128,16,128]{2,1,0:T(8,128)(2,1)}) custom-call(s32[6]{0:T(128)S(1)} %convert_element_type.3.flags, f32[64,640]{1,0:T(8,128)S(1)} %get-tuple-element.52.own, bf16[64,640]{1,0:T(8,128)(2,1)S(1)} %collective-permute-done.8.a, ...), custom_call_target="tpu_custom_call" | custom-call | flops 1207959552 | bytes 3522584 | tf_op jit(solution)/shard_map/fine_gradient/pallas_call | solution.py:421
  40.8 25.7 %all-to-all-start = ((bf16[128,16,128]{2,1,0:T(8,128)(2,1)}), bf16[128,16,128]{2,1,0:T(8,128)(2,1)S(1)}, u32[]{:S(2)}, u32[]{:S(2)}) async-start(bf16[128,16,128]{2,1,0:T(8,128)(2,1)} %get-tuple-element.68), calls=%async_computation | async-start | bytes 1048576 | tf_op jit(solution)/shard_map/all_to_all | solution.py:553
  66.5 1.6 %collective-permute-start.13 = (bf16[16,64,128]{2,1,0:T(8,128)(2,1)S(1)}, bf16[16,64,128]{2,1,0:T(8,128)(2,1)S(1)}, u32[]{:S(2)}, u32[]{:S(2)}) collective-permute-start(bf16[16,64,128]{2,1,0:T(8,128)(2,1)S(1)} %get-tuple-element.63.a.first), channel_id=1, source_target_pairs={{0,4},{4,0},{8,12},{12,8},{16,20},{20,16},{24,28},{28,24},{32,36},... | collective-permute-start | bytes 786440 | tf_op jit(solution)/shard_map/ppermute | solution.py:439
  68.7 11.3 %all-to-all-done.parts = bf16[128,16,128]{2,1,0:T(8,128)(2,1)S(1)} async-done(((bf16[128,16,128]{2,1,0:T(8,128)(2,1)}), bf16[128,16,128]{2,1,0:T(8,128)(2,1)S(1)}, u32[]{:S(2)}, u32[]{:S(2)}) %all-to-all-start) | async-done | bytes 524320 | tf_op jit(solution)/shard_map/all_to_all | solution.py:553
  81.1 4.7 %all-to-all-start.1 = ((bf16[128,24,128]{2,1,0:T(8,128)(2,1)}), bf16[128,24,128]{2,1,0:T(8,128)(2,1)S(1)}, u32[]{:S(2)}, u32[]{:S(2)}) async-start(bf16[128,24,128]{2,1,0:T(8,128)(2,1)} %sum_shares.1), calls=%async_computation.1 | async-start | bytes 1572864 | tf_op jit(solution)/shard_map/all_to_all | solution.py:561
  86.3 1.1 %collective-permute-start.15 = (bf16[4,64,128]{2,1,0:T(8,128)(2,1)S(1)}, bf16[4,64,128]{2,1,0:T(8,128)(2,1)S(1)}, u32[]{:S(2)}, u32[]{:S(2)}) collective-permute-start(bf16[4,64,128]{2,1,0:T(8,128)(2,1)S(1)} %get-tuple-element.65), channel_id=1, source_target_pairs={{0,1},{1,0},{2,3},{3,2},{4,5},{5,4},{6,7},{7,6},{8,9},{9,8},{10,11... | collective-permute-start | bytes 196616 | tf_op jit(solution)/shard_map/ppermute | solution.py:439
  87.5 2.6 %collective-permute-start.16 = (bf16[4,64,128]{2,1,0:T(8,128)(2,1)S(1)}, bf16[4,64,128]{2,1,0:T(8,128)(2,1)S(1)}, u32[]{:S(2)}, u32[]{:S(2)}) collective-permute-start(bf16[4,64,128]{2,1,0:T(8,128)(2,1)S(1)} %get-tuple-element.66), channel_id=1, source_target_pairs={{0,0},{3,3},{1,2},{2,1},{4,4},{7,7},{5,6},{6,5},{8,8},{11,11},{9,1... | collective-permute-start | bytes 196616 | tf_op jit(solution)/shard_map/ppermute | solution.py:438
  90.1 5.8 %collective-permute-done.16.eb = bf16[4,64,128]{2,1,0:T(8,128)(2,1)S(1)} collective-permute-done((bf16[4,64,128]{2,1,0:T(8,128)(2,1)S(1)}, bf16[4,64,128]{2,1,0:T(8,128)(2,1)S(1)}, u32[]{:S(2)}, u32[]{:S(2)}) %collective-permute-start.16) | collective-permute-done | bytes 65568 | tf_op jit(solution)/shard_map/ppermute | solution.py:438
  95.9 3.0 %input_gradient.1 = bf16[2,16,64,128]{3,2,1,0:T(8,128)(2,1)} custom-call(s32[6]{0:T(128)S(1)} %convert_element_type.3.flags, bf16[16,64,128]{2,1,0:T(8,128)(2,1)S(1)} %get-tuple-element.63.a.first, bf16[16,64,128]{2,1,0:T(8,128)(2,1)S(1)} %get-tuple-element.64.b.second, bf16[16,64,128]{2,1,0:T(8,128)(2,1)S(1)} %collective-permute-done.13.c.a, ...), custom_call_target="tpu_custom_call" | custom-call | flops 1207959552 | bytes 1769496 | tf_op jit(solution)/shard_map/input_gradient/pallas_call | solution.py:421
  98.9 2.9 %all-to-all-done.1.got = bf16[128,24,128]{2,1,0:T(8,128)(2,1)S(1)} async-done(((bf16[128,24,128]{2,1,0:T(8,128)(2,1)}), bf16[128,24,128]{2,1,0:T(8,128)(2,1)S(1)}, u32[]{:S(2)}, u32[]{:S(2)}) %all-to-all-start.1) | async-done | bytes 786464 | tf_op jit(solution)/shard_map/all_to_all | solution.py:561
  101.8 1.4 %unpack.1 = (f32[3,3,3,64,64]{4,3,2,1,0:T(8,128)}, f32[3,3,3,64,128]{4,3,2,1,0:T(8,128)}) custom-call(bf16[128,24,128]{2,1,0:T(8,128)(2,1)S(1)} %all-to-all-done.1.got), custom_call_target="tpu_custom_call" | custom-call | bytes 786432 | tf_op jit(solution)/shard_map/unpack/pallas_call | solution.py:421
  (40 shorter events, 10.4 us)
Async XLA Ops:
  0.6 7.5 %copy-start = (bf16[2,16,64,128]{3,2,1,0:T(8,128)(2,1)S(1)}, bf16[2,16,64,128]{3,2,1,0:T(8,128)(2,1)}, u32[]{:S(2)}) copy-start(bf16[2,16,64,128]{3,2,1,0:T(8,128)(2,1)} %own.3) | copy-start | bytes 1572868
  0.6 7.4 %copy-start.1 = (bf16[1,8,128,64]{2,3,1,0:T(8,128)(2,1)S(1)}, bf16[1,8,128,64]{2,3,1,0:T(8,128)(2,1)}, u32[]{:S(2)}) copy-start(bf16[1,8,128,64]{2,3,1,0:T(8,128)(2,1)} %param.7) | copy-start | bytes 393220
  0.7 18.3 %copy-start.3 = (bf16[3,3,3,64,128]{4,3,2,1,0:T(8,128)(2,1)S(1)}, bf16[3,3,3,64,128]{4,3,2,1,0:T(8,128)(2,1)}, u32[]{:S(2)}) copy-start(bf16[3,3,3,64,128]{4,3,2,1,0:T(8,128)(2,1)} %wc.1) | copy-start | bytes 1327108
  0.7 18.3 %copy-start.2 = (bf16[3,3,3,64,64]{4,3,2,1,0:T(8,128)(2,1)S(1)}, bf16[3,3,3,64,64]{4,3,2,1,0:T(8,128)(2,1)}, u32[]{:S(2)}) copy-start(bf16[3,3,3,64,64]{4,3,2,1,0:T(8,128)(2,1)} %wf.1) | copy-start | bytes 663556
  1.9 11.7 %collective-permute-start.1 = (bf16[16,64,128]{2,1,0:T(8,128)(2,1)S(1)}, bf16[16,64,128]{2,1,0:T(8,128)(2,1)S(1)}, u32[]{:S(2)}, u32[]{:S(2)}) collective-permute-start(bf16[16,64,128]{2,1,0:T(8,128)(2,1)S(1)} %get-tuple-element.71), channel_id=1, source_target_pairs={{0,0},{124,124},{4,8},{8,4},{12,16},{16,12},{20,24},{24,20},{28,32... | collective-permute-start | bytes 786440 | tf_op jit(solution)/shard_map/ppermute | solution.py:438
  2.6 11.1 %collective-permute-start = (bf16[16,64,128]{2,1,0:T(8,128)(2,1)S(1)}, bf16[16,64,128]{2,1,0:T(8,128)(2,1)S(1)}, u32[]{:S(2)}, u32[]{:S(2)}) collective-permute-start(bf16[16,64,128]{2,1,0:T(8,128)(2,1)S(1)} %get-tuple-element.72), channel_id=1, source_target_pairs={{0,4},{4,0},{8,12},{12,8},{16,20},{20,16},{24,28},{28,24},{32,36},... | collective-permute-start | bytes 786440 | tf_op jit(solution)/shard_map/ppermute | solution.py:439
  9.2 12.5 %collective-permute-start.2 = (bf16[11,64,128]{2,1,0:T(8,128)(2,1)S(1)}, bf16[11,64,128]{2,1,0:T(8,128)(2,1)S(1)}, u32[]{:S(2)}, u32[]{:S(2)}) collective-permute-start(bf16[11,64,128]{2,1,0:T(8,128)(2,1)S(1)} %get-tuple-element.40), channel_id=1, source_target_pairs={{0,1},{1,0},{2,3},{3,2},{4,5},{5,4},{6,7},{7,6},{8,9},{9,8},{10,11... | collective-permute-start | bytes 540680 | tf_op jit(solution)/shard_map/ppermute | solution.py:439
  10.5 11.2 %collective-permute-start.3 = (bf16[11,64,128]{2,1,0:T(8,128)(2,1)S(1)}, bf16[11,64,128]{2,1,0:T(8,128)(2,1)S(1)}, u32[]{:S(2)}, u32[]{:S(2)}) collective-permute-start(bf16[11,64,128]{2,1,0:T(8,128)(2,1)S(1)} %get-tuple-element.41), channel_id=1, source_target_pairs={{0,0},{3,3},{1,2},{2,1},{4,4},{7,7},{5,6},{6,5},{8,8},{11,11},{9,1... | collective-permute-start | bytes 540680 | tf_op jit(solution)/shard_map/ppermute | solution.py:438
  14.3 7.5 %collective-permute-start.4 = (bf16[10,64,128]{2,1,0:T(8,128)(2,1)S(1)}, bf16[10,64,128]{2,1,0:T(8,128)(2,1)S(1)}, u32[]{:S(2)}, u32[]{:S(2)}) collective-permute-start(bf16[10,64,128]{2,1,0:T(8,128)(2,1)S(1)} %get-tuple-element.42), channel_id=1, source_target_pairs={{0,1},{1,0},{2,3},{3,2},{4,5},{5,4},{6,7},{7,6},{8,9},{9,8},{10,11... | collective-permute-start | bytes 491528 | tf_op jit(solution)/shard_map/ppermute | solution.py:439
  15.9 6.6 %collective-permute-start.5 = (bf16[10,64,128]{2,1,0:T(8,128)(2,1)S(1)}, bf16[10,64,128]{2,1,0:T(8,128)(2,1)S(1)}, u32[]{:S(2)}, u32[]{:S(2)}) collective-permute-start(bf16[10,64,128]{2,1,0:T(8,128)(2,1)S(1)} %get-tuple-element.43), channel_id=1, source_target_pairs={{0,0},{3,3},{1,2},{2,1},{4,4},{7,7},{5,6},{6,5},{8,8},{11,11},{9,1... | collective-permute-start | bytes 491528 | tf_op jit(solution)/shard_map/ppermute | solution.py:438
  24.6 4.5 %collective-permute-start.7 = (bf16[64,896]{1,0:T(8,128)(2,1)S(1)}, bf16[64,896]{1,0:T(8,128)(2,1)S(1)}, u32[]{:S(2)}, u32[]{:S(2)}) collective-permute-start(bf16[64,896]{1,0:T(8,128)(2,1)S(1)} %get-tuple-element.44.own), channel_id=1, source_target_pairs={{0,0},{124,124},{4,8},{8,4},{12,16},{16,12},{20,24},{24,20},{28,32... | collective-permute-start | bytes 344072 | tf_op jit(solution)/shard_map/ppermute | solution.py:438
  25.3 5.0 %collective-permute-start.6 = (bf16[64,896]{1,0:T(8,128)(2,1)S(1)}, bf16[64,896]{1,0:T(8,128)(2,1)S(1)}, u32[]{:S(2)}, u32[]{:S(2)}) collective-permute-start(bf16[64,896]{1,0:T(8,128)(2,1)S(1)} %get-tuple-element.44.own), channel_id=1, source_target_pairs={{0,4},{4,0},{8,12},{12,8},{16,20},{20,16},{24,28},{28,24},{32,36},... | collective-permute-start | bytes 344072 | tf_op jit(solution)/shard_map/ppermute | solution.py:439
  32.1 5.4 %copy-start.4 = (bf16[2,16,64,128]{3,2,1,0:T(8,128)(2,1)S(1)}, bf16[2,16,64,128]{3,2,1,0:T(8,128)(2,1)}, u32[]{:S(2)}) copy-start(bf16[2,16,64,128]{3,2,1,0:T(8,128)(2,1)} %fc.1) | copy-start | bytes 1572868
  32.1 5.4 %collective-permute-start.8 = (bf16[64,640]{1,0:T(8,128)(2,1)S(1)}, bf16[64,640]{1,0:T(8,128)(2,1)S(1)}, u32[]{:S(2)}, u32[]{:S(2)}) collective-permute-start(bf16[64,640]{1,0:T(8,128)(2,1)S(1)} %get-tuple-element.53), channel_id=1, source_target_pairs={{0,4},{4,0},{8,12},{12,8},{16,20},{20,16},{24,28},{28,24},{32,36},... | collective-permute-start | bytes 245768 | tf_op jit(solution)/shard_map/ppermute | solution.py:439
  33.6 3.9 %collective-permute-start.9 = (bf16[64,640]{1,0:T(8,128)(2,1)S(1)}, bf16[64,640]{1,0:T(8,128)(2,1)S(1)}, u32[]{:S(2)}, u32[]{:S(2)}) collective-permute-start(bf16[64,640]{1,0:T(8,128)(2,1)S(1)} %get-tuple-element.54), channel_id=1, source_target_pairs={{0,0},{124,124},{4,8},{8,4},{12,16},{16,12},{20,24},{24,20},{28,32... | collective-permute-start | bytes 245768 | tf_op jit(solution)/shard_map/ppermute | solution.py:438
  35.6 1.3 %collective-permute-start.10 = (bf16[288,128]{1,0:T(8,128)(2,1)S(1)}, bf16[288,128]{1,0:T(8,128)(2,1)S(1)}, u32[]{:S(2)}, u32[]{:S(2)}) collective-permute-start(bf16[288,128]{1,0:T(8,128)(2,1)S(1)} %get-tuple-element.60), channel_id=1, source_target_pairs={{0,1},{1,0},{2,3},{3,2},{4,5},{5,4},{6,7},{7,6},{8,9},{9,8},{10,11... | collective-permute-start | bytes 221192 | tf_op jit(solution)/shard_map/ppermute | solution.py:526
  35.7 1.4 %collective-permute-start.11 = (bf16[288,128]{1,0:T(8,128)(2,1)S(1)}, bf16[288,128]{1,0:T(8,128)(2,1)S(1)}, u32[]{:S(2)}, u32[]{:S(2)}) collective-permute-start(bf16[288,128]{1,0:T(8,128)(2,1)S(1)} %get-tuple-element.61), channel_id=1, source_target_pairs={{0,1},{1,0},{2,3},{3,2},{4,5},{5,4},{6,7},{7,6},{8,9},{9,8},{10,11... | collective-permute-start | bytes 221192 | tf_op jit(solution)/shard_map/ppermute | solution.py:526
  36.2 1.3 %collective-permute-start.12 = (bf16[288,128]{1,0:T(8,128)(2,1)S(1)}, bf16[288,128]{1,0:T(8,128)(2,1)S(1)}, u32[]{:S(2)}, u32[]{:S(2)}) collective-permute-start(bf16[288,128]{1,0:T(8,128)(2,1)S(1)} %get-tuple-element.62), channel_id=1, source_target_pairs={{0,1},{1,0},{2,3},{3,2},{4,5},{5,4},{6,7},{7,6},{8,9},{9,8},{10,11... | collective-permute-start | bytes 221192 | tf_op jit(solution)/shard_map/ppermute | solution.py:526
  40.8 39.3 %all-to-all-start = ((bf16[128,16,128]{2,1,0:T(8,128)(2,1)}), bf16[128,16,128]{2,1,0:T(8,128)(2,1)S(1)}, u32[]{:S(2)}, u32[]{:S(2)}) async-start(bf16[128,16,128]{2,1,0:T(8,128)(2,1)} %get-tuple-element.68), calls=%async_computation | async-start | bytes 1048576 | tf_op jit(solution)/shard_map/all_to_all | solution.py:553
  66.5 19.3 %collective-permute-start.13 = (bf16[16,64,128]{2,1,0:T(8,128)(2,1)S(1)}, bf16[16,64,128]{2,1,0:T(8,128)(2,1)S(1)}, u32[]{:S(2)}, u32[]{:S(2)}) collective-permute-start(bf16[16,64,128]{2,1,0:T(8,128)(2,1)S(1)} %get-tuple-element.63.a.first), channel_id=1, source_target_pairs={{0,4},{4,0},{8,12},{12,8},{16,20},{20,16},{24,28},{28,24},{32,36},... | collective-permute-start | bytes 786440 | tf_op jit(solution)/shard_map/ppermute | solution.py:439
  68.1 17.7 %collective-permute-start.14 = (bf16[16,64,128]{2,1,0:T(8,128)(2,1)S(1)}, bf16[16,64,128]{2,1,0:T(8,128)(2,1)S(1)}, u32[]{:S(2)}, u32[]{:S(2)}) collective-permute-start(bf16[16,64,128]{2,1,0:T(8,128)(2,1)S(1)} %get-tuple-element.64.b.second), channel_id=1, source_target_pairs={{0,0},{124,124},{4,8},{8,4},{12,16},{16,12},{20,24},{24,20},{28,32... | collective-permute-start | bytes 786440 | tf_op jit(solution)/shard_map/ppermute | solution.py:438
  81.1 20.7 %all-to-all-start.1 = ((bf16[128,24,128]{2,1,0:T(8,128)(2,1)}), bf16[128,24,128]{2,1,0:T(8,128)(2,1)S(1)}, u32[]{:S(2)}, u32[]{:S(2)}) async-start(bf16[128,24,128]{2,1,0:T(8,128)(2,1)} %sum_shares.1), calls=%async_computation.1 | async-start | bytes 1572864 | tf_op jit(solution)/shard_map/all_to_all | solution.py:561
  86.3 3.8 %collective-permute-start.15 = (bf16[4,64,128]{2,1,0:T(8,128)(2,1)S(1)}, bf16[4,64,128]{2,1,0:T(8,128)(2,1)S(1)}, u32[]{:S(2)}, u32[]{:S(2)}) collective-permute-start(bf16[4,64,128]{2,1,0:T(8,128)(2,1)S(1)} %get-tuple-element.65), channel_id=1, source_target_pairs={{0,1},{1,0},{2,3},{3,2},{4,5},{5,4},{6,7},{7,6},{8,9},{9,8},{10,11... | collective-permute-start | bytes 196616 | tf_op jit(solution)/shard_map/ppermute | solution.py:439
  87.5 8.4 %collective-permute-start.16 = (bf16[4,64,128]{2,1,0:T(8,128)(2,1)S(1)}, bf16[4,64,128]{2,1,0:T(8,128)(2,1)S(1)}, u32[]{:S(2)}, u32[]{:S(2)}) collective-permute-start(bf16[4,64,128]{2,1,0:T(8,128)(2,1)S(1)} %get-tuple-element.66), channel_id=1, source_target_pairs={{0,0},{3,3},{1,2},{2,1},{4,4},{7,7},{5,6},{6,5},{8,8},{11,11},{9,1... | collective-permute-start | bytes 196616 | tf_op jit(solution)/shard_map/ppermute | solution.py:438

commit v6 on v5

--- a/solution.py
+++ b/solution.py
@@ -119,21 +119,24 @@
         c.wait()
 
 
-def own_edges_kernel(flags, own, cot, first, second, sems):
+def own_edges_kernel(flags, own, cot, first, second, far, sems):
     pairs = []
     for out, up in ((first, flags[5]), (second, 1 - flags[5])):
         y, cc = up * (16 - YH), up * 7
         for x in range(2):
             pairs.append((own.at[x, pl.ds(y, YH)], out.at[x * YH : (x + 1) * YH]))
         pairs.append((cot.at[pl.ds(cc, 1)], out.at[2 * YH : 2 * YH + 1]))
+    y = (1 - flags[5]) * (16 - YH)
+    pairs.append((own.at[flags[4], pl.ds(y, YH)], far))
     start_and_wait(pairs, sems)
 
 
 def corner_edges_kernel(flags, xa, xb, first, second):
-    for out, up in ((first, flags[5]), (second, 1 - flags[5])):
-        for n in range(YH):
-            out[n] = xa[up * (16 - YH) + n]
-            out[YH + n] = xb[up * (16 - YH) + n]
+    at = flags[5] * (16 - YH)
+    for n in range(YH):
+        first[n] = xa[at + n]
+        first[YH + n] = xb[at + n]
+        second[n] = xb[16 - YH - at + n]
 
 
 def interior_kernel(flags, own, xa, xb, weight, v2, slope, pooled):
@@ -153,7 +156,7 @@
 
 
 def border_kernel(
-    flags, v2, mid, aa, ab, ba, bb, weight, slope_lo, slope_hi, pooled, vedge, window
+    flags, v2, mid, aa, ab, nb, ba, bb, weight, slope_lo, slope_hi, pooled, vedge, window
 ):
     f = [flags[i] > 0 for i in range(6)]
     lane = iota((128, L), 1)
@@ -163,7 +166,7 @@
         first = 0 if side == 0 else 3
         for y in range(YH):
             at = slice((first + y) * L, (first + y + 1) * L)
-            xs = [pick(even, ba[n * YH + y], bb[n * YH + y]) for n in range(2)]
+            xs = [pick(even, ba[y], nb[y]), pick(even, ba[YH + y], bb[y])]
             win[0:64, at] = take(ok & f[0], pick(f[4], xs[1], xs[0]))
             win[64:128, at] = take(ok, pick(even, aa[y], ab[y]))
             win[128:192, at] = take(ok, pick(even, aa[YH + y], ab[YH + y]))
@@ -439,6 +442,12 @@
     return lax.ppermute(first, axis, pairs), other
 
 
+def diagonal_swap(far):
+    turn = (0, 2, 1, 3)
+    pairs = [(4 * i + j, 4 * (i ^ 1) + turn[j]) for i in range(32) for j in range(4)]
+    return lax.ppermute(far, ("slab", "sub"), pairs)
+
+
 def on_device(inputs, fine_cot, coarse_cot, weight_fine, weight_coarse):
     slab, sub = lax.axis_index("slab"), lax.axis_index("sub")
     flags = jnp.stack(
@@ -453,14 +462,16 @@
         "slab",
     )
     own_edge = ((2 * YH + 1, 64, L), BF)
-    first, second = call(
+    corner = ((YH, 64, L), BF)
+    first, second, far = call(
         own_edges_kernel,
         "own_edges",
-        (own_edge, own_edge),
+        (own_edge, own_edge, corner),
         (flags, inputs, cot),
-        copies=6,
+        copies=7,
     )
     aa, ab = swaps(first, second, "sub")
+    nb = diagonal_swap(far)
     w_fwd, w_bwd, c_fwd, c_own, c_part = call(
         prepare_kernel,
         "prepare_weights",
@@ -474,9 +485,9 @@
         (weight_fine, weight_coarse),
         flags=False,
     )
-    corner = ((2 * YH, 64, L), BF)
+    xa, xb, w_fwd = lax.optimization_barrier((xa, xb, w_fwd))
     first, second = call(
-        corner_edges_kernel, "corner_edges", (corner, corner), (flags, xa, xb)
+        corner_edges_kernel, "corner_edges", (((2 * YH, 64, L), BF), corner), (flags, xa, xb)
     )
     ba, bb = swaps(first, second, "sub")
     v2, slope, mid = call(
@@ -490,7 +501,7 @@
         border_kernel,
         "fine_forward_border",
         (((128, 2 * L), F32), ((128, 2 * L), F32), ((64, 7 * L), BF), ((256, 2 * L), BF)),
-        (flags, v2, mid, aa, ab, ba, bb, w_fwd),
+        (flags, v2, mid, aa, ab, nb, ba, bb, w_fwd),
         scratch=[pltpu.VMEM((2, 256, 8 * L), BF)],
         macs=384 * 768 * 12 * L,
     )

time: 104 us -> 103 us (level)
  starting transfers between devices: 57.9 us -> 56.5 us
    all_to_all x1, starting transfers between devices: 25.7 us -> 21.4 us  [on_device(): lax.all_to_all(mine.reshape(128 * 2 * R, L), ('slab', 'sub'), 0, 0, tiled...]
    ppermute x0 -> x1, starting transfers between devices: none -> 2.45 us  [diagonal_swap(): return lax.ppermute(far, ('slab', 'sub'), pairs)]
    ppermute x7, starting transfers between devices: 15.4 us -> 16.6 us  [swaps(): return (lax.ppermute(first, axis, pairs), other)]
  transfers between devices with their start and end apart: 19 -> 20, of which waited for: 9 -> 8; matrix products, arithmetic and copies ran while one was open for 0% -> 0% of each run, Pallas kernels for 11% -> 11%
where the time goes in v6:
time: 103 us; the launch traced here: 102 us
  starting transfers between devices  56.5 us (55%)
  waiting for transfers between devices  23.7 us (23%)
  Pallas kernels  19.9 us (19%)
  local copies, waits for them, and re-layouts  1.3 us (1%)
    all_to_all x1, starting transfers between devices, on_device(): lax.all_to_all(mine.reshape(128 * 2 * R, L), ('slab', 'sub'), 0, 0, tiled...  21.4 us
    pallas_call x13, Pallas kernels, call(): pl.pallas_call(kernel, out_shape=shapes, in_specs=specs, out_specs=tuple(...  19.9 us
    ppermute x7, starting transfers between devices, swaps(): return (lax.ppermute(first, axis, pairs), other)  16.6 us
    all_to_all x1, waiting for transfers between devices, on_device(): lax.all_to_all(mine.reshape(128 * 2 * R, L), ('slab', 'sub'), 0, 0, tiled...  11.3 us
    ppermute x7, starting transfers between devices, swaps(): other = lax.ppermute(second, axis, others)  10.7 us
    ppermute x7, waiting for transfers between devices, swaps(): other = lax.ppermute(second, axis, others)  7.15 us
    all_to_all x1, starting transfers between devices, on_device(): lax.all_to_all(total.reshape(128 * 3 * R, L), ('slab', 'sub'), 0, 0, tile...  4.67 us
    all_to_all x1, waiting for transfers between devices, on_device(): lax.all_to_all(total.reshape(128 * 3 * R, L), ('slab', 'sub'), 0, 0, tile...  2.88 us
  transfers between devices with their start and end apart: 20, of which 8 were waited for; matrix products, arithmetic and copies ran while one was open for 0% of the time, Pallas kernels for 11%

profile of v6, /device:TPU:1, one launch (start us, length us, event | category | flops | bytes accessed | tf_op | source)
XLA Modules:
  0.0 102.4 jit_solution(9338454251544265318)
XLA Ops:
  2.6 5.4 %collective-permute-start = (bf16[16,64,128]{2,1,0:T(8,128)(2,1)S(1)}, bf16[16,64,128]{2,1,0:T(8,128)(2,1)S(1)}, u32[]{:S(2)}, u32[]{:S(2)}) collective-permute-start(bf16[16,64,128]{2,1,0:T(8,128)(2,1)S(1)} %get-tuple-element.80), channel_id=1, source_target_pairs={{0,4},{4,0},{8,12},{12,8},{16,20},{20,16},{24,28},{28,24},{32,36},... | collective-permute-start | bytes 786440 | tf_op jit(solution)/shard_map/ppermute | solution.py:442
  8.1 1.2 %own_edges.1 = (bf16[11,64,128]{2,1,0:T(8,128)(2,1)S(1)}, bf16[11,64,128]{2,1,0:T(8,128)(2,1)S(1)}, bf16[5,64,128]{2,1,0:T(8,128)(2,1)S(1)}) custom-call(s32[6]{0:T(128)S(1)} %convert_element_type.3.flags, bf16[2,16,64,128]{3,2,1,0:T(8,128)(2,1)S(1)} %copy-done, bf16[8,64,128]{2,1,0:T(8,128)(2,1)S(1)} %bitcast.13), custom_call_target="tpu_custom_call" | custom-call | bytes 655384 | tf_op jit(solution)/shard_map/own_edges/pallas_call | solution.py:424
  9.3 1.3 %collective-permute-start.2 = (bf16[11,64,128]{2,1,0:T(8,128)(2,1)S(1)}, bf16[11,64,128]{2,1,0:T(8,128)(2,1)S(1)}, u32[]{:S(2)}, u32[]{:S(2)}) collective-permute-start(bf16[11,64,128]{2,1,0:T(8,128)(2,1)S(1)} %get-tuple-element.47), channel_id=1, source_target_pairs={{0,1},{1,0},{2,3},{3,2},{4,5},{5,4},{6,7},{7,6},{8,9},{9,8},{10,11... | collective-permute-start | bytes 540680 | tf_op jit(solution)/shard_map/ppermute | solution.py:442
  10.6 3.1 %collective-permute-start.3 = (bf16[11,64,128]{2,1,0:T(8,128)(2,1)S(1)}, bf16[11,64,128]{2,1,0:T(8,128)(2,1)S(1)}, u32[]{:S(2)}, u32[]{:S(2)}) collective-permute-start(bf16[11,64,128]{2,1,0:T(8,128)(2,1)S(1)} %get-tuple-element.48), channel_id=1, source_target_pairs={{0,0},{3,3},{1,2},{2,1},{4,4},{7,7},{5,6},{6,5},{8,8},{11,11},{9,1... | collective-permute-start | bytes 540680 | tf_op jit(solution)/shard_map/ppermute | solution.py:441
  15.9 2.5 %collective-permute-start.4 = (bf16[5,64,128]{2,1,0:T(8,128)(2,1)S(1)}, bf16[5,64,128]{2,1,0:T(8,128)(2,1)S(1)}, u32[]{:S(2)}, u32[]{:S(2)}) collective-permute-start(bf16[5,64,128]{2,1,0:T(8,128)(2,1)S(1)} %get-tuple-element.49), channel_id=1, source_target_pairs={{0,4},{1,6},{2,5},{3,7},{4,0},{5,2},{6,1},{7,3},{8,12},{9,14},{10,... | collective-permute-start | bytes 245768 | tf_op jit(solution)/shard_map/ppermute | solution.py:448
  18.3 2.4 %collective-permute-start.6 = (bf16[5,64,128]{2,1,0:T(8,128)(2,1)S(1)}, bf16[5,64,128]{2,1,0:T(8,128)(2,1)S(1)}, u32[]{:S(2)}, u32[]{:S(2)}) collective-permute-start(bf16[5,64,128]{2,1,0:T(8,128)(2,1)S(1)} %get-tuple-element.51), channel_id=1, source_target_pairs={{0,0},{3,3},{1,2},{2,1},{4,4},{7,7},{5,6},{6,5},{8,8},{11,11},{9,1... | collective-permute-start | bytes 245768 | tf_op jit(solution)/shard_map/ppermute | solution.py:441
  20.7 2.0 %fine_forward_interior.1 = (bf16[256,2048]{1,0:T(8,128)(2,1)S(1)}, f32[128,1536]{1,0:T(8,128)S(1)}, bf16[64,768]{1,0:T(8,128)(2,1)S(1)}) custom-call(s32[6]{0:T(128)S(1)} %convert_element_type.3.flags, bf16[2,16,64,128]{3,2,1,0:T(8,128)(2,1)S(1)} %copy-done, bf16[16,64,128]{2,1,0:T(8,128)(2,1)S(1)} %collective-permute-done.xa, ...), custom_call_target="tpu_custom_call" | custom-call | flops 905969664 | bytes 1638424 | tf_op jit(solution)/shard_map/fine_forward_interior/pallas_call | solution.py:424
  22.8 1.3 %collective-permute-done.6.bb = bf16[5,64,128]{2,1,0:T(8,128)(2,1)S(1)} collective-permute-done((bf16[5,64,128]{2,1,0:T(8,128)(2,1)S(1)}, bf16[5,64,128]{2,1,0:T(8,128)(2,1)S(1)}, u32[]{:S(2)}, u32[]{:S(2)}) %collective-permute-start.6) | collective-permute-done | bytes 81952 | tf_op jit(solution)/shard_map/ppermute | solution.py:441
  24.1 2.1 %fine_forward_border.1 = (f32[128,256]{1,0:T(8,128)S(1)}, f32[128,256]{1,0:T(8,128)S(1)}, bf16[64,896]{1,0:T(8,128)(2,1)S(1)}, bf16[256,256]{1,0:T(8,128)(2,1)S(1)}) custom-call(s32[6]{0:T(128)S(1)} %convert_element_type.3.flags, bf16[256,2048]{1,0:T(8,128)(2,1)S(1)} %get-tuple-element.45.v2, bf16[64,768]{1,0:T(8,128)(2,1)S(1)} %get-tuple-element.46.mid, ...), custom_call_target="tpu_custom_call" | custom-call | flops 905969664 | bytes 2424856 | tf_op jit(solution)/shard_map/fine_forward_border/pallas_call | solution.py:424
  26.9 4.7 %collective-permute-start.7 = (bf16[64,896]{1,0:T(8,128)(2,1)S(1)}, bf16[64,896]{1,0:T(8,128)(2,1)S(1)}, u32[]{:S(2)}, u32[]{:S(2)}) collective-permute-start(bf16[64,896]{1,0:T(8,128)(2,1)S(1)} %get-tuple-element.52.own), channel_id=1, source_target_pairs={{0,4},{4,0},{8,12},{12,8},{16,20},{20,16},{24,28},{28,24},{32,36},... | collective-permute-start | bytes 344072 | tf_op jit(solution)/shard_map/ppermute | solution.py:442
  32.6 1.2 %collective-permute-done.7.a = bf16[64,896]{1,0:T(8,128)(2,1)S(1)} collective-permute-done((bf16[64,896]{1,0:T(8,128)(2,1)S(1)}, bf16[64,896]{1,0:T(8,128)(2,1)S(1)}, u32[]{:S(2)}, u32[]{:S(2)}) %collective-permute-start.7) | collective-permute-done | bytes 114720 | tf_op jit(solution)/shard_map/ppermute | solution.py:442
  33.8 1.8 %coarse_forward.1 = (bf16[192,896]{1,0:T(8,128)(2,1)S(1)}, bf16[128,896]{1,0:T(8,128)(2,1)S(1)}, bf16[64,640]{1,0:T(8,128)(2,1)S(1)}, bf16[64,640]{1,0:T(8,128)(2,1)S(1)}) custom-call(s32[6]{0:T(128)S(1)} %convert_element_type.3.flags, bf16[64,896]{1,0:T(8,128)(2,1)S(1)} %get-tuple-element.52.own, bf16[64,896]{1,0:T(8,128)(2,1)S(1)} %collective-permute-done.7.a, ...), custom_call_target="tpu_custom_call" | custom-call | flops 566231040 | bytes 1409048 | tf_op jit(solution)/shard_map/coarse_forward/pallas_call | solution.py:424
  35.6 1.5 %collective-permute-start.9 = (bf16[64,640]{1,0:T(8,128)(2,1)S(1)}, bf16[64,640]{1,0:T(8,128)(2,1)S(1)}, u32[]{:S(2)}, u32[]{:S(2)}) collective-permute-start(bf16[64,640]{1,0:T(8,128)(2,1)S(1)} %get-tuple-element.61), channel_id=1, source_target_pairs={{0,4},{4,0},{8,12},{12,8},{16,20},{20,16},{24,28},{28,24},{32,36},... | collective-permute-start | bytes 245768 | tf_op jit(solution)/shard_map/ppermute | solution.py:442
  37.8 1.4 %coarse_correlate.1 = (f32[64,640]{1,0:T(8,128)S(1)}, bf16[864,128]{1,0:T(8,128)(2,1)S(1)}, bf16[288,128]{1,0:T(8,128)(2,1)S(1)}, bf16[288,128]{1,0:T(8,128)(2,1)S(1)}, bf16[288,128]{1,0:T(8,128)(2,1)S(1)}) custom-call(s32[6]{0:T(128)S(1)} %convert_element_type.3.flags, bf16[192,896]{1,0:T(8,128)(2,1)S(1)} %get-tuple-element.57.p2, ...), custom_call_target="tpu_custom_call" | custom-call | flops 452984832 | bytes 720920 | tf_op jit(solution)/shard_map/coarse_correlate/pallas_call | solution.py:424
  41.0 3.3 %fine_gradient.1 = (bf16[16,64,128]{2,1,0:T(8,128)(2,1)S(1)}, bf16[16,64,128]{2,1,0:T(8,128)(2,1)S(1)}, bf16[128,16,128]{2,1,0:T(8,128)(2,1)}) custom-call(s32[6]{0:T(128)S(1)} %convert_element_type.3.flags, f32[64,640]{1,0:T(8,128)S(1)} %get-tuple-element.60.own, bf16[64,640]{1,0:T(8,128)(2,1)S(1)} %collective-permute-done.9.a, ...), custom_call_target="tpu_custom_call" | custom-call | flops 1207959552 | bytes 3522584 | tf_op jit(solution)/shard_map/fine_gradient/pallas_call | solution.py:424
  44.3 21.4 %all-to-all-start = ((bf16[128,16,128]{2,1,0:T(8,128)(2,1)}), bf16[128,16,128]{2,1,0:T(8,128)(2,1)S(1)}, u32[]{:S(2)}, u32[]{:S(2)}) async-start(bf16[128,16,128]{2,1,0:T(8,128)(2,1)} %get-tuple-element.76), calls=%async_computation | async-start | bytes 1048576 | tf_op jit(solution)/shard_map/all_to_all | solution.py:564
  65.7 1.6 %collective-permute-start.14 = (bf16[16,64,128]{2,1,0:T(8,128)(2,1)S(1)}, bf16[16,64,128]{2,1,0:T(8,128)(2,1)S(1)}, u32[]{:S(2)}, u32[]{:S(2)}) collective-permute-start(bf16[16,64,128]{2,1,0:T(8,128)(2,1)S(1)} %get-tuple-element.71.a.first), channel_id=1, source_target_pairs={{0,4},{4,0},{8,12},{12,8},{16,20},{20,16},{24,28},{28,24},{32,36},... | collective-permute-start | bytes 786440 | tf_op jit(solution)/shard_map/ppermute | solution.py:442
  68.0 11.3 %all-to-all-done.parts = bf16[128,16,128]{2,1,0:T(8,128)(2,1)S(1)} async-done(((bf16[128,16,128]{2,1,0:T(8,128)(2,1)}), bf16[128,16,128]{2,1,0:T(8,128)(2,1)S(1)}, u32[]{:S(2)}, u32[]{:S(2)}) %all-to-all-start) | async-done | bytes 524320 | tf_op jit(solution)/shard_map/all_to_all | solution.py:564
  80.3 4.7 %all-to-all-start.1 = ((bf16[128,24,128]{2,1,0:T(8,128)(2,1)}), bf16[128,24,128]{2,1,0:T(8,128)(2,1)S(1)}, u32[]{:S(2)}, u32[]{:S(2)}) async-start(bf16[128,24,128]{2,1,0:T(8,128)(2,1)} %sum_shares.1), calls=%async_computation.1 | async-start | bytes 1572864 | tf_op jit(solution)/shard_map/all_to_all | solution.py:572
  86.7 2.6 %collective-permute-start.17 = (bf16[4,64,128]{2,1,0:T(8,128)(2,1)S(1)}, bf16[4,64,128]{2,1,0:T(8,128)(2,1)S(1)}, u32[]{:S(2)}, u32[]{:S(2)}) collective-permute-start(bf16[4,64,128]{2,1,0:T(8,128)(2,1)S(1)} %get-tuple-element.74), channel_id=1, source_target_pairs={{0,0},{3,3},{1,2},{2,1},{4,4},{7,7},{5,6},{6,5},{8,8},{11,11},{9,1... | collective-permute-start | bytes 196616 | tf_op jit(solution)/shard_map/ppermute | solution.py:441
  89.4 5.8 %collective-permute-done.17.eb = bf16[4,64,128]{2,1,0:T(8,128)(2,1)S(1)} collective-permute-done((bf16[4,64,128]{2,1,0:T(8,128)(2,1)S(1)}, bf16[4,64,128]{2,1,0:T(8,128)(2,1)S(1)}, u32[]{:S(2)}, u32[]{:S(2)}) %collective-permute-start.17) | collective-permute-done | bytes 65568 | tf_op jit(solution)/shard_map/ppermute | solution.py:441
  95.2 3.0 %input_gradient.1 = bf16[2,16,64,128]{3,2,1,0:T(8,128)(2,1)} custom-call(s32[6]{0:T(128)S(1)} %convert_element_type.3.flags, bf16[16,64,128]{2,1,0:T(8,128)(2,1)S(1)} %get-tuple-element.71.a.first, bf16[16,64,128]{2,1,0:T(8,128)(2,1)S(1)} %get-tuple-element.72.b.second, bf16[16,64,128]{2,1,0:T(8,128)(2,1)S(1)} %collective-permute-done.14.c.a, ...), custom_call_target="tpu_custom_call" | custom-call | flops 1207959552 | bytes 1769496 | tf_op jit(solution)/shard_map/input_gradient/pallas_call | solution.py:424
  98.1 2.9 %all-to-all-done.1.got = bf16[128,24,128]{2,1,0:T(8,128)(2,1)S(1)} async-done(((bf16[128,24,128]{2,1,0:T(8,128)(2,1)}), bf16[128,24,128]{2,1,0:T(8,128)(2,1)S(1)}, u32[]{:S(2)}, u32[]{:S(2)}) %all-to-all-start.1) | async-done | bytes 786464 | tf_op jit(solution)/shard_map/all_to_all | solution.py:572
  101.0 1.4 %unpack.1 = (f32[3,3,3,64,64]{4,3,2,1,0:T(8,128)}, f32[3,3,3,64,128]{4,3,2,1,0:T(8,128)}) custom-call(bf16[128,24,128]{2,1,0:T(8,128)(2,1)S(1)} %all-to-all-done.1.got), custom_call_target="tpu_custom_call" | custom-call | bytes 786432 | tf_op jit(solution)/shard_map/unpack/pallas_call | solution.py:424
  (42 shorter events, 11.7 us)
Async XLA Ops:
  0.6 7.5 %copy-start = (bf16[2,16,64,128]{3,2,1,0:T(8,128)(2,1)S(1)}, bf16[2,16,64,128]{3,2,1,0:T(8,128)(2,1)}, u32[]{:S(2)}) copy-start(bf16[2,16,64,128]{3,2,1,0:T(8,128)(2,1)} %own.3) | copy-start | bytes 1572868
  0.6 7.4 %copy-start.1 = (bf16[1,8,128,64]{2,3,1,0:T(8,128)(2,1)S(1)}, bf16[1,8,128,64]{2,3,1,0:T(8,128)(2,1)}, u32[]{:S(2)}) copy-start(bf16[1,8,128,64]{2,3,1,0:T(8,128)(2,1)} %param.7) | copy-start | bytes 393220
  0.7 13.1 %copy-start.3 = (bf16[3,3,3,64,128]{4,3,2,1,0:T(8,128)(2,1)S(1)}, bf16[3,3,3,64,128]{4,3,2,1,0:T(8,128)(2,1)}, u32[]{:S(2)}) copy-start(bf16[3,3,3,64,128]{4,3,2,1,0:T(8,128)(2,1)} %wc.1) | copy-start | bytes 1327108
  0.7 13.1 %copy-start.2 = (bf16[3,3,3,64,64]{4,3,2,1,0:T(8,128)(2,1)S(1)}, bf16[3,3,3,64,64]{4,3,2,1,0:T(8,128)(2,1)}, u32[]{:S(2)}) copy-start(bf16[3,3,3,64,64]{4,3,2,1,0:T(8,128)(2,1)} %wf.1) | copy-start | bytes 663556
  1.9 12.5 %collective-permute-start.1 = (bf16[16,64,128]{2,1,0:T(8,128)(2,1)S(1)}, bf16[16,64,128]{2,1,0:T(8,128)(2,1)S(1)}, u32[]{:S(2)}, u32[]{:S(2)}) collective-permute-start(bf16[16,64,128]{2,1,0:T(8,128)(2,1)S(1)} %get-tuple-element.79), channel_id=1, source_target_pairs={{0,0},{124,124},{4,8},{8,4},{12,16},{16,12},{20,24},{24,20},{28,32... | collective-permute-start | bytes 786440 | tf_op jit(solution)/shard_map/ppermute | solution.py:441
  2.6 11.9 %collective-permute-start = (bf16[16,64,128]{2,1,0:T(8,128)(2,1)S(1)}, bf16[16,64,128]{2,1,0:T(8,128)(2,1)S(1)}, u32[]{:S(2)}, u32[]{:S(2)}) collective-permute-start(bf16[16,64,128]{2,1,0:T(8,128)(2,1)S(1)} %get-tuple-element.80), channel_id=1, source_target_pairs={{0,4},{4,0},{8,12},{12,8},{16,20},{20,16},{24,28},{28,24},{32,36},... | collective-permute-start | bytes 786440 | tf_op jit(solution)/shard_map/ppermute | solution.py:442
  9.3 13.4 %collective-permute-start.2 = (bf16[11,64,128]{2,1,0:T(8,128)(2,1)S(1)}, bf16[11,64,128]{2,1,0:T(8,128)(2,1)S(1)}, u32[]{:S(2)}, u32[]{:S(2)}) collective-permute-start(bf16[11,64,128]{2,1,0:T(8,128)(2,1)S(1)} %get-tuple-element.47), channel_id=1, source_target_pairs={{0,1},{1,0},{2,3},{3,2},{4,5},{5,4},{6,7},{7,6},{8,9},{9,8},{10,11... | collective-permute-start | bytes 540680 | tf_op jit(solution)/shard_map/ppermute | solution.py:442
  10.6 12.1 %collective-permute-start.3 = (bf16[11,64,128]{2,1,0:T(8,128)(2,1)S(1)}, bf16[11,64,128]{2,1,0:T(8,128)(2,1)S(1)}, u32[]{:S(2)}, u32[]{:S(2)}) collective-permute-start(bf16[11,64,128]{2,1,0:T(8,128)(2,1)S(1)} %get-tuple-element.48), channel_id=1, source_target_pairs={{0,0},{3,3},{1,2},{2,1},{4,4},{7,7},{5,6},{6,5},{8,8},{11,11},{9,1... | collective-permute-start | bytes 540680 | tf_op jit(solution)/shard_map/ppermute | solution.py:441
  15.0 9.1 %collective-permute-start.5 = (bf16[10,64,128]{2,1,0:T(8,128)(2,1)S(1)}, bf16[10,64,128]{2,1,0:T(8,128)(2,1)S(1)}, u32[]{:S(2)}, u32[]{:S(2)}) collective-permute-start(bf16[10,64,128]{2,1,0:T(8,128)(2,1)S(1)} %get-tuple-element.50), channel_id=1, source_target_pairs={{0,1},{1,0},{2,3},{3,2},{4,5},{5,4},{6,7},{7,6},{8,9},{9,8},{10,11... | collective-permute-start | bytes 491528 | tf_op jit(solution)/shard_map/ppermute | solution.py:442
  15.9 6.8 %collective-permute-start.4 = (bf16[5,64,128]{2,1,0:T(8,128)(2,1)S(1)}, bf16[5,64,128]{2,1,0:T(8,128)(2,1)S(1)}, u32[]{:S(2)}, u32[]{:S(2)}) collective-permute-start(bf16[5,64,128]{2,1,0:T(8,128)(2,1)S(1)} %get-tuple-element.49), channel_id=1, source_target_pairs={{0,4},{1,6},{2,5},{3,7},{4,0},{5,2},{6,1},{7,3},{8,12},{9,14},{10,... | collective-permute-start | bytes 245768 | tf_op jit(solution)/shard_map/ppermute | solution.py:448
  18.3 5.7 %collective-permute-start.6 = (bf16[5,64,128]{2,1,0:T(8,128)(2,1)S(1)}, bf16[5,64,128]{2,1,0:T(8,128)(2,1)S(1)}, u32[]{:S(2)}, u32[]{:S(2)}) collective-permute-start(bf16[5,64,128]{2,1,0:T(8,128)(2,1)S(1)} %get-tuple-element.51), channel_id=1, source_target_pairs={{0,0},{3,3},{1,2},{2,1},{4,4},{7,7},{5,6},{6,5},{8,8},{11,11},{9,1... | collective-permute-start | bytes 245768 | tf_op jit(solution)/shard_map/ppermute | solution.py:441
  26.2 6.3 %collective-permute-start.8 = (bf16[64,896]{1,0:T(8,128)(2,1)S(1)}, bf16[64,896]{1,0:T(8,128)(2,1)S(1)}, u32[]{:S(2)}, u32[]{:S(2)}) collective-permute-start(bf16[64,896]{1,0:T(8,128)(2,1)S(1)} %get-tuple-element.52.own), channel_id=1, source_target_pairs={{0,0},{124,124},{4,8},{8,4},{12,16},{16,12},{20,24},{24,20},{28,32... | collective-permute-start | bytes 344072 | tf_op jit(solution)/shard_map/ppermute | solution.py:441
  26.9 6.9 %collective-permute-start.7 = (bf16[64,896]{1,0:T(8,128)(2,1)S(1)}, bf16[64,896]{1,0:T(8,128)(2,1)S(1)}, u32[]{:S(2)}, u32[]{:S(2)}) collective-permute-start(bf16[64,896]{1,0:T(8,128)(2,1)S(1)} %get-tuple-element.52.own), channel_id=1, source_target_pairs={{0,4},{4,0},{8,12},{12,8},{16,20},{20,16},{24,28},{28,24},{32,36},... | collective-permute-start | bytes 344072 | tf_op jit(solution)/shard_map/ppermute | solution.py:442
  35.6 5.4 %collective-permute-start.9 = (bf16[64,640]{1,0:T(8,128)(2,1)S(1)}, bf16[64,640]{1,0:T(8,128)(2,1)S(1)}, u32[]{:S(2)}, u32[]{:S(2)}) collective-permute-start(bf16[64,640]{1,0:T(8,128)(2,1)S(1)} %get-tuple-element.61), channel_id=1, source_target_pairs={{0,4},{4,0},{8,12},{12,8},{16,20},{20,16},{24,28},{28,24},{32,36},... | collective-permute-start | bytes 245768 | tf_op jit(solution)/shard_map/ppermute | solution.py:442
  37.1 3.9 %collective-permute-start.10 = (bf16[64,640]{1,0:T(8,128)(2,1)S(1)}, bf16[64,640]{1,0:T(8,128)(2,1)S(1)}, u32[]{:S(2)}, u32[]{:S(2)}) collective-permute-start(bf16[64,640]{1,0:T(8,128)(2,1)S(1)} %get-tuple-element.62), channel_id=1, source_target_pairs={{0,0},{124,124},{4,8},{8,4},{12,16},{16,12},{20,24},{24,20},{28,32... | collective-permute-start | bytes 245768 | tf_op jit(solution)/shard_map/ppermute | solution.py:441
  39.1 1.3 %collective-permute-start.11 = (bf16[288,128]{1,0:T(8,128)(2,1)S(1)}, bf16[288,128]{1,0:T(8,128)(2,1)S(1)}, u32[]{:S(2)}, u32[]{:S(2)}) collective-permute-start(bf16[288,128]{1,0:T(8,128)(2,1)S(1)} %get-tuple-element.68), channel_id=1, source_target_pairs={{0,1},{1,0},{2,3},{3,2},{4,5},{5,4},{6,7},{7,6},{8,9},{9,8},{10,11... | collective-permute-start | bytes 221192 | tf_op jit(solution)/shard_map/ppermute | solution.py:537
  39.2 1.4 %collective-permute-start.12 = (bf16[288,128]{1,0:T(8,128)(2,1)S(1)}, bf16[288,128]{1,0:T(8,128)(2,1)S(1)}, u32[]{:S(2)}, u32[]{:S(2)}) collective-permute-start(bf16[288,128]{1,0:T(8,128)(2,1)S(1)} %get-tuple-element.69), channel_id=1, source_target_pairs={{0,1},{1,0},{2,3},{3,2},{4,5},{5,4},{6,7},{7,6},{8,9},{9,8},{10,11... | collective-permute-start | bytes 221192 | tf_op jit(solution)/shard_map/ppermute | solution.py:537
  39.7 1.3 %collective-permute-start.13 = (bf16[288,128]{1,0:T(8,128)(2,1)S(1)}, bf16[288,128]{1,0:T(8,128)(2,1)S(1)}, u32[]{:S(2)}, u32[]{:S(2)}) collective-permute-start(bf16[288,128]{1,0:T(8,128)(2,1)S(1)} %get-tuple-element.70), channel_id=1, source_target_pairs={{0,1},{1,0},{2,3},{3,2},{4,5},{5,4},{6,7},{7,6},{8,9},{9,8},{10,11... | collective-permute-start | bytes 221192 | tf_op jit(solution)/shard_map/ppermute | solution.py:537
  44.3 35.0 %all-to-all-start = ((bf16[128,16,128]{2,1,0:T(8,128)(2,1)}), bf16[128,16,128]{2,1,0:T(8,128)(2,1)S(1)}, u32[]{:S(2)}, u32[]{:S(2)}) async-start(bf16[128,16,128]{2,1,0:T(8,128)(2,1)} %get-tuple-element.76), calls=%async_computation | async-start | bytes 1048576 | tf_op jit(solution)/shard_map/all_to_all | solution.py:564
  65.7 19.3 %collective-permute-start.14 = (bf16[16,64,128]{2,1,0:T(8,128)(2,1)S(1)}, bf16[16,64,128]{2,1,0:T(8,128)(2,1)S(1)}, u32[]{:S(2)}, u32[]{:S(2)}) collective-permute-start(bf16[16,64,128]{2,1,0:T(8,128)(2,1)S(1)} %get-tuple-element.71.a.first), channel_id=1, source_target_pairs={{0,4},{4,0},{8,12},{12,8},{16,20},{20,16},{24,28},{28,24},{32,36},... | collective-permute-start | bytes 786440 | tf_op jit(solution)/shard_map/ppermute | solution.py:442
  67.3 17.7 %collective-permute-start.15 = (bf16[16,64,128]{2,1,0:T(8,128)(2,1)S(1)}, bf16[16,64,128]{2,1,0:T(8,128)(2,1)S(1)}, u32[]{:S(2)}, u32[]{:S(2)}) collective-permute-start(bf16[16,64,128]{2,1,0:T(8,128)(2,1)S(1)} %get-tuple-element.72.b.second), channel_id=1, source_target_pairs={{0,0},{124,124},{4,8},{8,4},{12,16},{16,12},{20,24},{24,20},{28,32... | collective-permute-start | bytes 786440 | tf_op jit(solution)/shard_map/ppermute | solution.py:441
  80.3 20.7 %all-to-all-start.1 = ((bf16[128,24,128]{2,1,0:T(8,128)(2,1)}), bf16[128,24,128]{2,1,0:T(8,128)(2,1)S(1)}, u32[]{:S(2)}, u32[]{:S(2)}) async-start(bf16[128,24,128]{2,1,0:T(8,128)(2,1)} %sum_shares.1), calls=%async_computation.1 | async-start | bytes 1572864 | tf_op jit(solution)/shard_map/all_to_all | solution.py:572
  85.6 3.8 %collective-permute-start.16 = (bf16[4,64,128]{2,1,0:T(8,128)(2,1)S(1)}, bf16[4,64,128]{2,1,0:T(8,128)(2,1)S(1)}, u32[]{:S(2)}, u32[]{:S(2)}) collective-permute-start(bf16[4,64,128]{2,1,0:T(8,128)(2,1)S(1)} %get-tuple-element.73), channel_id=1, source_target_pairs={{0,1},{1,0},{2,3},{3,2},{4,5},{5,4},{6,7},{7,6},{8,9},{9,8},{10,11... | collective-permute-start | bytes 196616 | tf_op jit(solution)/shard_map/ppermute | solution.py:442
  86.7 8.4 %collective-permute-start.17 = (bf16[4,64,128]{2,1,0:T(8,128)(2,1)S(1)}, bf16[4,64,128]{2,1,0:T(8,128)(2,1)S(1)}, u32[]{:S(2)}, u32[]{:S(2)}) collective-permute-start(bf16[4,64,128]{2,1,0:T(8,128)(2,1)S(1)} %get-tuple-element.74), channel_id=1, source_target_pairs={{0,0},{3,3},{1,2},{2,1},{4,4},{7,7},{5,6},{6,5},{8,8},{11,11},{9,1... | collective-permute-start | bytes 196616 | tf_op jit(solution)/shard_map/ppermute | solution.py:441
  (1 other events, 5.4 us)

commit v7 on v6

--- a/solution.py
+++ b/solution.py
@@ -75,7 +75,7 @@
     sums, slps = [], []
     for pre in combine(acc, 128, tiles, lane):
         sig, slp = slopes(pre)
-        act = (pre * sig).astype(BF).astype(F32)
+        act = pre * sig
         sums.append(act[:64] + act[64:])
         slps.append(slp)
     means = []

time: 103 us -> 103 us (level)
  no operation moved by 1% of the time
where the time goes in v7:
time: 103 us; the launch traced here: 102 us
  starting transfers between devices  56.5 us (55%)
  waiting for transfers between devices  23.7 us (23%)
  Pallas kernels  19.9 us (19%)
  local copies, waits for them, and re-layouts  1.3 us (1%)
    all_to_all x1, starting transfers between devices, on_device(): lax.all_to_all(mine.reshape(128 * 2 * R, L), ('slab', 'sub'), 0, 0, tiled...  21.4 us
    pallas_call x13, Pallas kernels, call(): pl.pallas_call(kernel, out_shape=shapes, in_specs=specs, out_specs=tuple(...  19.9 us
    ppermute x7, starting transfers between devices, swaps(): return (lax.ppermute(first, axis, pairs), other)  16.5 us
    all_to_all x1, waiting for transfers between devices, on_device(): lax.all_to_all(mine.reshape(128 * 2 * R, L), ('slab', 'sub'), 0, 0, tiled...  11.3 us
    ppermute x7, starting transfers between devices, swaps(): other = lax.ppermute(second, axis, others)  10.7 us
    ppermute x7, waiting for transfers between devices, swaps(): other = lax.ppermute(second, axis, others)  7.15 us
    all_to_all x1, starting transfers between devices, on_device(): lax.all_to_all(total.reshape(128 * 3 * R, L), ('slab', 'sub'), 0, 0, tile...  4.67 us
    all_to_all x1, waiting for transfers between devices, on_device(): lax.all_to_all(total.reshape(128 * 3 * R, L), ('slab', 'sub'), 0, 0, tile...  2.88 us
  transfers between devices with their start and end apart: 20, of which 8 were waited for; matrix products, arithmetic and copies ran while one was open for 0% of the time, Pallas kernels for 11%

profile of v7, /device:TPU:1, one launch (start us, length us, event | category | flops | bytes accessed | tf_op | source)
XLA Modules:
  0.0 102.4 jit_solution(9828288933939062118)
XLA Ops:
  2.6 5.4 %collective-permute-start = (bf16[16,64,128]{2,1,0:T(8,128)(2,1)S(1)}, bf16[16,64,128]{2,1,0:T(8,128)(2,1)S(1)}, u32[]{:S(2)}, u32[]{:S(2)}) collective-permute-start(bf16[16,64,128]{2,1,0:T(8,128)(2,1)S(1)} %get-tuple-element.80), channel_id=1, source_target_pairs={{0,4},{4,0},{8,12},{12,8},{16,20},{20,16},{24,28},{28,24},{32,36},... | collective-permute-start | bytes 786440 | tf_op jit(solution)/shard_map/ppermute | solution.py:442
  8.1 1.2 %own_edges.1 = (bf16[11,64,128]{2,1,0:T(8,128)(2,1)S(1)}, bf16[11,64,128]{2,1,0:T(8,128)(2,1)S(1)}, bf16[5,64,128]{2,1,0:T(8,128)(2,1)S(1)}) custom-call(s32[6]{0:T(128)S(1)} %convert_element_type.3.flags, bf16[2,16,64,128]{3,2,1,0:T(8,128)(2,1)S(1)} %copy-done, bf16[8,64,128]{2,1,0:T(8,128)(2,1)S(1)} %bitcast.13), custom_call_target="tpu_custom_call" | custom-call | bytes 655384 | tf_op jit(solution)/shard_map/own_edges/pallas_call | solution.py:424
  9.3 1.3 %collective-permute-start.2 = (bf16[11,64,128]{2,1,0:T(8,128)(2,1)S(1)}, bf16[11,64,128]{2,1,0:T(8,128)(2,1)S(1)}, u32[]{:S(2)}, u32[]{:S(2)}) collective-permute-start(bf16[11,64,128]{2,1,0:T(8,128)(2,1)S(1)} %get-tuple-element.47), channel_id=1, source_target_pairs={{0,1},{1,0},{2,3},{3,2},{4,5},{5,4},{6,7},{7,6},{8,9},{9,8},{10,11... | collective-permute-start | bytes 540680 | tf_op jit(solution)/shard_map/ppermute | solution.py:442
  10.6 3.1 %collective-permute-start.3 = (bf16[11,64,128]{2,1,0:T(8,128)(2,1)S(1)}, bf16[11,64,128]{2,1,0:T(8,128)(2,1)S(1)}, u32[]{:S(2)}, u32[]{:S(2)}) collective-permute-start(bf16[11,64,128]{2,1,0:T(8,128)(2,1)S(1)} %get-tuple-element.48), channel_id=1, source_target_pairs={{0,0},{3,3},{1,2},{2,1},{4,4},{7,7},{5,6},{6,5},{8,8},{11,11},{9,1... | collective-permute-start | bytes 540680 | tf_op jit(solution)/shard_map/ppermute | solution.py:441
  15.9 2.5 %collective-permute-start.4 = (bf16[5,64,128]{2,1,0:T(8,128)(2,1)S(1)}, bf16[5,64,128]{2,1,0:T(8,128)(2,1)S(1)}, u32[]{:S(2)}, u32[]{:S(2)}) collective-permute-start(bf16[5,64,128]{2,1,0:T(8,128)(2,1)S(1)} %get-tuple-element.49), channel_id=1, source_target_pairs={{0,4},{1,6},{2,5},{3,7},{4,0},{5,2},{6,1},{7,3},{8,12},{9,14},{10,... | collective-permute-start | bytes 245768 | tf_op jit(solution)/shard_map/ppermute | solution.py:448
  18.3 2.4 %collective-permute-start.6 = (bf16[5,64,128]{2,1,0:T(8,128)(2,1)S(1)}, bf16[5,64,128]{2,1,0:T(8,128)(2,1)S(1)}, u32[]{:S(2)}, u32[]{:S(2)}) collective-permute-start(bf16[5,64,128]{2,1,0:T(8,128)(2,1)S(1)} %get-tuple-element.51), channel_id=1, source_target_pairs={{0,0},{3,3},{1,2},{2,1},{4,4},{7,7},{5,6},{6,5},{8,8},{11,11},{9,1... | collective-permute-start | bytes 245768 | tf_op jit(solution)/shard_map/ppermute | solution.py:441
  20.7 2.0 %fine_forward_interior.1 = (bf16[256,2048]{1,0:T(8,128)(2,1)S(1)}, f32[128,1536]{1,0:T(8,128)S(1)}, bf16[64,768]{1,0:T(8,128)(2,1)S(1)}) custom-call(s32[6]{0:T(128)S(1)} %convert_element_type.3.flags, bf16[2,16,64,128]{3,2,1,0:T(8,128)(2,1)S(1)} %copy-done, bf16[16,64,128]{2,1,0:T(8,128)(2,1)S(1)} %collective-permute-done.xa, ...), custom_call_target="tpu_custom_call" | custom-call | flops 905969664 | bytes 1638424 | tf_op jit(solution)/shard_map/fine_forward_interior/pallas_call | solution.py:424
  22.8 1.3 %collective-permute-done.6.bb = bf16[5,64,128]{2,1,0:T(8,128)(2,1)S(1)} collective-permute-done((bf16[5,64,128]{2,1,0:T(8,128)(2,1)S(1)}, bf16[5,64,128]{2,1,0:T(8,128)(2,1)S(1)}, u32[]{:S(2)}, u32[]{:S(2)}) %collective-permute-start.6) | collective-permute-done | bytes 81952 | tf_op jit(solution)/shard_map/ppermute | solution.py:441
  24.1 2.1 %fine_forward_border.1 = (f32[128,256]{1,0:T(8,128)S(1)}, f32[128,256]{1,0:T(8,128)S(1)}, bf16[64,896]{1,0:T(8,128)(2,1)S(1)}, bf16[256,256]{1,0:T(8,128)(2,1)S(1)}) custom-call(s32[6]{0:T(128)S(1)} %convert_element_type.3.flags, bf16[256,2048]{1,0:T(8,128)(2,1)S(1)} %get-tuple-element.45.v2, bf16[64,768]{1,0:T(8,128)(2,1)S(1)} %get-tuple-element.46.mid, ...), custom_call_target="tpu_custom_call" | custom-call | flops 905969664 | bytes 2424856 | tf_op jit(solution)/shard_map/fine_forward_border/pallas_call | solution.py:424
  26.9 4.7 %collective-permute-start.7 = (bf16[64,896]{1,0:T(8,128)(2,1)S(1)}, bf16[64,896]{1,0:T(8,128)(2,1)S(1)}, u32[]{:S(2)}, u32[]{:S(2)}) collective-permute-start(bf16[64,896]{1,0:T(8,128)(2,1)S(1)} %get-tuple-element.52.own), channel_id=1, source_target_pairs={{0,4},{4,0},{8,12},{12,8},{16,20},{20,16},{24,28},{28,24},{32,36},... | collective-permute-start | bytes 344072 | tf_op jit(solution)/shard_map/ppermute | solution.py:442
  32.6 1.2 %collective-permute-done.7.a = bf16[64,896]{1,0:T(8,128)(2,1)S(1)} collective-permute-done((bf16[64,896]{1,0:T(8,128)(2,1)S(1)}, bf16[64,896]{1,0:T(8,128)(2,1)S(1)}, u32[]{:S(2)}, u32[]{:S(2)}) %collective-permute-start.7) | collective-permute-done | bytes 114720 | tf_op jit(solution)/shard_map/ppermute | solution.py:442
  33.8 1.8 %coarse_forward.1 = (bf16[192,896]{1,0:T(8,128)(2,1)S(1)}, bf16[128,896]{1,0:T(8,128)(2,1)S(1)}, bf16[64,640]{1,0:T(8,128)(2,1)S(1)}, bf16[64,640]{1,0:T(8,128)(2,1)S(1)}) custom-call(s32[6]{0:T(128)S(1)} %convert_element_type.3.flags, bf16[64,896]{1,0:T(8,128)(2,1)S(1)} %get-tuple-element.52.own, bf16[64,896]{1,0:T(8,128)(2,1)S(1)} %collective-permute-done.7.a, ...), custom_call_target="tpu_custom_call" | custom-call | flops 566231040 | bytes 1409048 | tf_op jit(solution)/shard_map/coarse_forward/pallas_call | solution.py:424
  35.6 1.5 %collective-permute-start.9 = (bf16[64,640]{1,0:T(8,128)(2,1)S(1)}, bf16[64,640]{1,0:T(8,128)(2,1)S(1)}, u32[]{:S(2)}, u32[]{:S(2)}) collective-permute-start(bf16[64,640]{1,0:T(8,128)(2,1)S(1)} %get-tuple-element.61), channel_id=1, source_target_pairs={{0,4},{4,0},{8,12},{12,8},{16,20},{20,16},{24,28},{28,24},{32,36},... | collective-permute-start | bytes 245768 | tf_op jit(solution)/shard_map/ppermute | solution.py:442
  37.8 1.4 %coarse_correlate.1 = (f32[64,640]{1,0:T(8,128)S(1)}, bf16[864,128]{1,0:T(8,128)(2,1)S(1)}, bf16[288,128]{1,0:T(8,128)(2,1)S(1)}, bf16[288,128]{1,0:T(8,128)(2,1)S(1)}, bf16[288,128]{1,0:T(8,128)(2,1)S(1)}) custom-call(s32[6]{0:T(128)S(1)} %convert_element_type.3.flags, bf16[192,896]{1,0:T(8,128)(2,1)S(1)} %get-tuple-element.57.p2, ...), custom_call_target="tpu_custom_call" | custom-call | flops 452984832 | bytes 720920 | tf_op jit(solution)/shard_map/coarse_correlate/pallas_call | solution.py:424
  41.0 3.3 %fine_gradient.1 = (bf16[16,64,128]{2,1,0:T(8,128)(2,1)S(1)}, bf16[16,64,128]{2,1,0:T(8,128)(2,1)S(1)}, bf16[128,16,128]{2,1,0:T(8,128)(2,1)}) custom-call(s32[6]{0:T(128)S(1)} %convert_element_type.3.flags, f32[64,640]{1,0:T(8,128)S(1)} %get-tuple-element.60.own, bf16[64,640]{1,0:T(8,128)(2,1)S(1)} %collective-permute-done.9.a, ...), custom_call_target="tpu_custom_call" | custom-call | flops 1207959552 | bytes 3522584 | tf_op jit(solution)/shard_map/fine_gradient/pallas_call | solution.py:424
  44.3 21.4 %all-to-all-start = ((bf16[128,16,128]{2,1,0:T(8,128)(2,1)}), bf16[128,16,128]{2,1,0:T(8,128)(2,1)S(1)}, u32[]{:S(2)}, u32[]{:S(2)}) async-start(bf16[128,16,128]{2,1,0:T(8,128)(2,1)} %get-tuple-element.76), calls=%async_computation | async-start | bytes 1048576 | tf_op jit(solution)/shard_map/all_to_all | solution.py:564
  65.7 1.6 %collective-permute-start.14 = (bf16[16,64,128]{2,1,0:T(8,128)(2,1)S(1)}, bf16[16,64,128]{2,1,0:T(8,128)(2,1)S(1)}, u32[]{:S(2)}, u32[]{:S(2)}) collective-permute-start(bf16[16,64,128]{2,1,0:T(8,128)(2,1)S(1)} %get-tuple-element.71.a.first), channel_id=1, source_target_pairs={{0,4},{4,0},{8,12},{12,8},{16,20},{20,16},{24,28},{28,24},{32,36},... | collective-permute-start | bytes 786440 | tf_op jit(solution)/shard_map/ppermute | solution.py:442
  68.0 11.3 %all-to-all-done.parts = bf16[128,16,128]{2,1,0:T(8,128)(2,1)S(1)} async-done(((bf16[128,16,128]{2,1,0:T(8,128)(2,1)}), bf16[128,16,128]{2,1,0:T(8,128)(2,1)S(1)}, u32[]{:S(2)}, u32[]{:S(2)}) %all-to-all-start) | async-done | bytes 524320 | tf_op jit(solution)/shard_map/all_to_all | solution.py:564
  80.3 4.7 %all-to-all-start.1 = ((bf16[128,24,128]{2,1,0:T(8,128)(2,1)}), bf16[128,24,128]{2,1,0:T(8,128)(2,1)S(1)}, u32[]{:S(2)}, u32[]{:S(2)}) async-start(bf16[128,24,128]{2,1,0:T(8,128)(2,1)} %sum_shares.1), calls=%async_computation.1 | async-start | bytes 1572864 | tf_op jit(solution)/shard_map/all_to_all | solution.py:572
  86.7 2.6 %collective-permute-start.17 = (bf16[4,64,128]{2,1,0:T(8,128)(2,1)S(1)}, bf16[4,64,128]{2,1,0:T(8,128)(2,1)S(1)}, u32[]{:S(2)}, u32[]{:S(2)}) collective-permute-start(bf16[4,64,128]{2,1,0:T(8,128)(2,1)S(1)} %get-tuple-element.74), channel_id=1, source_target_pairs={{0,0},{3,3},{1,2},{2,1},{4,4},{7,7},{5,6},{6,5},{8,8},{11,11},{9,1... | collective-permute-start | bytes 196616 | tf_op jit(solution)/shard_map/ppermute | solution.py:441
  89.4 5.8 %collective-permute-done.17.eb = bf16[4,64,128]{2,1,0:T(8,128)(2,1)S(1)} collective-permute-done((bf16[4,64,128]{2,1,0:T(8,128)(2,1)S(1)}, bf16[4,64,128]{2,1,0:T(8,128)(2,1)S(1)}, u32[]{:S(2)}, u32[]{:S(2)}) %collective-permute-start.17) | collective-permute-done | bytes 65568 | tf_op jit(solution)/shard_map/ppermute | solution.py:441
  95.2 3.0 %input_gradient.1 = bf16[2,16,64,128]{3,2,1,0:T(8,128)(2,1)} custom-call(s32[6]{0:T(128)S(1)} %convert_element_type.3.flags, bf16[16,64,128]{2,1,0:T(8,128)(2,1)S(1)} %get-tuple-element.71.a.first, bf16[16,64,128]{2,1,0:T(8,128)(2,1)S(1)} %get-tuple-element.72.b.second, bf16[16,64,128]{2,1,0:T(8,128)(2,1)S(1)} %collective-permute-done.14.c.a, ...), custom_call_target="tpu_custom_call" | custom-call | flops 1207959552 | bytes 1769496 | tf_op jit(solution)/shard_map/input_gradient/pallas_call | solution.py:424
  98.1 2.9 %all-to-all-done.1.got = bf16[128,24,128]{2,1,0:T(8,128)(2,1)S(1)} async-done(((bf16[128,24,128]{2,1,0:T(8,128)(2,1)}), bf16[128,24,128]{2,1,0:T(8,128)(2,1)S(1)}, u32[]{:S(2)}, u32[]{:S(2)}) %all-to-all-start.1) | async-done | bytes 786464 | tf_op jit(solution)/shard_map/all_to_all | solution.py:572
  101.0 1.4 %unpack.1 = (f32[3,3,3,64,64]{4,3,2,1,0:T(8,128)}, f32[3,3,3,64,128]{4,3,2,1,0:T(8,128)}) custom-call(bf16[128,24,128]{2,1,0:T(8,128)(2,1)S(1)} %all-to-all-done.1.got), custom_call_target="tpu_custom_call" | custom-call | bytes 786432 | tf_op jit(solution)/shard_map/unpack/pallas_call | solution.py:424
  (42 shorter events, 11.7 us)
Async XLA Ops:
  0.6 7.5 %copy-start = (bf16[2,16,64,128]{3,2,1,0:T(8,128)(2,1)S(1)}, bf16[2,16,64,128]{3,2,1,0:T(8,128)(2,1)}, u32[]{:S(2)}) copy-start(bf16[2,16,64,128]{3,2,1,0:T(8,128)(2,1)} %own.3) | copy-start | bytes 1572868
  0.6 7.4 %copy-start.1 = (bf16[1,8,128,64]{2,3,1,0:T(8,128)(2,1)S(1)}, bf16[1,8,128,64]{2,3,1,0:T(8,128)(2,1)}, u32[]{:S(2)}) copy-start(bf16[1,8,128,64]{2,3,1,0:T(8,128)(2,1)} %param.7) | copy-start | bytes 393220
  0.7 13.1 %copy-start.3 = (bf16[3,3,3,64,128]{4,3,2,1,0:T(8,128)(2,1)S(1)}, bf16[3,3,3,64,128]{4,3,2,1,0:T(8,128)(2,1)}, u32[]{:S(2)}) copy-start(bf16[3,3,3,64,128]{4,3,2,1,0:T(8,128)(2,1)} %wc.1) | copy-start | bytes 1327108
  0.7 13.1 %copy-start.2 = (bf16[3,3,3,64,64]{4,3,2,1,0:T(8,128)(2,1)S(1)}, bf16[3,3,3,64,64]{4,3,2,1,0:T(8,128)(2,1)}, u32[]{:S(2)}) copy-start(bf16[3,3,3,64,64]{4,3,2,1,0:T(8,128)(2,1)} %wf.1) | copy-start | bytes 663556
  1.9 12.5 %collective-permute-start.1 = (bf16[16,64,128]{2,1,0:T(8,128)(2,1)S(1)}, bf16[16,64,128]{2,1,0:T(8,128)(2,1)S(1)}, u32[]{:S(2)}, u32[]{:S(2)}) collective-permute-start(bf16[16,64,128]{2,1,0:T(8,128)(2,1)S(1)} %get-tuple-element.79), channel_id=1, source_target_pairs={{0,0},{124,124},{4,8},{8,4},{12,16},{16,12},{20,24},{24,20},{28,32... | collective-permute-start | bytes 786440 | tf_op jit(solution)/shard_map/ppermute | solution.py:441
  2.6 11.9 %collective-permute-start = (bf16[16,64,128]{2,1,0:T(8,128)(2,1)S(1)}, bf16[16,64,128]{2,1,0:T(8,128)(2,1)S(1)}, u32[]{:S(2)}, u32[]{:S(2)}) collective-permute-start(bf16[16,64,128]{2,1,0:T(8,128)(2,1)S(1)} %get-tuple-element.80), channel_id=1, source_target_pairs={{0,4},{4,0},{8,12},{12,8},{16,20},{20,16},{24,28},{28,24},{32,36},... | collective-permute-start | bytes 786440 | tf_op jit(solution)/shard_map/ppermute | solution.py:442
  9.3 13.4 %collective-permute-start.2 = (bf16[11,64,128]{2,1,0:T(8,128)(2,1)S(1)}, bf16[11,64,128]{2,1,0:T(8,128)(2,1)S(1)}, u32[]{:S(2)}, u32[]{:S(2)}) collective-permute-start(bf16[11,64,128]{2,1,0:T(8,128)(2,1)S(1)} %get-tuple-element.47), channel_id=1, source_target_pairs={{0,1},{1,0},{2,3},{3,2},{4,5},{5,4},{6,7},{7,6},{8,9},{9,8},{10,11... | collective-permute-start | bytes 540680 | tf_op jit(solution)/shard_map/ppermute | solution.py:442
  10.6 12.1 %collective-permute-start.3 = (bf16[11,64,128]{2,1,0:T(8,128)(2,1)S(1)}, bf16[11,64,128]{2,1,0:T(8,128)(2,1)S(1)}, u32[]{:S(2)}, u32[]{:S(2)}) collective-permute-start(bf16[11,64,128]{2,1,0:T(8,128)(2,1)S(1)} %get-tuple-element.48), channel_id=1, source_target_pairs={{0,0},{3,3},{1,2},{2,1},{4,4},{7,7},{5,6},{6,5},{8,8},{11,11},{9,1... | collective-permute-start | bytes 540680 | tf_op jit(solution)/shard_map/ppermute | solution.py:441
  15.0 9.1 %collective-permute-start.5 = (bf16[10,64,128]{2,1,0:T(8,128)(2,1)S(1)}, bf16[10,64,128]{2,1,0:T(8,128)(2,1)S(1)}, u32[]{:S(2)}, u32[]{:S(2)}) collective-permute-start(bf16[10,64,128]{2,1,0:T(8,128)(2,1)S(1)} %get-tuple-element.50), channel_id=1, source_target_pairs={{0,1},{1,0},{2,3},{3,2},{4,5},{5,4},{6,7},{7,6},{8,9},{9,8},{10,11... | collective-permute-start | bytes 491528 | tf_op jit(solution)/shard_map/ppermute | solution.py:442
  15.9 6.8 %collective-permute-start.4 = (bf16[5,64,128]{2,1,0:T(8,128)(2,1)S(1)}, bf16[5,64,128]{2,1,0:T(8,128)(2,1)S(1)}, u32[]{:S(2)}, u32[]{:S(2)}) collective-permute-start(bf16[5,64,128]{2,1,0:T(8,128)(2,1)S(1)} %get-tuple-element.49), channel_id=1, source_target_pairs={{0,4},{1,6},{2,5},{3,7},{4,0},{5,2},{6,1},{7,3},{8,12},{9,14},{10,... | collective-permute-start | bytes 245768 | tf_op jit(solution)/shard_map/ppermute | solution.py:448
  18.3 5.7 %collective-permute-start.6 = (bf16[5,64,128]{2,1,0:T(8,128)(2,1)S(1)}, bf16[5,64,128]{2,1,0:T(8,128)(2,1)S(1)}, u32[]{:S(2)}, u32[]{:S(2)}) collective-permute-start(bf16[5,64,128]{2,1,0:T(8,128)(2,1)S(1)} %get-tuple-element.51), channel_id=1, source_target_pairs={{0,0},{3,3},{1,2},{2,1},{4,4},{7,7},{5,6},{6,5},{8,8},{11,11},{9,1... | collective-permute-start | bytes 245768 | tf_op jit(solution)/shard_map/ppermute | solution.py:441
  26.2 6.3 %collective-permute-start.8 = (bf16[64,896]{1,0:T(8,128)(2,1)S(1)}, bf16[64,896]{1,0:T(8,128)(2,1)S(1)}, u32[]{:S(2)}, u32[]{:S(2)}) collective-permute-start(bf16[64,896]{1,0:T(8,128)(2,1)S(1)} %get-tuple-element.52.own), channel_id=1, source_target_pairs={{0,0},{124,124},{4,8},{8,4},{12,16},{16,12},{20,24},{24,20},{28,32... | collective-permute-start | bytes 344072 | tf_op jit(solution)/shard_map/ppermute | solution.py:441
  26.9 6.9 %collective-permute-start.7 = (bf16[64,896]{1,0:T(8,128)(2,1)S(1)}, bf16[64,896]{1,0:T(8,128)(2,1)S(1)}, u32[]{:S(2)}, u32[]{:S(2)}) collective-permute-start(bf16[64,896]{1,0:T(8,128)(2,1)S(1)} %get-tuple-element.52.own), channel_id=1, source_target_pairs={{0,4},{4,0},{8,12},{12,8},{16,20},{20,16},{24,28},{28,24},{32,36},... | collective-permute-start | bytes 344072 | tf_op jit(solution)/shard_map/ppermute | solution.py:442
  35.6 5.4 %collective-permute-start.9 = (bf16[64,640]{1,0:T(8,128)(2,1)S(1)}, bf16[64,640]{1,0:T(8,128)(2,1)S(1)}, u32[]{:S(2)}, u32[]{:S(2)}) collective-permute-start(bf16[64,640]{1,0:T(8,128)(2,1)S(1)} %get-tuple-element.61), channel_id=1, source_target_pairs={{0,4},{4,0},{8,12},{12,8},{16,20},{20,16},{24,28},{28,24},{32,36},... | collective-permute-start | bytes 245768 | tf_op jit(solution)/shard_map/ppermute | solution.py:442
  37.1 3.9 %collective-permute-start.10 = (bf16[64,640]{1,0:T(8,128)(2,1)S(1)}, bf16[64,640]{1,0:T(8,128)(2,1)S(1)}, u32[]{:S(2)}, u32[]{:S(2)}) collective-permute-start(bf16[64,640]{1,0:T(8,128)(2,1)S(1)} %get-tuple-element.62), channel_id=1, source_target_pairs={{0,0},{124,124},{4,8},{8,4},{12,16},{16,12},{20,24},{24,20},{28,32... | collective-permute-start | bytes 245768 | tf_op jit(solution)/shard_map/ppermute | solution.py:441
  39.1 1.3 %collective-permute-start.11 = (bf16[288,128]{1,0:T(8,128)(2,1)S(1)}, bf16[288,128]{1,0:T(8,128)(2,1)S(1)}, u32[]{:S(2)}, u32[]{:S(2)}) collective-permute-start(bf16[288,128]{1,0:T(8,128)(2,1)S(1)} %get-tuple-element.68), channel_id=1, source_target_pairs={{0,1},{1,0},{2,3},{3,2},{4,5},{5,4},{6,7},{7,6},{8,9},{9,8},{10,11... | collective-permute-start | bytes 221192 | tf_op jit(solution)/shard_map/ppermute | solution.py:537
  39.2 1.4 %collective-permute-start.12 = (bf16[288,128]{1,0:T(8,128)(2,1)S(1)}, bf16[288,128]{1,0:T(8,128)(2,1)S(1)}, u32[]{:S(2)}, u32[]{:S(2)}) collective-permute-start(bf16[288,128]{1,0:T(8,128)(2,1)S(1)} %get-tuple-element.69), channel_id=1, source_target_pairs={{0,1},{1,0},{2,3},{3,2},{4,5},{5,4},{6,7},{7,6},{8,9},{9,8},{10,11... | collective-permute-start | bytes 221192 | tf_op jit(solution)/shard_map/ppermute | solution.py:537
  39.7 1.3 %collective-permute-start.13 = (bf16[288,128]{1,0:T(8,128)(2,1)S(1)}, bf16[288,128]{1,0:T(8,128)(2,1)S(1)}, u32[]{:S(2)}, u32[]{:S(2)}) collective-permute-start(bf16[288,128]{1,0:T(8,128)(2,1)S(1)} %get-tuple-element.70), channel_id=1, source_target_pairs={{0,1},{1,0},{2,3},{3,2},{4,5},{5,4},{6,7},{7,6},{8,9},{9,8},{10,11... | collective-permute-start | bytes 221192 | tf_op jit(solution)/shard_map/ppermute | solution.py:537
  44.3 35.0 %all-to-all-start = ((bf16[128,16,128]{2,1,0:T(8,128)(2,1)}), bf16[128,16,128]{2,1,0:T(8,128)(2,1)S(1)}, u32[]{:S(2)}, u32[]{:S(2)}) async-start(bf16[128,16,128]{2,1,0:T(8,128)(2,1)} %get-tuple-element.76), calls=%async_computation | async-start | bytes 1048576 | tf_op jit(solution)/shard_map/all_to_all | solution.py:564
  65.7 19.3 %collective-permute-start.14 = (bf16[16,64,128]{2,1,0:T(8,128)(2,1)S(1)}, bf16[16,64,128]{2,1,0:T(8,128)(2,1)S(1)}, u32[]{:S(2)}, u32[]{:S(2)}) collective-permute-start(bf16[16,64,128]{2,1,0:T(8,128)(2,1)S(1)} %get-tuple-element.71.a.first), channel_id=1, source_target_pairs={{0,4},{4,0},{8,12},{12,8},{16,20},{20,16},{24,28},{28,24},{32,36},... | collective-permute-start | bytes 786440 | tf_op jit(solution)/shard_map/ppermute | solution.py:442
  67.3 17.7 %collective-permute-start.15 = (bf16[16,64,128]{2,1,0:T(8,128)(2,1)S(1)}, bf16[16,64,128]{2,1,0:T(8,128)(2,1)S(1)}, u32[]{:S(2)}, u32[]{:S(2)}) collective-permute-start(bf16[16,64,128]{2,1,0:T(8,128)(2,1)S(1)} %get-tuple-element.72.b.second), channel_id=1, source_target_pairs={{0,0},{124,124},{4,8},{8,4},{12,16},{16,12},{20,24},{24,20},{28,32... | collective-permute-start | bytes 786440 | tf_op jit(solution)/shard_map/ppermute | solution.py:441
  80.3 20.7 %all-to-all-start.1 = ((bf16[128,24,128]{2,1,0:T(8,128)(2,1)}), bf16[128,24,128]{2,1,0:T(8,128)(2,1)S(1)}, u32[]{:S(2)}, u32[]{:S(2)}) async-start(bf16[128,24,128]{2,1,0:T(8,128)(2,1)} %sum_shares.1), calls=%async_computation.1 | async-start | bytes 1572864 | tf_op jit(solution)/shard_map/all_to_all | solution.py:572
  85.6 3.8 %collective-permute-start.16 = (bf16[4,64,128]{2,1,0:T(8,128)(2,1)S(1)}, bf16[4,64,128]{2,1,0:T(8,128)(2,1)S(1)}, u32[]{:S(2)}, u32[]{:S(2)}) collective-permute-start(bf16[4,64,128]{2,1,0:T(8,128)(2,1)S(1)} %get-tuple-element.73), channel_id=1, source_target_pairs={{0,1},{1,0},{2,3},{3,2},{4,5},{5,4},{6,7},{7,6},{8,9},{9,8},{10,11... | collective-permute-start | bytes 196616 | tf_op jit(solution)/shard_map/ppermute | solution.py:442
  86.7 8.4 %collective-permute-start.17 = (bf16[4,64,128]{2,1,0:T(8,128)(2,1)S(1)}, bf16[4,64,128]{2,1,0:T(8,128)(2,1)S(1)}, u32[]{:S(2)}, u32[]{:S(2)}) collective-permute-start(bf16[4,64,128]{2,1,0:T(8,128)(2,1)S(1)} %get-tuple-element.74), channel_id=1, source_target_pairs={{0,0},{3,3},{1,2},{2,1},{4,4},{7,7},{5,6},{6,5},{8,8},{11,11},{9,1... | collective-permute-start | bytes 196616 | tf_op jit(solution)/shard_map/ppermute | solution.py:441
  (1 other events, 5.4 us)

commit v8 on v7

--- a/solution.py
+++ b/solution.py
@@ -284,6 +284,8 @@
     mine,
     u3,
     pack,
+    held,
+    sems,
 ):
     f = [flags[i] > 0 for i in range(6)]
     lane = iota((64, L), 1)
@@ -318,6 +320,21 @@
                 u3[256 + x * 64 : 320 + x * 64, at] = shifted(tile, 1, lane).astype(BF)
             first[n] = pick(f[4], rows[1], rows[0])
             second[n] = pick(f[4], rows[0], rows[1])
+    got = jnp.concatenate([got0[...], got1[...], got2[...]], axis=0)
+    coarse = kept[...].astype(F32) + got.astype(F32)
+    none = jnp.zeros((R, L), F32)
+    copies = []
+
+    def send(start, stop):
+        for n in range(start, stop):
+            at = slice(n * R, (n + 1) * R)
+            top = coarse[at] if n < HALF // R else none
+            low = pack[at, :] if n < 896 // R else none
+            held[n] = jnp.concatenate([top, low], axis=0).astype(BF)
+        part = pl.ds(start, stop - start)
+        copies.append(pltpu.make_async_copy(held.at[part], mine.at[part], sems.at[len(copies)]))
+        copies[-1].start()
+
     halves = []
     for j in range(3):
         res = dot(u3[...], vt[j * L : (j + 16) * L, :]) * scale
@@ -326,19 +343,15 @@
             at = (3 * j + k) * 64
             pack[at : at + 64, :] = both[:, :L]
             halves.append(both[:, L:])
+        send(24 * j, 24 * j + 24)
     halves.append(jnp.zeros((64, L), F32))
     lane = iota((64, L), 1)
     for n in range(5):
         packed = jnp.where(lane < 64, halves[2 * n], pltpu.roll(halves[2 * n + 1], 64, 1))
         pack[576 + 64 * n : 640 + 64 * n, :] = packed
-    got = jnp.concatenate([got0[...], got1[...], got2[...]], axis=0)
-    coarse = kept[...].astype(F32) + got.astype(F32)
-    none = jnp.zeros((R, L), F32)
-    for n in range(128):
-        at = slice(n * R, (n + 1) * R)
-        top = coarse[at] if n < HALF // R else none
-        low = pack[at, :] if n < 896 // R else none
-        mine[n] = jnp.concatenate([top, low], axis=0).astype(BF)
+    send(72, 128)
+    for copy in copies:
+        copy.wait()
 
 
 def gradient_edges_kernel(flags, a, b, c, d, first, second):
@@ -412,7 +425,7 @@
                 fine[2, at // 3, at % 3] = part[64 * h : 64 * h + 64]
 
 
-def call(kernel, name, outs, args, scratch=(), flags=True, macs=0, copies=0):
+def call(kernel, name, outs, args, scratch=(), flags=True, macs=0, copies=0, far=()):
     space = pl.ANY if copies else pltpu.VMEM
     specs = [pl.BlockSpec(memory_space=space) for _ in args]
     if flags:
@@ -425,7 +438,9 @@
         kernel,
         out_shape=shapes,
         in_specs=specs,
-        out_specs=tuple(pl.BlockSpec(memory_space=space) for _ in shapes),
+        out_specs=tuple(
+            pl.BlockSpec(memory_space=pl.ANY if n in far else space) for n in range(len(shapes))
+        ),
         scratch_shapes=list(scratch),
         compiler_params=pltpu.CompilerParams(vmem_limit_bytes=VMEM),
         cost_estimate=pl.CostEstimate(flops=2 * macs, bytes_accessed=moved, transcendentals=0),
@@ -557,7 +572,10 @@
         scratch=[
             pltpu.VMEM((384, 16 * L), BF),
             pltpu.VMEM((896, L), F32),
+            pltpu.VMEM((128, 2 * R, L), BF),
+            pltpu.SemaphoreType.DMA((4,)),
         ],
+        far=(2,),
         macs=384 * 768 * 16 * L,
     )
     ha, hb = swaps(first, second, "slab")

time: 103 us -> 103 us (level)
  no operation moved by 1% of the time
where the time goes in v8:
time: 103 us; the launch traced here: 102 us
  starting transfers between devices  56.5 us (55%)
  waiting for transfers between devices  23.7 us (23%)
  Pallas kernels  19.9 us (19%)
  local copies, waits for them, and re-layouts  1.3 us (1%)
    all_to_all x1, starting transfers between devices, on_device(): lax.all_to_all(mine.reshape(128 * 2 * R, L), ('slab', 'sub'), 0, 0, tiled...  21.4 us
    pallas_call x13, Pallas kernels, call(): pl.pallas_call(kernel, out_shape=shapes, in_specs=specs, out_specs=tuple(...  19.9 us
    ppermute x7, starting transfers between devices, swaps(): return (lax.ppermute(first, axis, pairs), other)  16.5 us
    all_to_all x1, waiting for transfers between devices, on_device(): lax.all_to_all(mine.reshape(128 * 2 * R, L), ('slab', 'sub'), 0, 0, tiled...  11.3 us
    ppermute x7, starting transfers between devices, swaps(): other = lax.ppermute(second, axis, others)  10.7 us
    ppermute x7, waiting for transfers between devices, swaps(): other = lax.ppermute(second, axis, others)  7.15 us
    all_to_all x1, starting transfers between devices, on_device(): lax.all_to_all(total.reshape(128 * 3 * R, L), ('slab', 'sub'), 0, 0, tile...  4.67 us
    all_to_all x1, waiting for transfers between devices, on_device(): lax.all_to_all(total.reshape(128 * 3 * R, L), ('slab', 'sub'), 0, 0, tile...  2.88 us
  transfers between devices with their start and end apart: 20, of which 8 were waited for; matrix products, arithmetic and copies ran while one was open for 0% of the time, Pallas kernels for 11%

profile of v8, /device:TPU:1, one launch (start us, length us, event | category | flops | bytes accessed | tf_op | source)
XLA Modules:
  0.0 102.4 jit_solution(13640591544162845494)
XLA Ops:
  2.6 5.4 %collective-permute-start = (bf16[16,64,128]{2,1,0:T(8,128)(2,1)S(1)}, bf16[16,64,128]{2,1,0:T(8,128)(2,1)S(1)}, u32[]{:S(2)}, u32[]{:S(2)}) collective-permute-start(bf16[16,64,128]{2,1,0:T(8,128)(2,1)S(1)} %get-tuple-element.80), channel_id=1, source_target_pairs={{0,4},{4,0},{8,12},{12,8},{16,20},{20,16},{24,28},{28,24},{32,36},... | collective-permute-start | bytes 786440 | tf_op jit(solution)/shard_map/ppermute | solution.py:457
  8.1 1.2 %own_edges.1 = (bf16[11,64,128]{2,1,0:T(8,128)(2,1)S(1)}, bf16[11,64,128]{2,1,0:T(8,128)(2,1)S(1)}, bf16[5,64,128]{2,1,0:T(8,128)(2,1)S(1)}) custom-call(s32[6]{0:T(128)S(1)} %convert_element_type.3.flags, bf16[2,16,64,128]{3,2,1,0:T(8,128)(2,1)S(1)} %copy-done, bf16[8,64,128]{2,1,0:T(8,128)(2,1)S(1)} %bitcast.13), custom_call_target="tpu_custom_call" | custom-call | bytes 655384 | tf_op jit(solution)/shard_map/own_edges/pallas_call | solution.py:437
  9.3 1.3 %collective-permute-start.2 = (bf16[11,64,128]{2,1,0:T(8,128)(2,1)S(1)}, bf16[11,64,128]{2,1,0:T(8,128)(2,1)S(1)}, u32[]{:S(2)}, u32[]{:S(2)}) collective-permute-start(bf16[11,64,128]{2,1,0:T(8,128)(2,1)S(1)} %get-tuple-element.47), channel_id=1, source_target_pairs={{0,1},{1,0},{2,3},{3,2},{4,5},{5,4},{6,7},{7,6},{8,9},{9,8},{10,11... | collective-permute-start | bytes 540680 | tf_op jit(solution)/shard_map/ppermute | solution.py:457
  10.6 3.1 %collective-permute-start.3 = (bf16[11,64,128]{2,1,0:T(8,128)(2,1)S(1)}, bf16[11,64,128]{2,1,0:T(8,128)(2,1)S(1)}, u32[]{:S(2)}, u32[]{:S(2)}) collective-permute-start(bf16[11,64,128]{2,1,0:T(8,128)(2,1)S(1)} %get-tuple-element.48), channel_id=1, source_target_pairs={{0,0},{3,3},{1,2},{2,1},{4,4},{7,7},{5,6},{6,5},{8,8},{11,11},{9,1... | collective-permute-start | bytes 540680 | tf_op jit(solution)/shard_map/ppermute | solution.py:456
  15.9 2.5 %collective-permute-start.4 = (bf16[5,64,128]{2,1,0:T(8,128)(2,1)S(1)}, bf16[5,64,128]{2,1,0:T(8,128)(2,1)S(1)}, u32[]{:S(2)}, u32[]{:S(2)}) collective-permute-start(bf16[5,64,128]{2,1,0:T(8,128)(2,1)S(1)} %get-tuple-element.49), channel_id=1, source_target_pairs={{0,4},{1,6},{2,5},{3,7},{4,0},{5,2},{6,1},{7,3},{8,12},{9,14},{10,... | collective-permute-start | bytes 245768 | tf_op jit(solution)/shard_map/ppermute | solution.py:463
  18.3 2.4 %collective-permute-start.6 = (bf16[5,64,128]{2,1,0:T(8,128)(2,1)S(1)}, bf16[5,64,128]{2,1,0:T(8,128)(2,1)S(1)}, u32[]{:S(2)}, u32[]{:S(2)}) collective-permute-start(bf16[5,64,128]{2,1,0:T(8,128)(2,1)S(1)} %get-tuple-element.51), channel_id=1, source_target_pairs={{0,0},{3,3},{1,2},{2,1},{4,4},{7,7},{5,6},{6,5},{8,8},{11,11},{9,1... | collective-permute-start | bytes 245768 | tf_op jit(solution)/shard_map/ppermute | solution.py:456
  20.7 2.0 %fine_forward_interior.1 = (bf16[256,2048]{1,0:T(8,128)(2,1)S(1)}, f32[128,1536]{1,0:T(8,128)S(1)}, bf16[64,768]{1,0:T(8,128)(2,1)S(1)}) custom-call(s32[6]{0:T(128)S(1)} %convert_element_type.3.flags, bf16[2,16,64,128]{3,2,1,0:T(8,128)(2,1)S(1)} %copy-done, bf16[16,64,128]{2,1,0:T(8,128)(2,1)S(1)} %collective-permute-done.xa, ...), custom_call_target="tpu_custom_call" | custom-call | flops 905969664 | bytes 1638424 | tf_op jit(solution)/shard_map/fine_forward_interior/pallas_call | solution.py:437
  22.8 1.3 %collective-permute-done.6.bb = bf16[5,64,128]{2,1,0:T(8,128)(2,1)S(1)} collective-permute-done((bf16[5,64,128]{2,1,0:T(8,128)(2,1)S(1)}, bf16[5,64,128]{2,1,0:T(8,128)(2,1)S(1)}, u32[]{:S(2)}, u32[]{:S(2)}) %collective-permute-start.6) | collective-permute-done | bytes 81952 | tf_op jit(solution)/shard_map/ppermute | solution.py:456
  24.1 2.1 %fine_forward_border.1 = (f32[128,256]{1,0:T(8,128)S(1)}, f32[128,256]{1,0:T(8,128)S(1)}, bf16[64,896]{1,0:T(8,128)(2,1)S(1)}, bf16[256,256]{1,0:T(8,128)(2,1)S(1)}) custom-call(s32[6]{0:T(128)S(1)} %convert_element_type.3.flags, bf16[256,2048]{1,0:T(8,128)(2,1)S(1)} %get-tuple-element.45.v2, bf16[64,768]{1,0:T(8,128)(2,1)S(1)} %get-tuple-element.46.mid, ...), custom_call_target="tpu_custom_call" | custom-call | flops 905969664 | bytes 2424856 | tf_op jit(solution)/shard_map/fine_forward_border/pallas_call | solution.py:437
  26.9 4.7 %collective-permute-start.7 = (bf16[64,896]{1,0:T(8,128)(2,1)S(1)}, bf16[64,896]{1,0:T(8,128)(2,1)S(1)}, u32[]{:S(2)}, u32[]{:S(2)}) collective-permute-start(bf16[64,896]{1,0:T(8,128)(2,1)S(1)} %get-tuple-element.52.own), channel_id=1, source_target_pairs={{0,4},{4,0},{8,12},{12,8},{16,20},{20,16},{24,28},{28,24},{32,36},... | collective-permute-start | bytes 344072 | tf_op jit(solution)/shard_map/ppermute | solution.py:457
  32.6 1.2 %collective-permute-done.7.a = bf16[64,896]{1,0:T(8,128)(2,1)S(1)} collective-permute-done((bf16[64,896]{1,0:T(8,128)(2,1)S(1)}, bf16[64,896]{1,0:T(8,128)(2,1)S(1)}, u32[]{:S(2)}, u32[]{:S(2)}) %collective-permute-start.7) | collective-permute-done | bytes 114720 | tf_op jit(solution)/shard_map/ppermute | solution.py:457
  33.8 1.8 %coarse_forward.1 = (bf16[192,896]{1,0:T(8,128)(2,1)S(1)}, bf16[128,896]{1,0:T(8,128)(2,1)S(1)}, bf16[64,640]{1,0:T(8,128)(2,1)S(1)}, bf16[64,640]{1,0:T(8,128)(2,1)S(1)}) custom-call(s32[6]{0:T(128)S(1)} %convert_element_type.3.flags, bf16[64,896]{1,0:T(8,128)(2,1)S(1)} %get-tuple-element.52.own, bf16[64,896]{1,0:T(8,128)(2,1)S(1)} %collective-permute-done.7.a, ...), custom_call_target="tpu_custom_call" | custom-call | flops 566231040 | bytes 1409048 | tf_op jit(solution)/shard_map/coarse_forward/pallas_call | solution.py:437
  35.6 1.5 %collective-permute-start.9 = (bf16[64,640]{1,0:T(8,128)(2,1)S(1)}, bf16[64,640]{1,0:T(8,128)(2,1)S(1)}, u32[]{:S(2)}, u32[]{:S(2)}) collective-permute-start(bf16[64,640]{1,0:T(8,128)(2,1)S(1)} %get-tuple-element.61), channel_id=1, source_target_pairs={{0,4},{4,0},{8,12},{12,8},{16,20},{20,16},{24,28},{28,24},{32,36},... | collective-permute-start | bytes 245768 | tf_op jit(solution)/shard_map/ppermute | solution.py:457
  37.8 1.4 %coarse_correlate.1 = (f32[64,640]{1,0:T(8,128)S(1)}, bf16[864,128]{1,0:T(8,128)(2,1)S(1)}, bf16[288,128]{1,0:T(8,128)(2,1)S(1)}, bf16[288,128]{1,0:T(8,128)(2,1)S(1)}, bf16[288,128]{1,0:T(8,128)(2,1)S(1)}) custom-call(s32[6]{0:T(128)S(1)} %convert_element_type.3.flags, bf16[192,896]{1,0:T(8,128)(2,1)S(1)} %get-tuple-element.57.p2, ...), custom_call_target="tpu_custom_call" | custom-call | flops 452984832 | bytes 720920 | tf_op jit(solution)/shard_map/coarse_correlate/pallas_call | solution.py:437
  41.0 3.2 %fine_gradient.1 = (bf16[16,64,128]{2,1,0:T(8,128)(2,1)S(1)}, bf16[16,64,128]{2,1,0:T(8,128)(2,1)S(1)}, bf16[128,16,128]{2,1,0:T(8,128)(2,1)}) custom-call(s32[6]{0:T(128)S(1)} %convert_element_type.3.flags, f32[64,640]{1,0:T(8,128)S(1)} %get-tuple-element.60.own, bf16[64,640]{1,0:T(8,128)(2,1)S(1)} %collective-permute-done.9.a, ...), custom_call_target="tpu_custom_call" | custom-call | flops 1207959552 | bytes 3522584 | tf_op jit(solution)/shard_map/fine_gradient/pallas_call | solution.py:437
  44.2 21.4 %all-to-all-start = ((bf16[128,16,128]{2,1,0:T(8,128)(2,1)}), bf16[128,16,128]{2,1,0:T(8,128)(2,1)S(1)}, u32[]{:S(2)}, u32[]{:S(2)}) async-start(bf16[128,16,128]{2,1,0:T(8,128)(2,1)} %get-tuple-element.76), calls=%async_computation | async-start | bytes 1048576 | tf_op jit(solution)/shard_map/all_to_all | solution.py:582
  65.7 1.6 %collective-permute-start.14 = (bf16[16,64,128]{2,1,0:T(8,128)(2,1)S(1)}, bf16[16,64,128]{2,1,0:T(8,128)(2,1)S(1)}, u32[]{:S(2)}, u32[]{:S(2)}) collective-permute-start(bf16[16,64,128]{2,1,0:T(8,128)(2,1)S(1)} %get-tuple-element.71.a.first), channel_id=1, source_target_pairs={{0,4},{4,0},{8,12},{12,8},{16,20},{20,16},{24,28},{28,24},{32,36},... | collective-permute-start | bytes 786440 | tf_op jit(solution)/shard_map/ppermute | solution.py:457
  67.9 11.3 %all-to-all-done.parts = bf16[128,16,128]{2,1,0:T(8,128)(2,1)S(1)} async-done(((bf16[128,16,128]{2,1,0:T(8,128)(2,1)}), bf16[128,16,128]{2,1,0:T(8,128)(2,1)S(1)}, u32[]{:S(2)}, u32[]{:S(2)}) %all-to-all-start) | async-done | bytes 524320 | tf_op jit(solution)/shard_map/all_to_all | solution.py:582
  80.3 4.7 %all-to-all-start.1 = ((bf16[128,24,128]{2,1,0:T(8,128)(2,1)}), bf16[128,24,128]{2,1,0:T(8,128)(2,1)S(1)}, u32[]{:S(2)}, u32[]{:S(2)}) async-start(bf16[128,24,128]{2,1,0:T(8,128)(2,1)} %sum_shares.1), calls=%async_computation.1 | async-start | bytes 1572864 | tf_op jit(solution)/shard_map/all_to_all | solution.py:590
  86.7 2.6 %collective-permute-start.17 = (bf16[4,64,128]{2,1,0:T(8,128)(2,1)S(1)}, bf16[4,64,128]{2,1,0:T(8,128)(2,1)S(1)}, u32[]{:S(2)}, u32[]{:S(2)}) collective-permute-start(bf16[4,64,128]{2,1,0:T(8,128)(2,1)S(1)} %get-tuple-element.74), channel_id=1, source_target_pairs={{0,0},{3,3},{1,2},{2,1},{4,4},{7,7},{5,6},{6,5},{8,8},{11,11},{9,1... | collective-permute-start | bytes 196616 | tf_op jit(solution)/shard_map/ppermute | solution.py:456
  89.3 5.8 %collective-permute-done.17.eb = bf16[4,64,128]{2,1,0:T(8,128)(2,1)S(1)} collective-permute-done((bf16[4,64,128]{2,1,0:T(8,128)(2,1)S(1)}, bf16[4,64,128]{2,1,0:T(8,128)(2,1)S(1)}, u32[]{:S(2)}, u32[]{:S(2)}) %collective-permute-start.17) | collective-permute-done | bytes 65568 | tf_op jit(solution)/shard_map/ppermute | solution.py:456
  95.1 3.0 %input_gradient.1 = bf16[2,16,64,128]{3,2,1,0:T(8,128)(2,1)} custom-call(s32[6]{0:T(128)S(1)} %convert_element_type.3.flags, bf16[16,64,128]{2,1,0:T(8,128)(2,1)S(1)} %get-tuple-element.71.a.first, bf16[16,64,128]{2,1,0:T(8,128)(2,1)S(1)} %get-tuple-element.72.b.second, bf16[16,64,128]{2,1,0:T(8,128)(2,1)S(1)} %collective-permute-done.14.c.a, ...), custom_call_target="tpu_custom_call" | custom-call | flops 1207959552 | bytes 1769496 | tf_op jit(solution)/shard_map/input_gradient/pallas_call | solution.py:437
  98.1 2.9 %all-to-all-done.1.got = bf16[128,24,128]{2,1,0:T(8,128)(2,1)S(1)} async-done(((bf16[128,24,128]{2,1,0:T(8,128)(2,1)}), bf16[128,24,128]{2,1,0:T(8,128)(2,1)S(1)}, u32[]{:S(2)}, u32[]{:S(2)}) %all-to-all-start.1) | async-done | bytes 786464 | tf_op jit(solution)/shard_map/all_to_all | solution.py:590
  101.0 1.4 %unpack.1 = (f32[3,3,3,64,64]{4,3,2,1,0:T(8,128)}, f32[3,3,3,64,128]{4,3,2,1,0:T(8,128)}) custom-call(bf16[128,24,128]{2,1,0:T(8,128)(2,1)S(1)} %all-to-all-done.1.got), custom_call_target="tpu_custom_call" | custom-call | bytes 786432 | tf_op jit(solution)/shard_map/unpack/pallas_call | solution.py:437
  (42 shorter events, 11.7 us)
Async XLA Ops:
  0.6 7.5 %copy-start = (bf16[2,16,64,128]{3,2,1,0:T(8,128)(2,1)S(1)}, bf16[2,16,64,128]{3,2,1,0:T(8,128)(2,1)}, u32[]{:S(2)}) copy-start(bf16[2,16,64,128]{3,2,1,0:T(8,128)(2,1)} %own.3) | copy-start | bytes 1572868
  0.6 7.4 %copy-start.1 = (bf16[1,8,128,64]{2,3,1,0:T(8,128)(2,1)S(1)}, bf16[1,8,128,64]{2,3,1,0:T(8,128)(2,1)}, u32[]{:S(2)}) copy-start(bf16[1,8,128,64]{2,3,1,0:T(8,128)(2,1)} %param.7) | copy-start | bytes 393220
  0.7 13.1 %copy-start.3 = (bf16[3,3,3,64,128]{4,3,2,1,0:T(8,128)(2,1)S(1)}, bf16[3,3,3,64,128]{4,3,2,1,0:T(8,128)(2,1)}, u32[]{:S(2)}) copy-start(bf16[3,3,3,64,128]{4,3,2,1,0:T(8,128)(2,1)} %wc.1) | copy-start | bytes 1327108
  0.7 13.1 %copy-start.2 = (bf16[3,3,3,64,64]{4,3,2,1,0:T(8,128)(2,1)S(1)}, bf16[3,3,3,64,64]{4,3,2,1,0:T(8,128)(2,1)}, u32[]{:S(2)}) copy-start(bf16[3,3,3,64,64]{4,3,2,1,0:T(8,128)(2,1)} %wf.1) | copy-start | bytes 663556
  1.9 12.5 %collective-permute-start.1 = (bf16[16,64,128]{2,1,0:T(8,128)(2,1)S(1)}, bf16[16,64,128]{2,1,0:T(8,128)(2,1)S(1)}, u32[]{:S(2)}, u32[]{:S(2)}) collective-permute-start(bf16[16,64,128]{2,1,0:T(8,128)(2,1)S(1)} %get-tuple-element.79), channel_id=1, source_target_pairs={{0,0},{124,124},{4,8},{8,4},{12,16},{16,12},{20,24},{24,20},{28,32... | collective-permute-start | bytes 786440 | tf_op jit(solution)/shard_map/ppermute | solution.py:456
  2.6 11.9 %collective-permute-start = (bf16[16,64,128]{2,1,0:T(8,128)(2,1)S(1)}, bf16[16,64,128]{2,1,0:T(8,128)(2,1)S(1)}, u32[]{:S(2)}, u32[]{:S(2)}) collective-permute-start(bf16[16,64,128]{2,1,0:T(8,128)(2,1)S(1)} %get-tuple-element.80), channel_id=1, source_target_pairs={{0,4},{4,0},{8,12},{12,8},{16,20},{20,16},{24,28},{28,24},{32,36},... | collective-permute-start | bytes 786440 | tf_op jit(solution)/shard_map/ppermute | solution.py:457
  9.3 13.4 %collective-permute-start.2 = (bf16[11,64,128]{2,1,0:T(8,128)(2,1)S(1)}, bf16[11,64,128]{2,1,0:T(8,128)(2,1)S(1)}, u32[]{:S(2)}, u32[]{:S(2)}) collective-permute-start(bf16[11,64,128]{2,1,0:T(8,128)(2,1)S(1)} %get-tuple-element.47), channel_id=1, source_target_pairs={{0,1},{1,0},{2,3},{3,2},{4,5},{5,4},{6,7},{7,6},{8,9},{9,8},{10,11... | collective-permute-start | bytes 540680 | tf_op jit(solution)/shard_map/ppermute | solution.py:457
  10.6 12.1 %collective-permute-start.3 = (bf16[11,64,128]{2,1,0:T(8,128)(2,1)S(1)}, bf16[11,64,128]{2,1,0:T(8,128)(2,1)S(1)}, u32[]{:S(2)}, u32[]{:S(2)}) collective-permute-start(bf16[11,64,128]{2,1,0:T(8,128)(2,1)S(1)} %get-tuple-element.48), channel_id=1, source_target_pairs={{0,0},{3,3},{1,2},{2,1},{4,4},{7,7},{5,6},{6,5},{8,8},{11,11},{9,1... | collective-permute-start | bytes 540680 | tf_op jit(solution)/shard_map/ppermute | solution.py:456
  15.0 9.1 %collective-permute-start.5 = (bf16[10,64,128]{2,1,0:T(8,128)(2,1)S(1)}, bf16[10,64,128]{2,1,0:T(8,128)(2,1)S(1)}, u32[]{:S(2)}, u32[]{:S(2)}) collective-permute-start(bf16[10,64,128]{2,1,0:T(8,128)(2,1)S(1)} %get-tuple-element.50), channel_id=1, source_target_pairs={{0,1},{1,0},{2,3},{3,2},{4,5},{5,4},{6,7},{7,6},{8,9},{9,8},{10,11... | collective-permute-start | bytes 491528 | tf_op jit(solution)/shard_map/ppermute | solution.py:457
  15.9 6.8 %collective-permute-start.4 = (bf16[5,64,128]{2,1,0:T(8,128)(2,1)S(1)}, bf16[5,64,128]{2,1,0:T(8,128)(2,1)S(1)}, u32[]{:S(2)}, u32[]{:S(2)}) collective-permute-start(bf16[5,64,128]{2,1,0:T(8,128)(2,1)S(1)} %get-tuple-element.49), channel_id=1, source_target_pairs={{0,4},{1,6},{2,5},{3,7},{4,0},{5,2},{6,1},{7,3},{8,12},{9,14},{10,... | collective-permute-start | bytes 245768 | tf_op jit(solution)/shard_map/ppermute | solution.py:463
  18.3 5.7 %collective-permute-start.6 = (bf16[5,64,128]{2,1,0:T(8,128)(2,1)S(1)}, bf16[5,64,128]{2,1,0:T(8,128)(2,1)S(1)}, u32[]{:S(2)}, u32[]{:S(2)}) collective-permute-start(bf16[5,64,128]{2,1,0:T(8,128)(2,1)S(1)} %get-tuple-element.51), channel_id=1, source_target_pairs={{0,0},{3,3},{1,2},{2,1},{4,4},{7,7},{5,6},{6,5},{8,8},{11,11},{9,1... | collective-permute-start | bytes 245768 | tf_op jit(solution)/shard_map/ppermute | solution.py:456
  26.2 6.3 %collective-permute-start.8 = (bf16[64,896]{1,0:T(8,128)(2,1)S(1)}, bf16[64,896]{1,0:T(8,128)(2,1)S(1)}, u32[]{:S(2)}, u32[]{:S(2)}) collective-permute-start(bf16[64,896]{1,0:T(8,128)(2,1)S(1)} %get-tuple-element.52.own), channel_id=1, source_target_pairs={{0,0},{124,124},{4,8},{8,4},{12,16},{16,12},{20,24},{24,20},{28,32... | collective-permute-start | bytes 344072 | tf_op jit(solution)/shard_map/ppermute | solution.py:456
  26.9 6.9 %collective-permute-start.7 = (bf16[64,896]{1,0:T(8,128)(2,1)S(1)}, bf16[64,896]{1,0:T(8,128)(2,1)S(1)}, u32[]{:S(2)}, u32[]{:S(2)}) collective-permute-start(bf16[64,896]{1,0:T(8,128)(2,1)S(1)} %get-tuple-element.52.own), channel_id=1, source_target_pairs={{0,4},{4,0},{8,12},{12,8},{16,20},{20,16},{24,28},{28,24},{32,36},... | collective-permute-start | bytes 344072 | tf_op jit(solution)/shard_map/ppermute | solution.py:457
  35.6 5.4 %collective-permute-start.9 = (bf16[64,640]{1,0:T(8,128)(2,1)S(1)}, bf16[64,640]{1,0:T(8,128)(2,1)S(1)}, u32[]{:S(2)}, u32[]{:S(2)}) collective-permute-start(bf16[64,640]{1,0:T(8,128)(2,1)S(1)} %get-tuple-element.61), channel_id=1, source_target_pairs={{0,4},{4,0},{8,12},{12,8},{16,20},{20,16},{24,28},{28,24},{32,36},... | collective-permute-start | bytes 245768 | tf_op jit(solution)/shard_map/ppermute | solution.py:457
  37.1 3.9 %collective-permute-start.10 = (bf16[64,640]{1,0:T(8,128)(2,1)S(1)}, bf16[64,640]{1,0:T(8,128)(2,1)S(1)}, u32[]{:S(2)}, u32[]{:S(2)}) collective-permute-start(bf16[64,640]{1,0:T(8,128)(2,1)S(1)} %get-tuple-element.62), channel_id=1, source_target_pairs={{0,0},{124,124},{4,8},{8,4},{12,16},{16,12},{20,24},{24,20},{28,32... | collective-permute-start | bytes 245768 | tf_op jit(solution)/shard_map/ppermute | solution.py:456
  39.1 1.3 %collective-permute-start.11 = (bf16[288,128]{1,0:T(8,128)(2,1)S(1)}, bf16[288,128]{1,0:T(8,128)(2,1)S(1)}, u32[]{:S(2)}, u32[]{:S(2)}) collective-permute-start(bf16[288,128]{1,0:T(8,128)(2,1)S(1)} %get-tuple-element.68), channel_id=1, source_target_pairs={{0,1},{1,0},{2,3},{3,2},{4,5},{5,4},{6,7},{7,6},{8,9},{9,8},{10,11... | collective-permute-start | bytes 221192 | tf_op jit(solution)/shard_map/ppermute | solution.py:552
  39.2 1.4 %collective-permute-start.12 = (bf16[288,128]{1,0:T(8,128)(2,1)S(1)}, bf16[288,128]{1,0:T(8,128)(2,1)S(1)}, u32[]{:S(2)}, u32[]{:S(2)}) collective-permute-start(bf16[288,128]{1,0:T(8,128)(2,1)S(1)} %get-tuple-element.69), channel_id=1, source_target_pairs={{0,1},{1,0},{2,3},{3,2},{4,5},{5,4},{6,7},{7,6},{8,9},{9,8},{10,11... | collective-permute-start | bytes 221192 | tf_op jit(solution)/shard_map/ppermute | solution.py:552
  39.7 1.3 %collective-permute-start.13 = (bf16[288,128]{1,0:T(8,128)(2,1)S(1)}, bf16[288,128]{1,0:T(8,128)(2,1)S(1)}, u32[]{:S(2)}, u32[]{:S(2)}) collective-permute-start(bf16[288,128]{1,0:T(8,128)(2,1)S(1)} %get-tuple-element.70), channel_id=1, source_target_pairs={{0,1},{1,0},{2,3},{3,2},{4,5},{5,4},{6,7},{7,6},{8,9},{9,8},{10,11... | collective-permute-start | bytes 221192 | tf_op jit(solution)/shard_map/ppermute | solution.py:552
  44.2 35.0 %all-to-all-start = ((bf16[128,16,128]{2,1,0:T(8,128)(2,1)}), bf16[128,16,128]{2,1,0:T(8,128)(2,1)S(1)}, u32[]{:S(2)}, u32[]{:S(2)}) async-start(bf16[128,16,128]{2,1,0:T(8,128)(2,1)} %get-tuple-element.76), calls=%async_computation | async-start | bytes 1048576 | tf_op jit(solution)/shard_map/all_to_all | solution.py:582
  65.7 19.3 %collective-permute-start.14 = (bf16[16,64,128]{2,1,0:T(8,128)(2,1)S(1)}, bf16[16,64,128]{2,1,0:T(8,128)(2,1)S(1)}, u32[]{:S(2)}, u32[]{:S(2)}) collective-permute-start(bf16[16,64,128]{2,1,0:T(8,128)(2,1)S(1)} %get-tuple-element.71.a.first), channel_id=1, source_target_pairs={{0,4},{4,0},{8,12},{12,8},{16,20},{20,16},{24,28},{28,24},{32,36},... | collective-permute-start | bytes 786440 | tf_op jit(solution)/shard_map/ppermute | solution.py:457
  67.3 17.7 %collective-permute-start.15 = (bf16[16,64,128]{2,1,0:T(8,128)(2,1)S(1)}, bf16[16,64,128]{2,1,0:T(8,128)(2,1)S(1)}, u32[]{:S(2)}, u32[]{:S(2)}) collective-permute-start(bf16[16,64,128]{2,1,0:T(8,128)(2,1)S(1)} %get-tuple-element.72.b.second), channel_id=1, source_target_pairs={{0,0},{124,124},{4,8},{8,4},{12,16},{16,12},{20,24},{24,20},{28,32... | collective-permute-start | bytes 786440 | tf_op jit(solution)/shard_map/ppermute | solution.py:456
  80.3 20.7 %all-to-all-start.1 = ((bf16[128,24,128]{2,1,0:T(8,128)(2,1)}), bf16[128,24,128]{2,1,0:T(8,128)(2,1)S(1)}, u32[]{:S(2)}, u32[]{:S(2)}) async-start(bf16[128,24,128]{2,1,0:T(8,128)(2,1)} %sum_shares.1), calls=%async_computation.1 | async-start | bytes 1572864 | tf_op jit(solution)/shard_map/all_to_all | solution.py:590
  85.5 3.8 %collective-permute-start.16 = (bf16[4,64,128]{2,1,0:T(8,128)(2,1)S(1)}, bf16[4,64,128]{2,1,0:T(8,128)(2,1)S(1)}, u32[]{:S(2)}, u32[]{:S(2)}) collective-permute-start(bf16[4,64,128]{2,1,0:T(8,128)(2,1)S(1)} %get-tuple-element.73), channel_id=1, source_target_pairs={{0,1},{1,0},{2,3},{3,2},{4,5},{5,4},{6,7},{7,6},{8,9},{9,8},{10,11... | collective-permute-start | bytes 196616 | tf_op jit(solution)/shard_map/ppermute | solution.py:457
  86.7 8.4 %collective-permute-start.17 = (bf16[4,64,128]{2,1,0:T(8,128)(2,1)S(1)}, bf16[4,64,128]{2,1,0:T(8,128)(2,1)S(1)}, u32[]{:S(2)}, u32[]{:S(2)}) collective-permute-start(bf16[4,64,128]{2,1,0:T(8,128)(2,1)S(1)} %get-tuple-element.74), channel_id=1, source_target_pairs={{0,0},{3,3},{1,2},{2,1},{4,4},{7,7},{5,6},{6,5},{8,8},{11,11},{9,1... | collective-permute-start | bytes 196616 | tf_op jit(solution)/shard_map/ppermute | solution.py:456
  (1 other events, 5.4 us)

commit v9 on v7

--- a/solution.py
+++ b/solution.py
@@ -384,35 +384,45 @@
         out[n] = total
 
 
-def unpack_kernel(got, fine, coarse):
+def unpack_kernel(got, fine, coarse, fine_v, coarse_v, sems):
+    copies = []
+
+    def send(held, out, i):
+        copies.append(pltpu.make_async_copy(held.at[i], out.at[i], sems.at[len(copies)]))
+        copies[-1].start()
+
     def coarse_rows(q):
         half, at = q // (HALF // R), q % (HALF // R)
         return got[at].astype(F32)[half * R : (half + 1) * R]
 
-    for j in range(3):
-        for k in range(3):
-            for i in range(3):
-                q = ((3 * j + k) * 192 + i * 64) // R
-                rows = [coarse_rows(q + m) for m in range(64 // R)]
-                coarse[i, j, k] = jnp.concatenate(rows, axis=0)
-
     def tile(n):
         rows = [got[m].astype(F32)[2 * R :] for m in range(n * 64 // R, (n + 1) * 64 // R)]
         return jnp.concatenate(rows, axis=0).T
 
     for n in range(9):
         part = tile(n)
-        fine[0, n // 3, n % 3] = part[:64]
-        fine[1, n // 3, n % 3] = part[64:]
+        fine_v[0, n // 3, n % 3] = part[:64]
+        fine_v[1, n // 3, n % 3] = part[64:]
+    send(fine_v, fine, 0)
+    send(fine_v, fine, 1)
     for n in range(5):
         part = tile(9 + n)
         for h in range(2):
             at = 2 * n + h
             if at < 9:
-                fine[2, at // 3, at % 3] = part[64 * h : 64 * h + 64]
-
-
-def call(kernel, name, outs, args, scratch=(), flags=True, macs=0, copies=0):
+                fine_v[2, at // 3, at % 3] = part[64 * h : 64 * h + 64]
+    send(fine_v, fine, 2)
+    for i in range(3):
+        for n in range(9):
+            q = (n * 192 + i * 64) // R
+            rows = [coarse_rows(q + m) for m in range(64 // R)]
+            coarse_v[i, n // 3, n % 3] = jnp.concatenate(rows, axis=0)
+        send(coarse_v, coarse, i)
+    for copy in copies:
+        copy.wait()
+
+
+def call(kernel, name, outs, args, scratch=(), flags=True, macs=0, copies=0, far=()):
     space = pl.ANY if copies else pltpu.VMEM
     specs = [pl.BlockSpec(memory_space=space) for _ in args]
     if flags:
@@ -425,7 +435,9 @@
         kernel,
         out_shape=shapes,
         in_specs=specs,
-        out_specs=tuple(pl.BlockSpec(memory_space=space) for _ in shapes),
+        out_specs=tuple(
+            pl.BlockSpec(memory_space=pl.ANY if n in far else space) for n in range(len(shapes))
+        ),
         scratch_shapes=list(scratch),
         compiler_params=pltpu.CompilerParams(vmem_limit_bytes=VMEM),
         cost_estimate=pl.CostEstimate(flops=2 * macs, bytes_accessed=moved, transcendentals=0),
@@ -591,7 +603,13 @@
         "unpack",
         (((3, 3, 3, 64, 64), F32), ((3, 3, 3, 64, 128), F32)),
         (everything.reshape(128, 3 * R, L),),
+        scratch=[
+            pltpu.VMEM((3, 3, 3, 64, 64), F32),
+            pltpu.VMEM((3, 3, 3, 64, 128), F32),
+            pltpu.SemaphoreType.DMA((6,)),
+        ],
         flags=False,
+        far=(0, 1),
     )
     return (grad_input, grad_fine, grad_coarse)
 

time: 103 us -> 103 us (level)
  no operation moved by 1% of the time
where the time goes in v9:
time: 103 us
  starting transfers between devices  56.5 us (55%)
  waiting for transfers between devices  23.7 us (23%)
  Pallas kernels  20 us (19%)
  local copies, waits for them, and re-layouts  1.3 us (1%)
  between operations  1.1 us (1%)
    all_to_all x1, starting transfers between devices, on_device(): lax.all_to_all(mine.reshape(128 * 2 * R, L), ('slab', 'sub'), 0, 0, tiled...  21.4 us
    pallas_call x13, Pallas kernels, call(): pl.pallas_call(kernel, out_shape=shapes, in_specs=specs, out_specs=tuple(...  20 us
    ppermute x7, starting transfers between devices, swaps(): return (lax.ppermute(first, axis, pairs), other)  16.5 us
    all_to_all x1, waiting for transfers between devices, on_device(): lax.all_to_all(mine.reshape(128 * 2 * R, L), ('slab', 'sub'), 0, 0, tiled...  11.3 us
    ppermute x7, starting transfers between devices, swaps(): other = lax.ppermute(second, axis, others)  10.7 us
    ppermute x7, waiting for transfers between devices, swaps(): other = lax.ppermute(second, axis, others)  7.15 us
    all_to_all x1, starting transfers between devices, on_device(): lax.all_to_all(total.reshape(128 * 3 * R, L), ('slab', 'sub'), 0, 0, tile...  4.67 us
    all_to_all x1, waiting for transfers between devices, on_device(): lax.all_to_all(total.reshape(128 * 3 * R, L), ('slab', 'sub'), 0, 0, tile...  2.88 us
  transfers between devices with their start and end apart: 20, of which 8 were waited for; matrix products, arithmetic and copies ran while one was open for 0% of the time, Pallas kernels for 11%

profile of v9, /device:TPU:1, one launch (start us, length us, event | category | flops | bytes accessed | tf_op | source)
XLA Modules:
  0.0 102.6 jit_solution(10467066015563103665)
XLA Ops:
  2.6 5.4 %collective-permute-start = (bf16[16,64,128]{2,1,0:T(8,128)(2,1)S(1)}, bf16[16,64,128]{2,1,0:T(8,128)(2,1)S(1)}, u32[]{:S(2)}, u32[]{:S(2)}) collective-permute-start(bf16[16,64,128]{2,1,0:T(8,128)(2,1)S(1)} %get-tuple-element.80), channel_id=1, source_target_pairs={{0,4},{4,0},{8,12},{12,8},{16,20},{20,16},{24,28},{28,24},{32,36},... | collective-permute-start | bytes 786440 | tf_op jit(solution)/shard_map/ppermute | solution.py:454
  8.1 1.2 %own_edges.1 = (bf16[11,64,128]{2,1,0:T(8,128)(2,1)S(1)}, bf16[11,64,128]{2,1,0:T(8,128)(2,1)S(1)}, bf16[5,64,128]{2,1,0:T(8,128)(2,1)S(1)}) custom-call(s32[6]{0:T(128)S(1)} %convert_element_type.3.flags, bf16[2,16,64,128]{3,2,1,0:T(8,128)(2,1)S(1)} %copy-done, bf16[8,64,128]{2,1,0:T(8,128)(2,1)S(1)} %bitcast.13), custom_call_target="tpu_custom_call" | custom-call | bytes 655384 | tf_op jit(solution)/shard_map/own_edges/pallas_call | solution.py:434
  9.3 1.3 %collective-permute-start.2 = (bf16[11,64,128]{2,1,0:T(8,128)(2,1)S(1)}, bf16[11,64,128]{2,1,0:T(8,128)(2,1)S(1)}, u32[]{:S(2)}, u32[]{:S(2)}) collective-permute-start(bf16[11,64,128]{2,1,0:T(8,128)(2,1)S(1)} %get-tuple-element.47), channel_id=1, source_target_pairs={{0,1},{1,0},{2,3},{3,2},{4,5},{5,4},{6,7},{7,6},{8,9},{9,8},{10,11... | collective-permute-start | bytes 540680 | tf_op jit(solution)/shard_map/ppermute | solution.py:454
  10.6 3.1 %collective-permute-start.3 = (bf16[11,64,128]{2,1,0:T(8,128)(2,1)S(1)}, bf16[11,64,128]{2,1,0:T(8,128)(2,1)S(1)}, u32[]{:S(2)}, u32[]{:S(2)}) collective-permute-start(bf16[11,64,128]{2,1,0:T(8,128)(2,1)S(1)} %get-tuple-element.48), channel_id=1, source_target_pairs={{0,0},{3,3},{1,2},{2,1},{4,4},{7,7},{5,6},{6,5},{8,8},{11,11},{9,1... | collective-permute-start | bytes 540680 | tf_op jit(solution)/shard_map/ppermute | solution.py:453
  15.9 2.5 %collective-permute-start.4 = (bf16[5,64,128]{2,1,0:T(8,128)(2,1)S(1)}, bf16[5,64,128]{2,1,0:T(8,128)(2,1)S(1)}, u32[]{:S(2)}, u32[]{:S(2)}) collective-permute-start(bf16[5,64,128]{2,1,0:T(8,128)(2,1)S(1)} %get-tuple-element.49), channel_id=1, source_target_pairs={{0,4},{1,6},{2,5},{3,7},{4,0},{5,2},{6,1},{7,3},{8,12},{9,14},{10,... | collective-permute-start | bytes 245768 | tf_op jit(solution)/shard_map/ppermute | solution.py:460
  18.3 2.4 %collective-permute-start.6 = (bf16[5,64,128]{2,1,0:T(8,128)(2,1)S(1)}, bf16[5,64,128]{2,1,0:T(8,128)(2,1)S(1)}, u32[]{:S(2)}, u32[]{:S(2)}) collective-permute-start(bf16[5,64,128]{2,1,0:T(8,128)(2,1)S(1)} %get-tuple-element.51), channel_id=1, source_target_pairs={{0,0},{3,3},{1,2},{2,1},{4,4},{7,7},{5,6},{6,5},{8,8},{11,11},{9,1... | collective-permute-start | bytes 245768 | tf_op jit(solution)/shard_map/ppermute | solution.py:453
  20.7 2.0 %fine_forward_interior.1 = (bf16[256,2048]{1,0:T(8,128)(2,1)S(1)}, f32[128,1536]{1,0:T(8,128)S(1)}, bf16[64,768]{1,0:T(8,128)(2,1)S(1)}) custom-call(s32[6]{0:T(128)S(1)} %convert_element_type.3.flags, bf16[2,16,64,128]{3,2,1,0:T(8,128)(2,1)S(1)} %copy-done, bf16[16,64,128]{2,1,0:T(8,128)(2,1)S(1)} %collective-permute-done.xa, ...), custom_call_target="tpu_custom_call" | custom-call | flops 905969664 | bytes 1638424 | tf_op jit(solution)/shard_map/fine_forward_interior/pallas_call | solution.py:434
  22.8 1.3 %collective-permute-done.6.bb = bf16[5,64,128]{2,1,0:T(8,128)(2,1)S(1)} collective-permute-done((bf16[5,64,128]{2,1,0:T(8,128)(2,1)S(1)}, bf16[5,64,128]{2,1,0:T(8,128)(2,1)S(1)}, u32[]{:S(2)}, u32[]{:S(2)}) %collective-permute-start.6) | collective-permute-done | bytes 81952 | tf_op jit(solution)/shard_map/ppermute | solution.py:453
  24.1 2.1 %fine_forward_border.1 = (f32[128,256]{1,0:T(8,128)S(1)}, f32[128,256]{1,0:T(8,128)S(1)}, bf16[64,896]{1,0:T(8,128)(2,1)S(1)}, bf16[256,256]{1,0:T(8,128)(2,1)S(1)}) custom-call(s32[6]{0:T(128)S(1)} %convert_element_type.3.flags, bf16[256,2048]{1,0:T(8,128)(2,1)S(1)} %get-tuple-element.45.v2, bf16[64,768]{1,0:T(8,128)(2,1)S(1)} %get-tuple-element.46.mid, ...), custom_call_target="tpu_custom_call" | custom-call | flops 905969664 | bytes 2424856 | tf_op jit(solution)/shard_map/fine_forward_border/pallas_call | solution.py:434
  26.9 4.7 %collective-permute-start.7 = (bf16[64,896]{1,0:T(8,128)(2,1)S(1)}, bf16[64,896]{1,0:T(8,128)(2,1)S(1)}, u32[]{:S(2)}, u32[]{:S(2)}) collective-permute-start(bf16[64,896]{1,0:T(8,128)(2,1)S(1)} %get-tuple-element.52.own), channel_id=1, source_target_pairs={{0,4},{4,0},{8,12},{12,8},{16,20},{20,16},{24,28},{28,24},{32,36},... | collective-permute-start | bytes 344072 | tf_op jit(solution)/shard_map/ppermute | solution.py:454
  32.6 1.2 %collective-permute-done.7.a = bf16[64,896]{1,0:T(8,128)(2,1)S(1)} collective-permute-done((bf16[64,896]{1,0:T(8,128)(2,1)S(1)}, bf16[64,896]{1,0:T(8,128)(2,1)S(1)}, u32[]{:S(2)}, u32[]{:S(2)}) %collective-permute-start.7) | collective-permute-done | bytes 114720 | tf_op jit(solution)/shard_map/ppermute | solution.py:454
  33.8 1.8 %coarse_forward.1 = (bf16[192,896]{1,0:T(8,128)(2,1)S(1)}, bf16[128,896]{1,0:T(8,128)(2,1)S(1)}, bf16[64,640]{1,0:T(8,128)(2,1)S(1)}, bf16[64,640]{1,0:T(8,128)(2,1)S(1)}) custom-call(s32[6]{0:T(128)S(1)} %convert_element_type.3.flags, bf16[64,896]{1,0:T(8,128)(2,1)S(1)} %get-tuple-element.52.own, bf16[64,896]{1,0:T(8,128)(2,1)S(1)} %collective-permute-done.7.a, ...), custom_call_target="tpu_custom_call" | custom-call | flops 566231040 | bytes 1409048 | tf_op jit(solution)/shard_map/coarse_forward/pallas_call | solution.py:434
  35.6 1.5 %collective-permute-start.9 = (bf16[64,640]{1,0:T(8,128)(2,1)S(1)}, bf16[64,640]{1,0:T(8,128)(2,1)S(1)}, u32[]{:S(2)}, u32[]{:S(2)}) collective-permute-start(bf16[64,640]{1,0:T(8,128)(2,1)S(1)} %get-tuple-element.61), channel_id=1, source_target_pairs={{0,4},{4,0},{8,12},{12,8},{16,20},{20,16},{24,28},{28,24},{32,36},... | collective-permute-start | bytes 245768 | tf_op jit(solution)/shard_map/ppermute | solution.py:454
  37.8 1.4 %coarse_correlate.1 = (f32[64,640]{1,0:T(8,128)S(1)}, bf16[864,128]{1,0:T(8,128)(2,1)S(1)}, bf16[288,128]{1,0:T(8,128)(2,1)S(1)}, bf16[288,128]{1,0:T(8,128)(2,1)S(1)}, bf16[288,128]{1,0:T(8,128)(2,1)S(1)}) custom-call(s32[6]{0:T(128)S(1)} %convert_element_type.3.flags, bf16[192,896]{1,0:T(8,128)(2,1)S(1)} %get-tuple-element.57.p2, ...), custom_call_target="tpu_custom_call" | custom-call | flops 452984832 | bytes 720920 | tf_op jit(solution)/shard_map/coarse_correlate/pallas_call | solution.py:434
  41.0 3.3 %fine_gradient.1 = (bf16[16,64,128]{2,1,0:T(8,128)(2,1)S(1)}, bf16[16,64,128]{2,1,0:T(8,128)(2,1)S(1)}, bf16[128,16,128]{2,1,0:T(8,128)(2,1)}) custom-call(s32[6]{0:T(128)S(1)} %convert_element_type.3.flags, f32[64,640]{1,0:T(8,128)S(1)} %get-tuple-element.60.own, bf16[64,640]{1,0:T(8,128)(2,1)S(1)} %collective-permute-done.9.a, ...), custom_call_target="tpu_custom_call" | custom-call | flops 1207959552 | bytes 3522584 | tf_op jit(solution)/shard_map/fine_gradient/pallas_call | solution.py:434
  44.3 21.4 %all-to-all-start = ((bf16[128,16,128]{2,1,0:T(8,128)(2,1)}), bf16[128,16,128]{2,1,0:T(8,128)(2,1)S(1)}, u32[]{:S(2)}, u32[]{:S(2)}) async-start(bf16[128,16,128]{2,1,0:T(8,128)(2,1)} %get-tuple-element.76), calls=%async_computation | async-start | bytes 1048576 | tf_op jit(solution)/shard_map/all_to_all | solution.py:576
  65.7 1.6 %collective-permute-start.14 = (bf16[16,64,128]{2,1,0:T(8,128)(2,1)S(1)}, bf16[16,64,128]{2,1,0:T(8,128)(2,1)S(1)}, u32[]{:S(2)}, u32[]{:S(2)}) collective-permute-start(bf16[16,64,128]{2,1,0:T(8,128)(2,1)S(1)} %get-tuple-element.71.a.first), channel_id=1, source_target_pairs={{0,4},{4,0},{8,12},{12,8},{16,20},{20,16},{24,28},{28,24},{32,36},... | collective-permute-start | bytes 786440 | tf_op jit(solution)/shard_map/ppermute | solution.py:454
  68.0 11.3 %all-to-all-done.parts = bf16[128,16,128]{2,1,0:T(8,128)(2,1)S(1)} async-done(((bf16[128,16,128]{2,1,0:T(8,128)(2,1)}), bf16[128,16,128]{2,1,0:T(8,128)(2,1)S(1)}, u32[]{:S(2)}, u32[]{:S(2)}) %all-to-all-start) | async-done | bytes 524320 | tf_op jit(solution)/shard_map/all_to_all | solution.py:576
  80.3 4.7 %all-to-all-start.1 = ((bf16[128,24,128]{2,1,0:T(8,128)(2,1)}), bf16[128,24,128]{2,1,0:T(8,128)(2,1)S(1)}, u32[]{:S(2)}, u32[]{:S(2)}) async-start(bf16[128,24,128]{2,1,0:T(8,128)(2,1)} %sum_shares.1), calls=%async_computation.1 | async-start | bytes 1572864 | tf_op jit(solution)/shard_map/all_to_all | solution.py:584
  86.7 2.6 %collective-permute-start.17 = (bf16[4,64,128]{2,1,0:T(8,128)(2,1)S(1)}, bf16[4,64,128]{2,1,0:T(8,128)(2,1)S(1)}, u32[]{:S(2)}, u32[]{:S(2)}) collective-permute-start(bf16[4,64,128]{2,1,0:T(8,128)(2,1)S(1)} %get-tuple-element.74), channel_id=1, source_target_pairs={{0,0},{3,3},{1,2},{2,1},{4,4},{7,7},{5,6},{6,5},{8,8},{11,11},{9,1... | collective-permute-start | bytes 196616 | tf_op jit(solution)/shard_map/ppermute | solution.py:453
  89.4 5.8 %collective-permute-done.17.eb = bf16[4,64,128]{2,1,0:T(8,128)(2,1)S(1)} collective-permute-done((bf16[4,64,128]{2,1,0:T(8,128)(2,1)S(1)}, bf16[4,64,128]{2,1,0:T(8,128)(2,1)S(1)}, u32[]{:S(2)}, u32[]{:S(2)}) %collective-permute-start.17) | collective-permute-done | bytes 65568 | tf_op jit(solution)/shard_map/ppermute | solution.py:453
  95.2 3.0 %input_gradient.1 = bf16[2,16,64,128]{3,2,1,0:T(8,128)(2,1)} custom-call(s32[6]{0:T(128)S(1)} %convert_element_type.3.flags, bf16[16,64,128]{2,1,0:T(8,128)(2,1)S(1)} %get-tuple-element.71.a.first, bf16[16,64,128]{2,1,0:T(8,128)(2,1)S(1)} %get-tuple-element.72.b.second, bf16[16,64,128]{2,1,0:T(8,128)(2,1)S(1)} %collective-permute-done.14.c.a, ...), custom_call_target="tpu_custom_call" | custom-call | flops 1207959552 | bytes 1769496 | tf_op jit(solution)/shard_map/input_gradient/pallas_call | solution.py:434
  98.1 2.9 %all-to-all-done.1.got = bf16[128,24,128]{2,1,0:T(8,128)(2,1)S(1)} async-done(((bf16[128,24,128]{2,1,0:T(8,128)(2,1)}), bf16[128,24,128]{2,1,0:T(8,128)(2,1)S(1)}, u32[]{:S(2)}, u32[]{:S(2)}) %all-to-all-start.1) | async-done | bytes 786464 | tf_op jit(solution)/shard_map/all_to_all | solution.py:584
  101.0 1.4 %unpack.1 = (f32[3,3,3,64,64]{4,3,2,1,0:T(8,128)}, f32[3,3,3,64,128]{4,3,2,1,0:T(8,128)}) custom-call(bf16[128,24,128]{2,1,0:T(8,128)(2,1)S(1)} %all-to-all-done.1.got), custom_call_target="tpu_custom_call" | custom-call | bytes 786432 | tf_op jit(solution)/shard_map/unpack/pallas_call | solution.py:434
  (42 shorter events, 11.7 us)
Async XLA Ops:
  0.6 7.5 %copy-start = (bf16[2,16,64,128]{3,2,1,0:T(8,128)(2,1)S(1)}, bf16[2,16,64,128]{3,2,1,0:T(8,128)(2,1)}, u32[]{:S(2)}) copy-start(bf16[2,16,64,128]{3,2,1,0:T(8,128)(2,1)} %own.3) | copy-start | bytes 1572868
  0.6 7.4 %copy-start.1 = (bf16[1,8,128,64]{2,3,1,0:T(8,128)(2,1)S(1)}, bf16[1,8,128,64]{2,3,1,0:T(8,128)(2,1)}, u32[]{:S(2)}) copy-start(bf16[1,8,128,64]{2,3,1,0:T(8,128)(2,1)} %param.7) | copy-start | bytes 393220
  0.7 13.1 %copy-start.3 = (bf16[3,3,3,64,128]{4,3,2,1,0:T(8,128)(2,1)S(1)}, bf16[3,3,3,64,128]{4,3,2,1,0:T(8,128)(2,1)}, u32[]{:S(2)}) copy-start(bf16[3,3,3,64,128]{4,3,2,1,0:T(8,128)(2,1)} %wc.1) | copy-start | bytes 1327108
  0.7 13.1 %copy-start.2 = (bf16[3,3,3,64,64]{4,3,2,1,0:T(8,128)(2,1)S(1)}, bf16[3,3,3,64,64]{4,3,2,1,0:T(8,128)(2,1)}, u32[]{:S(2)}) copy-start(bf16[3,3,3,64,64]{4,3,2,1,0:T(8,128)(2,1)} %wf.1) | copy-start | bytes 663556
  1.9 12.5 %collective-permute-start.1 = (bf16[16,64,128]{2,1,0:T(8,128)(2,1)S(1)}, bf16[16,64,128]{2,1,0:T(8,128)(2,1)S(1)}, u32[]{:S(2)}, u32[]{:S(2)}) collective-permute-start(bf16[16,64,128]{2,1,0:T(8,128)(2,1)S(1)} %get-tuple-element.79), channel_id=1, source_target_pairs={{0,0},{124,124},{4,8},{8,4},{12,16},{16,12},{20,24},{24,20},{28,32... | collective-permute-start | bytes 786440 | tf_op jit(solution)/shard_map/ppermute | solution.py:453
  2.6 11.9 %collective-permute-start = (bf16[16,64,128]{2,1,0:T(8,128)(2,1)S(1)}, bf16[16,64,128]{2,1,0:T(8,128)(2,1)S(1)}, u32[]{:S(2)}, u32[]{:S(2)}) collective-permute-start(bf16[16,64,128]{2,1,0:T(8,128)(2,1)S(1)} %get-tuple-element.80), channel_id=1, source_target_pairs={{0,4},{4,0},{8,12},{12,8},{16,20},{20,16},{24,28},{28,24},{32,36},... | collective-permute-start | bytes 786440 | tf_op jit(solution)/shard_map/ppermute | solution.py:454
  9.3 13.4 %collective-permute-start.2 = (bf16[11,64,128]{2,1,0:T(8,128)(2,1)S(1)}, bf16[11,64,128]{2,1,0:T(8,128)(2,1)S(1)}, u32[]{:S(2)}, u32[]{:S(2)}) collective-permute-start(bf16[11,64,128]{2,1,0:T(8,128)(2,1)S(1)} %get-tuple-element.47), channel_id=1, source_target_pairs={{0,1},{1,0},{2,3},{3,2},{4,5},{5,4},{6,7},{7,6},{8,9},{9,8},{10,11... | collective-permute-start | bytes 540680 | tf_op jit(solution)/shard_map/ppermute | solution.py:454
  10.6 12.1 %collective-permute-start.3 = (bf16[11,64,128]{2,1,0:T(8,128)(2,1)S(1)}, bf16[11,64,128]{2,1,0:T(8,128)(2,1)S(1)}, u32[]{:S(2)}, u32[]{:S(2)}) collective-permute-start(bf16[11,64,128]{2,1,0:T(8,128)(2,1)S(1)} %get-tuple-element.48), channel_id=1, source_target_pairs={{0,0},{3,3},{1,2},{2,1},{4,4},{7,7},{5,6},{6,5},{8,8},{11,11},{9,1... | collective-permute-start | bytes 540680 | tf_op jit(solution)/shard_map/ppermute | solution.py:453
  15.0 9.1 %collective-permute-start.5 = (bf16[10,64,128]{2,1,0:T(8,128)(2,1)S(1)}, bf16[10,64,128]{2,1,0:T(8,128)(2,1)S(1)}, u32[]{:S(2)}, u32[]{:S(2)}) collective-permute-start(bf16[10,64,128]{2,1,0:T(8,128)(2,1)S(1)} %get-tuple-element.50), channel_id=1, source_target_pairs={{0,1},{1,0},{2,3},{3,2},{4,5},{5,4},{6,7},{7,6},{8,9},{9,8},{10,11... | collective-permute-start | bytes 491528 | tf_op jit(solution)/shard_map/ppermute | solution.py:454
  15.9 6.8 %collective-permute-start.4 = (bf16[5,64,128]{2,1,0:T(8,128)(2,1)S(1)}, bf16[5,64,128]{2,1,0:T(8,128)(2,1)S(1)}, u32[]{:S(2)}, u32[]{:S(2)}) collective-permute-start(bf16[5,64,128]{2,1,0:T(8,128)(2,1)S(1)} %get-tuple-element.49), channel_id=1, source_target_pairs={{0,4},{1,6},{2,5},{3,7},{4,0},{5,2},{6,1},{7,3},{8,12},{9,14},{10,... | collective-permute-start | bytes 245768 | tf_op jit(solution)/shard_map/ppermute | solution.py:460
  18.3 5.7 %collective-permute-start.6 = (bf16[5,64,128]{2,1,0:T(8,128)(2,1)S(1)}, bf16[5,64,128]{2,1,0:T(8,128)(2,1)S(1)}, u32[]{:S(2)}, u32[]{:S(2)}) collective-permute-start(bf16[5,64,128]{2,1,0:T(8,128)(2,1)S(1)} %get-tuple-element.51), channel_id=1, source_target_pairs={{0,0},{3,3},{1,2},{2,1},{4,4},{7,7},{5,6},{6,5},{8,8},{11,11},{9,1... | collective-permute-start | bytes 245768 | tf_op jit(solution)/shard_map/ppermute | solution.py:453
  26.2 6.3 %collective-permute-start.8 = (bf16[64,896]{1,0:T(8,128)(2,1)S(1)}, bf16[64,896]{1,0:T(8,128)(2,1)S(1)}, u32[]{:S(2)}, u32[]{:S(2)}) collective-permute-start(bf16[64,896]{1,0:T(8,128)(2,1)S(1)} %get-tuple-element.52.own), channel_id=1, source_target_pairs={{0,0},{124,124},{4,8},{8,4},{12,16},{16,12},{20,24},{24,20},{28,32... | collective-permute-start | bytes 344072 | tf_op jit(solution)/shard_map/ppermute | solution.py:453
  26.9 6.9 %collective-permute-start.7 = (bf16[64,896]{1,0:T(8,128)(2,1)S(1)}, bf16[64,896]{1,0:T(8,128)(2,1)S(1)}, u32[]{:S(2)}, u32[]{:S(2)}) collective-permute-start(bf16[64,896]{1,0:T(8,128)(2,1)S(1)} %get-tuple-element.52.own), channel_id=1, source_target_pairs={{0,4},{4,0},{8,12},{12,8},{16,20},{20,16},{24,28},{28,24},{32,36},... | collective-permute-start | bytes 344072 | tf_op jit(solution)/shard_map/ppermute | solution.py:454
  35.6 5.4 %collective-permute-start.9 = (bf16[64,640]{1,0:T(8,128)(2,1)S(1)}, bf16[64,640]{1,0:T(8,128)(2,1)S(1)}, u32[]{:S(2)}, u32[]{:S(2)}) collective-permute-start(bf16[64,640]{1,0:T(8,128)(2,1)S(1)} %get-tuple-element.61), channel_id=1, source_target_pairs={{0,4},{4,0},{8,12},{12,8},{16,20},{20,16},{24,28},{28,24},{32,36},... | collective-permute-start | bytes 245768 | tf_op jit(solution)/shard_map/ppermute | solution.py:454
  37.1 3.9 %collective-permute-start.10 = (bf16[64,640]{1,0:T(8,128)(2,1)S(1)}, bf16[64,640]{1,0:T(8,128)(2,1)S(1)}, u32[]{:S(2)}, u32[]{:S(2)}) collective-permute-start(bf16[64,640]{1,0:T(8,128)(2,1)S(1)} %get-tuple-element.62), channel_id=1, source_target_pairs={{0,0},{124,124},{4,8},{8,4},{12,16},{16,12},{20,24},{24,20},{28,32... | collective-permute-start | bytes 245768 | tf_op jit(solution)/shard_map/ppermute | solution.py:453
  39.1 1.3 %collective-permute-start.11 = (bf16[288,128]{1,0:T(8,128)(2,1)S(1)}, bf16[288,128]{1,0:T(8,128)(2,1)S(1)}, u32[]{:S(2)}, u32[]{:S(2)}) collective-permute-start(bf16[288,128]{1,0:T(8,128)(2,1)S(1)} %get-tuple-element.68), channel_id=1, source_target_pairs={{0,1},{1,0},{2,3},{3,2},{4,5},{5,4},{6,7},{7,6},{8,9},{9,8},{10,11... | collective-permute-start | bytes 221192 | tf_op jit(solution)/shard_map/ppermute | solution.py:549
  39.2 1.4 %collective-permute-start.12 = (bf16[288,128]{1,0:T(8,128)(2,1)S(1)}, bf16[288,128]{1,0:T(8,128)(2,1)S(1)}, u32[]{:S(2)}, u32[]{:S(2)}) collective-permute-start(bf16[288,128]{1,0:T(8,128)(2,1)S(1)} %get-tuple-element.69), channel_id=1, source_target_pairs={{0,1},{1,0},{2,3},{3,2},{4,5},{5,4},{6,7},{7,6},{8,9},{9,8},{10,11... | collective-permute-start | bytes 221192 | tf_op jit(solution)/shard_map/ppermute | solution.py:549
  39.7 1.3 %collective-permute-start.13 = (bf16[288,128]{1,0:T(8,128)(2,1)S(1)}, bf16[288,128]{1,0:T(8,128)(2,1)S(1)}, u32[]{:S(2)}, u32[]{:S(2)}) collective-permute-start(bf16[288,128]{1,0:T(8,128)(2,1)S(1)} %get-tuple-element.70), channel_id=1, source_target_pairs={{0,1},{1,0},{2,3},{3,2},{4,5},{5,4},{6,7},{7,6},{8,9},{9,8},{10,11... | collective-permute-start | bytes 221192 | tf_op jit(solution)/shard_map/ppermute | solution.py:549
  44.3 35.0 %all-to-all-start = ((bf16[128,16,128]{2,1,0:T(8,128)(2,1)}), bf16[128,16,128]{2,1,0:T(8,128)(2,1)S(1)}, u32[]{:S(2)}, u32[]{:S(2)}) async-start(bf16[128,16,128]{2,1,0:T(8,128)(2,1)} %get-tuple-element.76), calls=%async_computation | async-start | bytes 1048576 | tf_op jit(solution)/shard_map/all_to_all | solution.py:576
  65.7 19.3 %collective-permute-start.14 = (bf16[16,64,128]{2,1,0:T(8,128)(2,1)S(1)}, bf16[16,64,128]{2,1,0:T(8,128)(2,1)S(1)}, u32[]{:S(2)}, u32[]{:S(2)}) collective-permute-start(bf16[16,64,128]{2,1,0:T(8,128)(2,1)S(1)} %get-tuple-element.71.a.first), channel_id=1, source_target_pairs={{0,4},{4,0},{8,12},{12,8},{16,20},{20,16},{24,28},{28,24},{32,36},... | collective-permute-start | bytes 786440 | tf_op jit(solution)/shard_map/ppermute | solution.py:454
  67.3 17.7 %collective-permute-start.15 = (bf16[16,64,128]{2,1,0:T(8,128)(2,1)S(1)}, bf16[16,64,128]{2,1,0:T(8,128)(2,1)S(1)}, u32[]{:S(2)}, u32[]{:S(2)}) collective-permute-start(bf16[16,64,128]{2,1,0:T(8,128)(2,1)S(1)} %get-tuple-element.72.b.second), channel_id=1, source_target_pairs={{0,0},{124,124},{4,8},{8,4},{12,16},{16,12},{20,24},{24,20},{28,32... | collective-permute-start | bytes 786440 | tf_op jit(solution)/shard_map/ppermute | solution.py:453
  80.3 20.7 %all-to-all-start.1 = ((bf16[128,24,128]{2,1,0:T(8,128)(2,1)}), bf16[128,24,128]{2,1,0:T(8,128)(2,1)S(1)}, u32[]{:S(2)}, u32[]{:S(2)}) async-start(bf16[128,24,128]{2,1,0:T(8,128)(2,1)} %sum_shares.1), calls=%async_computation.1 | async-start | bytes 1572864 | tf_op jit(solution)/shard_map/all_to_all | solution.py:584
  85.6 3.8 %collective-permute-start.16 = (bf16[4,64,128]{2,1,0:T(8,128)(2,1)S(1)}, bf16[4,64,128]{2,1,0:T(8,128)(2,1)S(1)}, u32[]{:S(2)}, u32[]{:S(2)}) collective-permute-start(bf16[4,64,128]{2,1,0:T(8,128)(2,1)S(1)} %get-tuple-element.73), channel_id=1, source_target_pairs={{0,1},{1,0},{2,3},{3,2},{4,5},{5,4},{6,7},{7,6},{8,9},{9,8},{10,11... | collective-permute-start | bytes 196616 | tf_op jit(solution)/shard_map/ppermute | solution.py:454
  86.7 8.4 %collective-permute-start.17 = (bf16[4,64,128]{2,1,0:T(8,128)(2,1)S(1)}, bf16[4,64,128]{2,1,0:T(8,128)(2,1)S(1)}, u32[]{:S(2)}, u32[]{:S(2)}) collective-permute-start(bf16[4,64,128]{2,1,0:T(8,128)(2,1)S(1)} %get-tuple-element.74), channel_id=1, source_target_pairs={{0,0},{3,3},{1,2},{2,1},{4,4},{7,7},{5,6},{6,5},{8,8},{11,11},{9,1... | collective-permute-start | bytes 196616 | tf_op jit(solution)/shard_map/ppermute | solution.py:453
  (1 other events, 5.4 us)
